TPU v7x, 32 devices: a whole 2x2x4 slice. The times are simulated.
32 devices in a mesh: segment: 4 (over y, core), ctx: 8 (over z, x).
Axes of the slice: x: 2, y: 2, z: 4, core: 2. Of those that a mesh axis runs over, the one named last changes fastest.
Arguments:
- queries: bfloat16 [128, 8192], P(('segment', 'ctx')), may hold values from -9 to 9
- cache: bfloat16 [65536, 2048], P(('segment', 'ctx')), may hold values from -9 to 9
- out_weight: bfloat16 [32768, 8192], P('segment', 'ctx'), may hold values from -2 to 2
- offsets: int32 [4], P('segment'), may hold values from 5461 to 16352, as said below
- starts: int32 [4], P('segment'), may hold values from 0 to 7261, as said below
Outputs:
- advanced: bfloat16 [128, 8192], P('segment', 'ctx')
Inputs may be any that keep to these rules, and one draw needn't show every extreme that they name: `offsets`: each section's slice ends inside its cache; some section's slice ends at its last cache position. A section's document starts no later than its first query; some section's document starts at 0.
All inputs are finite; a program needn't handle non-finite values.
Results may differ from a plain program's by a relative error of at most 0.0054.
Values may be sent and summed in bfloat16 or wider, within the bound.
No kernel may reach another device: no remote copies, remote signals or barrier semaphores. Data moves between devices by JAX's collectives and lax.ppermute only.
A program may use at most 192 MiB of HBM per device.

v0:
```python
import jax
import jax.numpy as jnp
from jax import lax
from jax.sharding import PartitionSpec as P

H = 64
KVH = 8
HD = 128


def from_behind(value, axis, by):
    devices = lax.axis_size(axis)
    return lax.ppermute(value, axis, [(i, (i + by) % devices) for i in range(devices)])


def block_state(gathered, cache, offset, doc_start, first_position):
    rows = gathered.shape[0]
    span = cache.shape[0]
    group = H // KVH
    positions = first_position + jnp.arange(span, dtype=jnp.int32)
    query_pos = offset + jnp.arange(rows, dtype=jnp.int32)
    visible = ((positions[None, :] >= doc_start) & (positions[None, :] <= query_pos[:, None]))[
        :, None, :
    ]
    score_scale = HD ** (-0.5)

    def per_group(group_index, carry):
        maxima, sums, outputs = carry
        query_part = lax.dynamic_slice_in_dim(
            gathered, group_index * group * HD, group * HD, 1
        ).reshape(rows * group, HD)
        key_part = lax.dynamic_slice_in_dim(cache, group_index * HD, HD, 1)
        value_part = lax.dynamic_slice_in_dim(cache, (KVH + group_index) * HD, HD, 1)
        scores = lax.dot_general(
            query_part, key_part, (((1,), (1,)), ((), ())), preferred_element_type=jnp.float32
        )
        scores = scores.reshape(rows, group, span) * score_scale
        masked = jnp.where(visible, scores, -1e30)
        row_max = jnp.max(masked, axis=-1)
        weights = jnp.where(visible, jnp.exp(masked - row_max[..., None]), 0.0)
        weight_sum = jnp.sum(weights, axis=-1)
        numerator = jnp.dot(
            weights.astype(jnp.bfloat16).reshape(rows * group, span),
            value_part,
            preferred_element_type=jnp.float32,
        )
        normalized = numerator.reshape(rows, group, HD) / jnp.maximum(weight_sum, 1.0)[..., None]
        head_start = group_index * group
        maxima = lax.dynamic_update_slice_in_dim(maxima, row_max, head_start, 1)
        sums = lax.dynamic_update_slice_in_dim(sums, weight_sum, head_start, 1)
        outputs = lax.dynamic_update_slice_in_dim(outputs, normalized, head_start, 1)
        return (maxima, sums, outputs)

    initial = (
        jnp.zeros((rows, H), jnp.float32),
        jnp.zeros((rows, H), jnp.float32),
        jnp.zeros((rows, H, HD), jnp.float32),
    )
    return lax.fori_loop(0, KVH, per_group, initial)


def tile_state(gathered, tile, offset, doc_start, first_position):
    rows = gathered.shape[0]
    span = tile.shape[0]
    hidden_tile = (first_position + span - 1 < doc_start) | (first_position > offset + rows - 1)

    def skipped(unused):
        return (
            jnp.full((rows, H), -1e30, jnp.float32),
            jnp.zeros((rows, H), jnp.float32),
            jnp.zeros((rows, H, HD), jnp.float32),
        )

    def computed(unused):
        return block_state(gathered, tile, offset, doc_start, first_position)

    return lax.cond(hidden_tile, skipped, computed, 0)


def combine_parts(first, second):
    max_first, sum_first, out_first = first
    max_second, sum_second, out_second = second
    joint = jnp.maximum(max_first, max_second)
    factor_first = sum_first * jnp.exp(max_first - joint)
    factor_second = sum_second * jnp.exp(max_second - joint)
    total = factor_first + factor_second
    mixed = (
        factor_first[..., None] * out_first + factor_second[..., None] * out_second
    ) / jnp.maximum(total, 1.0)[..., None]
    return (joint, total, mixed)


def settle(parts):
    maxima_all, sums_all, outs_all = parts
    blocks, rows, heads_here = maxima_all.shape
    overall = jnp.max(maxima_all, axis=0)
    factors = sums_all * jnp.exp(maxima_all - overall[None])
    head_outs = outs_all.reshape(blocks, rows, heads_here, HD)
    merged = jnp.sum(factors[..., None] * head_outs, axis=0) / jnp.sum(factors, axis=0)[..., None]
    return merged.reshape(rows, heads_here * HD).astype(jnp.bfloat16)


def per_device(queries, cache, out_weight, offsets, starts):
    offset = offsets[0]
    doc_start = starts[0]
    gathered = lax.all_gather(queries, "ctx", axis=0, tiled=True)
    span = cache.shape[0]
    half = span // 2
    position = lax.axis_index("ctx")
    own_state = tile_state(gathered, cache[:half], offset, doc_start, position * span)
    other_state = tile_state(gathered, cache[half:], offset, doc_start, position * span + half)
    maxima, sums, outputs = combine_parts(own_state, other_state)
    rows = gathered.shape[0]
    local_heads = settle(
        (
            lax.all_to_all(maxima[None], "ctx", split_axis=2, concat_axis=0, tiled=True),
            lax.all_to_all(sums[None], "ctx", split_axis=2, concat_axis=0, tiled=True),
            lax.all_to_all(
                outputs.reshape(1, rows, H * HD), "ctx", split_axis=2, concat_axis=0, tiled=True
            ),
        )
    )
    projected = jnp.dot(
        lax.all_gather(local_heads, "ctx", axis=1, tiled=True),
        out_weight,
        preferred_element_type=jnp.float32,
    )
    return from_behind(projected.astype(jnp.bfloat16), "segment", 1)


def solution(mesh):
    in_specs = (
        P(("segment", "ctx"), None),
        P(("segment", "ctx"), None),
        P("segment", "ctx"),
        P("segment"),
        P("segment"),
    )
    out_specs = P("segment", "ctx")
    return jax.shard_map(
        per_device, mesh=mesh, in_specs=in_specs, out_specs=out_specs, check_vma=False
    )
```

profile of v0, /device:TPU:0, one launch (start us, length us, event | category | flops | bytes accessed | tf_op | source)
XLA Modules:
  0.0 271.6 jit_solution(14714719832399195303)
XLA Ops:
  1.3 33.2 %all-gather = bf16[8,4,8192]{2,1,0:T(4,128)(2,1)S(1)} all-gather(bf16[1,4,8192]{2,1,0:T(4,128)(2,1)} %bitcast.101), channel_id=1, replica_groups=mesh['segment'=4,'ctx'=8] {'ctx'}, dimensions={0}, use_global_device_ids=true | all-gather | bytes 589824 | tf_op jit(solution)/shard_map/all_gather | solution.py:106
  34.7 38.3 %conditional.3 = (f32[32,64]{1,0:T(8,128)S(1)}, f32[32,64]{1,0:T(8,128)S(1)}, f32[32,64,128]{2,1,0:T(8,128)S(1)}) conditional(s32[]{:T(128)} %convert_element_type.33, (bf16[2048,2048]{1,0:T(8,128)(2,1)}, s32[]{:T(128)}, s32[]{:T(128)}, s32[]{:T(128)}, bf16[32,8192]{1,0:T(8,128)(2,1)S(1)}) %tuple.67, () %tuple.68), branch_computations={%region_6.11_spmd, %region_11.12_spmd} | conditional | flops 136678176 | bytes 13766469 | solution.py:77
  34.7 4.7 %slice.7 = bf16[1024,2048]{1,0:T(8,128)(2,1)} slice(bf16[2048,2048]{1,0:T(8,128)(2,1)} %get-tuple-element.389), slice={[1024:2048], [0:2048]} | slice | bytes 8388608 | tf_op jit(solution)/shard_map/slice | solution.py:111
  40.9 32.1 %while.39 = (s32[]{:T(128)}, f32[32,64]{1,0:T(8,128)S(1)}, f32[32,64]{1,0:T(8,128)S(1)}, f32[32,64,128]{2,1,0:T(8,128)S(1)}, bf16[32,8192]{1,0:T(8,128)(2,1)S(1)...) while((s32[]{:T(128)}, f32[32,64]{1,0:T(8,128)S(1)}, ...), condition=%wide.region_10.10_spmd.clone, body=%wide.region_7.9_spmd.clone.sunk | while | flops 136675072 | bytes 4307457 | solution.py:59
  41.0 1.4 fusion.58
  44.9 1.4 fusion.58
  47.4 1.3 fusion.60
  48.9 1.4 fusion.58
  51.4 1.3 fusion.60
  52.9 1.4 fusion.58
  55.4 1.3 fusion.60
  57.0 1.4 fusion.58
  59.5 1.3 fusion.60
  61.0 1.4 fusion.58
  63.5 1.3 fusion.60
  65.0 1.4 fusion.58
  67.5 1.3 fusion.60
  69.1 1.4 fusion.58
  71.6 1.3 fusion.60
  72.9 45.1 %conditional.2 = (f32[32,64]{1,0:T(8,128)S(1)}, f32[32,64]{1,0:T(8,128)S(1)}, f32[32,64,128]{2,1,0:T(8,128)S(1)}) conditional(s32[]{:T(128)} %convert_element_type.32, (bf16[2048,2048]{1,0:T(8,128)(2,1)}, s32[]{:T(128)}, s32[]{:T(128)}, s32[]{:T(128)}, bf16[32,8192]{1,0:T(8,128)(2,1)S(1)}) %tuple.65, () %tuple.66), branch_computations={%region_0.5_spmd, %region_5.6_spmd} | conditional | flops 136678176 | bytes 15863649 | solution.py:77
  73.0 4.9 %slice.6 = bf16[1024,2048]{1,0:T(8,128)(2,1)} slice(bf16[2048,2048]{1,0:T(8,128)(2,1)} %get-tuple-element.373), slice={[0:1024], [0:2048]} | slice | bytes 8388608 | tf_op jit(solution)/shard_map/slice | solution.py:110
  79.3 38.7 %while.38 = (s32[]{:T(128)}, f32[32,64]{1,0:T(8,128)S(1)}, f32[32,64]{1,0:T(8,128)S(1)}, f32[32,64,128]{2,1,0:T(8,128)S(1)}, bf16[32,8192]{1,0:T(8,128)(2,1)}, /...) while((s32[]{:T(128)}, f32[32,64]{1,0:T(8,128)S(1)}, ...), condition=%wide.region_4.4_spmd.clone, body=%wide.region_1.3_spmd.clone.sunk | while | flops 136675072 | bytes 4307457 | solution.py:59
  80.3 1.4 fusion.64
  85.0 1.4 fusion.64
  87.5 1.3 fusion.66
  89.8 1.4 fusion.64
  94.7 1.4 fusion.64
  97.2 1.3 fusion.66
  99.6 1.4 fusion.64
  104.4 1.4 fusion.64
  106.9 1.3 fusion.66
  109.3 1.4 fusion.64
  111.8 1.3 fusion.66
  114.2 1.4 fusion.64
  120.1 5.7 %all-to-all-start = ((f32[8,1,256]{2,1,0:T(1,128)}), f32[8,1,256]{2,1,0:T(1,128)S(1)}, u32[]{:S(2)}, u32[]{:S(2)}) async-start(f32[8,1,256]{2,1,0:T(1,128)} %reshape.238), calls=%async_computation | async-start | bytes 16384 | tf_op jit(solution)/shard_map/all_to_all | solution.py:117
  127.2 5.0 %all-to-all-done = f32[8,1,256]{2,1,0:T(1,128)S(1)} async-done(((f32[8,1,256]{2,1,0:T(1,128)}), f32[8,1,256]{2,1,0:T(1,128)S(1)}, u32[]{:S(2)}, u32[]{:S(2)}) %all-to-all-start) | async-done | bytes 8224 | tf_op jit(solution)/shard_map/all_to_all | solution.py:117
  132.2 3.3 %all-to-all-start.1 = ((f32[8,1,256]{2,1,0:T(1,128)}), f32[8,1,256]{2,1,0:T(1,128)S(1)}, u32[]{:S(2)}, u32[]{:S(2)}) async-start(f32[8,1,256]{2,1,0:T(1,128)} %reshape.240), calls=%async_computation.1 | async-start | bytes 16384 | tf_op jit(solution)/shard_map/all_to_all | solution.py:116
  136.5 2.7 copy.42
  139.2 38.3 %reduce.2 = f32[8192,32]{1,0:T(8,128)} reduce(f32[8192,1,32]{2,1,0:T(1,128)} %bitcast.93, f32[]{:T(128)} %broadcast.228), dimensions={1}, to_apply=%bitcast.51.reduce_sub_computation | reduce | bytes 2097156
  177.5 4.8 %reshape.236 = f32[8,1,32768]{2,1,0:T(1,128)} reshape(f32[8192,32]{1,0:T(8,128)} %reduce.2) | data formatting | bytes 2097152
  182.4 5.9 %all-to-all-start.2 = ((f32[8,1,32768]{2,1,0:T(1,128)}), f32[8,1,32768]{2,1,0:T(1,128)S(1)}, u32[]{:S(2)}, u32[]{:S(2)}) async-start(f32[8,1,32768]{2,1,0:T(1,128)} %reshape.236), calls=%async_computation.2 | async-start | bytes 2097152 | tf_op jit(solution)/shard_map/all_to_all | solution.py:118
  189.9 14.8 %all-to-all-done.2 = f32[8,1,32768]{2,1,0:T(1,128)S(1)} async-done(((f32[8,1,32768]{2,1,0:T(1,128)}), f32[8,1,32768]{2,1,0:T(1,128)S(1)}, u32[]{:S(2)}, u32[]{:S(2)}) %all-to-all-start.2) | async-done | bytes 1048608 | tf_op jit(solution)/shard_map/all_to_all | solution.py:118
  204.7 3.1 %reduce.3 = f32[8,32768]{1,0:T(8,128)S(1)} reduce(f32[8,1,32768]{2,1,0:T(1,128)S(1)} %all-to-all-done.2, f32[]{:T(128)} %broadcast.228), dimensions={1}, to_apply=%all_to_all.45.reduce_sub_computation | reduce | bytes 2097156 | tf_op jit(solution)/shard_map/all_to_all | solution.py:118
  207.8 8.7 %reshape.237 = f32[8192,1,32]{2,1,0:T(1,128)} reshape(f32[8,32768]{1,0:T(8,128)S(1)} %reduce.3) | data formatting | bytes 2097152
  216.5 2.7 fusion.34
  219.3 39.0 %all_gather.7 = bf16[32,8192]{0,1:T(8,128)(2,1)S(1)} all-gather(bf16[32,1024]{0,1:T(8,128)(2,1)S(1)} %fusion.35), channel_id=1, replica_groups=mesh['segment'=4,'ctx'=8] {'ctx'}, dimensions={1}, use_global_device_ids=true | all-gather | bytes 589824 | tf_op jit(solution)/shard_map/all_gather | solution.py:124
  258.3 8.9 %convolution_convert_fusion = bf16[32,1024]{1,0:T(8,128)(2,1)S(1)} fusion(bf16[32,8192]{0,1:T(8,128)(2,1)S(1)} %all_gather.7, bf16[8192,1024]{1,0:T(8,128)(2,1)} %param.15), kind=kOutput, calls=%fused_computation.50 | convolution fusion | flops 536903680 | bytes 17367040 | tf_op jit(solution)/shard_map/dot_general | solution.py:123
  267.3 3.7 %collective-permute-done = bf16[32,1024]{1,0:T(8,128)(2,1)S(1)} collective-permute-done((bf16[32,1024]{1,0:T(8,128)(2,1)S(1)}, bf16[32,1024]{1,0:T(8,128)(2,1)S(1)}, u32[]{:S(2)}, u32[]{:S(2)}) %collective-permute-start) | collective-permute-done | bytes 65568 | tf_op jit(solution)/shard_map/ppermute | solution.py:13
  (152 shorter events, 41.9 us)
Async XLA Ops:
  73.0 4.9 %copy-start = (bf16[32,8192]{1,0:T(8,128)(2,1)}, bf16[32,8192]{1,0:T(8,128)(2,1)S(1)}, u32[]{:S(2)}) copy-start(bf16[32,8192]{1,0:T(8,128)(2,1)S(1)} %get-tuple-element.670) | copy-start | bytes 1572868 | tf_op jit(solution)/shard_map/cond
  120.1 12.2 %all-to-all-start = ((f32[8,1,256]{2,1,0:T(1,128)}), f32[8,1,256]{2,1,0:T(1,128)S(1)}, u32[]{:S(2)}, u32[]{:S(2)}) async-start(f32[8,1,256]{2,1,0:T(1,128)} %reshape.238), calls=%async_computation | async-start | bytes 16384 | tf_op jit(solution)/shard_map/all_to_all | solution.py:117
  132.2 50.1 %all-to-all-start.1 = ((f32[8,1,256]{2,1,0:T(1,128)}), f32[8,1,256]{2,1,0:T(1,128)S(1)}, u32[]{:S(2)}, u32[]{:S(2)}) async-start(f32[8,1,256]{2,1,0:T(1,128)} %reshape.240), calls=%async_computation.1 | async-start | bytes 16384 | tf_op jit(solution)/shard_map/all_to_all | solution.py:116
  182.4 22.3 %all-to-all-start.2 = ((f32[8,1,32768]{2,1,0:T(1,128)}), f32[8,1,32768]{2,1,0:T(1,128)S(1)}, u32[]{:S(2)}, u32[]{:S(2)}) async-start(f32[8,1,32768]{2,1,0:T(1,128)} %reshape.236), calls=%async_computation.2 | async-start | bytes 2097152 | tf_op jit(solution)/shard_map/all_to_all | solution.py:118
  267.2 3.7 %collective-permute-start = (bf16[32,1024]{1,0:T(8,128)(2,1)S(1)}, bf16[32,1024]{1,0:T(8,128)(2,1)S(1)}, u32[]{:S(2)}, u32[]{:S(2)}) collective-permute-start(bf16[32,1024]{1,0:T(8,128)(2,1)S(1)} %convolution_convert_fusion), channel_id=1, source_target_pairs={{0,8},{8,16},{16,24},{24,0},{1,9},{9,17},{17,25},{25,1},{2,10},{10... | collective-permute-start | bytes 196616 | tf_op jit(solution)/shard_map/ppermute | solution.py:13
where the time goes:
time: 277 us; the launch traced here: 272 us
  blocking collectives  72.3 us (26%)
  other arithmetic  58.5 us (21%)
  matrix products  52.7 us (19%)
  local copies, waits for them, and re-layouts  46.6 us (17%)
  waiting for transfers between devices  23.5 us (8%)
  starting transfers between devices  14.9 us (5%)
    unnamed x3, other arithmetic  39.8 us
    all_gather x1, blocking collectives, per_device(): lax.all_gather(local_heads, 'ctx', axis=1, tiled=True)  39 us
    all_gather x1, blocking collectives, per_device(): gathered = lax.all_gather(queries, 'ctx', axis=0, tiled=True)  33.2 us
    dot_general x16, matrix products, per_group(): lax.dot_general(query_part, key_part, (((1,), (1,)), ((), ())), preferred...  22.4 us
    dot_general x16, matrix products, per_group(): jnp.dot(weights.astype(jnp.bfloat16).reshape(rows * group, span), value_p...  21.5 us
    unnamed x9, local copies, waits for them, and re-layouts  16.4 us
    all_to_all x1, waiting for transfers between devices, per_device(): lax.all_to_all(outputs.reshape(1, rows, H * HD), 'ctx', split_axis=2, con...  14.8 us
    dot_general x1, matrix products, per_device(): jnp.dot(lax.all_gather(local_heads, 'ctx', axis=1, tiled=True), out_weigh...  8.88 us
  transfers between devices with their start and end apart: 4, of which 3 were waited for; matrix products, arithmetic and copies ran while one was open for 18% of the time, Pallas kernels for 0%

commit v1 on v0

v1 whole, which is shorter than its diff:
```python
import functools
import math

import jax
import jax.numpy as jnp
from jax import lax
from jax.experimental import pallas as pl
from jax.experimental.pallas import tpu as pltpu
from jax.sharding import PartitionSpec as P

H = 64
KVH = 8
HD = 128
GROUP = H // KVH
LOG2_SCALE = HD ** (-0.5) * math.log2(math.e)
STEP = 8.0
FLOOR = -4096.0
HIDDEN = -1e30
STATS = 16
VMEM_LIMIT = 24 * 1024 * 1024


def swap(value, axis, bits):
    devices = lax.axis_size(axis)
    return lax.ppermute(value, axis, [(i, i ^ bits) for i in range(devices)])


def from_behind(value, axis, by):
    devices = lax.axis_size(axis)
    return lax.ppermute(value, axis, [(i, (i + by) % devices) for i in range(devices)])


class Plan:
    def __init__(self, ctx, rows_here):
        self.ctx = ctx
        self.half = ctx // 2
        self.rows_here = rows_here
        self.rows = ctx * rows_here
        self.heads = H // self.half
        self.unit_heads = min(self.heads, GROUP)
        self.units = self.heads // self.unit_heads
        self.unit_rows = self.unit_heads * self.rows
        self.stat_blocks = self.unit_rows // 128
        self.num_rows = self.units * self.unit_rows
        self.payload_rows = self.num_rows + self.units * self.stat_blocks * STATS

    def stats_at(self, unit):
        return self.num_rows + unit * self.stat_blocks * STATS


def pack_stats(plan, out_ref, unit, peak, total):
    lane = lax.broadcasted_iota(jnp.int32, (plan.unit_rows, 128), 1)
    high = total.astype(jnp.bfloat16).astype(jnp.float32)
    table = jnp.where(lane == 0, peak, jnp.where(lane == 1, high, total - high))
    turned = jnp.transpose(table)[:STATS].astype(jnp.bfloat16)
    for block in range(plan.stat_blocks):
        at = plan.stats_at(unit) + block * STATS
        out_ref[at : at + STATS, :] = turned[:, block * 128 : (block + 1) * 128]


def unpack_stats(plan, ref, unit):
    at = plan.stats_at(unit)
    rows = jnp.concatenate(
        [ref[at + b * STATS : at + (b + 1) * STATS, :] for b in range(plan.stat_blocks)], axis=1
    ).astype(jnp.float32)
    padded = jnp.concatenate([rows, jnp.zeros((128 - STATS, plan.unit_rows), jnp.float32)], axis=0)
    table = jnp.transpose(padded)
    return table[:, 0:1], table[:, 1:2] + table[:, 2:3]


def attend_kernel(plan, part, offset_ref, start_ref, *refs):
    *query_refs, cache_ref, out_ref, score_ref, bias_ref = refs
    span = cache_ref.shape[0]
    chunk = min(span, 512)
    me = lax.axis_index("ctx")
    low, high = me % plan.half, me // plan.half
    offset, start = offset_ref[0], start_ref[0]
    first = me * span
    none = (first + span - 1 < start) | (first > offset + plan.rows - 1)
    every = (first >= start) & (first + span - 1 <= offset)
    mine = low ^ part

    @pl.when(none)
    def _():
        out_ref[...] = jnp.zeros_like(out_ref)
        for unit in range(plan.units):
            pack_stats(
                plan,
                out_ref,
                unit,
                jnp.full((plan.unit_rows, 128), FLOOR / STEP, jnp.float32),
                jnp.zeros((plan.unit_rows, 128), jnp.float32),
            )

    @pl.when(every)
    def _():
        bias_ref[...] = jnp.zeros_like(bias_ref)

    @pl.when(jnp.logical_not(every | none))
    def _():
        position = first + lax.broadcasted_iota(jnp.int32, (span, 128), 0)
        last = offset + lax.broadcasted_iota(jnp.int32, (span, 128), 1)
        shown = (position >= start) & (position <= last)
        bias_ref[...] = jnp.where(shown, 0.0, HIDDEN).astype(jnp.bfloat16)

    @pl.when(jnp.logical_not(none))
    def _():
        source_rows = GROUP * plan.rows
        row = lax.broadcasted_iota(jnp.int32, (plan.unit_rows, source_rows), 0)
        column = lax.broadcasted_iota(jnp.int32, (plan.unit_rows, source_rows), 1)
        query = lax.rem(row, plan.rows)
        device = lax.div(query, plan.rows_here)
        block = 2 * (lax.rem(device, plan.half) ^ low) + (lax.div(device, plan.half) ^ high)
        first_head = (mine * plan.heads) % GROUP
        head = first_head + lax.div(row, plan.rows)
        origin = (block * GROUP + head) * plan.rows_here + lax.rem(query, plan.rows_here)
        order = jnp.where(column == origin, 1.0, 0.0).astype(jnp.bfloat16)
        one_hot = jnp.where(
            lax.rem(lax.broadcasted_iota(jnp.int32, (plan.unit_rows, 128), 0), plan.rows)
            == lax.broadcasted_iota(jnp.int32, (plan.unit_rows, 128), 1),
            1.0,
            0.0,
        ).astype(jnp.bfloat16)
        ones = jnp.ones((chunk, 128), jnp.bfloat16)
        for unit in range(plan.units):
            group = (mine * plan.heads + unit * plan.unit_heads) // GROUP
            stacked = jnp.concatenate([ref[group] for ref in query_refs], axis=0)
            queries = jnp.dot(order, stacked, preferred_element_type=jnp.float32)
            queries = jnp.concatenate([queries.astype(jnp.bfloat16), one_hot], axis=1)
            key_at = pl.multiple_of(group * HD, HD)
            value_at = pl.multiple_of((KVH + group) * HD, HD)
            peak = None
            for at in range(0, span, chunk):
                keys = jnp.concatenate(
                    [cache_ref[at : at + chunk, pl.ds(key_at, HD)], bias_ref[at : at + chunk, :]], axis=1
                )
                scores = lax.dot_general(
                    queries, keys, (((1,), (1,)), ((), ())), preferred_element_type=jnp.float32
                )
                score_ref[unit, :, at : at + chunk] = scores
                for lane in range(0, chunk, 128):
                    piece = scores[:, lane : lane + 128]
                    peak = piece if peak is None else jnp.maximum(peak, piece)
            peak = jnp.max(peak, axis=1, keepdims=True) * LOG2_SCALE
            peak = jnp.maximum(jnp.ceil(peak * (1.0 / STEP)), FLOOR / STEP)
            shift = peak * STEP
            both = jnp.zeros((plan.unit_rows, 2 * HD), jnp.float32)
            for at in range(0, span, chunk):
                weights = jnp.exp2(score_ref[unit, :, at : at + chunk] * LOG2_SCALE - shift)
                values = jnp.concatenate([cache_ref[at : at + chunk, pl.ds(value_at, HD)], ones], axis=1)
                both += jnp.dot(weights.astype(jnp.bfloat16), values, preferred_element_type=jnp.float32)
            at = unit * plan.unit_rows
            out_ref[at : at + plan.unit_rows, :] = both[:, :HD].astype(jnp.bfloat16)
            pack_stats(plan, out_ref, unit, peak, both[:, HD:])


def attend(plan, part, offsets, starts, queries, cache):
    span = cache.shape[0]
    smem = pl.BlockSpec(memory_space=pltpu.SMEM)
    vmem = pl.BlockSpec(memory_space=pltpu.VMEM)
    return pl.pallas_call(
        functools.partial(attend_kernel, plan, part),
        out_shape=jax.ShapeDtypeStruct((plan.payload_rows, HD), jnp.bfloat16),
        in_specs=[smem, smem] + [vmem] * (len(queries) + 1),
        out_specs=vmem,
        scratch_shapes=[
            pltpu.VMEM((plan.units, plan.unit_rows, span), jnp.float32),
            pltpu.VMEM((span, 128), jnp.bfloat16),
        ],
        compiler_params=pltpu.CompilerParams(vmem_limit_bytes=VMEM_LIMIT),
        cost_estimate=pl.CostEstimate(
            flops=4 * plan.num_rows * span * HD,
            bytes_accessed=2 * plan.units * span * HD * 2,
            transcendentals=plan.num_rows * span,
        ),
        name="attend",
    )(offsets, starts, *queries, cache)


def merged(plan, refs, unit):
    stats = [unpack_stats(plan, ref, unit) for ref in refs]
    joint = functools.reduce(jnp.maximum, [peak for peak, _ in stats])
    at = unit * plan.unit_rows
    mixed, total = None, None
    for ref, (peak, weight) in zip(refs, stats):
        factor = jnp.exp2((peak - joint) * STEP)
        term = factor * ref[at : at + plan.unit_rows, :].astype(jnp.float32)
        mixed = term if mixed is None else mixed + term
        total = factor * weight if total is None else total + factor * weight
    return joint, total, mixed


def merge_kernel(plan, *refs):
    *parts, out_ref = refs
    for unit in range(plan.units):
        joint, total, mixed = merged(plan, parts, unit)
        at = unit * plan.unit_rows
        out_ref[at : at + plan.unit_rows, :] = mixed.astype(jnp.bfloat16)
        pack_stats(plan, out_ref, unit, joint, total)


def settle_kernel(plan, *refs):
    *parts, out_ref = refs
    for unit in range(plan.units):
        _, total, mixed = merged(plan, parts, unit)
        done = (mixed / total).astype(jnp.bfloat16)
        for head in range(plan.unit_heads):
            at = (unit * plan.unit_heads + head) * HD
            out_ref[:, at : at + HD] = done[head * plan.rows : (head + 1) * plan.rows, :]


def merge(plan, parts):
    vmem = pl.BlockSpec(memory_space=pltpu.VMEM)
    return pl.pallas_call(
        functools.partial(merge_kernel, plan),
        out_shape=jax.ShapeDtypeStruct((plan.payload_rows, HD), jnp.bfloat16),
        in_specs=[vmem] * len(parts),
        out_specs=vmem,
        compiler_params=pltpu.CompilerParams(vmem_limit_bytes=VMEM_LIMIT),
        name="merge",
    )(*parts)


def settle(plan, parts):
    vmem = pl.BlockSpec(memory_space=pltpu.VMEM)
    return pl.pallas_call(
        functools.partial(settle_kernel, plan),
        out_shape=jax.ShapeDtypeStruct((plan.rows, plan.heads * HD), jnp.bfloat16),
        in_specs=[vmem] * len(parts),
        out_specs=vmem,
        compiler_params=pltpu.CompilerParams(vmem_limit_bytes=VMEM_LIMIT),
        name="settle",
    )(*parts)


def project_kernel(plan, first, last, *refs):
    *refs, weight_ref, out_ref = refs
    depth = plan.heads * HD
    low = lax.axis_index("ctx") % plan.half
    total = None
    for k, ref in zip(range(first, last), refs):
        at = pl.multiple_of((low ^ k) * depth, depth)
        term = jnp.dot(ref[...], weight_ref[pl.ds(at, depth), :], preferred_element_type=jnp.float32)
        total = term if total is None else total + term
    if len(refs) > last - first:
        total = total + refs[-1][...]
    out_ref[...] = total.astype(out_ref.dtype)


def project(plan, first, blocks, weight, before, dtype):
    vmem = pl.BlockSpec(memory_space=pltpu.VMEM)
    extra = [] if before is None else [before]
    return pl.pallas_call(
        functools.partial(project_kernel, plan, first, first + len(blocks)),
        out_shape=jax.ShapeDtypeStruct((plan.rows, weight.shape[1]), dtype),
        in_specs=[vmem] * (len(blocks) + len(extra) + 1),
        out_specs=vmem,
        compiler_params=pltpu.CompilerParams(vmem_limit_bytes=VMEM_LIMIT),
        name="project",
    )(*blocks, *extra, weight)


def per_device(queries, cache, out_weight, offsets, starts):
    plan = Plan(lax.axis_size("ctx"), queries.shape[0])
    half = plan.half
    cache = pltpu.with_memory_space_constraint(cache, pltpu.VMEM)
    out_weight = pltpu.with_memory_space_constraint(out_weight, pltpu.VMEM)

    own = queries.reshape(plan.rows_here, KVH, GROUP, HD)
    own = own.transpose(1, 2, 0, 3).reshape(KVH, GROUP * plan.rows_here, HD)
    pair = jnp.concatenate([own, swap(own, "ctx", half)], axis=1)
    gathered = [pair] + [swap(pair, "ctx", k) for k in range(1, half)]

    received = []
    for part in range(1, half):
        piece = attend(plan, part, offsets, starts, gathered, cache)
        received.append(swap(piece, "ctx", part))
    kept = attend(plan, 0, offsets, starts, gathered, cache)
    near = merge(plan, [kept] + received)
    block = settle(plan, [near, swap(near, "ctx", half)])

    blocks = [block] + [swap(block, "ctx", k) for k in range(1, half)]
    begun = project(plan, 0, blocks[:1], out_weight, None, jnp.float32)
    projected = project(plan, 1, blocks[1:], out_weight, begun, jnp.bfloat16)
    return from_behind(projected, "segment", 1)


def solution(mesh):
    in_specs = (
        P(("segment", "ctx"), None),
        P(("segment", "ctx"), None),
        P("segment", "ctx"),
        P("segment"),
        P("segment"),
    )
    out_specs = P("segment", "ctx")
    return jax.shard_map(
        per_device, mesh=mesh, in_specs=in_specs, out_specs=out_specs, check_vma=False
    )
```

time: 277 us -> 62.5 us (0.23); the launches traced: 272 us -> 61.6 us
  blocking collectives: 72.3 us -> 0 us
  other arithmetic: 58.5 us -> 0.85 us
  matrix products: 52.7 us -> 0 us
  local copies, waits for them, and re-layouts: 46.6 us -> 4.03 us
  starting transfers between devices: 14.9 us -> 27.7 us
  Pallas kernels: 0 us -> 5.6 us
    all_gather x2 -> x0, blocking collectives: 72.3 us -> none  [the longest x1 39 us: per_device(): lax.all_gather(local_heads, 'ctx', axis=1, tiled=True)]
    dot_general x33 -> x0, matrix products: 52.7 us -> none  [the longest x16 22.4 us: per_group(): lax.dot_general(query_part, key_part, (((1,), (1,)), ((), ())), preferred...]
    unnamed x3 -> x1, other arithmetic: 39.8 us -> 0.01 us
    ppermute x0 -> x11, starting transfers between devices: none -> 27.7 us  [swap(): return lax.ppermute(value, axis, [(i, i ^ bits) for i in range(devices)])]
    all_to_all x3 -> x0, waiting for transfers between devices: 19.9 us -> none  [the longest x1 14.8 us: per_device(): lax.all_to_all(outputs.reshape(1, rows, H * HD), 'ctx', split_axis=2, con...]
    ppermute x0 -> x11, waiting for transfers between devices: none -> 18.4 us  [swap(): return lax.ppermute(value, axis, [(i, i ^ bits) for i in range(devices)])]
    all_to_all x3 -> x0, starting transfers between devices: 14.8 us -> none  [the longest x1 5.92 us: per_device(): lax.all_to_all(outputs.reshape(1, rows, H * HD), 'ctx', split_axis=2, con...]
    unnamed x9 -> x11, local copies, waits for them, and re-layouts: 16.4 us -> 4.03 us
  transfers between devices with their start and end apart: 4 -> 12, of which waited for: 3 -> 9; matrix products, arithmetic and copies ran while one was open for 18% -> 0% of each run, Pallas kernels for 0% -> 2%
where the time goes in v1:
time: 62.5 us; the launch traced here: 61.6 us
  starting transfers between devices  27.7 us (44%)
  waiting for transfers between devices  22.1 us (35%)
  Pallas kernels  5.6 us (9%)
  local copies, waits for them, and re-layouts  4.03 us (6%)
  between operations  1.38 us (2%)
  other arithmetic  0.85 us (1%)
    ppermute x11, starting transfers between devices, swap(): return lax.ppermute(value, axis, [(i, i ^ bits) for i in range(devices)])  27.7 us
    ppermute x11, waiting for transfers between devices, swap(): return lax.ppermute(value, axis, [(i, i ^ bits) for i in range(devices)])  18.4 us
    unnamed x11, local copies, waits for them, and re-layouts  4.03 us
    ppermute x1, waiting for transfers between devices, from_behind(): lax.ppermute(value, axis, [(i, (i + by) % devices) for i in range(devices)])  3.69 us
    pallas_call x2, Pallas kernels, project(): pl.pallas_call(functools.partial(project_kernel, plan, first, first + len...  3.09 us
    pallas_call x1, Pallas kernels, merge(): pl.pallas_call(functools.partial(merge_kernel, plan), out_shape=jax.Shape...  1.35 us
  transfers between devices with their start and end apart: 12, of which 9 were waited for; matrix products, arithmetic and copies ran while one was open for 0% of the time, Pallas kernels for 2%

profile of v1, /device:TPU:0, one launch (start us, length us, event | category | flops | bytes accessed | tf_op | source)
XLA Modules:
  0.0 61.6 jit_solution(8570690251774035832)
XLA Ops:
  0.0 4.0 %collective-permute-start = (bf16[8,32,128]{2,1,0:T(8,128)(2,1)}, bf16[8,32,128]{2,1,0:T(8,128)(2,1)S(1)}, u32[]{:S(2)}, u32[]{:S(2)}) collective-permute-start(bf16[8,32,128]{2,1,0:T(8,128)(2,1)} %bitcast.7), channel_id=1, source_target_pairs={{0,4},{1,5},{2,6},{3,7},{4,0},{5,1},{6,2},{7,3},{8,12},{9,13},{10,... | collective-permute-start | bytes 196616 | tf_op jit(solution)/shard_map/ppermute | solution.py:25
  4.0 3.9 %collective-permute-done = bf16[8,32,128]{2,1,0:T(8,128)(2,1)S(1)} collective-permute-done((bf16[8,32,128]{2,1,0:T(8,128)(2,1)}, bf16[8,32,128]{2,1,0:T(8,128)(2,1)S(1)}, u32[]{:S(2)}, u32[]{:S(2)}) %collective-permute-start) | collective-permute-done | bytes 65568 | tf_op jit(solution)/shard_map/ppermute | solution.py:25
  7.9 0.8 %pad_maximum_fusion.refs_0_ = bf16[8,64,128]{2,1,0:T(8,128)(2,1)S(1)} fusion(bf16[8,32,128]{2,1,0:T(8,128)(2,1)S(1)} %collective-permute-done, bf16[8,32,128]{2,1,0:T(8,128)(2,1)} %bitcast.8), kind=kLoop, calls=%fused_computation | loop fusion | flops 262144 | bytes 262144 | tf_op jit(solution)/shard_map/concatenate | solution.py:271
  8.7 1.7 %collective-permute-start.3 = (bf16[8,64,128]{2,1,0:T(8,128)(2,1)S(1)}, bf16[8,64,128]{2,1,0:T(8,128)(2,1)S(1)}, u32[]{:S(2)}, u32[]{:S(2)}) collective-permute-start(bf16[8,64,128]{2,1,0:T(8,128)(2,1)S(1)} %pad_maximum_fusion.refs_0_), channel_id=1, source_target_pairs={{0,3},{1,2},{2,1},{3,0},{4,7},{5,6},{6,5},{7,4},{8,11},{9,10},{10,... | collective-permute-start | bytes 393224 | tf_op jit(solution)/shard_map/ppermute | solution.py:25
  10.4 1.6 %collective-permute-start.2 = (bf16[8,64,128]{2,1,0:T(8,128)(2,1)S(1)}, bf16[8,64,128]{2,1,0:T(8,128)(2,1)S(1)}, u32[]{:S(2)}, u32[]{:S(2)}) collective-permute-start(bf16[8,64,128]{2,1,0:T(8,128)(2,1)S(1)} %pad_maximum_fusion.refs_0_), channel_id=1, source_target_pairs={{0,2},{1,3},{2,0},{3,1},{4,6},{5,7},{6,4},{7,5},{8,10},{9,11},{10,... | collective-permute-start | bytes 393224 | tf_op jit(solution)/shard_map/ppermute | solution.py:25
  12.0 0.3 collective-permute-start.1
  13.6 1.5 %collective-permute-done.3.refs_3_ = bf16[8,64,128]{2,1,0:T(8,128)(2,1)S(1)} collective-permute-done((bf16[8,64,128]{2,1,0:T(8,128)(2,1)S(1)}, bf16[8,64,128]{2,1,0:T(8,128)(2,1)S(1)}, u32[]{:S(2)}, u32[]{:S(2)}) %collective-permute-start.3) | collective-permute-done | bytes 131104 | tf_op jit(solution)/shard_map/ppermute | solution.py:25
  15.1 1.4 %collective-permute-done.2.refs_2_ = bf16[8,64,128]{2,1,0:T(8,128)(2,1)S(1)} collective-permute-done((bf16[8,64,128]{2,1,0:T(8,128)(2,1)S(1)}, bf16[8,64,128]{2,1,0:T(8,128)(2,1)S(1)}, u32[]{:S(2)}, u32[]{:S(2)}) %collective-permute-start.2) | collective-permute-done | bytes 131104 | tf_op jit(solution)/shard_map/ppermute | solution.py:25
  16.5 0.5 collective-permute-done.1.refs_1_
  16.9 0.0 copy-start
  16.9 3.4 %copy-done = bf16[2048,2048]{1,0:T(8,128)(2,1)S(1)} copy-done((bf16[2048,2048]{1,0:T(8,128)(2,1)S(1)}, bf16[2048,2048]{1,0:T(8,128)(2,1)}, u32[]{:S(2)}) %copy-start) | copy-done | bytes 8388632
  20.3 0.0 slice-start
  20.3 0.1 attend.5
  20.4 0.0 slice-start.1
  20.4 1.0 %collective-permute-start.4 = (bf16[576,128]{1,0:T(8,128)(2,1)S(1)}, bf16[576,128]{1,0:T(8,128)(2,1)S(1)}, u32[]{:S(2)}, u32[]{:S(2)}) collective-permute-start(bf16[576,128]{1,0:T(8,128)(2,1)S(1)} %attend.5), channel_id=1, source_target_pairs={{0,1},{1,0},{2,3},{3,2},{4,5},{5,4},{6,7},{7,6},{8,9},{9,8},{10,11... | collective-permute-start | bytes 442376 | tf_op jit(solution)/shard_map/ppermute | solution.py:25
  21.4 0.1 attend.6
  21.5 0.0 slice-start.2
  21.5 4.4 %collective-permute-start.5 = (bf16[576,128]{1,0:T(8,128)(2,1)S(1)}, bf16[576,128]{1,0:T(8,128)(2,1)S(1)}, u32[]{:S(2)}, u32[]{:S(2)}) collective-permute-start(bf16[576,128]{1,0:T(8,128)(2,1)S(1)} %attend.6), channel_id=1, source_target_pairs={{0,2},{1,3},{2,0},{3,1},{4,6},{5,7},{6,4},{7,5},{8,10},{9,11},{10,... | collective-permute-start | bytes 442376 | tf_op jit(solution)/shard_map/ppermute | solution.py:25
  25.9 0.1 attend.7
  25.9 0.0 slice-start.3
  25.9 4.8 %collective-permute-start.6 = (bf16[576,128]{1,0:T(8,128)(2,1)S(1)}, bf16[576,128]{1,0:T(8,128)(2,1)S(1)}, u32[]{:S(2)}, u32[]{:S(2)}) collective-permute-start(bf16[576,128]{1,0:T(8,128)(2,1)S(1)} %attend.7), channel_id=1, source_target_pairs={{0,3},{1,2},{2,1},{3,0},{4,7},{5,6},{6,5},{7,4},{8,11},{9,10},{10,... | collective-permute-start | bytes 442376 | tf_op jit(solution)/shard_map/ppermute | solution.py:25
  30.7 0.2 attend.4.refs_0_
  30.9 0.0 collective-permute-done.4.refs_1_
  31.0 0.0 collective-permute-done.5.refs_2_
  31.0 4.2 %collective-permute-done.6.refs_3_ = bf16[576,128]{1,0:T(8,128)(2,1)S(1)} collective-permute-done((bf16[576,128]{1,0:T(8,128)(2,1)S(1)}, bf16[576,128]{1,0:T(8,128)(2,1)S(1)}, u32[]{:S(2)}, u32[]{:S(2)}) %collective-permute-start.6) | collective-permute-done | bytes 147488 | tf_op jit(solution)/shard_map/ppermute | solution.py:25
  35.1 1.4 %merge.1.refs_0_ = bf16[576,128]{1,0:T(8,128)(2,1)S(1)} custom-call(bf16[576,128]{1,0:T(8,128)(2,1)S(1)} %attend.4.refs_0_, bf16[576,128]{1,0:T(8,128)(2,1)S(1)} %collective-permute-done.4.refs_1_, bf16[576,128]{1,0:T(8,128)(2,1)S(1)} %collective-permute-done.5.refs_2_, bf16[576,128]{1,0:T(8,128)(2,1)S(1)} %collective-permute-done.6.refs_3_), custom_call_target="tpu_custom_call" | custom-call | tf_op jit(solution)/shard_map/merge/pallas_call | solution.py:214
  36.5 6.3 %collective-permute-start.7 = (bf16[576,128]{1,0:T(8,128)(2,1)S(1)}, bf16[576,128]{1,0:T(8,128)(2,1)S(1)}, u32[]{:S(2)}, u32[]{:S(2)}) collective-permute-start(bf16[576,128]{1,0:T(8,128)(2,1)S(1)} %merge.1.refs_0_), channel_id=1, source_target_pairs={{0,4},{1,5},{2,6},{3,7},{4,0},{5,1},{6,2},{7,3},{8,12},{9,13},{10,... | collective-permute-start | bytes 442376 | tf_op jit(solution)/shard_map/ppermute | solution.py:25
  42.8 4.1 %collective-permute-done.7.refs_1_ = bf16[576,128]{1,0:T(8,128)(2,1)S(1)} collective-permute-done((bf16[576,128]{1,0:T(8,128)(2,1)S(1)}, bf16[576,128]{1,0:T(8,128)(2,1)S(1)}, u32[]{:S(2)}, u32[]{:S(2)}) %collective-permute-start.7) | collective-permute-done | bytes 147488 | tf_op jit(solution)/shard_map/ppermute | solution.py:25
  46.9 0.8 %settle.1.refs_0_ = bf16[32,2048]{1,0:T(8,128)(2,1)S(1)} custom-call(bf16[576,128]{1,0:T(8,128)(2,1)S(1)} %merge.1.refs_0_, bf16[576,128]{1,0:T(8,128)(2,1)S(1)} %collective-permute-done.7.refs_1_), custom_call_target="tpu_custom_call" | custom-call | tf_op jit(solution)/shard_map/settle/pallas_call | solution.py:226
  47.7 0.1 collective-permute-start.10
  47.8 1.6 %collective-permute-start.9 = (bf16[32,2048]{1,0:T(8,128)(2,1)S(1)}, bf16[32,2048]{1,0:T(8,128)(2,1)S(1)}, u32[]{:S(2)}, u32[]{:S(2)}) collective-permute-start(bf16[32,2048]{1,0:T(8,128)(2,1)S(1)} %settle.1.refs_0_), channel_id=1, source_target_pairs={{0,2},{1,3},{2,0},{3,1},{4,6},{5,7},{6,4},{7,5},{8,10},{9,11},{10,... | collective-permute-start | bytes 393224 | tf_op jit(solution)/shard_map/ppermute | solution.py:25
  49.4 1.9 %collective-permute-start.8 = (bf16[32,2048]{1,0:T(8,128)(2,1)S(1)}, bf16[32,2048]{1,0:T(8,128)(2,1)S(1)}, u32[]{:S(2)}, u32[]{:S(2)}) collective-permute-start(bf16[32,2048]{1,0:T(8,128)(2,1)S(1)} %settle.1.refs_0_), channel_id=1, source_target_pairs={{0,1},{1,0},{2,3},{3,2},{4,5},{5,4},{6,7},{7,6},{8,9},{9,8},{10,11... | collective-permute-start | bytes 393224 | tf_op jit(solution)/shard_map/ppermute | solution.py:25
  51.2 0.0 slice-done
  51.3 0.0 slice-done.1
  51.3 0.0 slice-done.2
  51.3 0.0 slice-done.3
  51.3 0.8 %project.2.refs_3_ = f32[32,1024]{1,0:T(8,128)S(1)} custom-call(bf16[32,2048]{1,0:T(8,128)(2,1)S(1)} %settle.1.refs_0_, bf16[8192,1024]{1,0:T(8,128)(2,1)S(1)} %bitcast.6), custom_call_target="tpu_custom_call" | custom-call | tf_op jit(solution)/shard_map/project/pallas_call | solution.py:253
  52.1 1.6 %collective-permute-done.10.refs_2_ = bf16[32,2048]{1,0:T(8,128)(2,1)S(1)} collective-permute-done((bf16[32,2048]{1,0:T(8,128)(2,1)S(1)}, bf16[32,2048]{1,0:T(8,128)(2,1)S(1)}, u32[]{:S(2)}, u32[]{:S(2)}) %collective-permute-start.10) | collective-permute-done | bytes 131104 | tf_op jit(solution)/shard_map/ppermute | solution.py:25
  53.7 0.0 collective-permute-done.9.refs_1_
  53.7 1.3 %collective-permute-done.8.refs_0_ = bf16[32,2048]{1,0:T(8,128)(2,1)S(1)} collective-permute-done((bf16[32,2048]{1,0:T(8,128)(2,1)S(1)}, bf16[32,2048]{1,0:T(8,128)(2,1)S(1)}, u32[]{:S(2)}, u32[]{:S(2)}) %collective-permute-start.8) | collective-permute-done | bytes 131104 | tf_op jit(solution)/shard_map/ppermute | solution.py:25
  55.0 2.3 %project.3 = bf16[32,1024]{1,0:T(8,128)(2,1)S(1)} custom-call(bf16[32,2048]{1,0:T(8,128)(2,1)S(1)} %collective-permute-done.8.refs_0_, bf16[32,2048]{1,0:T(8,128)(2,1)S(1)} %collective-permute-done.9.refs_1_, bf16[32,2048]{1,0:T(8,128)(2,1)S(1)} %collective-permute-done.10.refs_2_, f32[32,1024]{1,0:T(8,128)S(1)} %project.2.refs_3_, ...), custom_call_target="tpu_custom_call" | custom-call | tf_op jit(solution)/shard_map/project/pallas_call | solution.py:253
  57.3 0.0 collective-permute-start.11
  57.3 3.7 %collective-permute-done.11 = bf16[32,1024]{1,0:T(8,128)(2,1)S(1)} collective-permute-done((bf16[32,1024]{1,0:T(8,128)(2,1)S(1)}, bf16[32,1024]{1,0:T(8,128)(2,1)S(1)}, u32[]{:S(2)}, u32[]{:S(2)}) %collective-permute-start.11) | collective-permute-done | bytes 65568 | tf_op jit(solution)/shard_map/ppermute | solution.py:30
  61.0 0.6 %copy.10 = bf16[32,1024]{1,0:T(8,128)(2,1)} copy(bf16[32,1024]{1,0:T(8,128)(2,1)S(1)} %collective-permute-done.11) | data formatting | bytes 131072
  (1 shorter events, 0.0 us)
Async XLA Ops:
  0.0 7.9 %collective-permute-start = (bf16[8,32,128]{2,1,0:T(8,128)(2,1)}, bf16[8,32,128]{2,1,0:T(8,128)(2,1)S(1)}, u32[]{:S(2)}, u32[]{:S(2)}) collective-permute-start(bf16[8,32,128]{2,1,0:T(8,128)(2,1)} %bitcast.7), channel_id=1, source_target_pairs={{0,4},{1,5},{2,6},{3,7},{4,0},{5,1},{6,2},{7,3},{8,12},{9,13},{10,... | collective-permute-start | bytes 196616 | tf_op jit(solution)/shard_map/ppermute | solution.py:25
  8.7 6.3 %collective-permute-start.3 = (bf16[8,64,128]{2,1,0:T(8,128)(2,1)S(1)}, bf16[8,64,128]{2,1,0:T(8,128)(2,1)S(1)}, u32[]{:S(2)}, u32[]{:S(2)}) collective-permute-start(bf16[8,64,128]{2,1,0:T(8,128)(2,1)S(1)} %pad_maximum_fusion.refs_0_), channel_id=1, source_target_pairs={{0,3},{1,2},{2,1},{3,0},{4,7},{5,6},{6,5},{7,4},{8,11},{9,10},{10,... | collective-permute-start | bytes 393224 | tf_op jit(solution)/shard_map/ppermute | solution.py:25
  10.4 6.1 %collective-permute-start.2 = (bf16[8,64,128]{2,1,0:T(8,128)(2,1)S(1)}, bf16[8,64,128]{2,1,0:T(8,128)(2,1)S(1)}, u32[]{:S(2)}, u32[]{:S(2)}) collective-permute-start(bf16[8,64,128]{2,1,0:T(8,128)(2,1)S(1)} %pad_maximum_fusion.refs_0_), channel_id=1, source_target_pairs={{0,2},{1,3},{2,0},{3,1},{4,6},{5,7},{6,4},{7,5},{8,10},{9,11},{10,... | collective-permute-start | bytes 393224 | tf_op jit(solution)/shard_map/ppermute | solution.py:25
  12.0 5.0 %collective-permute-start.1 = (bf16[8,64,128]{2,1,0:T(8,128)(2,1)S(1)}, bf16[8,64,128]{2,1,0:T(8,128)(2,1)S(1)}, u32[]{:S(2)}, u32[]{:S(2)}) collective-permute-start(bf16[8,64,128]{2,1,0:T(8,128)(2,1)S(1)} %pad_maximum_fusion.refs_0_), channel_id=1, source_target_pairs={{0,1},{1,0},{2,3},{3,2},{4,5},{5,4},{6,7},{7,6},{8,9},{9,8},{10,11... | collective-permute-start | bytes 393224 | tf_op jit(solution)/shard_map/ppermute | solution.py:25
  16.9 3.4 %copy-start = (bf16[2048,2048]{1,0:T(8,128)(2,1)S(1)}, bf16[2048,2048]{1,0:T(8,128)(2,1)}, u32[]{:S(2)}) copy-start(bf16[2048,2048]{1,0:T(8,128)(2,1)} %refs_4_.8) | copy-start | bytes 25165828
  20.3 30.9 %slice-start = ((s8[16777216]{0:T(1024)(128)(4,1)}), s8[4194304]{0:T(1024)(128)(4,1)S(1)}, s32[]{:S(2)}) async-start(s8[16777216]{0:T(1024)(128)(4,1)} %bitcast.5), calls=%async_computation | async-start | bytes 8388608
  20.4 30.9 %slice-start.1 = ((s8[16777216]{0:T(1024)(128)(4,1)}), s8[4194304]{0:T(1024)(128)(4,1)S(1)}, s32[]{:S(2)}) async-start(s8[16777216]{0:T(1024)(128)(4,1)} %bitcast.5), calls=%async_computation.1 | async-start | bytes 8388608
  20.4 10.6 %collective-permute-start.4 = (bf16[576,128]{1,0:T(8,128)(2,1)S(1)}, bf16[576,128]{1,0:T(8,128)(2,1)S(1)}, u32[]{:S(2)}, u32[]{:S(2)}) collective-permute-start(bf16[576,128]{1,0:T(8,128)(2,1)S(1)} %attend.5), channel_id=1, source_target_pairs={{0,1},{1,0},{2,3},{3,2},{4,5},{5,4},{6,7},{7,6},{8,9},{9,8},{10,11... | collective-permute-start | bytes 442376 | tf_op jit(solution)/shard_map/ppermute | solution.py:25
  21.5 29.8 %slice-start.2 = ((s8[16777216]{0:T(1024)(128)(4,1)}), s8[4194304]{0:T(1024)(128)(4,1)S(1)}, s32[]{:S(2)}) async-start(s8[16777216]{0:T(1024)(128)(4,1)} %bitcast.5), calls=%async_computation.2 | async-start | bytes 8388608
  21.5 9.5 %collective-permute-start.5 = (bf16[576,128]{1,0:T(8,128)(2,1)S(1)}, bf16[576,128]{1,0:T(8,128)(2,1)S(1)}, u32[]{:S(2)}, u32[]{:S(2)}) collective-permute-start(bf16[576,128]{1,0:T(8,128)(2,1)S(1)} %attend.6), channel_id=1, source_target_pairs={{0,2},{1,3},{2,0},{3,1},{4,6},{5,7},{6,4},{7,5},{8,10},{9,11},{10,... | collective-permute-start | bytes 442376 | tf_op jit(solution)/shard_map/ppermute | solution.py:25
  25.9 25.3 %slice-start.3 = ((s8[16777216]{0:T(1024)(128)(4,1)}), s8[4194304]{0:T(1024)(128)(4,1)S(1)}, s32[]{:S(2)}) async-start(s8[16777216]{0:T(1024)(128)(4,1)} %bitcast.5), calls=%async_computation.3 | async-start | bytes 8388608
  25.9 9.2 %collective-permute-start.6 = (bf16[576,128]{1,0:T(8,128)(2,1)S(1)}, bf16[576,128]{1,0:T(8,128)(2,1)S(1)}, u32[]{:S(2)}, u32[]{:S(2)}) collective-permute-start(bf16[576,128]{1,0:T(8,128)(2,1)S(1)} %attend.7), channel_id=1, source_target_pairs={{0,3},{1,2},{2,1},{3,0},{4,7},{5,6},{6,5},{7,4},{8,11},{9,10},{10,... | collective-permute-start | bytes 442376 | tf_op jit(solution)/shard_map/ppermute | solution.py:25
  36.5 10.4 %collective-permute-start.7 = (bf16[576,128]{1,0:T(8,128)(2,1)S(1)}, bf16[576,128]{1,0:T(8,128)(2,1)S(1)}, u32[]{:S(2)}, u32[]{:S(2)}) collective-permute-start(bf16[576,128]{1,0:T(8,128)(2,1)S(1)} %merge.1.refs_0_), channel_id=1, source_target_pairs={{0,4},{1,5},{2,6},{3,7},{4,0},{5,1},{6,2},{7,3},{8,12},{9,13},{10,... | collective-permute-start | bytes 442376 | tf_op jit(solution)/shard_map/ppermute | solution.py:25
  47.7 6.0 %collective-permute-start.10 = (bf16[32,2048]{1,0:T(8,128)(2,1)S(1)}, bf16[32,2048]{1,0:T(8,128)(2,1)S(1)}, u32[]{:S(2)}, u32[]{:S(2)}) collective-permute-start(bf16[32,2048]{1,0:T(8,128)(2,1)S(1)} %settle.1.refs_0_), channel_id=1, source_target_pairs={{0,3},{1,2},{2,1},{3,0},{4,7},{5,6},{6,5},{7,4},{8,11},{9,10},{10,... | collective-permute-start | bytes 393224 | tf_op jit(solution)/shard_map/ppermute | solution.py:25
  47.8 5.9 %collective-permute-start.9 = (bf16[32,2048]{1,0:T(8,128)(2,1)S(1)}, bf16[32,2048]{1,0:T(8,128)(2,1)S(1)}, u32[]{:S(2)}, u32[]{:S(2)}) collective-permute-start(bf16[32,2048]{1,0:T(8,128)(2,1)S(1)} %settle.1.refs_0_), channel_id=1, source_target_pairs={{0,2},{1,3},{2,0},{3,1},{4,6},{5,7},{6,4},{7,5},{8,10},{9,11},{10,... | collective-permute-start | bytes 393224 | tf_op jit(solution)/shard_map/ppermute | solution.py:25
  49.4 5.7 %collective-permute-start.8 = (bf16[32,2048]{1,0:T(8,128)(2,1)S(1)}, bf16[32,2048]{1,0:T(8,128)(2,1)S(1)}, u32[]{:S(2)}, u32[]{:S(2)}) collective-permute-start(bf16[32,2048]{1,0:T(8,128)(2,1)S(1)} %settle.1.refs_0_), channel_id=1, source_target_pairs={{0,1},{1,0},{2,3},{3,2},{4,5},{5,4},{6,7},{7,6},{8,9},{9,8},{10,11... | collective-permute-start | bytes 393224 | tf_op jit(solution)/shard_map/ppermute | solution.py:25
  57.3 3.7 %collective-permute-start.11 = (bf16[32,1024]{1,0:T(8,128)(2,1)S(1)}, bf16[32,1024]{1,0:T(8,128)(2,1)S(1)}, u32[]{:S(2)}, u32[]{:S(2)}) collective-permute-start(bf16[32,1024]{1,0:T(8,128)(2,1)S(1)} %project.3), channel_id=1, source_target_pairs={{0,8},{8,16},{16,24},{24,0},{1,9},{9,17},{17,25},{25,1},{2,10},{10... | collective-permute-start | bytes 196616 | tf_op jit(solution)/shard_map/ppermute | solution.py:30

commit v2 on v1

v2 whole, which is shorter than its diff:
```python
import functools
import math

import jax
import jax.numpy as jnp
from jax import lax
from jax.experimental import pallas as pl
from jax.experimental.pallas import tpu as pltpu
from jax.sharding import PartitionSpec as P

H = 64
KVH = 8
HD = 128
GROUP = H // KVH
LOG2_SCALE = HD ** (-0.5) * math.log2(math.e)
STEP = 8.0
FLOOR = -4096.0
HIDDEN = -1e30
STATS = 16
VMEM_LIMIT = 12 * 1024 * 1024


def swap(value, axis, bits):
    devices = lax.axis_size(axis)
    return lax.ppermute(value, axis, [(i, i ^ bits) for i in range(devices)])


def from_behind(value, axis, by):
    devices = lax.axis_size(axis)
    return lax.ppermute(value, axis, [(i, (i + by) % devices) for i in range(devices)])


class Plan:
    def __init__(self, ctx, rows_here):
        self.ctx = ctx
        self.half = ctx // 2
        self.rows_here = rows_here
        self.rows = ctx * rows_here
        self.heads = H // self.half
        self.unit_heads = min(self.heads, GROUP)
        self.units = self.heads // self.unit_heads
        self.unit_rows = self.unit_heads * self.rows
        self.stat_blocks = self.unit_rows // 128
        self.num_rows = self.units * self.unit_rows
        self.payload_rows = self.num_rows + self.units * self.stat_blocks * STATS

    def stats_at(self, unit):
        return self.num_rows + unit * self.stat_blocks * STATS


def stage_kernel(rows, offset_ref, start_ref, cache_ref, staged_ref, bias_ref, sem):
    copy = pltpu.make_async_copy(cache_ref, staged_ref, sem)
    copy.start()
    span = cache_ref.shape[0]
    offset, start = offset_ref[0], start_ref[0]
    first = lax.axis_index("ctx") * span
    every = (first >= start) & (first + span - 1 <= offset)

    @pl.when(every)
    def _():
        bias_ref[...] = jnp.zeros_like(bias_ref)

    @pl.when(jnp.logical_not(every))
    def _():
        position = first + lax.broadcasted_iota(jnp.int32, (span, 128), 0)
        last = offset + lax.broadcasted_iota(jnp.int32, (span, 128), 1)
        shown = (position >= start) & (position <= last)
        bias_ref[...] = jnp.where(shown, 0.0, HIDDEN).astype(jnp.bfloat16)

    copy.wait()


def stage(plan, offsets, starts, cache):
    smem = pl.BlockSpec(memory_space=pltpu.SMEM)
    vmem = pl.BlockSpec(memory_space=pltpu.VMEM)
    return pl.pallas_call(
        functools.partial(stage_kernel, plan.rows),
        out_shape=[
            pltpu.VMEM(cache.shape, cache.dtype),
            pltpu.VMEM((cache.shape[0], 128), jnp.bfloat16),
        ],
        in_specs=[smem, smem, pl.BlockSpec(memory_space=pltpu.HBM)],
        out_specs=[vmem, vmem],
        scratch_shapes=[pltpu.SemaphoreType.DMA],
        compiler_params=pltpu.CompilerParams(vmem_limit_bytes=VMEM_LIMIT),
        cost_estimate=pl.CostEstimate(
            flops=0, bytes_accessed=2 * cache.shape[0] * cache.shape[1] * 2, transcendentals=0
        ),
        name="stage",
    )(offsets, starts, cache)


def pack_stats(plan, out_ref, unit, peak, total):
    lane = lax.broadcasted_iota(jnp.int32, (plan.unit_rows, 128), 1)
    high = total.astype(jnp.bfloat16).astype(jnp.float32)
    table = jnp.where(lane == 0, peak, jnp.where(lane == 1, high, total - high))
    turned = jnp.transpose(table)[:STATS].astype(jnp.bfloat16)
    for block in range(plan.stat_blocks):
        at = plan.stats_at(unit) + block * STATS
        out_ref[at : at + STATS, :] = turned[:, block * 128 : (block + 1) * 128]


def attend_kernel(plan, part, offset_ref, start_ref, *refs):
    *query_refs, cache_ref, bias_ref, out_ref = refs[: -1 - (part == 0)]
    score_ref = refs[-1]
    wide_ref = refs[-2] if part == 0 else None
    span = cache_ref.shape[0]
    me = lax.axis_index("ctx")
    low, high = me % plan.half, me // plan.half
    offset, start = offset_ref[0], start_ref[0]
    first = me * span
    none = (first + span - 1 < start) | (first > offset + plan.rows - 1)
    mine = low ^ part

    @pl.when(none)
    def _():
        out_ref[...] = jnp.zeros_like(out_ref)
        if wide_ref is not None:
            wide_ref[...] = jnp.zeros_like(wide_ref)
        for unit in range(plan.units):
            pack_stats(
                plan,
                out_ref,
                unit,
                jnp.full((plan.unit_rows, 128), FLOOR / STEP, jnp.float32),
                jnp.zeros((plan.unit_rows, 128), jnp.float32),
            )

    @pl.when(jnp.logical_not(none))
    def _():
        row = lax.broadcasted_iota(jnp.int32, (plan.unit_rows, 128), 0)
        lane = lax.broadcasted_iota(jnp.int32, (plan.unit_rows, 128), 1)
        query = lax.rem(row, plan.rows)
        device = lax.div(query, plan.rows_here)
        block = 2 * (lax.rem(device, plan.half) ^ low) + (lax.div(device, plan.half) ^ high)
        head = (mine * plan.heads) % GROUP + lax.div(row, plan.rows)
        origin = (block * GROUP + head) * plan.rows_here + lax.rem(query, plan.rows_here)
        order = jnp.concatenate(
            [
                jnp.where(lane + at == origin, 1.0, 0.0).astype(jnp.bfloat16)
                for at in range(0, GROUP * plan.rows, 128)
            ],
            axis=1,
        )
        one_hot = jnp.where(query == lane, 1.0, 0.0).astype(jnp.bfloat16)
        ones = jnp.ones((span, HD), jnp.bfloat16)
        groups = [(mine * plan.heads + unit * plan.unit_heads) // GROUP for unit in range(plan.units)]
        peaks = []
        for unit, group in enumerate(groups):
            stacked = jnp.concatenate([ref[group] for ref in query_refs], axis=0)
            queries = jnp.dot(order, stacked, preferred_element_type=jnp.float32)
            queries = jnp.concatenate([queries.astype(jnp.bfloat16), one_hot], axis=1)
            key_at = pl.multiple_of(group * HD, HD)
            keys = jnp.concatenate([cache_ref[:, pl.ds(key_at, HD)], bias_ref[...]], axis=1)
            scores = lax.dot_general(
                queries, keys, (((1,), (1,)), ((), ())), preferred_element_type=jnp.float32
            )
            score_ref[unit] = scores
            peak = [scores[:, at : at + 128] for at in range(0, span, 128)]
            while len(peak) > 1:
                peak = [jnp.maximum(*peak[i : i + 2]) for i in range(0, len(peak) - 1, 2)] + (
                    peak[-1:] if len(peak) % 2 else []
                )
            peak = jnp.max(peak[0], axis=1, keepdims=True) * LOG2_SCALE
            peaks.append(jnp.maximum(jnp.ceil(peak * (1.0 / STEP)), FLOOR / STEP))
        for unit, group in enumerate(groups):
            weights = jnp.exp2(score_ref[unit] * LOG2_SCALE - peaks[unit] * STEP)
            value_at = pl.multiple_of((KVH + group) * HD, HD)
            values = jnp.concatenate([cache_ref[:, pl.ds(value_at, HD)], ones], axis=1)
            both = jnp.dot(weights.astype(jnp.bfloat16), values, preferred_element_type=jnp.float32)
            at = unit * plan.unit_rows
            if wide_ref is not None:
                wide_ref[at : at + plan.unit_rows, :] = both[:, :HD]
            else:
                out_ref[at : at + plan.unit_rows, :] = both[:, :HD].astype(jnp.bfloat16)
            pack_stats(plan, out_ref, unit, peaks[unit], both[:, HD:])


def attend(plan, part, offsets, starts, queries, cache, bias):
    span = cache.shape[0]
    smem = pl.BlockSpec(memory_space=pltpu.SMEM)
    vmem = pl.BlockSpec(memory_space=pltpu.VMEM)
    out_shape = [jax.ShapeDtypeStruct((plan.payload_rows, HD), jnp.bfloat16)]
    if part == 0:
        out_shape.append(jax.ShapeDtypeStruct((plan.num_rows, HD), jnp.float32))
    return pl.pallas_call(
        functools.partial(attend_kernel, plan, part),
        out_shape=out_shape,
        in_specs=[smem, smem] + [vmem] * (len(queries) + 2),
        out_specs=[vmem] * len(out_shape),
        scratch_shapes=[pltpu.VMEM((plan.units, plan.unit_rows, span), jnp.float32)],
        compiler_params=pltpu.CompilerParams(vmem_limit_bytes=VMEM_LIMIT),
        cost_estimate=pl.CostEstimate(
            flops=4 * plan.num_rows * span * HD,
            bytes_accessed=2 * plan.units * span * HD * 2,
            transcendentals=plan.num_rows * span,
        ),
        name="attend",
    )(offsets, starts, *queries, cache, bias)


def columns(rows):
    index = lax.broadcasted_iota(jnp.int32, (128, 128), 0)
    table = jnp.zeros((128, 128), jnp.float32)
    for i, row in enumerate(rows):
        table = jnp.where(index == i, row, table)
    turned = jnp.transpose(table)
    return [turned[:, i : i + 1] for i in range(len(rows))]


def factors(plan, refs, unit, block):
    at = plan.stats_at(unit) + block * STATS
    stats = [ref[at : at + STATS, :].astype(jnp.float32) for ref in refs]
    joint = functools.reduce(jnp.maximum, [stat[0:1] for stat in stats])
    scale = [jnp.exp2((stat[0:1] - joint) * STEP) for stat in stats]
    total = functools.reduce(
        jnp.add, [factor * (stat[1:2] + stat[2:3]) for factor, stat in zip(scale, stats)]
    )
    return joint, scale, total


def mix(wide_ref, refs, at, scale):
    mixed = scale[0] * wide_ref[at : at + 128, :]
    for ref, factor in zip(refs[1:], scale[1:]):
        mixed = mixed + factor * ref[at : at + 128, :].astype(jnp.float32)
    return mixed


def merge_kernel(plan, wide_ref, *refs):
    *parts, out_ref, wide_out_ref = refs
    index = lax.broadcasted_iota(jnp.int32, (STATS, 128), 0)
    for unit in range(plan.units):
        for block in range(plan.stat_blocks):
            joint, scale, total = factors(plan, parts, unit, block)
            high = total.astype(jnp.bfloat16).astype(jnp.float32)
            at = plan.stats_at(unit) + block * STATS
            table = jnp.where(index == 0, joint, jnp.where(index == 1, high, total - high))
            out_ref[at : at + STATS, :] = table.astype(jnp.bfloat16)
            at = unit * plan.unit_rows + block * 128
            mixed = mix(wide_ref, parts, at, columns(scale))
            wide_out_ref[at : at + 128, :] = mixed
            out_ref[at : at + 128, :] = mixed.astype(jnp.bfloat16)


def settle_kernel(plan, wide_ref, *refs):
    *parts, out_ref = refs
    for unit in range(plan.units):
        for block in range(plan.stat_blocks):
            _, scale, total = factors(plan, parts, unit, block)
            at = unit * plan.unit_rows + block * 128
            done = mix(wide_ref, parts, at, columns([factor / total for factor in scale]))
            done = done.astype(jnp.bfloat16)
            for row in range(0, 128, plan.rows):
                to = (at + row) // plan.rows * HD
                out_ref[:, to : to + HD] = done[row : row + plan.rows, :]


def merge(plan, wide, parts):
    vmem = pl.BlockSpec(memory_space=pltpu.VMEM)
    return pl.pallas_call(
        functools.partial(merge_kernel, plan),
        out_shape=[
            jax.ShapeDtypeStruct((plan.payload_rows, HD), jnp.bfloat16),
            jax.ShapeDtypeStruct((plan.num_rows, HD), jnp.float32),
        ],
        in_specs=[vmem] * (len(parts) + 1),
        out_specs=[vmem, vmem],
        compiler_params=pltpu.CompilerParams(vmem_limit_bytes=VMEM_LIMIT),
        name="merge",
    )(wide, *parts)


def settle(plan, wide, parts):
    vmem = pl.BlockSpec(memory_space=pltpu.VMEM)
    return pl.pallas_call(
        functools.partial(settle_kernel, plan),
        out_shape=jax.ShapeDtypeStruct((plan.rows, plan.heads * HD), jnp.bfloat16),
        in_specs=[vmem] * (len(parts) + 1),
        out_specs=vmem,
        compiler_params=pltpu.CompilerParams(vmem_limit_bytes=VMEM_LIMIT),
        name="settle",
    )(wide, *parts)


def project_kernel(plan, first, last, *refs):
    *refs, weight_ref, out_ref = refs
    depth = plan.heads * HD
    low = lax.axis_index("ctx") % plan.half
    total = None
    for k, ref in zip(range(first, last), refs):
        at = pl.multiple_of((low ^ k) * depth, depth)
        term = jnp.dot(ref[...], weight_ref[pl.ds(at, depth), :], preferred_element_type=jnp.float32)
        total = term if total is None else total + term
    if len(refs) > last - first:
        total = total + refs[-1][...]
    out_ref[...] = total.astype(out_ref.dtype)


def project(plan, first, blocks, weight, before, dtype):
    vmem = pl.BlockSpec(memory_space=pltpu.VMEM)
    extra = [] if before is None else [before]
    return pl.pallas_call(
        functools.partial(project_kernel, plan, first, first + len(blocks)),
        out_shape=jax.ShapeDtypeStruct((plan.rows, weight.shape[1]), dtype),
        in_specs=[vmem] * (len(blocks) + len(extra) + 1),
        out_specs=vmem,
        compiler_params=pltpu.CompilerParams(vmem_limit_bytes=VMEM_LIMIT),
        name="project",
    )(*blocks, *extra, weight)


def per_device(queries, cache, out_weight, offsets, starts):
    plan = Plan(lax.axis_size("ctx"), queries.shape[0])
    half = plan.half
    cache = pltpu.with_memory_space_constraint(cache, pltpu.HBM)
    out_weight = pltpu.with_memory_space_constraint(out_weight, pltpu.VMEM)

    own = queries.reshape(plan.rows_here, KVH, GROUP, HD)
    own = own.transpose(1, 2, 0, 3).reshape(KVH, GROUP * plan.rows_here, HD)
    staged, bias = stage(plan, offsets, starts, cache)
    staged = pltpu.with_memory_space_constraint(staged, pltpu.VMEM)
    pair = jnp.concatenate([own, swap(own, "ctx", half)], axis=1)
    gathered = [pair] + [swap(pair, "ctx", k) for k in range(1, half)]

    received = []
    for part in reversed(range(1, half)):
        (piece,) = attend(plan, part, offsets, starts, gathered, staged, bias)
        received.append(swap(piece, "ctx", part))
    kept, wide = attend(plan, 0, offsets, starts, gathered, staged, bias)
    near, wide = merge(plan, wide, [kept] + received)
    block = settle(plan, wide, [near, swap(near, "ctx", half)])

    blocks = [block] + [swap(block, "ctx", k) for k in range(1, half)]
    total = project(plan, 0, blocks[:1], out_weight, None, jnp.float32)
    for k in range(1, half):
        last = k == half - 1
        total = project(plan, k, blocks[k : k + 1], out_weight, total, jnp.bfloat16 if last else jnp.float32)
    return from_behind(total, "segment", 1)


def solution(mesh):
    in_specs = (
        P(("segment", "ctx"), None),
        P(("segment", "ctx"), None),
        P("segment", "ctx"),
        P("segment"),
        P("segment"),
    )
    out_specs = P("segment", "ctx")
    return jax.shard_map(
        per_device, mesh=mesh, in_specs=in_specs, out_specs=out_specs, check_vma=False
    )
```

time: 62.5 us -> 53.2 us (0.85); the launches traced: 61.6 us -> 53 us
  starting transfers between devices: 27.7 us -> 23.3 us
  local copies, waits for them, and re-layouts: 4.03 us -> 0.65 us
  waiting for transfers between devices: 22.1 us -> 18.9 us
  Pallas kernels: 5.6 us -> 7.93 us
    ppermute x11, starting transfers between devices: 27.7 us -> 23.3 us  [swap(): return lax.ppermute(value, axis, [(i, i ^ bits) for i in range(devices)])]
    unnamed x11 -> x9, local copies, waits for them, and re-layouts: 4.03 us -> 0.65 us
    ppermute x11, waiting for transfers between devices: 18.4 us -> 15.2 us  [swap(): return lax.ppermute(value, axis, [(i, i ^ bits) for i in range(devices)])]
    pallas_call x5 -> x6, Pallas kernels: 1.75 us -> 4.21 us  [the longest x1 3.39 us: stage(): pl.pallas_call(functools.partial(stage_kernel, plan.rows), out_shape=[plt...]
    pallas_call x2 -> x4, Pallas kernels: 3.09 us -> 3.3 us  [project(): pl.pallas_call(functools.partial(project_kernel, plan, first, first + len...]
  transfers between devices with their start and end apart: 12 -> 12, of which waited for: 9 -> 7; matrix products, arithmetic and copies ran while one was open for 0% -> 0% of each run, Pallas kernels for 2% -> 11%
where the time goes in v2:
time: 53.2 us; the launch traced here: 53 us
  starting transfers between devices  23.3 us (44%)
  waiting for transfers between devices  18.9 us (36%)
  Pallas kernels  7.93 us (15%)
  between operations  1.39 us (3%)
  other arithmetic  0.85 us (2%)
  local copies, waits for them, and re-layouts  0.65 us (1%)
    ppermute x11, starting transfers between devices, swap(): return lax.ppermute(value, axis, [(i, i ^ bits) for i in range(devices)])  23.3 us
    ppermute x11, waiting for transfers between devices, swap(): return lax.ppermute(value, axis, [(i, i ^ bits) for i in range(devices)])  15.2 us
    ppermute x1, waiting for transfers between devices, from_behind(): lax.ppermute(value, axis, [(i, (i + by) % devices) for i in range(devices)])  3.69 us
    pallas_call x1, Pallas kernels, stage(): pl.pallas_call(functools.partial(stage_kernel, plan.rows), out_shape=[plt...  3.39 us
    pallas_call x4, Pallas kernels, project(): pl.pallas_call(functools.partial(project_kernel, plan, first, first + len...  3.3 us
  transfers between devices with their start and end apart: 12, of which 7 were waited for; matrix products, arithmetic and copies ran while one was open for 0% of the time, Pallas kernels for 11%

profile of v2, /device:TPU:0, one launch (start us, length us, event | category | flops | bytes accessed | tf_op | source)
XLA Modules:
  0.0 53.0 jit_solution(13088772542006197958)
XLA Ops:
  0.0 4.0 %collective-permute-start = (bf16[8,32,128]{2,1,0:T(8,128)(2,1)}, bf16[8,32,128]{2,1,0:T(8,128)(2,1)S(1)}, u32[]{:S(2)}, u32[]{:S(2)}) collective-permute-start(bf16[8,32,128]{2,1,0:T(8,128)(2,1)} %bitcast.7), channel_id=1, source_target_pairs={{0,4},{1,5},{2,6},{3,7},{4,0},{5,1},{6,2},{7,3},{8,12},{9,13},{10,... | collective-permute-start | bytes 196616 | tf_op jit(solution)/shard_map/ppermute | solution.py:25
  4.0 3.9 %collective-permute-done = bf16[8,32,128]{2,1,0:T(8,128)(2,1)S(1)} collective-permute-done((bf16[8,32,128]{2,1,0:T(8,128)(2,1)}, bf16[8,32,128]{2,1,0:T(8,128)(2,1)S(1)}, u32[]{:S(2)}, u32[]{:S(2)}) %collective-permute-start) | collective-permute-done | bytes 65568 | tf_op jit(solution)/shard_map/ppermute | solution.py:25
  7.9 0.8 %pad_maximum_fusion.refs_0_ = bf16[8,64,128]{2,1,0:T(8,128)(2,1)S(1)} fusion(bf16[8,32,128]{2,1,0:T(8,128)(2,1)S(1)} %collective-permute-done, bf16[8,32,128]{2,1,0:T(8,128)(2,1)} %bitcast.8), kind=kLoop, calls=%fused_computation | loop fusion | flops 262144 | bytes 262144 | tf_op jit(solution)/shard_map/concatenate | solution.py:322
  8.7 1.7 %collective-permute-start.3 = (bf16[8,64,128]{2,1,0:T(8,128)(2,1)S(1)}, bf16[8,64,128]{2,1,0:T(8,128)(2,1)S(1)}, u32[]{:S(2)}, u32[]{:S(2)}) collective-permute-start(bf16[8,64,128]{2,1,0:T(8,128)(2,1)S(1)} %pad_maximum_fusion.refs_0_), channel_id=1, source_target_pairs={{0,3},{1,2},{2,1},{3,0},{4,7},{5,6},{6,5},{7,4},{8,11},{9,10},{10,... | collective-permute-start | bytes 393224 | tf_op jit(solution)/shard_map/ppermute | solution.py:25
  10.4 1.6 %collective-permute-start.2 = (bf16[8,64,128]{2,1,0:T(8,128)(2,1)S(1)}, bf16[8,64,128]{2,1,0:T(8,128)(2,1)S(1)}, u32[]{:S(2)}, u32[]{:S(2)}) collective-permute-start(bf16[8,64,128]{2,1,0:T(8,128)(2,1)S(1)} %pad_maximum_fusion.refs_0_), channel_id=1, source_target_pairs={{0,2},{1,3},{2,0},{3,1},{4,6},{5,7},{6,4},{7,5},{8,10},{9,11},{10,... | collective-permute-start | bytes 393224 | tf_op jit(solution)/shard_map/ppermute | solution.py:25
  12.0 0.3 collective-permute-start.1
  13.6 3.4 %stage.1 = (bf16[2048,2048]{1,0:T(8,128)(2,1)S(1)}, bf16[2048,128]{1,0:T(8,128)(2,1)S(1)}) custom-call(s32[1]{0:T(128)S(6)} %copy.8.offset_ref, s32[1]{0:T(128)S(6)} %copy.9.start_ref, bf16[2048,2048]{1,0:T(8,128)(2,1)} %cache_ref.1), custom_call_target="tpu_custom_call" | custom-call | bytes 16777216 | tf_op jit(solution)/shard_map/stage/pallas_call | solution.py:76
  17.0 0.0 collective-permute-done.3.refs_3_
  17.0 0.0 collective-permute-done.2.refs_2_
  17.0 0.0 collective-permute-done.1.refs_1_
  17.0 0.0 slice-start
  17.0 0.1 attend.5
  17.1 0.0 slice-start.1
  17.1 3.8 %collective-permute-start.4 = (bf16[576,128]{1,0:T(8,128)(2,1)S(1)}, bf16[576,128]{1,0:T(8,128)(2,1)S(1)}, u32[]{:S(2)}, u32[]{:S(2)}) collective-permute-start(bf16[576,128]{1,0:T(8,128)(2,1)S(1)} %attend.5), channel_id=1, source_target_pairs={{0,3},{1,2},{2,1},{3,0},{4,7},{5,6},{6,5},{7,4},{8,11},{9,10},{10,... | collective-permute-start | bytes 442376 | tf_op jit(solution)/shard_map/ppermute | solution.py:25
  21.0 0.1 attend.6
  21.0 0.0 slice-start.2
  21.0 3.1 %collective-permute-start.5 = (bf16[576,128]{1,0:T(8,128)(2,1)S(1)}, bf16[576,128]{1,0:T(8,128)(2,1)S(1)}, u32[]{:S(2)}, u32[]{:S(2)}) collective-permute-start(bf16[576,128]{1,0:T(8,128)(2,1)S(1)} %attend.6), channel_id=1, source_target_pairs={{0,2},{1,3},{2,0},{3,1},{4,6},{5,7},{6,4},{7,5},{8,10},{9,11},{10,... | collective-permute-start | bytes 442376 | tf_op jit(solution)/shard_map/ppermute | solution.py:25
  24.1 0.1 attend.7
  24.2 0.0 slice-start.3
  24.2 1.4 %collective-permute-start.6 = (bf16[576,128]{1,0:T(8,128)(2,1)S(1)}, bf16[576,128]{1,0:T(8,128)(2,1)S(1)}, u32[]{:S(2)}, u32[]{:S(2)}) collective-permute-start(bf16[576,128]{1,0:T(8,128)(2,1)S(1)} %attend.7), channel_id=1, source_target_pairs={{0,1},{1,0},{2,3},{3,2},{4,5},{5,4},{6,7},{7,6},{8,9},{9,8},{10,11... | collective-permute-start | bytes 442376 | tf_op jit(solution)/shard_map/ppermute | solution.py:25
  25.6 0.1 attend.4
  25.7 0.0 collective-permute-done.4.refs_1_
  25.7 2.8 %collective-permute-done.5.refs_2_ = bf16[576,128]{1,0:T(8,128)(2,1)S(1)} collective-permute-done((bf16[576,128]{1,0:T(8,128)(2,1)S(1)}, bf16[576,128]{1,0:T(8,128)(2,1)S(1)}, u32[]{:S(2)}, u32[]{:S(2)}) %collective-permute-start.5) | collective-permute-done | bytes 147488 | tf_op jit(solution)/shard_map/ppermute | solution.py:25
  28.5 1.4 %collective-permute-done.6.refs_3_ = bf16[576,128]{1,0:T(8,128)(2,1)S(1)} collective-permute-done((bf16[576,128]{1,0:T(8,128)(2,1)S(1)}, bf16[576,128]{1,0:T(8,128)(2,1)S(1)}, u32[]{:S(2)}, u32[]{:S(2)}) %collective-permute-start.6) | collective-permute-done | bytes 147488 | tf_op jit(solution)/shard_map/ppermute | solution.py:25
  29.9 0.5 %merge.1 = (bf16[576,128]{1,0:T(8,128)(2,1)S(1)}, f32[512,128]{1,0:T(8,128)S(1)}) custom-call(f32[512,128]{1,0:T(8,128)S(1)} %get-tuple-element.13.wide_ref, bf16[576,128]{1,0:T(8,128)(2,1)S(1)} %get-tuple-element.14.refs_0_, bf16[576,128]{1,0:T(8,128)(2,1)S(1)} %collective-permute-done.4.refs_1_, bf16[576,128]{1,0:T(8,128)(2,1)S(1)} %collective-permute-done.5.refs_2_, ...), custom_call_target="tpu_custom_call" | custom-call | tf_op jit(solution)/shard_map/merge/pallas_call | solution.py:260
  30.4 3.7 %collective-permute-start.7 = (bf16[576,128]{1,0:T(8,128)(2,1)S(1)}, bf16[576,128]{1,0:T(8,128)(2,1)S(1)}, u32[]{:S(2)}, u32[]{:S(2)}) collective-permute-start(bf16[576,128]{1,0:T(8,128)(2,1)S(1)} %get-tuple-element.16.refs_0_), channel_id=1, source_target_pairs={{0,4},{1,5},{2,6},{3,7},{4,0},{5,1},{6,2},{7,3},{8,12},{9,13},{10,... | collective-permute-start | bytes 442376 | tf_op jit(solution)/shard_map/ppermute | solution.py:25
  34.2 5.3 %collective-permute-done.7.refs_1_ = bf16[576,128]{1,0:T(8,128)(2,1)S(1)} collective-permute-done((bf16[576,128]{1,0:T(8,128)(2,1)S(1)}, bf16[576,128]{1,0:T(8,128)(2,1)S(1)}, u32[]{:S(2)}, u32[]{:S(2)}) %collective-permute-start.7) | collective-permute-done | bytes 147488 | tf_op jit(solution)/shard_map/ppermute | solution.py:25
  39.5 0.4 settle.1.refs_0_
  39.9 0.7 %collective-permute-start.10 = (bf16[32,2048]{1,0:T(8,128)(2,1)S(1)}, bf16[32,2048]{1,0:T(8,128)(2,1)S(1)}, u32[]{:S(2)}, u32[]{:S(2)}) collective-permute-start(bf16[32,2048]{1,0:T(8,128)(2,1)S(1)} %settle.1.refs_0_), channel_id=1, source_target_pairs={{0,1},{1,0},{2,3},{3,2},{4,5},{5,4},{6,7},{7,6},{8,9},{9,8},{10,11... | collective-permute-start | bytes 393224 | tf_op jit(solution)/shard_map/ppermute | solution.py:25
  40.6 0.7 %collective-permute-start.9 = (bf16[32,2048]{1,0:T(8,128)(2,1)S(1)}, bf16[32,2048]{1,0:T(8,128)(2,1)S(1)}, u32[]{:S(2)}, u32[]{:S(2)}) collective-permute-start(bf16[32,2048]{1,0:T(8,128)(2,1)S(1)} %settle.1.refs_0_), channel_id=1, source_target_pairs={{0,2},{1,3},{2,0},{3,1},{4,6},{5,7},{6,4},{7,5},{8,10},{9,11},{10,... | collective-permute-start | bytes 393224 | tf_op jit(solution)/shard_map/ppermute | solution.py:25
  41.3 2.2 %collective-permute-start.8 = (bf16[32,2048]{1,0:T(8,128)(2,1)S(1)}, bf16[32,2048]{1,0:T(8,128)(2,1)S(1)}, u32[]{:S(2)}, u32[]{:S(2)}) collective-permute-start(bf16[32,2048]{1,0:T(8,128)(2,1)S(1)} %settle.1.refs_0_), channel_id=1, source_target_pairs={{0,3},{1,2},{2,1},{3,0},{4,7},{5,6},{6,5},{7,4},{8,11},{9,10},{10,... | collective-permute-start | bytes 393224 | tf_op jit(solution)/shard_map/ppermute | solution.py:25
  43.5 0.0 slice-done
  43.5 0.0 slice-done.1
  43.5 0.0 slice-done.2
  43.5 0.0 slice-done.3
  43.5 0.8 %project.4.refs_1_ = f32[32,1024]{1,0:T(8,128)S(1)} custom-call(bf16[32,2048]{1,0:T(8,128)(2,1)S(1)} %settle.1.refs_0_, bf16[8192,1024]{1,0:T(8,128)(2,1)S(1)} %bitcast.6), custom_call_target="tpu_custom_call" | custom-call | tf_op jit(solution)/shard_map/project/pallas_call | solution.py:302
  44.3 1.2 %collective-permute-done.10.refs_0_ = bf16[32,2048]{1,0:T(8,128)(2,1)S(1)} collective-permute-done((bf16[32,2048]{1,0:T(8,128)(2,1)S(1)}, bf16[32,2048]{1,0:T(8,128)(2,1)S(1)}, u32[]{:S(2)}, u32[]{:S(2)}) %collective-permute-start.10) | collective-permute-done | bytes 131104 | tf_op jit(solution)/shard_map/ppermute | solution.py:25
  45.5 0.8 %project.5.refs_1_ = f32[32,1024]{1,0:T(8,128)S(1)} custom-call(bf16[32,2048]{1,0:T(8,128)(2,1)S(1)} %collective-permute-done.10.refs_0_, f32[32,1024]{1,0:T(8,128)S(1)} %project.4.refs_1_, bf16[8192,1024]{1,0:T(8,128)(2,1)S(1)} %bitcast.6), custom_call_target="tpu_custom_call" | custom-call | tf_op jit(solution)/shard_map/project/pallas_call | solution.py:302
  46.3 0.0 collective-permute-done.9.refs_0_
  46.3 0.8 %project.6.refs_1_ = f32[32,1024]{1,0:T(8,128)S(1)} custom-call(bf16[32,2048]{1,0:T(8,128)(2,1)S(1)} %collective-permute-done.9.refs_0_, f32[32,1024]{1,0:T(8,128)S(1)} %project.5.refs_1_, bf16[8192,1024]{1,0:T(8,128)(2,1)S(1)} %bitcast.6), custom_call_target="tpu_custom_call" | custom-call | tf_op jit(solution)/shard_map/project/pallas_call | solution.py:302
  47.2 0.7 %collective-permute-done.8.refs_0_ = bf16[32,2048]{1,0:T(8,128)(2,1)S(1)} collective-permute-done((bf16[32,2048]{1,0:T(8,128)(2,1)S(1)}, bf16[32,2048]{1,0:T(8,128)(2,1)S(1)}, u32[]{:S(2)}, u32[]{:S(2)}) %collective-permute-start.8) | collective-permute-done | bytes 131104 | tf_op jit(solution)/shard_map/ppermute | solution.py:25
  47.8 0.8 %project.7 = bf16[32,1024]{1,0:T(8,128)(2,1)S(1)} custom-call(bf16[32,2048]{1,0:T(8,128)(2,1)S(1)} %collective-permute-done.8.refs_0_, f32[32,1024]{1,0:T(8,128)S(1)} %project.6.refs_1_, bf16[8192,1024]{1,0:T(8,128)(2,1)S(1)} %bitcast.6), custom_call_target="tpu_custom_call" | custom-call | tf_op jit(solution)/shard_map/project/pallas_call | solution.py:302
  48.6 0.0 collective-permute-start.11
  48.7 3.7 %collective-permute-done.11 = bf16[32,1024]{1,0:T(8,128)(2,1)S(1)} collective-permute-done((bf16[32,1024]{1,0:T(8,128)(2,1)S(1)}, bf16[32,1024]{1,0:T(8,128)(2,1)S(1)}, u32[]{:S(2)}, u32[]{:S(2)}) %collective-permute-start.11) | collective-permute-done | bytes 65568 | tf_op jit(solution)/shard_map/ppermute | solution.py:30
  52.3 0.6 %copy.10 = bf16[32,1024]{1,0:T(8,128)(2,1)} copy(bf16[32,1024]{1,0:T(8,128)(2,1)S(1)} %collective-permute-done.11) | data formatting | bytes 131072
  (1 shorter events, 0.0 us)
Async XLA Ops:
  0.0 7.9 %collective-permute-start = (bf16[8,32,128]{2,1,0:T(8,128)(2,1)}, bf16[8,32,128]{2,1,0:T(8,128)(2,1)S(1)}, u32[]{:S(2)}, u32[]{:S(2)}) collective-permute-start(bf16[8,32,128]{2,1,0:T(8,128)(2,1)} %bitcast.7), channel_id=1, source_target_pairs={{0,4},{1,5},{2,6},{3,7},{4,0},{5,1},{6,2},{7,3},{8,12},{9,13},{10,... | collective-permute-start | bytes 196616 | tf_op jit(solution)/shard_map/ppermute | solution.py:25
  8.7 8.3 %collective-permute-start.3 = (bf16[8,64,128]{2,1,0:T(8,128)(2,1)S(1)}, bf16[8,64,128]{2,1,0:T(8,128)(2,1)S(1)}, u32[]{:S(2)}, u32[]{:S(2)}) collective-permute-start(bf16[8,64,128]{2,1,0:T(8,128)(2,1)S(1)} %pad_maximum_fusion.refs_0_), channel_id=1, source_target_pairs={{0,3},{1,2},{2,1},{3,0},{4,7},{5,6},{6,5},{7,4},{8,11},{9,10},{10,... | collective-permute-start | bytes 393224 | tf_op jit(solution)/shard_map/ppermute | solution.py:25
  10.4 6.6 %collective-permute-start.2 = (bf16[8,64,128]{2,1,0:T(8,128)(2,1)S(1)}, bf16[8,64,128]{2,1,0:T(8,128)(2,1)S(1)}, u32[]{:S(2)}, u32[]{:S(2)}) collective-permute-start(bf16[8,64,128]{2,1,0:T(8,128)(2,1)S(1)} %pad_maximum_fusion.refs_0_), channel_id=1, source_target_pairs={{0,2},{1,3},{2,0},{3,1},{4,6},{5,7},{6,4},{7,5},{8,10},{9,11},{10,... | collective-permute-start | bytes 393224 | tf_op jit(solution)/shard_map/ppermute | solution.py:25
  12.0 5.0 %collective-permute-start.1 = (bf16[8,64,128]{2,1,0:T(8,128)(2,1)S(1)}, bf16[8,64,128]{2,1,0:T(8,128)(2,1)S(1)}, u32[]{:S(2)}, u32[]{:S(2)}) collective-permute-start(bf16[8,64,128]{2,1,0:T(8,128)(2,1)S(1)} %pad_maximum_fusion.refs_0_), channel_id=1, source_target_pairs={{0,1},{1,0},{2,3},{3,2},{4,5},{5,4},{6,7},{7,6},{8,9},{9,8},{10,11... | collective-permute-start | bytes 393224 | tf_op jit(solution)/shard_map/ppermute | solution.py:25
  17.0 26.4 %slice-start = ((s8[16777216]{0:T(1024)(128)(4,1)}), s8[4194304]{0:T(1024)(128)(4,1)S(1)}, s32[]{:S(2)}) async-start(s8[16777216]{0:T(1024)(128)(4,1)} %bitcast.5), calls=%async_computation | async-start | bytes 8388608
  17.1 26.3 %slice-start.1 = ((s8[16777216]{0:T(1024)(128)(4,1)}), s8[4194304]{0:T(1024)(128)(4,1)S(1)}, s32[]{:S(2)}) async-start(s8[16777216]{0:T(1024)(128)(4,1)} %bitcast.5), calls=%async_computation.1 | async-start | bytes 8388608
  17.1 8.6 %collective-permute-start.4 = (bf16[576,128]{1,0:T(8,128)(2,1)S(1)}, bf16[576,128]{1,0:T(8,128)(2,1)S(1)}, u32[]{:S(2)}, u32[]{:S(2)}) collective-permute-start(bf16[576,128]{1,0:T(8,128)(2,1)S(1)} %attend.5), channel_id=1, source_target_pairs={{0,3},{1,2},{2,1},{3,0},{4,7},{5,6},{6,5},{7,4},{8,11},{9,10},{10,... | collective-permute-start | bytes 442376 | tf_op jit(solution)/shard_map/ppermute | solution.py:25
  21.0 22.4 %slice-start.2 = ((s8[16777216]{0:T(1024)(128)(4,1)}), s8[4194304]{0:T(1024)(128)(4,1)S(1)}, s32[]{:S(2)}) async-start(s8[16777216]{0:T(1024)(128)(4,1)} %bitcast.5), calls=%async_computation.2 | async-start | bytes 8388608
  21.0 7.5 %collective-permute-start.5 = (bf16[576,128]{1,0:T(8,128)(2,1)S(1)}, bf16[576,128]{1,0:T(8,128)(2,1)S(1)}, u32[]{:S(2)}, u32[]{:S(2)}) collective-permute-start(bf16[576,128]{1,0:T(8,128)(2,1)S(1)} %attend.6), channel_id=1, source_target_pairs={{0,2},{1,3},{2,0},{3,1},{4,6},{5,7},{6,4},{7,5},{8,10},{9,11},{10,... | collective-permute-start | bytes 442376 | tf_op jit(solution)/shard_map/ppermute | solution.py:25
  24.2 19.3 %slice-start.3 = ((s8[16777216]{0:T(1024)(128)(4,1)}), s8[4194304]{0:T(1024)(128)(4,1)S(1)}, s32[]{:S(2)}) async-start(s8[16777216]{0:T(1024)(128)(4,1)} %bitcast.5), calls=%async_computation.3 | async-start | bytes 8388608
  24.2 5.7 %collective-permute-start.6 = (bf16[576,128]{1,0:T(8,128)(2,1)S(1)}, bf16[576,128]{1,0:T(8,128)(2,1)S(1)}, u32[]{:S(2)}, u32[]{:S(2)}) collective-permute-start(bf16[576,128]{1,0:T(8,128)(2,1)S(1)} %attend.7), channel_id=1, source_target_pairs={{0,1},{1,0},{2,3},{3,2},{4,5},{5,4},{6,7},{7,6},{8,9},{9,8},{10,11... | collective-permute-start | bytes 442376 | tf_op jit(solution)/shard_map/ppermute | solution.py:25
  30.4 9.0 %collective-permute-start.7 = (bf16[576,128]{1,0:T(8,128)(2,1)S(1)}, bf16[576,128]{1,0:T(8,128)(2,1)S(1)}, u32[]{:S(2)}, u32[]{:S(2)}) collective-permute-start(bf16[576,128]{1,0:T(8,128)(2,1)S(1)} %get-tuple-element.16.refs_0_), channel_id=1, source_target_pairs={{0,4},{1,5},{2,6},{3,7},{4,0},{5,1},{6,2},{7,3},{8,12},{9,13},{10,... | collective-permute-start | bytes 442376 | tf_op jit(solution)/shard_map/ppermute | solution.py:25
  39.9 5.6 %collective-permute-start.10 = (bf16[32,2048]{1,0:T(8,128)(2,1)S(1)}, bf16[32,2048]{1,0:T(8,128)(2,1)S(1)}, u32[]{:S(2)}, u32[]{:S(2)}) collective-permute-start(bf16[32,2048]{1,0:T(8,128)(2,1)S(1)} %settle.1.refs_0_), channel_id=1, source_target_pairs={{0,1},{1,0},{2,3},{3,2},{4,5},{5,4},{6,7},{7,6},{8,9},{9,8},{10,11... | collective-permute-start | bytes 393224 | tf_op jit(solution)/shard_map/ppermute | solution.py:25
  40.6 5.7 %collective-permute-start.9 = (bf16[32,2048]{1,0:T(8,128)(2,1)S(1)}, bf16[32,2048]{1,0:T(8,128)(2,1)S(1)}, u32[]{:S(2)}, u32[]{:S(2)}) collective-permute-start(bf16[32,2048]{1,0:T(8,128)(2,1)S(1)} %settle.1.refs_0_), channel_id=1, source_target_pairs={{0,2},{1,3},{2,0},{3,1},{4,6},{5,7},{6,4},{7,5},{8,10},{9,11},{10,... | collective-permute-start | bytes 393224 | tf_op jit(solution)/shard_map/ppermute | solution.py:25
  41.3 6.5 %collective-permute-start.8 = (bf16[32,2048]{1,0:T(8,128)(2,1)S(1)}, bf16[32,2048]{1,0:T(8,128)(2,1)S(1)}, u32[]{:S(2)}, u32[]{:S(2)}) collective-permute-start(bf16[32,2048]{1,0:T(8,128)(2,1)S(1)} %settle.1.refs_0_), channel_id=1, source_target_pairs={{0,3},{1,2},{2,1},{3,0},{4,7},{5,6},{6,5},{7,4},{8,11},{9,10},{10,... | collective-permute-start | bytes 393224 | tf_op jit(solution)/shard_map/ppermute | solution.py:25
  48.6 3.7 %collective-permute-start.11 = (bf16[32,1024]{1,0:T(8,128)(2,1)S(1)}, bf16[32,1024]{1,0:T(8,128)(2,1)S(1)}, u32[]{:S(2)}, u32[]{:S(2)}) collective-permute-start(bf16[32,1024]{1,0:T(8,128)(2,1)S(1)} %project.7), channel_id=1, source_target_pairs={{0,8},{8,16},{16,24},{24,0},{1,9},{9,17},{17,25},{25,1},{2,10},{10... | collective-permute-start | bytes 196616 | tf_op jit(solution)/shard_map/ppermute | solution.py:30

commit v3 on v2

v3 whole, which is shorter than its diff:
```python
import functools
import math

import jax
import jax.numpy as jnp
from jax import lax
from jax.experimental import pallas as pl
from jax.experimental.pallas import tpu as pltpu
from jax.sharding import PartitionSpec as P

H = 64
KVH = 8
HD = 128
GROUP = H // KVH
LOG2_SCALE = HD ** (-0.5) * math.log2(math.e)
STEP = 8.0
FLOOR = -4096.0
HIDDEN = -1e30
STATS = 16
VMEM_LIMIT = 12 * 1024 * 1024


def swap(value, axis, bits):
    devices = lax.axis_size(axis)
    return lax.ppermute(value, axis, [(i, i ^ bits) for i in range(devices)])


def from_behind(value, axis, by):
    devices = lax.axis_size(axis)
    return lax.ppermute(value, axis, [(i, (i + by) % devices) for i in range(devices)])


class Plan:
    def __init__(self, ctx, rows_here):
        self.ctx = ctx
        self.half = ctx // 2
        self.rows_here = rows_here
        self.rows = ctx * rows_here
        self.group_rows = GROUP * self.rows
        self.heads = H // self.half
        self.unit_heads = min(self.heads, GROUP)
        self.units = self.heads // self.unit_heads
        self.unit_rows = self.unit_heads * self.rows
        self.blocks = self.unit_rows // 128
        self.share_rows = self.units * self.unit_rows


def stat_rows(blocks):
    return -(-3 * blocks // 16) * 16


def local(kernel, out_shape, spaces, name, scratch=(), cost=None):
    return pl.pallas_call(
        kernel,
        out_shape=out_shape,
        in_specs=[pl.BlockSpec(memory_space=space) for space in spaces],
        out_specs=jax.tree.map(lambda _: pl.BlockSpec(memory_space=pltpu.VMEM), out_shape),
        scratch_shapes=list(scratch),
        compiler_params=pltpu.CompilerParams(vmem_limit_bytes=VMEM_LIMIT),
        cost_estimate=cost,
        name=name,
    )


def ready_kernel(plan, own_ref, held_ref, order_ref, one_hot_ref, sem):
    copy = pltpu.make_async_copy(own_ref, held_ref, sem)
    copy.start()
    me = lax.axis_index("ctx")
    low, high = me % plan.half, me // plan.half
    row = lax.broadcasted_iota(jnp.int32, (plan.group_rows, 128), 0)
    lane = lax.broadcasted_iota(jnp.int32, (plan.group_rows, 128), 1)
    query = lax.rem(row, plan.rows)
    device = lax.div(query, plan.rows_here)
    block = 2 * (lax.rem(device, plan.half) ^ low) + (lax.div(device, plan.half) ^ high)
    origin = (block * GROUP + lax.div(row, plan.rows)) * plan.rows_here + lax.rem(query, plan.rows_here)
    for at in range(0, plan.group_rows, 128):
        order_ref[:, at : at + 128] = jnp.where(lane + at == origin, 1.0, 0.0).astype(jnp.bfloat16)
    one_hot_ref[...] = jnp.where(query == lane, 1.0, 0.0).astype(jnp.bfloat16)
    copy.wait()


def ready(plan, own):
    return local(
        functools.partial(ready_kernel, plan),
        [
            pltpu.VMEM(own.shape, own.dtype),
            jax.ShapeDtypeStruct((plan.group_rows, plan.group_rows), jnp.bfloat16),
            jax.ShapeDtypeStruct((plan.group_rows, 128), jnp.bfloat16),
        ],
        [pltpu.HBM],
        "ready",
        [pltpu.SemaphoreType.DMA],
    )(pltpu.with_memory_space_constraint(own, pltpu.HBM))


def stage_kernel(plan, offset_ref, start_ref, cache_ref, staged_ref, bias_ref, sem):
    copy = pltpu.make_async_copy(cache_ref, staged_ref, sem)
    copy.start()
    span = cache_ref.shape[0]
    offset, start = offset_ref[0], start_ref[0]
    first = lax.axis_index("ctx") * span
    every = (first >= start) & (first + span - 1 <= offset)

    @pl.when(every)
    def _():
        bias_ref[...] = jnp.zeros_like(bias_ref)

    @pl.when(jnp.logical_not(every))
    def _():
        position = first + lax.broadcasted_iota(jnp.int32, (span, 128), 0)
        last = offset + lax.broadcasted_iota(jnp.int32, (span, 128), 1)
        shown = (position >= start) & (position <= last)
        bias_ref[...] = jnp.where(shown, 0.0, HIDDEN).astype(jnp.bfloat16)

    copy.wait()


def stage(plan, offsets, starts, cache):
    return local(
        functools.partial(stage_kernel, plan),
        [
            pltpu.VMEM(cache.shape, cache.dtype),
            jax.ShapeDtypeStruct((cache.shape[0], 128), jnp.bfloat16),
        ],
        [pltpu.SMEM, pltpu.SMEM, pltpu.HBM],
        "stage",
        [pltpu.SemaphoreType.DMA],
        pl.CostEstimate(flops=0, bytes_accessed=2 * cache.size * 2, transcendentals=0),
    )(offsets, starts, pltpu.with_memory_space_constraint(cache, pltpu.HBM))


def join_kernel(first_ref, second_ref, out_ref):
    rows = first_ref.shape[1]
    out_ref[:, :rows, :] = first_ref[...]
    out_ref[:, rows:, :] = second_ref[...]


def join(first, second):
    groups, rows, width = first.shape
    return local(
        join_kernel,
        jax.ShapeDtypeStruct((groups, 2 * rows, width), first.dtype),
        [pltpu.VMEM] * 2,
        "join",
    )(first, second)


def write_stats(ref, at, rows):
    values = []
    for peak, total in zip(rows[::2], rows[1::2]):
        high = total.astype(jnp.bfloat16).astype(jnp.float32)
        values += [peak, high, total - high]
    size = stat_rows(len(rows) // 2)
    index = lax.broadcasted_iota(jnp.int32, (size, 128), 0)
    table = jnp.zeros((size, 128), jnp.float32)
    for i, value in enumerate(values):
        table = jnp.where(index == i, value, table)
    ref[at : at + size, :] = table.astype(jnp.bfloat16)


def attend_kernel(plan, part, offset_ref, start_ref, *refs):
    *query_refs, cache_ref, bias_ref, order_ref, one_hot_ref, out_ref = refs[: -1 - (part == 0)]
    score_ref = refs[-1]
    value_ref, stat_ref, stat_at = (out_ref, refs[-2], 0) if part == 0 else (out_ref, out_ref, plan.share_rows)
    span = cache_ref.shape[0]
    me = lax.axis_index("ctx")
    first = me * span
    none = (first + span - 1 < start_ref[0]) | (first > offset_ref[0] + plan.rows - 1)
    mine = (me % plan.half) ^ part

    @pl.when(none)
    def _():
        value_ref[: plan.share_rows, :] = jnp.zeros((plan.share_rows, HD), value_ref.dtype)
        empty = [jnp.full((1, 128), FLOOR / STEP, jnp.float32), jnp.zeros((1, 128), jnp.float32)]
        write_stats(stat_ref, stat_at, empty * (plan.units * plan.blocks))

    @pl.when(jnp.logical_not(none))
    def _():
        row_at = pl.multiple_of((mine * plan.heads) % GROUP * plan.rows, plan.unit_rows)
        order = order_ref[pl.ds(row_at, plan.unit_rows), :]
        one_hot = one_hot_ref[pl.ds(row_at, plan.unit_rows), :]
        ones = jnp.ones((span, HD), jnp.bfloat16)
        groups = [(mine * plan.heads + unit * plan.unit_heads) // GROUP for unit in range(plan.units)]
        peaks = []
        for unit, group in enumerate(groups):
            stacked = jnp.concatenate([ref[group] for ref in query_refs], axis=0)
            queries = jnp.dot(order, stacked, preferred_element_type=jnp.float32)
            queries = jnp.concatenate([queries.astype(jnp.bfloat16), one_hot], axis=1)
            key_at = pl.multiple_of(group * HD, HD)
            keys = jnp.concatenate([cache_ref[:, pl.ds(key_at, HD)], bias_ref[...]], axis=1)
            scores = lax.dot_general(
                queries, keys, (((1,), (1,)), ((), ())), preferred_element_type=jnp.float32
            )
            score_ref[unit] = scores
            peak = [scores[:, at : at + 128] for at in range(0, span, 128)]
            while len(peak) > 1:
                peak = [jnp.maximum(*peak[i : i + 2]) for i in range(0, len(peak) - 1, 2)] + (
                    peak[-1:] if len(peak) % 2 else []
                )
            peak = jnp.max(peak[0], axis=1, keepdims=True) * LOG2_SCALE
            peak = jnp.maximum(jnp.ceil(peak * (1.0 / STEP)), FLOOR / STEP)
            peaks.append(jnp.broadcast_to(peak, (plan.unit_rows, 128)))
        same = lax.broadcasted_iota(jnp.int32, (128, 128), 0) == lax.broadcasted_iota(
            jnp.int32, (128, 128), 1
        )
        stats = []
        for unit, group in enumerate(groups):
            shift = jnp.concatenate([peaks[unit] * STEP] * (span // 128), axis=1)
            weights = jnp.exp2(score_ref[unit] * LOG2_SCALE - shift)
            value_at = pl.multiple_of((KVH + group) * HD, HD)
            values = jnp.concatenate([cache_ref[:, pl.ds(value_at, HD)], ones], axis=1)
            both = jnp.dot(weights.astype(jnp.bfloat16), values, preferred_element_type=jnp.float32)
            at = unit * plan.unit_rows
            value_ref[at : at + plan.unit_rows, :] = both[:, :HD].astype(value_ref.dtype)
            for block in range(0, plan.unit_rows, 128):
                for wide in (peaks[unit], both[:, HD:]):
                    chosen = jnp.where(same, wide[block : block + 128, :], 0.0)
                    stats.append(jnp.sum(chosen, axis=0, keepdims=True))
        write_stats(stat_ref, stat_at, stats)


def attend(plan, part, offsets, starts, queries, cache, *tables):
    span = cache.shape[0]
    size = stat_rows(plan.units * plan.blocks)
    if part == 0:
        out_shape = [
            jax.ShapeDtypeStruct((plan.share_rows, HD), jnp.float32),
            jax.ShapeDtypeStruct((size, HD), jnp.bfloat16),
        ]
    else:
        out_shape = [jax.ShapeDtypeStruct((plan.share_rows + size, HD), jnp.bfloat16)]
    return local(
        functools.partial(attend_kernel, plan, part),
        out_shape,
        [pltpu.SMEM] * 2 + [pltpu.VMEM] * (len(queries) + 1 + len(tables)),
        "attend",
        [pltpu.VMEM((plan.units, plan.unit_rows, span), jnp.float32)],
        pl.CostEstimate(
            flops=4 * plan.share_rows * span * HD,
            bytes_accessed=2 * plan.units * span * HD * 2,
            transcendentals=plan.share_rows * span,
        ),
    )(offsets, starts, *queries, cache, *tables)


def columns(rows):
    index = lax.broadcasted_iota(jnp.int32, (128, 128), 0)
    table = jnp.zeros((128, 128), jnp.float32)
    for i, row in enumerate(rows):
        table = jnp.where(index == i, row, table)
    turned = jnp.transpose(table)
    return [turned[:, i : i + 1] for i in range(len(rows))]


def factors(stats, block):
    parts = []
    for ref, at in stats:
        base = 3 * block // 16 * 16
        tile = ref[at + base : at + min(base + 32, stat_rows(block + 1)), :].astype(jnp.float32)
        begin = 3 * block - base
        parts.append([tile[begin + i : begin + i + 1] for i in range(3)])
    joint = functools.reduce(jnp.maximum, [peak for peak, _, _ in parts])
    scale = [jnp.exp2((peak - joint) * STEP) for peak, _, _ in parts]
    total = functools.reduce(jnp.add, [f * (high + low) for f, (_, high, low) in zip(scale, parts)])
    return joint, scale, total


def mix(refs, at, scale):
    terms = [f * ref[at : at + 128, :].astype(jnp.float32) for ref, f in zip(refs, scale)]
    return functools.reduce(jnp.add, terms)


def merge_kernel(plan, unit, wide_ref, stat_ref, *refs):
    *parts, out_ref, wide_out_ref = refs
    stats = [(stat_ref, 0)] + [(ref, plan.share_rows) for ref in parts]
    rows = []
    for block in range(plan.blocks):
        joint, scale, total = factors(stats, unit * plan.blocks + block)
        rows += [joint, total]
        to = block * 128
        mixed = mix([wide_ref] + parts, unit * plan.unit_rows + to, columns(scale))
        wide_out_ref[to : to + 128, :] = mixed
        out_ref[to : to + 128, :] = mixed.astype(jnp.bfloat16)
    write_stats(out_ref, plan.unit_rows, rows)


def merge(plan, unit, wide, stats, parts):
    rows = plan.unit_rows + stat_rows(plan.blocks)
    return local(
        functools.partial(merge_kernel, plan, unit),
        [
            jax.ShapeDtypeStruct((rows, HD), jnp.bfloat16),
            jax.ShapeDtypeStruct((plan.unit_rows, HD), jnp.float32),
        ],
        [pltpu.VMEM] * (len(parts) + 2),
        "merge",
    )(wide, stats, *parts)


def settle_kernel(plan, wide_ref, own_ref, other_ref, out_ref):
    stats = [(own_ref, plan.unit_rows), (other_ref, plan.unit_rows)]
    for block in range(plan.blocks):
        _, scale, total = factors(stats, block)
        done = mix([wide_ref, other_ref], block * 128, columns([f / total for f in scale]))
        done = done.astype(jnp.bfloat16)
        for row in range(0, 128, plan.rows):
            to = (block * 128 + row) // plan.rows * HD
            out_ref[:, to : to + HD] = done[row : row + plan.rows, :]


def settle(plan, wide, own, other):
    return local(
        functools.partial(settle_kernel, plan),
        jax.ShapeDtypeStruct((plan.rows, plan.unit_heads * HD), jnp.bfloat16),
        [pltpu.VMEM] * 3,
        "settle",
    )(wide, own, other)


def project_kernel(plan, part, unit, *refs):
    block_ref, weight_ref, *before, out_ref = refs
    depth = plan.unit_heads * HD
    share = (lax.axis_index("ctx") % plan.half) ^ part
    at = pl.multiple_of((share * plan.units + unit) * depth, depth)
    total = jnp.dot(block_ref[...], weight_ref[pl.ds(at, depth), :], preferred_element_type=jnp.float32)
    for ref in before:
        total = total + ref[...]
    out_ref[...] = total.astype(out_ref.dtype)


def project(plan, part, unit, block, weight, before, dtype):
    operands = [block, weight] + ([] if before is None else [before])
    return local(
        functools.partial(project_kernel, plan, part, unit),
        jax.ShapeDtypeStruct((plan.rows, weight.shape[1]), dtype),
        [pltpu.VMEM] * len(operands),
        "project",
    )(*operands)


def per_device(queries, cache, out_weight, offsets, starts):
    plan = Plan(lax.axis_size("ctx"), queries.shape[0])
    half = plan.half
    out_weight = pltpu.with_memory_space_constraint(out_weight, pltpu.VMEM)

    own = queries.reshape(plan.rows_here, KVH, GROUP, HD)
    own = own.transpose(1, 2, 0, 3).reshape(KVH, GROUP * plan.rows_here, HD)
    held, *order = ready(plan, own)
    staged, bias = stage(plan, offsets, starts, cache)
    staged = pltpu.with_memory_space_constraint(staged, pltpu.VMEM)
    pair = join(held, swap(own, "ctx", half))
    gathered = [pair] + [swap(pair, "ctx", k) for k in range(1, half)]

    received = []
    for part in reversed(range(1, half)):
        (piece,) = attend(plan, part, offsets, starts, gathered, staged, bias, *order)
        received.append(swap(piece, "ctx", part))
    wide, stats = attend(plan, 0, offsets, starts, gathered, staged, bias, *order)

    blocks = []
    for unit in range(plan.units):
        near, near_wide = merge(plan, unit, wide, stats, received)
        block = settle(plan, near_wide, near, swap(near, "ctx", half))
        blocks.append([block] + [swap(block, "ctx", k) for k in range(1, half)])

    steps = [(part, unit) for unit in range(plan.units) for part in range(half)]
    total = None
    for part, unit in steps:
        dtype = jnp.bfloat16 if (part, unit) == steps[-1] else jnp.float32
        total = project(plan, part, unit, blocks[unit][part], out_weight, total, dtype)
    return from_behind(total, "segment", 1)


def solution(mesh):
    in_specs = (
        P(("segment", "ctx"), None),
        P(("segment", "ctx"), None),
        P("segment", "ctx"),
        P("segment"),
        P("segment"),
    )
    out_specs = P("segment", "ctx")
    return jax.shard_map(
        per_device, mesh=mesh, in_specs=in_specs, out_specs=out_specs, check_vma=False
    )
```

time: 53.2 us -> 53.7 us (level)
  Pallas kernels: 7.93 us -> 16.7 us
  waiting for transfers between devices: 18.9 us -> 13.6 us
  starting transfers between devices: 23.3 us -> 21.1 us
  other arithmetic: 0.85 us -> 0.01 us
    pallas_call x11 -> x19, Pallas kernels: 7.93 us -> 16.7 us  [the longest x4 7.56 us: attend(): local(functools.partial(attend_kernel, plan, part), out_shape, [pltpu.SME...]
    ppermute x11 -> x15, waiting for transfers between devices: 15.2 us -> 9.86 us  [swap(): return lax.ppermute(value, axis, [(i, i ^ bits) for i in range(devices)])]
    ppermute x11 -> x15, starting transfers between devices: 23.3 us -> 21.1 us  [swap(): return lax.ppermute(value, axis, [(i, i ^ bits) for i in range(devices)])]
    concatenate x1 -> x0, other arithmetic: 0.85 us -> none  [per_device(): pair = jnp.concatenate([own, swap(own, 'ctx', half)], axis=1)]
  transfers between devices with their start and end apart: 12 -> 16, of which waited for: 7 -> 5; matrix products, arithmetic and copies ran while one was open for 0% -> 0% of each run, Pallas kernels for 11% -> 26%
where the time goes in v3:
time: 53.7 us; the launch traced here: 53.5 us
  starting transfers between devices  21.1 us (39%)
  Pallas kernels  16.7 us (31%)
  waiting for transfers between devices  13.6 us (25%)
  between operations  1.49 us (3%)
  local copies, waits for them, and re-layouts  0.65 us (1%)
    ppermute x15, starting transfers between devices, swap(): return lax.ppermute(value, axis, [(i, i ^ bits) for i in range(devices)])  21.1 us
    ppermute x15, waiting for transfers between devices, swap(): return lax.ppermute(value, axis, [(i, i ^ bits) for i in range(devices)])  9.86 us
    pallas_call x4, Pallas kernels, attend(): local(functools.partial(attend_kernel, plan, part), out_shape, [pltpu.SME...  7.56 us
    pallas_call x8, Pallas kernels, project(): local(functools.partial(project_kernel, plan, part, unit), jax.ShapeDtype...  3.8 us
    ppermute x1, waiting for transfers between devices, from_behind(): lax.ppermute(value, axis, [(i, (i + by) % devices) for i in range(devices)])  3.69 us
    pallas_call x1, Pallas kernels, stage(): local(functools.partial(stage_kernel, plan), [pltpu.VMEM(cache.shape, cac...  3.39 us
  transfers between devices with their start and end apart: 16, of which 5 were waited for; matrix products, arithmetic and copies ran while one was open for 0% of the time, Pallas kernels for 26%

profile of v3, /device:TPU:0, one launch (start us, length us, event | category | flops | bytes accessed | tf_op | source)
XLA Modules:
  0.0 53.5 jit_solution(12227576722738064290)
XLA Ops:
  0.0 4.0 %collective-permute-start = (bf16[8,32,128]{2,1,0:T(8,128)(2,1)}, bf16[8,32,128]{2,1,0:T(8,128)(2,1)S(1)}, u32[]{:S(2)}, u32[]{:S(2)}) collective-permute-start(bf16[8,32,128]{2,1,0:T(8,128)(2,1)} %bitcast.7), channel_id=1, source_target_pairs={{0,4},{1,5},{2,6},{3,7},{4,0},{5,1},{6,2},{7,3},{8,12},{9,13},{10,... | collective-permute-start | bytes 196616 | tf_op jit(solution)/shard_map/ppermute | solution.py:25
  4.0 0.9 %ready.1 = (bf16[8,32,128]{2,1,0:T(8,128)(2,1)S(1)}, bf16[256,256]{1,0:T(8,128)(2,1)S(1)}, bf16[256,128]{1,0:T(8,128)(2,1)S(1)}) custom-call(bf16[8,32,128]{2,1,0:T(8,128)(2,1)} %bitcast.8), custom_call_target="tpu_custom_call" | custom-call | tf_op jit(solution)/shard_map/ready/pallas_call | solution.py:83
  4.9 3.0 %collective-permute-done.second_ref = bf16[8,32,128]{2,1,0:T(8,128)(2,1)S(1)} collective-permute-done((bf16[8,32,128]{2,1,0:T(8,128)(2,1)}, bf16[8,32,128]{2,1,0:T(8,128)(2,1)S(1)}, u32[]{:S(2)}, u32[]{:S(2)}) %collective-permute-start) | collective-permute-done | bytes 65568 | tf_op jit(solution)/shard_map/ppermute | solution.py:25
  7.9 1.7 %collective-permute-start.3 = (bf16[8,64,128]{2,1,0:T(8,128)(2,1)S(1)}, bf16[8,64,128]{2,1,0:T(8,128)(2,1)S(1)}, u32[]{:S(2)}, u32[]{:S(2)}) collective-permute-start(bf16[8,64,128]{2,1,0:T(8,128)(2,1)S(1)} %join.1.refs_0_), channel_id=1, source_target_pairs={{0,3},{1,2},{2,1},{3,0},{4,7},{5,6},{6,5},{7,4},{8,11},{9,10},{10,... | collective-permute-start | bytes 393224 | tf_op jit(solution)/shard_map/ppermute | solution.py:25
  9.6 1.6 %collective-permute-start.2 = (bf16[8,64,128]{2,1,0:T(8,128)(2,1)S(1)}, bf16[8,64,128]{2,1,0:T(8,128)(2,1)S(1)}, u32[]{:S(2)}, u32[]{:S(2)}) collective-permute-start(bf16[8,64,128]{2,1,0:T(8,128)(2,1)S(1)} %join.1.refs_0_), channel_id=1, source_target_pairs={{0,2},{1,3},{2,0},{3,1},{4,6},{5,7},{6,4},{7,5},{8,10},{9,11},{10,... | collective-permute-start | bytes 393224 | tf_op jit(solution)/shard_map/ppermute | solution.py:25
  11.1 0.3 collective-permute-start.1
  12.8 3.4 %stage.1 = (bf16[2048,2048]{1,0:T(8,128)(2,1)S(1)}, bf16[2048,128]{1,0:T(8,128)(2,1)S(1)}) custom-call(s32[1]{0:T(128)S(6)} %copy.8.offset_ref, s32[1]{0:T(128)S(6)} %copy.9.start_ref, bf16[2048,2048]{1,0:T(8,128)(2,1)} %cache_ref.1), custom_call_target="tpu_custom_call" | custom-call | bytes 16777216 | tf_op jit(solution)/shard_map/stage/pallas_call | solution.py:119
  16.2 0.0 collective-permute-done.3.refs_3_
  16.2 1.9 %attend.5 = bf16[528,128]{1,0:T(8,128)(2,1)S(1)} custom-call(s32[1]{0:T(128)S(6)} %copy.8.offset_ref, s32[1]{0:T(128)S(6)} %copy.9.start_ref, bf16[8,64,128]{2,1,0:T(8,128)(2,1)S(1)} %join.1.refs_0_, bf16[8,64,128]{2,1,0:T(8,128)(2,1)S(1)} %collective-permute-done.1.refs_1_, bf16[8,64,128]{2,1,0:T(8,128)(2,1)S(1)} %collective-permute-done.2.refs_2_, ...), custom_call_target="tpu_custom_call" | custom-call | flops 536870912 | bytes 2097152 | tf_op jit(solution)/shard_map/attend/pallas_call | solution.py:232
  18.1 2.0 %collective-permute-start.4 = (bf16[528,128]{1,0:T(8,128)(2,1)S(1)}, bf16[528,128]{1,0:T(8,128)(2,1)S(1)}, u32[]{:S(2)}, u32[]{:S(2)}) collective-permute-start(bf16[528,128]{1,0:T(8,128)(2,1)S(1)} %attend.5), channel_id=1, source_target_pairs={{0,3},{1,2},{2,1},{3,0},{4,7},{5,6},{6,5},{7,4},{8,11},{9,10},{10,... | collective-permute-start | bytes 405512 | tf_op jit(solution)/shard_map/ppermute | solution.py:25
  20.1 1.9 %attend.6 = bf16[528,128]{1,0:T(8,128)(2,1)S(1)} custom-call(s32[1]{0:T(128)S(6)} %copy.8.offset_ref, s32[1]{0:T(128)S(6)} %copy.9.start_ref, bf16[8,64,128]{2,1,0:T(8,128)(2,1)S(1)} %join.1.refs_0_, bf16[8,64,128]{2,1,0:T(8,128)(2,1)S(1)} %collective-permute-done.1.refs_1_, bf16[8,64,128]{2,1,0:T(8,128)(2,1)S(1)} %collective-permute-done.2.refs_2_, ...), custom_call_target="tpu_custom_call" | custom-call | flops 536870912 | bytes 2097152 | tf_op jit(solution)/shard_map/attend/pallas_call | solution.py:232
  22.1 0.0 slice-start.2
  22.1 1.2 %collective-permute-start.5 = (bf16[528,128]{1,0:T(8,128)(2,1)S(1)}, bf16[528,128]{1,0:T(8,128)(2,1)S(1)}, u32[]{:S(2)}, u32[]{:S(2)}) collective-permute-start(bf16[528,128]{1,0:T(8,128)(2,1)S(1)} %attend.6), channel_id=1, source_target_pairs={{0,2},{1,3},{2,0},{3,1},{4,6},{5,7},{6,4},{7,5},{8,10},{9,11},{10,... | collective-permute-start | bytes 405512 | tf_op jit(solution)/shard_map/ppermute | solution.py:25
  23.3 1.9 %attend.7 = bf16[528,128]{1,0:T(8,128)(2,1)S(1)} custom-call(s32[1]{0:T(128)S(6)} %copy.8.offset_ref, s32[1]{0:T(128)S(6)} %copy.9.start_ref, bf16[8,64,128]{2,1,0:T(8,128)(2,1)S(1)} %join.1.refs_0_, bf16[8,64,128]{2,1,0:T(8,128)(2,1)S(1)} %collective-permute-done.1.refs_1_, bf16[8,64,128]{2,1,0:T(8,128)(2,1)S(1)} %collective-permute-done.2.refs_2_, ...), custom_call_target="tpu_custom_call" | custom-call | flops 536870912 | bytes 2097152 | tf_op jit(solution)/shard_map/attend/pallas_call | solution.py:232
  25.2 0.0 slice-start.3
  25.2 0.4 collective-permute-start.6
  25.6 1.8 %attend.4 = (f32[512,128]{1,0:T(8,128)S(1)}, bf16[16,128]{1,0:T(8,128)(2,1)S(1)}) custom-call(s32[1]{0:T(128)S(6)} %copy.8.offset_ref, s32[1]{0:T(128)S(6)} %copy.9.start_ref, bf16[8,64,128]{2,1,0:T(8,128)(2,1)S(1)} %join.1.refs_0_, bf16[8,64,128]{2,1,0:T(8,128)(2,1)S(1)} %collective-permute-done.1.refs_1_, ...), custom_call_target="tpu_custom_call" | custom-call | flops 536870912 | bytes 2097152 | tf_op jit(solution)/shard_map/attend/pallas_call | solution.py:232
  27.4 2.8 %collective-permute-done.6.refs_2_ = bf16[528,128]{1,0:T(8,128)(2,1)S(1)} collective-permute-done((bf16[528,128]{1,0:T(8,128)(2,1)S(1)}, bf16[528,128]{1,0:T(8,128)(2,1)S(1)}, u32[]{:S(2)}, u32[]{:S(2)}) %collective-permute-start.6) | collective-permute-done | bytes 135200 | tf_op jit(solution)/shard_map/ppermute | solution.py:25
  30.3 0.3 merge.3
  30.6 2.3 %collective-permute-start.11 = (bf16[272,128]{1,0:T(8,128)(2,1)S(1)}, bf16[272,128]{1,0:T(8,128)(2,1)S(1)}, u32[]{:S(2)}, u32[]{:S(2)}) collective-permute-start(bf16[272,128]{1,0:T(8,128)(2,1)S(1)} %get-tuple-element.26.own_ref), channel_id=1, source_target_pairs={{0,4},{1,5},{2,6},{3,7},{4,0},{5,1},{6,2},{7,3},{8,12},{9,13},{10,... | collective-permute-start | bytes 208904 | tf_op jit(solution)/shard_map/ppermute | solution.py:25
  32.9 0.3 merge.2
  33.2 0.7 %collective-permute-start.7 = (bf16[272,128]{1,0:T(8,128)(2,1)S(1)}, bf16[272,128]{1,0:T(8,128)(2,1)S(1)}, u32[]{:S(2)}, u32[]{:S(2)}) collective-permute-start(bf16[272,128]{1,0:T(8,128)(2,1)S(1)} %get-tuple-element.24.own_ref), channel_id=1, source_target_pairs={{0,4},{1,5},{2,6},{3,7},{4,0},{5,1},{6,2},{7,3},{8,12},{9,13},{10,... | collective-permute-start | bytes 208904 | tf_op jit(solution)/shard_map/ppermute | solution.py:25
  34.0 3.7 %collective-permute-done.11.other_ref = bf16[272,128]{1,0:T(8,128)(2,1)S(1)} collective-permute-done((bf16[272,128]{1,0:T(8,128)(2,1)S(1)}, bf16[272,128]{1,0:T(8,128)(2,1)S(1)}, u32[]{:S(2)}, u32[]{:S(2)}) %collective-permute-start.11) | collective-permute-done | bytes 69664 | tf_op jit(solution)/shard_map/ppermute | solution.py:25
  37.7 0.2 settle.3.refs_0_
  37.9 0.7 %collective-permute-start.14 = (bf16[32,1024]{1,0:T(8,128)(2,1)S(1)}, bf16[32,1024]{1,0:T(8,128)(2,1)S(1)}, u32[]{:S(2)}, u32[]{:S(2)}) collective-permute-start(bf16[32,1024]{1,0:T(8,128)(2,1)S(1)} %settle.3.refs_0_), channel_id=1, source_target_pairs={{0,1},{1,0},{2,3},{3,2},{4,5},{5,4},{6,7},{7,6},{8,9},{9,8},{10,11... | collective-permute-start | bytes 196616 | tf_op jit(solution)/shard_map/ppermute | solution.py:25
  38.6 0.3 collective-permute-start.13
  38.8 2.6 %collective-permute-start.12 = (bf16[32,1024]{1,0:T(8,128)(2,1)S(1)}, bf16[32,1024]{1,0:T(8,128)(2,1)S(1)}, u32[]{:S(2)}, u32[]{:S(2)}) collective-permute-start(bf16[32,1024]{1,0:T(8,128)(2,1)S(1)} %settle.3.refs_0_), channel_id=1, source_target_pairs={{0,3},{1,2},{2,1},{3,0},{4,7},{5,6},{6,5},{7,4},{8,11},{9,10},{10,... | collective-permute-start | bytes 196616 | tf_op jit(solution)/shard_map/ppermute | solution.py:25
  41.5 0.2 settle.2.refs_0_
  41.7 0.7 %collective-permute-start.10 = (bf16[32,1024]{1,0:T(8,128)(2,1)S(1)}, bf16[32,1024]{1,0:T(8,128)(2,1)S(1)}, u32[]{:S(2)}, u32[]{:S(2)}) collective-permute-start(bf16[32,1024]{1,0:T(8,128)(2,1)S(1)} %settle.2.refs_0_), channel_id=1, source_target_pairs={{0,1},{1,0},{2,3},{3,2},{4,5},{5,4},{6,7},{7,6},{8,9},{9,8},{10,11... | collective-permute-start | bytes 196616 | tf_op jit(solution)/shard_map/ppermute | solution.py:25
  42.4 0.3 collective-permute-start.9
  42.6 0.3 collective-permute-done.14.refs_0_
  42.9 2.3 %collective-permute-start.8 = (bf16[32,1024]{1,0:T(8,128)(2,1)S(1)}, bf16[32,1024]{1,0:T(8,128)(2,1)S(1)}, u32[]{:S(2)}, u32[]{:S(2)}) collective-permute-start(bf16[32,1024]{1,0:T(8,128)(2,1)S(1)} %settle.2.refs_0_), channel_id=1, source_target_pairs={{0,3},{1,2},{2,1},{3,0},{4,7},{5,6},{6,5},{7,4},{8,11},{9,10},{10,... | collective-permute-start | bytes 196616 | tf_op jit(solution)/shard_map/ppermute | solution.py:25
  45.3 0.5 project.8.refs_2_
  45.7 0.5 project.9.refs_2_
  46.2 0.0 collective-permute-done.13.refs_0_
  46.2 0.5 project.10.refs_2_
  46.7 0.0 collective-permute-done.12.refs_0_
  46.7 0.5 project.11.refs_2_
  47.2 0.5 project.12.refs_2_
  47.7 0.0 collective-permute-done.10.refs_0_
  47.7 0.5 project.13.refs_2_
  48.2 0.0 collective-permute-done.9.refs_0_
  48.2 0.5 project.14.refs_2_
  48.7 0.0 collective-permute-done.8.refs_0_
  48.7 0.5 project.15
  49.2 0.0 collective-permute-start.15
  49.2 3.7 %collective-permute-done.15 = bf16[32,1024]{1,0:T(8,128)(2,1)S(1)} collective-permute-done((bf16[32,1024]{1,0:T(8,128)(2,1)S(1)}, bf16[32,1024]{1,0:T(8,128)(2,1)S(1)}, u32[]{:S(2)}, u32[]{:S(2)}) %collective-permute-start.15) | collective-permute-done | bytes 65568 | tf_op jit(solution)/shard_map/ppermute | solution.py:30
  52.9 0.6 %copy.10 = bf16[32,1024]{1,0:T(8,128)(2,1)} copy(bf16[32,1024]{1,0:T(8,128)(2,1)S(1)} %collective-permute-done.15) | data formatting | bytes 131072
  (13 shorter events, 0.0 us)
Async XLA Ops:
  0.0 7.9 %collective-permute-start = (bf16[8,32,128]{2,1,0:T(8,128)(2,1)}, bf16[8,32,128]{2,1,0:T(8,128)(2,1)S(1)}, u32[]{:S(2)}, u32[]{:S(2)}) collective-permute-start(bf16[8,32,128]{2,1,0:T(8,128)(2,1)} %bitcast.7), channel_id=1, source_target_pairs={{0,4},{1,5},{2,6},{3,7},{4,0},{5,1},{6,2},{7,3},{8,12},{9,13},{10,... | collective-permute-start | bytes 196616 | tf_op jit(solution)/shard_map/ppermute | solution.py:25
  7.9 8.3 %collective-permute-start.3 = (bf16[8,64,128]{2,1,0:T(8,128)(2,1)S(1)}, bf16[8,64,128]{2,1,0:T(8,128)(2,1)S(1)}, u32[]{:S(2)}, u32[]{:S(2)}) collective-permute-start(bf16[8,64,128]{2,1,0:T(8,128)(2,1)S(1)} %join.1.refs_0_), channel_id=1, source_target_pairs={{0,3},{1,2},{2,1},{3,0},{4,7},{5,6},{6,5},{7,4},{8,11},{9,10},{10,... | collective-permute-start | bytes 393224 | tf_op jit(solution)/shard_map/ppermute | solution.py:25
  9.6 6.6 %collective-permute-start.2 = (bf16[8,64,128]{2,1,0:T(8,128)(2,1)S(1)}, bf16[8,64,128]{2,1,0:T(8,128)(2,1)S(1)}, u32[]{:S(2)}, u32[]{:S(2)}) collective-permute-start(bf16[8,64,128]{2,1,0:T(8,128)(2,1)S(1)} %join.1.refs_0_), channel_id=1, source_target_pairs={{0,2},{1,3},{2,0},{3,1},{4,6},{5,7},{6,4},{7,5},{8,10},{9,11},{10,... | collective-permute-start | bytes 393224 | tf_op jit(solution)/shard_map/ppermute | solution.py:25
  11.1 5.0 %collective-permute-start.1 = (bf16[8,64,128]{2,1,0:T(8,128)(2,1)S(1)}, bf16[8,64,128]{2,1,0:T(8,128)(2,1)S(1)}, u32[]{:S(2)}, u32[]{:S(2)}) collective-permute-start(bf16[8,64,128]{2,1,0:T(8,128)(2,1)S(1)} %join.1.refs_0_), channel_id=1, source_target_pairs={{0,1},{1,0},{2,3},{3,2},{4,5},{5,4},{6,7},{7,6},{8,9},{9,8},{10,11... | collective-permute-start | bytes 393224 | tf_op jit(solution)/shard_map/ppermute | solution.py:25
  18.1 9.3 %collective-permute-start.4 = (bf16[528,128]{1,0:T(8,128)(2,1)S(1)}, bf16[528,128]{1,0:T(8,128)(2,1)S(1)}, u32[]{:S(2)}, u32[]{:S(2)}) collective-permute-start(bf16[528,128]{1,0:T(8,128)(2,1)S(1)} %attend.5), channel_id=1, source_target_pairs={{0,3},{1,2},{2,1},{3,0},{4,7},{5,6},{6,5},{7,4},{8,11},{9,10},{10,... | collective-permute-start | bytes 405512 | tf_op jit(solution)/shard_map/ppermute | solution.py:25
  20.1 25.1 %slice-start = ((s8[16777216]{0:T(1024)(128)(4,1)}), s8[4194304]{0:T(1024)(128)(4,1)S(1)}, s32[]{:S(2)}) async-start(s8[16777216]{0:T(1024)(128)(4,1)} %bitcast.5), calls=%async_computation | async-start | bytes 8388608
  20.1 25.1 %slice-start.1 = ((s8[16777216]{0:T(1024)(128)(4,1)}), s8[4194304]{0:T(1024)(128)(4,1)S(1)}, s32[]{:S(2)}) async-start(s8[16777216]{0:T(1024)(128)(4,1)} %bitcast.5), calls=%async_computation.1 | async-start | bytes 8388608
  22.1 23.2 %slice-start.2 = ((s8[16777216]{0:T(1024)(128)(4,1)}), s8[4194304]{0:T(1024)(128)(4,1)S(1)}, s32[]{:S(2)}) async-start(s8[16777216]{0:T(1024)(128)(4,1)} %bitcast.5), calls=%async_computation.2 | async-start | bytes 8388608
  22.1 5.4 %collective-permute-start.5 = (bf16[528,128]{1,0:T(8,128)(2,1)S(1)}, bf16[528,128]{1,0:T(8,128)(2,1)S(1)}, u32[]{:S(2)}, u32[]{:S(2)}) collective-permute-start(bf16[528,128]{1,0:T(8,128)(2,1)S(1)} %attend.6), channel_id=1, source_target_pairs={{0,2},{1,3},{2,0},{3,1},{4,6},{5,7},{6,4},{7,5},{8,10},{9,11},{10,... | collective-permute-start | bytes 405512 | tf_op jit(solution)/shard_map/ppermute | solution.py:25
  25.2 20.1 %slice-start.3 = ((s8[16777216]{0:T(1024)(128)(4,1)}), s8[4194304]{0:T(1024)(128)(4,1)S(1)}, s32[]{:S(2)}) async-start(s8[16777216]{0:T(1024)(128)(4,1)} %bitcast.5), calls=%async_computation.3 | async-start | bytes 8388608
  25.2 5.1 %collective-permute-start.6 = (bf16[528,128]{1,0:T(8,128)(2,1)S(1)}, bf16[528,128]{1,0:T(8,128)(2,1)S(1)}, u32[]{:S(2)}, u32[]{:S(2)}) collective-permute-start(bf16[528,128]{1,0:T(8,128)(2,1)S(1)} %attend.7), channel_id=1, source_target_pairs={{0,1},{1,0},{2,3},{3,2},{4,5},{5,4},{6,7},{7,6},{8,9},{9,8},{10,11... | collective-permute-start | bytes 405512 | tf_op jit(solution)/shard_map/ppermute | solution.py:25
  30.6 7.1 %collective-permute-start.11 = (bf16[272,128]{1,0:T(8,128)(2,1)S(1)}, bf16[272,128]{1,0:T(8,128)(2,1)S(1)}, u32[]{:S(2)}, u32[]{:S(2)}) collective-permute-start(bf16[272,128]{1,0:T(8,128)(2,1)S(1)} %get-tuple-element.26.own_ref), channel_id=1, source_target_pairs={{0,4},{1,5},{2,6},{3,7},{4,0},{5,1},{6,2},{7,3},{8,12},{9,13},{10,... | collective-permute-start | bytes 208904 | tf_op jit(solution)/shard_map/ppermute | solution.py:25
  33.2 8.2 %collective-permute-start.7 = (bf16[272,128]{1,0:T(8,128)(2,1)S(1)}, bf16[272,128]{1,0:T(8,128)(2,1)S(1)}, u32[]{:S(2)}, u32[]{:S(2)}) collective-permute-start(bf16[272,128]{1,0:T(8,128)(2,1)S(1)} %get-tuple-element.24.own_ref), channel_id=1, source_target_pairs={{0,4},{1,5},{2,6},{3,7},{4,0},{5,1},{6,2},{7,3},{8,12},{9,13},{10,... | collective-permute-start | bytes 208904 | tf_op jit(solution)/shard_map/ppermute | solution.py:25
  37.9 5.0 %collective-permute-start.14 = (bf16[32,1024]{1,0:T(8,128)(2,1)S(1)}, bf16[32,1024]{1,0:T(8,128)(2,1)S(1)}, u32[]{:S(2)}, u32[]{:S(2)}) collective-permute-start(bf16[32,1024]{1,0:T(8,128)(2,1)S(1)} %settle.3.refs_0_), channel_id=1, source_target_pairs={{0,1},{1,0},{2,3},{3,2},{4,5},{5,4},{6,7},{7,6},{8,9},{9,8},{10,11... | collective-permute-start | bytes 196616 | tf_op jit(solution)/shard_map/ppermute | solution.py:25
  38.6 7.7 %collective-permute-start.13 = (bf16[32,1024]{1,0:T(8,128)(2,1)S(1)}, bf16[32,1024]{1,0:T(8,128)(2,1)S(1)}, u32[]{:S(2)}, u32[]{:S(2)}) collective-permute-start(bf16[32,1024]{1,0:T(8,128)(2,1)S(1)} %settle.3.refs_0_), channel_id=1, source_target_pairs={{0,2},{1,3},{2,0},{3,1},{4,6},{5,7},{6,4},{7,5},{8,10},{9,11},{10,... | collective-permute-start | bytes 196616 | tf_op jit(solution)/shard_map/ppermute | solution.py:25
  38.8 7.9 %collective-permute-start.12 = (bf16[32,1024]{1,0:T(8,128)(2,1)S(1)}, bf16[32,1024]{1,0:T(8,128)(2,1)S(1)}, u32[]{:S(2)}, u32[]{:S(2)}) collective-permute-start(bf16[32,1024]{1,0:T(8,128)(2,1)S(1)} %settle.3.refs_0_), channel_id=1, source_target_pairs={{0,3},{1,2},{2,1},{3,0},{4,7},{5,6},{6,5},{7,4},{8,11},{9,10},{10,... | collective-permute-start | bytes 196616 | tf_op jit(solution)/shard_map/ppermute | solution.py:25
  41.7 6.0 %collective-permute-start.10 = (bf16[32,1024]{1,0:T(8,128)(2,1)S(1)}, bf16[32,1024]{1,0:T(8,128)(2,1)S(1)}, u32[]{:S(2)}, u32[]{:S(2)}) collective-permute-start(bf16[32,1024]{1,0:T(8,128)(2,1)S(1)} %settle.2.refs_0_), channel_id=1, source_target_pairs={{0,1},{1,0},{2,3},{3,2},{4,5},{5,4},{6,7},{7,6},{8,9},{9,8},{10,11... | collective-permute-start | bytes 196616 | tf_op jit(solution)/shard_map/ppermute | solution.py:25
  42.4 5.8 %collective-permute-start.9 = (bf16[32,1024]{1,0:T(8,128)(2,1)S(1)}, bf16[32,1024]{1,0:T(8,128)(2,1)S(1)}, u32[]{:S(2)}, u32[]{:S(2)}) collective-permute-start(bf16[32,1024]{1,0:T(8,128)(2,1)S(1)} %settle.2.refs_0_), channel_id=1, source_target_pairs={{0,2},{1,3},{2,0},{3,1},{4,6},{5,7},{6,4},{7,5},{8,10},{9,11},{10,... | collective-permute-start | bytes 196616 | tf_op jit(solution)/shard_map/ppermute | solution.py:25
  42.9 5.8 %collective-permute-start.8 = (bf16[32,1024]{1,0:T(8,128)(2,1)S(1)}, bf16[32,1024]{1,0:T(8,128)(2,1)S(1)}, u32[]{:S(2)}, u32[]{:S(2)}) collective-permute-start(bf16[32,1024]{1,0:T(8,128)(2,1)S(1)} %settle.2.refs_0_), channel_id=1, source_target_pairs={{0,3},{1,2},{2,1},{3,0},{4,7},{5,6},{6,5},{7,4},{8,11},{9,10},{10,... | collective-permute-start | bytes 196616 | tf_op jit(solution)/shard_map/ppermute | solution.py:25
  49.2 3.7 %collective-permute-start.15 = (bf16[32,1024]{1,0:T(8,128)(2,1)S(1)}, bf16[32,1024]{1,0:T(8,128)(2,1)S(1)}, u32[]{:S(2)}, u32[]{:S(2)}) collective-permute-start(bf16[32,1024]{1,0:T(8,128)(2,1)S(1)} %project.15), channel_id=1, source_target_pairs={{0,8},{8,16},{16,24},{24,0},{1,9},{9,17},{17,25},{25,1},{2,10},{10... | collective-permute-start | bytes 196616 | tf_op jit(solution)/shard_map/ppermute | solution.py:30

commit v4 on v3

v4 whole, which is shorter than its diff:
```python
import functools
import math

import jax
import jax.numpy as jnp
from jax import lax
from jax.experimental import pallas as pl
from jax.experimental.pallas import tpu as pltpu
from jax.sharding import PartitionSpec as P

H = 64
KVH = 8
HD = 128
GROUP = H // KVH
LOG2_SCALE = HD ** (-0.5) * math.log2(math.e)
STEP = 8.0
FLOOR = -4096.0
HIDDEN = -1e30
STATS = 16
VMEM_LIMIT = 12 * 1024 * 1024


def swap(value, axis, bits):
    devices = lax.axis_size(axis)
    return lax.ppermute(value, axis, [(i, i ^ bits) for i in range(devices)])


def from_behind(value, axis, by):
    devices = lax.axis_size(axis)
    return lax.ppermute(value, axis, [(i, (i + by) % devices) for i in range(devices)])


class Plan:
    def __init__(self, ctx, rows_here):
        self.ctx = ctx
        self.half = ctx // 2
        self.fold = self.half // 2
        self.across = self.half | self.fold
        self.rows_here = rows_here
        self.rows = ctx * rows_here
        self.group_rows = GROUP * self.rows
        self.heads = H // self.half
        self.unit_heads = min(self.heads, GROUP)
        self.units = self.heads // self.unit_heads
        self.unit_rows = self.unit_heads * self.rows
        self.blocks = self.unit_rows // 128
        self.share_rows = self.units * self.unit_rows

    def share(self, part):
        me = lax.axis_index("ctx")
        return (me % self.half) ^ (me // self.half * self.fold) ^ part


def stat_rows(blocks):
    return -(-3 * blocks // 16) * 16


def local(kernel, out_shape, spaces, name, scratch=(), cost=None):
    return pl.pallas_call(
        kernel,
        out_shape=out_shape,
        in_specs=[pl.BlockSpec(memory_space=space) for space in spaces],
        out_specs=jax.tree.map(lambda _: pl.BlockSpec(memory_space=pltpu.VMEM), out_shape),
        scratch_shapes=list(scratch),
        compiler_params=pltpu.CompilerParams(vmem_limit_bytes=VMEM_LIMIT),
        cost_estimate=cost,
        name=name,
    )


def ready_kernel(plan, offset_ref, start_ref, own_ref, held_ref, order_ref, one_hot_ref, bias_ref, sem):
    copy = pltpu.make_async_copy(own_ref, held_ref, sem)
    copy.start()
    me = lax.axis_index("ctx")
    low, high = me % plan.half, me // plan.half
    row = lax.broadcasted_iota(jnp.int32, (plan.group_rows, 128), 0)
    lane = lax.broadcasted_iota(jnp.int32, (plan.group_rows, 128), 1)
    query = lax.rem(row, plan.rows)
    device = lax.div(query, plan.rows_here)
    block = 2 * (lax.rem(device, plan.half) ^ low) + (lax.div(device, plan.half) ^ high)
    origin = (block * GROUP + lax.div(row, plan.rows)) * plan.rows_here + lax.rem(query, plan.rows_here)
    for at in range(0, plan.group_rows, 128):
        order_ref[:, at : at + 128] = jnp.where(lane + at == origin, 1.0, 0.0).astype(jnp.bfloat16)
    one_hot_ref[...] = jnp.where(query == lane, 1.0, 0.0).astype(jnp.bfloat16)
    span = bias_ref.shape[0]
    offset, start = offset_ref[0], start_ref[0]
    first = me * span
    every = (first >= start) & (first + span - 1 <= offset)

    @pl.when(every)
    def _():
        bias_ref[...] = jnp.zeros_like(bias_ref)

    @pl.when(jnp.logical_not(every))
    def _():
        position = first + lax.broadcasted_iota(jnp.int32, (span, 128), 0)
        last = offset + lax.broadcasted_iota(jnp.int32, (span, 128), 1)
        shown = (position >= start) & (position <= last)
        bias_ref[...] = jnp.where(shown, 0.0, HIDDEN).astype(jnp.bfloat16)

    copy.wait()


def ready(plan, span, offsets, starts, own):
    return local(
        functools.partial(ready_kernel, plan),
        [
            pltpu.VMEM(own.shape, own.dtype),
            jax.ShapeDtypeStruct((plan.group_rows, plan.group_rows), jnp.bfloat16),
            jax.ShapeDtypeStruct((plan.group_rows, 128), jnp.bfloat16),
            jax.ShapeDtypeStruct((span, 128), jnp.bfloat16),
        ],
        [pltpu.SMEM, pltpu.SMEM, pltpu.HBM],
        "ready",
        [pltpu.SemaphoreType.DMA],
        pl.CostEstimate(flops=8_000_000_000, bytes_accessed=4 * span * HD, transcendentals=0),
    )(offsets, starts, pltpu.with_memory_space_constraint(own, pltpu.HBM))


def write_stats(ref, at, rows):
    values = []
    for peak, total in zip(rows[::2], rows[1::2]):
        high = total.astype(jnp.bfloat16).astype(jnp.float32)
        values += [peak, high, total - high]
    size = stat_rows(len(rows) // 2)
    index = lax.broadcasted_iota(jnp.int32, (size, 128), 0)
    table = jnp.zeros((size, 128), jnp.float32)
    for i, value in enumerate(values):
        table = jnp.where(index == i, value, table)
    ref[at : at + size, :] = table.astype(jnp.bfloat16)


def attend_kernel(plan, part, *refs):
    *query_refs, cache_ref, bias_ref, order_ref, one_hot_ref, out_ref = refs[: -1 - (part == 0)]
    score_ref = refs[-1]
    value_ref, stat_ref, stat_at = (out_ref, refs[-2], 0) if part == 0 else (out_ref, out_ref, plan.share_rows)
    span = cache_ref.shape[0]
    mine = plan.share(part)
    row_at = pl.multiple_of((mine * plan.heads) % GROUP * plan.rows, plan.unit_rows)
    order = order_ref[pl.ds(row_at, plan.unit_rows), :]
    one_hot = one_hot_ref[pl.ds(row_at, plan.unit_rows), :]
    ones = jnp.ones((span, HD), jnp.bfloat16)
    groups = [(mine * plan.heads + unit * plan.unit_heads) // GROUP for unit in range(plan.units)]
    peaks = []
    for unit, group in enumerate(groups):
        stacked = jnp.concatenate([ref[group] for ref in query_refs], axis=0)
        queries = jnp.dot(order, stacked, preferred_element_type=jnp.float32)
        queries = jnp.concatenate([queries.astype(jnp.bfloat16), one_hot], axis=1)
        key_at = pl.multiple_of(group * HD, HD)
        keys = jnp.concatenate([cache_ref[:, pl.ds(key_at, HD)], bias_ref[...]], axis=1)
        scores = lax.dot_general(queries, keys, (((1,), (1,)), ((), ())), preferred_element_type=jnp.float32)
        score_ref[unit] = scores
        peak = [scores[:, at : at + 128] for at in range(0, span, 128)]
        while len(peak) > 1:
            peak = [jnp.maximum(*peak[i : i + 2]) for i in range(0, len(peak) - 1, 2)] + (
                peak[-1:] if len(peak) % 2 else []
            )
        peak = jnp.max(peak[0], axis=1, keepdims=True) * LOG2_SCALE
        peak = jnp.maximum(jnp.ceil(peak * (1.0 / STEP)), FLOOR / STEP)
        peaks.append(jnp.broadcast_to(peak, (plan.unit_rows, 128)))
    same = lax.broadcasted_iota(jnp.int32, (128, 128), 0) == lax.broadcasted_iota(jnp.int32, (128, 128), 1)
    stats = []
    for unit, group in enumerate(groups):
        shift = jnp.concatenate([peaks[unit] * STEP] * (span // 128), axis=1)
        weights = jnp.exp2(score_ref[unit] * LOG2_SCALE - shift)
        value_at = pl.multiple_of((KVH + group) * HD, HD)
        values = jnp.concatenate([cache_ref[:, pl.ds(value_at, HD)], ones], axis=1)
        both = jnp.dot(weights.astype(jnp.bfloat16), values, preferred_element_type=jnp.float32)
        at = unit * plan.unit_rows
        value_ref[at : at + plan.unit_rows, :] = both[:, :HD].astype(value_ref.dtype)
        for block in range(0, plan.unit_rows, 128):
            for wide in (peaks[unit], both[:, HD:]):
                chosen = jnp.where(same, wide[block : block + 128, :], 0.0)
                stats.append(jnp.sum(chosen, axis=0, keepdims=True))
    write_stats(stat_ref, stat_at, stats)


def attend(plan, part, queries, cache, *tables):
    span = cache.shape[0]
    size = stat_rows(plan.units * plan.blocks)
    if part == 0:
        out_shape = [
            jax.ShapeDtypeStruct((plan.share_rows, HD), jnp.float32),
            jax.ShapeDtypeStruct((size, HD), jnp.bfloat16),
        ]
    else:
        out_shape = [jax.ShapeDtypeStruct((plan.share_rows + size, HD), jnp.bfloat16)]
    return local(
        functools.partial(attend_kernel, plan, part),
        out_shape,
        [pltpu.VMEM] * (len(queries) + 1 + len(tables)),
        "attend",
        [pltpu.VMEM((plan.units, plan.unit_rows, span), jnp.float32)],
        pl.CostEstimate(
            flops=4 * plan.share_rows * span * HD,
            bytes_accessed=2 * plan.units * span * HD * 2,
            transcendentals=plan.share_rows * span,
        ),
    )(*queries, cache, *tables)


def columns(rows):
    index = lax.broadcasted_iota(jnp.int32, (128, 128), 0)
    table = jnp.zeros((128, 128), jnp.float32)
    for i, row in enumerate(rows):
        table = jnp.where(index == i, row, table)
    turned = jnp.transpose(table)
    return [turned[:, i : i + 1] for i in range(len(rows))]


def factors(stats, block):
    parts = []
    for ref, at in stats:
        base = 3 * block // 16 * 16
        tile = ref[at + base : at + min(base + 32, stat_rows(block + 1)), :].astype(jnp.float32)
        begin = 3 * block - base
        parts.append([tile[begin + i : begin + i + 1] for i in range(3)])
    joint = functools.reduce(jnp.maximum, [peak for peak, _, _ in parts])
    scale = [jnp.exp2((peak - joint) * STEP) for peak, _, _ in parts]
    total = functools.reduce(jnp.add, [f * (high + low) for f, (_, high, low) in zip(scale, parts)])
    return joint, scale, total


def mix(refs, at, scale):
    terms = [f * ref[at : at + 128, :].astype(jnp.float32) for ref, f in zip(refs, scale)]
    return functools.reduce(jnp.add, terms)


def merge_kernel(plan, wide_ref, stat_ref, *refs):
    *parts, out_ref, wide_out_ref = refs
    stats = [(stat_ref, 0)] + [(ref, plan.share_rows) for ref in parts]
    rows = []
    for block in range(plan.units * plan.blocks):
        joint, scale, total = factors(stats, block)
        rows += [joint, total]
        at = block * 128
        mixed = mix([wide_ref] + parts, at, columns(scale))
        wide_out_ref[at : at + 128, :] = mixed
        out_ref[at : at + 128, :] = mixed.astype(jnp.bfloat16)
    write_stats(out_ref, plan.share_rows, rows)


def merge(plan, wide, stats, parts):
    rows = plan.share_rows + stat_rows(plan.units * plan.blocks)
    return local(
        functools.partial(merge_kernel, plan),
        [
            jax.ShapeDtypeStruct((rows, HD), jnp.bfloat16),
            jax.ShapeDtypeStruct((plan.share_rows, HD), jnp.float32),
        ],
        [pltpu.VMEM] * (len(parts) + 2),
        "merge",
    )(wide, stats, *parts)


def settle_kernel(plan, wide_ref, own_ref, other_ref, out_ref):
    stats = [(own_ref, plan.share_rows), (other_ref, plan.share_rows)]
    for block in range(plan.units * plan.blocks):
        _, scale, total = factors(stats, block)
        done = mix([wide_ref, other_ref], block * 128, columns([f / total for f in scale]))
        done = done.astype(jnp.bfloat16)
        for row in range(0, 128, plan.rows):
            to = (block * 128 + row) // plan.rows * HD
            out_ref[:, to : to + HD] = done[row : row + plan.rows, :]


def settle(plan, wide, own, other):
    return local(
        functools.partial(settle_kernel, plan),
        jax.ShapeDtypeStruct((plan.rows, plan.heads * HD), jnp.bfloat16),
        [pltpu.VMEM] * 3,
        "settle",
    )(wide, own, other)


def project_kernel(plan, part, *refs):
    block_ref, weight_ref, *before, out_ref = refs
    depth = plan.heads * HD
    at = pl.multiple_of(plan.share(part) * depth, depth)
    total = jnp.dot(block_ref[...], weight_ref[pl.ds(at, depth), :], preferred_element_type=jnp.float32)
    for ref in before:
        total = total + ref[...]
    out_ref[...] = total.astype(out_ref.dtype)


def project(plan, part, block, weight, before, dtype):
    operands = [block, weight] + ([] if before is None else [before])
    return local(
        functools.partial(project_kernel, plan, part),
        jax.ShapeDtypeStruct((plan.rows, weight.shape[1]), dtype),
        [pltpu.VMEM] * len(operands),
        "project",
    )(*operands)


def per_device(queries, cache, out_weight, offsets, starts):
    plan = Plan(lax.axis_size("ctx"), queries.shape[0])
    half = plan.half
    cache = pltpu.with_memory_space_constraint(cache, pltpu.VMEM)
    out_weight = pltpu.with_memory_space_constraint(out_weight, pltpu.VMEM)

    own = queries.reshape(plan.rows_here, KVH, GROUP, HD)
    own = own.transpose(1, 2, 0, 3).reshape(KVH, GROUP * plan.rows_here, HD)
    held, order, one_hot, bias = ready(plan, cache.shape[0], offsets, starts, own)
    far = swap(own, "ctx", half)
    if own.shape[1] % 16 == 0:
        gathered = [held, far]
        near = [swap(own, "ctx", k) for k in range(1, half)]
        for k in range(1, half):
            gathered += [near[k - 1], swap(far, "ctx", k)]
    else:
        pair = jnp.concatenate([own, far], axis=1)
        gathered = [pair] + [swap(pair, "ctx", k) for k in range(1, half)]

    received = []
    for part in reversed(range(1, half)):
        (piece,) = attend(plan, part, gathered, cache, bias, order, one_hot)
        received.append(swap(piece, "ctx", part))
    wide, stats = attend(plan, 0, gathered, cache, bias, order, one_hot)

    near, near_wide = merge(plan, wide, stats, received)
    block = settle(plan, near_wide, near, swap(near, "ctx", plan.across))

    total = project(plan, 0, block, out_weight, None, jnp.float32)
    blocks = [swap(block, "ctx", k) for k in range(1, half)]
    for k in range(1, half):
        dtype = jnp.float32 if k < half - 1 else jnp.bfloat16
        total = project(plan, k, blocks[k - 1], out_weight, total, dtype)
    return from_behind(total, "segment", 1)


def solution(mesh):
    in_specs = (
        P(("segment", "ctx"), None),
        P(("segment", "ctx"), None),
        P("segment", "ctx"),
        P("segment"),
        P("segment"),
    )
    out_specs = P("segment", "ctx")
    return jax.shard_map(
        per_device, mesh=mesh, in_specs=in_specs, out_specs=out_specs, check_vma=False
    )
```

time: 53.7 us -> 51 us (0.950)
  Pallas kernels: 16.7 us -> 12.7 us
  waiting for transfers between devices: 13.6 us -> 15.2 us
    pallas_call x16 -> x9, Pallas kernels: 15.4 us -> 11.4 us  [the longest x4 7.56 us: attend(): local(functools.partial(attend_kernel, plan, part), out_shape, [pltpu.VME...]
    ppermute x15 -> x14, waiting for transfers between devices: 9.86 us -> 11.6 us  [swap(): return lax.ppermute(value, axis, [(i, i ^ bits) for i in range(devices)])]
    ppermute x15 -> x14, starting transfers between devices: 21.1 us -> 20.8 us  [swap(): return lax.ppermute(value, axis, [(i, i ^ bits) for i in range(devices)])]
  transfers between devices with their start and end apart: 16 -> 15, of which waited for: 5 -> 9; matrix products, arithmetic and copies ran while one was open for 0% -> 0% of each run, Pallas kernels for 26% -> 18%
where the time goes in v4:
time: 51 us; the launch traced here: 50.8 us
  starting transfers between devices  20.8 us (41%)
  waiting for transfers between devices  15.2 us (30%)
  Pallas kernels  12.7 us (25%)
  between operations  1.45 us (3%)
  local copies, waits for them, and re-layouts  0.67 us (1%)
    ppermute x14, starting transfers between devices, swap(): return lax.ppermute(value, axis, [(i, i ^ bits) for i in range(devices)])  20.8 us
    ppermute x14, waiting for transfers between devices, swap(): return lax.ppermute(value, axis, [(i, i ^ bits) for i in range(devices)])  11.6 us
    pallas_call x4, Pallas kernels, attend(): local(functools.partial(attend_kernel, plan, part), out_shape, [pltpu.VME...  7.56 us
    ppermute x1, waiting for transfers between devices, from_behind(): lax.ppermute(value, axis, [(i, (i + by) % devices) for i in range(devices)])  3.69 us
    pallas_call x4, Pallas kernels, project(): local(functools.partial(project_kernel, plan, part), jax.ShapeDtypeStruct...  3.29 us
  transfers between devices with their start and end apart: 15, of which 9 were waited for; matrix products, arithmetic and copies ran while one was open for 0% of the time, Pallas kernels for 18%

profile of v4, /device:TPU:0, one launch (start us, length us, event | category | flops | bytes accessed | tf_op | source)
XLA Modules:
  0.0 50.8 jit_solution(16701673872601285519)
XLA Ops:
  0.0 4.0 %collective-permute-start = (bf16[8,32,128]{2,1,0:T(8,128)(2,1)}, bf16[8,32,128]{2,1,0:T(8,128)(2,1)S(1)}, u32[]{:S(2)}, u32[]{:S(2)}) collective-permute-start(bf16[8,32,128]{2,1,0:T(8,128)(2,1)} %bitcast.9), channel_id=1, source_target_pairs={{0,4},{1,5},{2,6},{3,7},{4,0},{5,1},{6,2},{7,3},{8,12},{9,13},{10,... | collective-permute-start | bytes 196616 | tf_op jit(solution)/shard_map/ppermute | solution.py:25
  4.0 2.5 %collective-permute-start.5 = (bf16[8,32,128]{2,1,0:T(8,128)(2,1)}, bf16[8,32,128]{2,1,0:T(8,128)(2,1)S(1)}, u32[]{:S(2)}, u32[]{:S(2)}) collective-permute-start(bf16[8,32,128]{2,1,0:T(8,128)(2,1)} %bitcast.10), channel_id=1, source_target_pairs={{0,3},{1,2},{2,1},{3,0},{4,7},{5,6},{6,5},{7,4},{8,11},{9,10},{10,... | collective-permute-start | bytes 196616 | tf_op jit(solution)/shard_map/ppermute | solution.py:25
  6.5 0.4 collective-permute-start.3
  7.0 0.5 %collective-permute-start.1 = (bf16[8,32,128]{2,1,0:T(8,128)(2,1)}, bf16[8,32,128]{2,1,0:T(8,128)(2,1)S(1)}, u32[]{:S(2)}, u32[]{:S(2)}) collective-permute-start(bf16[8,32,128]{2,1,0:T(8,128)(2,1)} %bitcast.12), channel_id=1, source_target_pairs={{0,1},{1,0},{2,3},{3,2},{4,5},{5,4},{6,7},{7,6},{8,9},{9,8},{10,11... | collective-permute-start | bytes 196616 | tf_op jit(solution)/shard_map/ppermute | solution.py:25
  8.8 0.0 slice-start.5
  8.8 0.0 collective-permute-done.refs_1_
  8.8 2.6 %collective-permute-start.6 = (bf16[8,32,128]{2,1,0:T(8,128)(2,1)S(1)}, bf16[8,32,128]{2,1,0:T(8,128)(2,1)S(1)}, u32[]{:S(2)}, u32[]{:S(2)}) collective-permute-start(bf16[8,32,128]{2,1,0:T(8,128)(2,1)S(1)} %collective-permute-done.refs_1_), channel_id=1, source_target_pairs={{0,3},{1,2},{2,1},{3,0},{4,7},{5,6},{6,5},{7,4},{8,11},{9,10},{10,... | collective-permute-start | bytes 196616 | tf_op jit(solution)/shard_map/ppermute | solution.py:25
  11.4 0.4 collective-permute-start.4
  11.9 0.0 collective-permute-done.5.refs_6_
  11.9 0.5 %collective-permute-start.2 = (bf16[8,32,128]{2,1,0:T(8,128)(2,1)S(1)}, bf16[8,32,128]{2,1,0:T(8,128)(2,1)S(1)}, u32[]{:S(2)}, u32[]{:S(2)}) collective-permute-start(bf16[8,32,128]{2,1,0:T(8,128)(2,1)S(1)} %collective-permute-done.refs_1_), channel_id=1, source_target_pairs={{0,1},{1,0},{2,3},{3,2},{4,5},{5,4},{6,7},{7,6},{8,9},{9,8},{10,11... | collective-permute-start | bytes 196616 | tf_op jit(solution)/shard_map/ppermute | solution.py:25
  12.4 0.8 %ready.1 = (bf16[8,32,128]{2,1,0:T(8,128)(2,1)S(1)}, bf16[256,256]{1,0:T(8,128)(2,1)S(1)}, bf16[256,128]{1,0:T(8,128)(2,1)S(1)}, bf16[2048,128]{1,0:T(8,128)(2,1)S(1)}) custom-call(s32[1]{0:T(128)S(6)} %copy.8.offset_ref, s32[1]{0:T(128)S(6)} %copy.9.start_ref, bf16[8,32,128]{2,1,0:T(8,128)(2,1)} %bitcast.13), custom_call_target="tpu_custom_call" | custom-call | flops 8000000000 | bytes 1048576 | tf_op jit(solution)/shard_map/ready/pallas_call | solution.py:105
  13.3 0.0 collective-permute-done.3.refs_4_
  13.3 0.0 collective-permute-done.1.refs_2_
  13.3 0.8 %collective-permute-done.6.refs_7_ = bf16[8,32,128]{2,1,0:T(8,128)(2,1)S(1)} collective-permute-done((bf16[8,32,128]{2,1,0:T(8,128)(2,1)S(1)}, bf16[8,32,128]{2,1,0:T(8,128)(2,1)S(1)}, u32[]{:S(2)}, u32[]{:S(2)}) %collective-permute-start.6) | collective-permute-done | bytes 65568 | tf_op jit(solution)/shard_map/ppermute | solution.py:25
  14.1 1.6 %collective-permute-done.4.refs_5_ = bf16[8,32,128]{2,1,0:T(8,128)(2,1)S(1)} collective-permute-done((bf16[8,32,128]{2,1,0:T(8,128)(2,1)S(1)}, bf16[8,32,128]{2,1,0:T(8,128)(2,1)S(1)}, u32[]{:S(2)}, u32[]{:S(2)}) %collective-permute-start.4) | collective-permute-done | bytes 65568 | tf_op jit(solution)/shard_map/ppermute | solution.py:25
  15.7 0.5 collective-permute-done.2.refs_3_
  16.1 0.0 slice-done.4
  16.1 1.9 %attend.5 = bf16[528,128]{1,0:T(8,128)(2,1)S(1)} custom-call(bf16[8,32,128]{2,1,0:T(8,128)(2,1)S(1)} %get-tuple-element.13.refs_0_, bf16[8,32,128]{2,1,0:T(8,128)(2,1)S(1)} %collective-permute-done.refs_1_, bf16[8,32,128]{2,1,0:T(8,128)(2,1)S(1)} %collective-permute-done.1.refs_2_, bf16[8,32,128]{2,1,0:T(8,128)(2,1)S(1)} %collective-permute-done.2.refs_3_, ...), custom_call_target="tpu_custom_call" | custom-call | flops 536870912 | bytes 2097152 | tf_op jit(solution)/shard_map/attend/pallas_call | solution.py:188
  18.1 0.0 slice-start
  18.1 0.0 slice-start.1
  18.1 1.5 %collective-permute-start.7 = (bf16[528,128]{1,0:T(8,128)(2,1)S(1)}, bf16[528,128]{1,0:T(8,128)(2,1)S(1)}, u32[]{:S(2)}, u32[]{:S(2)}) collective-permute-start(bf16[528,128]{1,0:T(8,128)(2,1)S(1)} %attend.5), channel_id=1, source_target_pairs={{0,3},{1,2},{2,1},{3,0},{4,7},{5,6},{6,5},{7,4},{8,11},{9,10},{10,... | collective-permute-start | bytes 405512 | tf_op jit(solution)/shard_map/ppermute | solution.py:25
  19.6 1.9 %attend.6 = bf16[528,128]{1,0:T(8,128)(2,1)S(1)} custom-call(bf16[8,32,128]{2,1,0:T(8,128)(2,1)S(1)} %get-tuple-element.13.refs_0_, bf16[8,32,128]{2,1,0:T(8,128)(2,1)S(1)} %collective-permute-done.refs_1_, bf16[8,32,128]{2,1,0:T(8,128)(2,1)S(1)} %collective-permute-done.1.refs_2_, bf16[8,32,128]{2,1,0:T(8,128)(2,1)S(1)} %collective-permute-done.2.refs_3_, ...), custom_call_target="tpu_custom_call" | custom-call | flops 536870912 | bytes 2097152 | tf_op jit(solution)/shard_map/attend/pallas_call | solution.py:188
  21.6 0.0 slice-start.2
  21.6 0.5 %collective-permute-start.8 = (bf16[528,128]{1,0:T(8,128)(2,1)S(1)}, bf16[528,128]{1,0:T(8,128)(2,1)S(1)}, u32[]{:S(2)}, u32[]{:S(2)}) collective-permute-start(bf16[528,128]{1,0:T(8,128)(2,1)S(1)} %attend.6), channel_id=1, source_target_pairs={{0,2},{1,3},{2,0},{3,1},{4,6},{5,7},{6,4},{7,5},{8,10},{9,11},{10,... | collective-permute-start | bytes 405512 | tf_op jit(solution)/shard_map/ppermute | solution.py:25
  22.1 1.9 %attend.7 = bf16[528,128]{1,0:T(8,128)(2,1)S(1)} custom-call(bf16[8,32,128]{2,1,0:T(8,128)(2,1)S(1)} %get-tuple-element.13.refs_0_, bf16[8,32,128]{2,1,0:T(8,128)(2,1)S(1)} %collective-permute-done.refs_1_, bf16[8,32,128]{2,1,0:T(8,128)(2,1)S(1)} %collective-permute-done.1.refs_2_, bf16[8,32,128]{2,1,0:T(8,128)(2,1)S(1)} %collective-permute-done.2.refs_3_, ...), custom_call_target="tpu_custom_call" | custom-call | flops 536870912 | bytes 2097152 | tf_op jit(solution)/shard_map/attend/pallas_call | solution.py:188
  24.0 0.0 slice-start.3
  24.0 1.5 %collective-permute-start.9 = (bf16[528,128]{1,0:T(8,128)(2,1)S(1)}, bf16[528,128]{1,0:T(8,128)(2,1)S(1)}, u32[]{:S(2)}, u32[]{:S(2)}) collective-permute-start(bf16[528,128]{1,0:T(8,128)(2,1)S(1)} %attend.7), channel_id=1, source_target_pairs={{0,1},{1,0},{2,3},{3,2},{4,5},{5,4},{6,7},{7,6},{8,9},{9,8},{10,11... | collective-permute-start | bytes 405512 | tf_op jit(solution)/shard_map/ppermute | solution.py:25
  25.5 1.8 %attend.4 = (f32[512,128]{1,0:T(8,128)S(1)}, bf16[16,128]{1,0:T(8,128)(2,1)S(1)}) custom-call(bf16[8,32,128]{2,1,0:T(8,128)(2,1)S(1)} %get-tuple-element.13.refs_0_, bf16[8,32,128]{2,1,0:T(8,128)(2,1)S(1)} %collective-permute-done.refs_1_, bf16[8,32,128]{2,1,0:T(8,128)(2,1)S(1)} %collective-permute-done.1.refs_2_, ...), custom_call_target="tpu_custom_call" | custom-call | flops 536870912 | bytes 2097152 | tf_op jit(solution)/shard_map/attend/pallas_call | solution.py:188
  27.4 0.0 collective-permute-done.7.refs_0_
  27.4 0.0 collective-permute-done.8.refs_1_
  27.4 1.7 %collective-permute-done.9.refs_2_ = bf16[528,128]{1,0:T(8,128)(2,1)S(1)} collective-permute-done((bf16[528,128]{1,0:T(8,128)(2,1)S(1)}, bf16[528,128]{1,0:T(8,128)(2,1)S(1)}, u32[]{:S(2)}, u32[]{:S(2)}) %collective-permute-start.9) | collective-permute-done | bytes 135200 | tf_op jit(solution)/shard_map/ppermute | solution.py:25
  29.1 0.6 %merge.1 = (bf16[528,128]{1,0:T(8,128)(2,1)S(1)}, f32[512,128]{1,0:T(8,128)S(1)}) custom-call(f32[512,128]{1,0:T(8,128)S(1)} %get-tuple-element.17.wide_ref, bf16[16,128]{1,0:T(8,128)(2,1)S(1)} %get-tuple-element.18.stat_ref, bf16[528,128]{1,0:T(8,128)(2,1)S(1)} %collective-permute-done.7.refs_0_, bf16[528,128]{1,0:T(8,128)(2,1)S(1)} %collective-permute-done.8.refs_1_, ...), custom_call_target="tpu_custom_call" | custom-call | tf_op jit(solution)/shard_map/merge/pallas_call | solution.py:245
  29.6 2.5 %collective-permute-start.10 = (bf16[528,128]{1,0:T(8,128)(2,1)S(1)}, bf16[528,128]{1,0:T(8,128)(2,1)S(1)}, u32[]{:S(2)}, u32[]{:S(2)}) collective-permute-start(bf16[528,128]{1,0:T(8,128)(2,1)S(1)} %get-tuple-element.20.own_ref), channel_id=1, source_target_pairs={{0,6},{1,7},{2,4},{3,5},{4,2},{5,3},{6,0},{7,1},{8,14},{9,15},{10,... | collective-permute-start | bytes 405512 | tf_op jit(solution)/shard_map/ppermute | solution.py:25
  32.2 4.5 %collective-permute-done.10.other_ref = bf16[528,128]{1,0:T(8,128)(2,1)S(1)} collective-permute-done((bf16[528,128]{1,0:T(8,128)(2,1)S(1)}, bf16[528,128]{1,0:T(8,128)(2,1)S(1)}, u32[]{:S(2)}, u32[]{:S(2)}) %collective-permute-start.10) | collective-permute-done | bytes 135200 | tf_op jit(solution)/shard_map/ppermute | solution.py:25
  36.7 0.4 settle.1.refs_0_
  37.1 1.6 %collective-permute-start.13 = (bf16[32,2048]{1,0:T(8,128)(2,1)S(1)}, bf16[32,2048]{1,0:T(8,128)(2,1)S(1)}, u32[]{:S(2)}, u32[]{:S(2)}) collective-permute-start(bf16[32,2048]{1,0:T(8,128)(2,1)S(1)} %settle.1.refs_0_), channel_id=1, source_target_pairs={{0,1},{1,0},{2,3},{3,2},{4,5},{5,4},{6,7},{7,6},{8,9},{9,8},{10,11... | collective-permute-start | bytes 393224 | tf_op jit(solution)/shard_map/ppermute | solution.py:25
  38.7 1.1 %collective-permute-start.12 = (bf16[32,2048]{1,0:T(8,128)(2,1)S(1)}, bf16[32,2048]{1,0:T(8,128)(2,1)S(1)}, u32[]{:S(2)}, u32[]{:S(2)}) collective-permute-start(bf16[32,2048]{1,0:T(8,128)(2,1)S(1)} %settle.1.refs_0_), channel_id=1, source_target_pairs={{0,2},{1,3},{2,0},{3,1},{4,6},{5,7},{6,4},{7,5},{8,10},{9,11},{10,... | collective-permute-start | bytes 393224 | tf_op jit(solution)/shard_map/ppermute | solution.py:25
  39.8 0.9 %collective-permute-start.11 = (bf16[32,2048]{1,0:T(8,128)(2,1)S(1)}, bf16[32,2048]{1,0:T(8,128)(2,1)S(1)}, u32[]{:S(2)}, u32[]{:S(2)}) collective-permute-start(bf16[32,2048]{1,0:T(8,128)(2,1)S(1)} %settle.1.refs_0_), channel_id=1, source_target_pairs={{0,3},{1,2},{2,1},{3,0},{4,7},{5,6},{6,5},{7,4},{8,11},{9,10},{10,... | collective-permute-start | bytes 393224 | tf_op jit(solution)/shard_map/ppermute | solution.py:25
  40.7 0.8 %project.4.refs_2_ = f32[32,1024]{1,0:T(8,128)S(1)} custom-call(bf16[32,2048]{1,0:T(8,128)(2,1)S(1)} %settle.1.refs_0_, bf16[8192,1024]{1,0:T(8,128)(2,1)S(1)} %bitcast.6), custom_call_target="tpu_custom_call" | custom-call | tf_op jit(solution)/shard_map/project/pallas_call | solution.py:288
  41.5 0.6 %collective-permute-done.13.refs_0_ = bf16[32,2048]{1,0:T(8,128)(2,1)S(1)} collective-permute-done((bf16[32,2048]{1,0:T(8,128)(2,1)S(1)}, bf16[32,2048]{1,0:T(8,128)(2,1)S(1)}, u32[]{:S(2)}, u32[]{:S(2)}) %collective-permute-start.13) | collective-permute-done | bytes 131104 | tf_op jit(solution)/shard_map/ppermute | solution.py:25
  42.1 0.8 %project.5.refs_2_ = f32[32,1024]{1,0:T(8,128)S(1)} custom-call(bf16[32,2048]{1,0:T(8,128)(2,1)S(1)} %collective-permute-done.13.refs_0_, bf16[8192,1024]{1,0:T(8,128)(2,1)S(1)} %bitcast.6, f32[32,1024]{1,0:T(8,128)S(1)} %project.4.refs_2_), custom_call_target="tpu_custom_call" | custom-call | tf_op jit(solution)/shard_map/project/pallas_call | solution.py:288
  42.9 0.7 %collective-permute-done.12.refs_0_ = bf16[32,2048]{1,0:T(8,128)(2,1)S(1)} collective-permute-done((bf16[32,2048]{1,0:T(8,128)(2,1)S(1)}, bf16[32,2048]{1,0:T(8,128)(2,1)S(1)}, u32[]{:S(2)}, u32[]{:S(2)}) %collective-permute-start.12) | collective-permute-done | bytes 131104 | tf_op jit(solution)/shard_map/ppermute | solution.py:25
  43.6 0.8 %project.6.refs_2_ = f32[32,1024]{1,0:T(8,128)S(1)} custom-call(bf16[32,2048]{1,0:T(8,128)(2,1)S(1)} %collective-permute-done.12.refs_0_, bf16[8192,1024]{1,0:T(8,128)(2,1)S(1)} %bitcast.6, f32[32,1024]{1,0:T(8,128)S(1)} %project.5.refs_2_), custom_call_target="tpu_custom_call" | custom-call | tf_op jit(solution)/shard_map/project/pallas_call | solution.py:288
  44.5 1.2 %collective-permute-done.11.refs_0_ = bf16[32,2048]{1,0:T(8,128)(2,1)S(1)} collective-permute-done((bf16[32,2048]{1,0:T(8,128)(2,1)S(1)}, bf16[32,2048]{1,0:T(8,128)(2,1)S(1)}, u32[]{:S(2)}, u32[]{:S(2)}) %collective-permute-start.11) | collective-permute-done | bytes 131104 | tf_op jit(solution)/shard_map/ppermute | solution.py:25
  45.7 0.8 %project.7 = bf16[32,1024]{1,0:T(8,128)(2,1)S(1)} custom-call(bf16[32,2048]{1,0:T(8,128)(2,1)S(1)} %collective-permute-done.11.refs_0_, bf16[8192,1024]{1,0:T(8,128)(2,1)S(1)} %bitcast.6, f32[32,1024]{1,0:T(8,128)S(1)} %project.6.refs_2_), custom_call_target="tpu_custom_call" | custom-call | tf_op jit(solution)/shard_map/project/pallas_call | solution.py:288
  46.5 0.0 collective-permute-start.14
  46.5 3.7 %collective-permute-done.14 = bf16[32,1024]{1,0:T(8,128)(2,1)S(1)} collective-permute-done((bf16[32,1024]{1,0:T(8,128)(2,1)S(1)}, bf16[32,1024]{1,0:T(8,128)(2,1)S(1)}, u32[]{:S(2)}, u32[]{:S(2)}) %collective-permute-start.14) | collective-permute-done | bytes 65568 | tf_op jit(solution)/shard_map/ppermute | solution.py:30
  50.2 0.6 %copy.10 = bf16[32,1024]{1,0:T(8,128)(2,1)} copy(bf16[32,1024]{1,0:T(8,128)(2,1)S(1)} %collective-permute-done.14) | data formatting | bytes 131072
  (8 shorter events, 0.0 us)
Async XLA Ops:
  0.0 16.1 %slice-start.4 = ((s8[8388608]{0:T(1024)(128)(4,1)}), s8[4194304]{0:T(1024)(128)(4,1)S(1)}, s32[]{:S(2)}) async-start(s8[8388608]{0:T(1024)(128)(4,1)} %bitcast.7), calls=%async_computation.4 | async-start | bytes 8388608
  0.0 8.8 %collective-permute-start = (bf16[8,32,128]{2,1,0:T(8,128)(2,1)}, bf16[8,32,128]{2,1,0:T(8,128)(2,1)S(1)}, u32[]{:S(2)}, u32[]{:S(2)}) collective-permute-start(bf16[8,32,128]{2,1,0:T(8,128)(2,1)} %bitcast.9), channel_id=1, source_target_pairs={{0,4},{1,5},{2,6},{3,7},{4,0},{5,1},{6,2},{7,3},{8,12},{9,13},{10,... | collective-permute-start | bytes 196616 | tf_op jit(solution)/shard_map/ppermute | solution.py:25
  4.0 7.8 %collective-permute-start.5 = (bf16[8,32,128]{2,1,0:T(8,128)(2,1)}, bf16[8,32,128]{2,1,0:T(8,128)(2,1)S(1)}, u32[]{:S(2)}, u32[]{:S(2)}) collective-permute-start(bf16[8,32,128]{2,1,0:T(8,128)(2,1)} %bitcast.10), channel_id=1, source_target_pairs={{0,3},{1,2},{2,1},{3,0},{4,7},{5,6},{6,5},{7,4},{8,11},{9,10},{10,... | collective-permute-start | bytes 196616 | tf_op jit(solution)/shard_map/ppermute | solution.py:25
  6.5 6.7 %collective-permute-start.3 = (bf16[8,32,128]{2,1,0:T(8,128)(2,1)}, bf16[8,32,128]{2,1,0:T(8,128)(2,1)S(1)}, u32[]{:S(2)}, u32[]{:S(2)}) collective-permute-start(bf16[8,32,128]{2,1,0:T(8,128)(2,1)} %bitcast.11), channel_id=1, source_target_pairs={{0,2},{1,3},{2,0},{3,1},{4,6},{5,7},{6,4},{7,5},{8,10},{9,11},{10,... | collective-permute-start | bytes 196616 | tf_op jit(solution)/shard_map/ppermute | solution.py:25
  7.0 6.3 %collective-permute-start.1 = (bf16[8,32,128]{2,1,0:T(8,128)(2,1)}, bf16[8,32,128]{2,1,0:T(8,128)(2,1)S(1)}, u32[]{:S(2)}, u32[]{:S(2)}) collective-permute-start(bf16[8,32,128]{2,1,0:T(8,128)(2,1)} %bitcast.12), channel_id=1, source_target_pairs={{0,1},{1,0},{2,3},{3,2},{4,5},{5,4},{6,7},{7,6},{8,9},{9,8},{10,11... | collective-permute-start | bytes 196616 | tf_op jit(solution)/shard_map/ppermute | solution.py:25
  8.8 7.3 %slice-start.5 = ((s8[8388608]{0:T(1024)(128)(4,1)}), s8[4194304]{0:T(1024)(128)(4,1)S(1)}, s32[]{:S(2)}) async-start(s8[8388608]{0:T(1024)(128)(4,1)} %bitcast.7), calls=%async_computation.5 | async-start | bytes 8388608
  8.8 5.2 %collective-permute-start.6 = (bf16[8,32,128]{2,1,0:T(8,128)(2,1)S(1)}, bf16[8,32,128]{2,1,0:T(8,128)(2,1)S(1)}, u32[]{:S(2)}, u32[]{:S(2)}) collective-permute-start(bf16[8,32,128]{2,1,0:T(8,128)(2,1)S(1)} %collective-permute-done.refs_1_), channel_id=1, source_target_pairs={{0,3},{1,2},{2,1},{3,0},{4,7},{5,6},{6,5},{7,4},{8,11},{9,10},{10,... | collective-permute-start | bytes 196616 | tf_op jit(solution)/shard_map/ppermute | solution.py:25
  11.4 4.3 %collective-permute-start.4 = (bf16[8,32,128]{2,1,0:T(8,128)(2,1)S(1)}, bf16[8,32,128]{2,1,0:T(8,128)(2,1)S(1)}, u32[]{:S(2)}, u32[]{:S(2)}) collective-permute-start(bf16[8,32,128]{2,1,0:T(8,128)(2,1)S(1)} %collective-permute-done.refs_1_), channel_id=1, source_target_pairs={{0,2},{1,3},{2,0},{3,1},{4,6},{5,7},{6,4},{7,5},{8,10},{9,11},{10,... | collective-permute-start | bytes 196616 | tf_op jit(solution)/shard_map/ppermute | solution.py:25
  11.9 4.3 %collective-permute-start.2 = (bf16[8,32,128]{2,1,0:T(8,128)(2,1)S(1)}, bf16[8,32,128]{2,1,0:T(8,128)(2,1)S(1)}, u32[]{:S(2)}, u32[]{:S(2)}) collective-permute-start(bf16[8,32,128]{2,1,0:T(8,128)(2,1)S(1)} %collective-permute-done.refs_1_), channel_id=1, source_target_pairs={{0,1},{1,0},{2,3},{3,2},{4,5},{5,4},{6,7},{7,6},{8,9},{9,8},{10,11... | collective-permute-start | bytes 196616 | tf_op jit(solution)/shard_map/ppermute | solution.py:25
  18.1 22.6 %slice-start = ((s8[16777216]{0:T(1024)(128)(4,1)}), s8[4194304]{0:T(1024)(128)(4,1)S(1)}, s32[]{:S(2)}) async-start(s8[16777216]{0:T(1024)(128)(4,1)} %bitcast.5), calls=%async_computation | async-start | bytes 8388608
  18.1 22.6 %slice-start.1 = ((s8[16777216]{0:T(1024)(128)(4,1)}), s8[4194304]{0:T(1024)(128)(4,1)S(1)}, s32[]{:S(2)}) async-start(s8[16777216]{0:T(1024)(128)(4,1)} %bitcast.5), calls=%async_computation.1 | async-start | bytes 8388608
  18.1 9.3 %collective-permute-start.7 = (bf16[528,128]{1,0:T(8,128)(2,1)S(1)}, bf16[528,128]{1,0:T(8,128)(2,1)S(1)}, u32[]{:S(2)}, u32[]{:S(2)}) collective-permute-start(bf16[528,128]{1,0:T(8,128)(2,1)S(1)} %attend.5), channel_id=1, source_target_pairs={{0,3},{1,2},{2,1},{3,0},{4,7},{5,6},{6,5},{7,4},{8,11},{9,10},{10,... | collective-permute-start | bytes 405512 | tf_op jit(solution)/shard_map/ppermute | solution.py:25
  21.6 19.1 %slice-start.2 = ((s8[16777216]{0:T(1024)(128)(4,1)}), s8[4194304]{0:T(1024)(128)(4,1)S(1)}, s32[]{:S(2)}) async-start(s8[16777216]{0:T(1024)(128)(4,1)} %bitcast.5), calls=%async_computation.2 | async-start | bytes 8388608
  21.6 5.8 %collective-permute-start.8 = (bf16[528,128]{1,0:T(8,128)(2,1)S(1)}, bf16[528,128]{1,0:T(8,128)(2,1)S(1)}, u32[]{:S(2)}, u32[]{:S(2)}) collective-permute-start(bf16[528,128]{1,0:T(8,128)(2,1)S(1)} %attend.6), channel_id=1, source_target_pairs={{0,2},{1,3},{2,0},{3,1},{4,6},{5,7},{6,4},{7,5},{8,10},{9,11},{10,... | collective-permute-start | bytes 405512 | tf_op jit(solution)/shard_map/ppermute | solution.py:25
  24.0 16.7 %slice-start.3 = ((s8[16777216]{0:T(1024)(128)(4,1)}), s8[4194304]{0:T(1024)(128)(4,1)S(1)}, s32[]{:S(2)}) async-start(s8[16777216]{0:T(1024)(128)(4,1)} %bitcast.5), calls=%async_computation.3 | async-start | bytes 8388608
  24.0 5.1 %collective-permute-start.9 = (bf16[528,128]{1,0:T(8,128)(2,1)S(1)}, bf16[528,128]{1,0:T(8,128)(2,1)S(1)}, u32[]{:S(2)}, u32[]{:S(2)}) collective-permute-start(bf16[528,128]{1,0:T(8,128)(2,1)S(1)} %attend.7), channel_id=1, source_target_pairs={{0,1},{1,0},{2,3},{3,2},{4,5},{5,4},{6,7},{7,6},{8,9},{9,8},{10,11... | collective-permute-start | bytes 405512 | tf_op jit(solution)/shard_map/ppermute | solution.py:25
  29.6 7.0 %collective-permute-start.10 = (bf16[528,128]{1,0:T(8,128)(2,1)S(1)}, bf16[528,128]{1,0:T(8,128)(2,1)S(1)}, u32[]{:S(2)}, u32[]{:S(2)}) collective-permute-start(bf16[528,128]{1,0:T(8,128)(2,1)S(1)} %get-tuple-element.20.own_ref), channel_id=1, source_target_pairs={{0,6},{1,7},{2,4},{3,5},{4,2},{5,3},{6,0},{7,1},{8,14},{9,15},{10,... | collective-permute-start | bytes 405512 | tf_op jit(solution)/shard_map/ppermute | solution.py:25
  37.1 5.0 %collective-permute-start.13 = (bf16[32,2048]{1,0:T(8,128)(2,1)S(1)}, bf16[32,2048]{1,0:T(8,128)(2,1)S(1)}, u32[]{:S(2)}, u32[]{:S(2)}) collective-permute-start(bf16[32,2048]{1,0:T(8,128)(2,1)S(1)} %settle.1.refs_0_), channel_id=1, source_target_pairs={{0,1},{1,0},{2,3},{3,2},{4,5},{5,4},{6,7},{7,6},{8,9},{9,8},{10,11... | collective-permute-start | bytes 393224 | tf_op jit(solution)/shard_map/ppermute | solution.py:25
  38.7 5.0 %collective-permute-start.12 = (bf16[32,2048]{1,0:T(8,128)(2,1)S(1)}, bf16[32,2048]{1,0:T(8,128)(2,1)S(1)}, u32[]{:S(2)}, u32[]{:S(2)}) collective-permute-start(bf16[32,2048]{1,0:T(8,128)(2,1)S(1)} %settle.1.refs_0_), channel_id=1, source_target_pairs={{0,2},{1,3},{2,0},{3,1},{4,6},{5,7},{6,4},{7,5},{8,10},{9,11},{10,... | collective-permute-start | bytes 393224 | tf_op jit(solution)/shard_map/ppermute | solution.py:25
  39.8 5.9 %collective-permute-start.11 = (bf16[32,2048]{1,0:T(8,128)(2,1)S(1)}, bf16[32,2048]{1,0:T(8,128)(2,1)S(1)}, u32[]{:S(2)}, u32[]{:S(2)}) collective-permute-start(bf16[32,2048]{1,0:T(8,128)(2,1)S(1)} %settle.1.refs_0_), channel_id=1, source_target_pairs={{0,3},{1,2},{2,1},{3,0},{4,7},{5,6},{6,5},{7,4},{8,11},{9,10},{10,... | collective-permute-start | bytes 393224 | tf_op jit(solution)/shard_map/ppermute | solution.py:25
  46.5 3.7 %collective-permute-start.14 = (bf16[32,1024]{1,0:T(8,128)(2,1)S(1)}, bf16[32,1024]{1,0:T(8,128)(2,1)S(1)}, u32[]{:S(2)}, u32[]{:S(2)}) collective-permute-start(bf16[32,1024]{1,0:T(8,128)(2,1)S(1)} %project.7), channel_id=1, source_target_pairs={{0,8},{8,16},{16,24},{24,0},{1,9},{9,17},{17,25},{25,1},{2,10},{10... | collective-permute-start | bytes 196616 | tf_op jit(solution)/shard_map/ppermute | solution.py:30

commit v5 on v4

v5 whole, which is shorter than its diff:
```python
import functools
import math

import jax
import jax.numpy as jnp
from jax import lax
from jax.experimental import pallas as pl
from jax.experimental.pallas import tpu as pltpu
from jax.sharding import PartitionSpec as P

H = 64
KVH = 8
HD = 128
GROUP = H // KVH
LOG2_SCALE = HD ** (-0.5) * math.log2(math.e)
STEP = 8.0
FLOOR = -4096.0
HIDDEN = -1e30
STATS = 16
VMEM_LIMIT = 12 * 1024 * 1024


def swap(value, axis, bits):
    devices = lax.axis_size(axis)
    return lax.ppermute(value, axis, [(i, i ^ bits) for i in range(devices)])


def from_behind(value, axis, by):
    devices = lax.axis_size(axis)
    return lax.ppermute(value, axis, [(i, (i + by) % devices) for i in range(devices)])


class Plan:
    def __init__(self, ctx, rows_here):
        self.ctx = ctx
        self.half = ctx // 2
        self.fold = self.half // 2
        self.across = self.half | self.fold
        self.rows_here = rows_here
        self.rows = ctx * rows_here
        self.side_rows = self.rows // 2
        self.group_rows = GROUP * self.side_rows
        self.heads = H // self.half
        self.unit_heads = min(self.heads, GROUP)
        self.units = self.heads // self.unit_heads
        self.piece = self.unit_heads * self.side_rows
        self.side = self.units * self.piece
        self.share_rows = 2 * self.side
        self.stats = stat_rows(2 * self.units)

    def share(self, part):
        me = lax.axis_index("ctx")
        return (me % self.half) ^ (me // self.half * self.fold) ^ part


def stat_rows(pieces):
    return -(-3 * pieces // 16) * 16


def local(kernel, out_shape, spaces, name, scratch=(), cost=None):
    return pl.pallas_call(
        kernel,
        out_shape=out_shape,
        in_specs=[pl.BlockSpec(memory_space=space) for space in spaces],
        out_specs=jax.tree.map(lambda _: pl.BlockSpec(memory_space=pltpu.VMEM), out_shape),
        scratch_shapes=list(scratch),
        compiler_params=pltpu.CompilerParams(vmem_limit_bytes=VMEM_LIMIT),
        cost_estimate=cost,
        name=name,
    )


def ready_kernel(plan, offset_ref, start_ref, after_ref, order_ref, one_hot_ref, bias_ref):
    del after_ref
    me = lax.axis_index("ctx")
    low, high = me % plan.half, me // plan.half
    row = lax.broadcasted_iota(jnp.int32, (plan.group_rows, 128), 0)
    lane = lax.broadcasted_iota(jnp.int32, (plan.group_rows, 128), 1)
    query = lax.rem(row, plan.side_rows)
    block = lax.div(query, plan.rows_here) ^ low
    origin = (block * GROUP + lax.div(row, plan.side_rows)) * plan.rows_here + lax.rem(query, plan.rows_here)
    for at in range(0, plan.group_rows, 128):
        order_ref[:, at : at + 128] = jnp.where(lane + at == origin, 1.0, 0.0).astype(jnp.bfloat16)
    for side in range(2):
        here = jnp.where(query + side * plan.side_rows == lane, 1.0, 0.0)
        one_hot_ref[side] = here.astype(jnp.bfloat16)
    span = bias_ref.shape[1]
    first = me * span
    position = first + lax.broadcasted_iota(jnp.int32, (plan.rows, span), 1)
    index = lax.broadcasted_iota(jnp.int32, (plan.rows, span), 0)
    asked = jnp.where(index < plan.side_rows, index + high * plan.side_rows, index - high * plan.side_rows)
    shown = (position >= start_ref[...]) & (position <= offset_ref[...] + asked)
    bias_ref[: plan.rows, :] = jnp.where(shown, 0.0, HIDDEN).astype(jnp.bfloat16)
    bias_ref[plan.rows :, :] = jnp.zeros((128 - plan.rows, span), jnp.bfloat16)


def ready(plan, span, offsets, starts, after):
    return local(
        functools.partial(ready_kernel, plan),
        [
            jax.ShapeDtypeStruct((plan.group_rows, plan.group_rows), jnp.bfloat16),
            jax.ShapeDtypeStruct((2, plan.group_rows, 128), jnp.bfloat16),
            jax.ShapeDtypeStruct((128, span), jnp.bfloat16),
        ],
        [pltpu.VMEM, pltpu.VMEM, pl.ANY],
        "ready",
    )(offsets.reshape(1, 1), starts.reshape(1, 1), after)


def turn_kernel(cache_ref, after_ref, out_ref, held_ref, sems):
    del after_ref
    copies = [
        pltpu.make_async_copy(cache_ref.at[:, pl.ds(group * HD, HD)], held_ref.at[group], sems.at[group])
        for group in range(KVH)
    ]
    for copy in copies:
        copy.start()
    for group, copy in enumerate(copies):
        copy.wait()
        out_ref[group] = jnp.transpose(held_ref[group])


def turn(cache, after):
    span = cache.shape[0]
    return local(
        turn_kernel,
        pltpu.VMEM((KVH, HD, span), cache.dtype),
        [pltpu.HBM, pl.ANY],
        "turn",
        [pltpu.VMEM((KVH, span, HD), cache.dtype), pltpu.SemaphoreType.DMA((KVH,))],
        pl.CostEstimate(flops=8_000_000_000, bytes_accessed=4 * KVH * HD * span, transcendentals=0),
    )(pltpu.with_memory_space_constraint(cache, pltpu.HBM), after)


def write_stats(ref, at, rows, begin, kept=None):
    values = []
    for peak, total in zip(rows[::2], rows[1::2]):
        high = total.astype(jnp.bfloat16).astype(jnp.float32)
        values += [peak, high, total - high]
    size = stat_rows(begin + len(rows) // 2) if kept is None else kept.shape[0]
    index = lax.broadcasted_iota(jnp.int32, (size, 128), 0)
    table = jnp.zeros((size, 128), jnp.float32) if kept is None else kept.astype(jnp.float32)
    for i, value in enumerate(values):
        table = jnp.where(index == 3 * begin + i, value, table)
    ref[at : at + size, :] = table.astype(jnp.bfloat16)


def attend_kernel(plan, part, side, *refs):
    refs, score_ref = refs[:-1], refs[-1]
    outs = 2 if part == 0 else 1
    refs, outs = refs[:-outs], refs[-outs:]
    earlier = ()
    if side == 1:
        refs, earlier = refs[:-1], refs[-1:]
    *query_refs, keys_ref, cache_ref, bias_ref, order_ref, one_hot_ref = refs
    span = cache_ref.shape[0]
    mine = plan.share(part)
    row_at = pl.multiple_of((mine * plan.heads) % GROUP * plan.side_rows, plan.piece)
    order = order_ref[pl.ds(row_at, plan.piece), :]
    one_hot = one_hot_ref[side, pl.ds(row_at, plan.piece), :]
    ones = jnp.ones((span, HD), jnp.bfloat16)
    groups = [(mine * plan.heads + unit * plan.unit_heads) // GROUP for unit in range(plan.units)]
    peaks = []
    for unit, group in enumerate(groups):
        stacked = jnp.concatenate([ref[group] for ref in query_refs], axis=0)
        queries = jnp.dot(order, stacked, preferred_element_type=jnp.float32)
        queries = jnp.concatenate([queries.astype(jnp.bfloat16), one_hot], axis=1)
        keys = jnp.concatenate([keys_ref[group], bias_ref[...]], axis=0)
        scores = jnp.dot(queries, keys, preferred_element_type=jnp.float32)
        score_ref[unit] = scores
        peak = [scores[:, at : at + 128] for at in range(0, span, 128)]
        while len(peak) > 1:
            peak = [jnp.maximum(*peak[i : i + 2]) for i in range(0, len(peak) - 1, 2)] + (
                peak[-1:] if len(peak) % 2 else []
            )
        peak = jnp.max(peak[0], axis=1, keepdims=True) * LOG2_SCALE
        peak = jnp.maximum(jnp.ceil(peak * (1.0 / STEP)), FLOOR / STEP)
        peaks.append(jnp.broadcast_to(peak, (plan.piece, 128)))
    same = lax.broadcasted_iota(jnp.int32, (plan.piece, 128), 0) == lax.broadcasted_iota(
        jnp.int32, (plan.piece, 128), 1
    )
    stats = []
    at = side * plan.side if part != 0 else 0
    for unit, group in enumerate(groups):
        shift = jnp.concatenate([peaks[unit] * STEP] * (span // 128), axis=1)
        weights = jnp.exp2(score_ref[unit] * LOG2_SCALE - shift)
        value_at = pl.multiple_of((KVH + group) * HD, HD)
        values = jnp.concatenate([cache_ref[:, pl.ds(value_at, HD)], ones], axis=1)
        both = jnp.dot(weights.astype(jnp.bfloat16), values, preferred_element_type=jnp.float32)
        outs[0][at : at + plan.piece, :] = both[:, :HD].astype(outs[0].dtype)
        at += plan.piece
        for wide in (peaks[unit], both[:, HD:]):
            stats.append(jnp.sum(jnp.where(same, wide, 0.0), axis=0, keepdims=True))
    if part == 0:
        kept = earlier[0][...] if earlier else None
        write_stats(outs[1], 0, stats, side * plan.units, kept)
    else:
        kept = None
        if earlier:
            outs[0][: plan.side, :] = earlier[0][: plan.side, :]
            kept = earlier[0][plan.side :, :]
        write_stats(outs[0], at, stats, side * plan.units, kept)


def attend(plan, part, side, queries, *tables):
    span = tables[1].shape[0]
    if part == 0:
        out_shape = [
            jax.ShapeDtypeStruct((plan.side, HD), jnp.float32),
            jax.ShapeDtypeStruct((plan.stats, HD), jnp.bfloat16),
        ]
    else:
        out_shape = [jax.ShapeDtypeStruct(((side + 1) * plan.side + plan.stats, HD), jnp.bfloat16)]
    return local(
        functools.partial(attend_kernel, plan, part, side),
        out_shape,
        [pltpu.VMEM] * (len(queries) + len(tables)),
        "attend",
        [pltpu.VMEM((plan.units, plan.piece, span), jnp.float32)],
        pl.CostEstimate(
            flops=4 * plan.side * span * HD,
            bytes_accessed=2 * plan.units * span * HD * 2,
            transcendentals=plan.side * span,
        ),
    )(*queries, *tables)


def columns(plan, rows):
    index = lax.broadcasted_iota(jnp.int32, (128, 128), 0)
    table = jnp.zeros((128, 128), jnp.float32)
    for i, row in enumerate(rows):
        table = jnp.where(index == i, row, table)
    turned = jnp.transpose(table)[: plan.piece]
    return [turned[:, i : i + 1] for i in range(len(rows))]


def factors(stats, pieces):
    parts = [[stat[3 * piece + i : 3 * piece + i + 1] for i in range(3)] for stat, piece in zip(stats, pieces)]
    joint = functools.reduce(jnp.maximum, [peak for peak, _, _ in parts])
    scale = [jnp.exp2((peak - joint) * STEP) for peak, _, _ in parts]
    total = functools.reduce(jnp.add, [f * (high + low) for f, (_, high, low) in zip(scale, parts)])
    return joint, scale, total


def mix(parts, scale):
    terms = [f * part.astype(jnp.float32) for part, f in zip(parts, scale)]
    return functools.reduce(jnp.add, terms)


def merge_kernel(plan, first_ref, second_ref, stat_ref, *refs):
    *parts, out_ref, wide_ref = refs
    stats = [stat_ref[...].astype(jnp.float32)]
    stats += [ref[plan.share_rows :, :].astype(jnp.float32) for ref in parts]
    rows = []
    for piece in range(2 * plan.units):
        joint, scale, total = factors(stats, [piece] * len(stats))
        rows += [joint, total]
        at, own_at = piece * plan.piece, piece % plan.units * plan.piece
        own_ref = (first_ref, second_ref)[piece // plan.units]
        values = [own_ref[own_at : own_at + plan.piece, :]]
        values += [ref[at : at + plan.piece, :] for ref in parts]
        mixed = mix(values, columns(plan, scale))
        wide_ref[at : at + plan.piece, :] = mixed
        out_ref[at : at + plan.piece, :] = mixed.astype(jnp.bfloat16)
    write_stats(out_ref, plan.share_rows, rows, 0)


def merge(plan, first, second, stats, parts):
    return local(
        functools.partial(merge_kernel, plan),
        [
            jax.ShapeDtypeStruct((plan.share_rows + plan.stats, HD), jnp.bfloat16),
            jax.ShapeDtypeStruct((plan.share_rows, HD), jnp.float32),
        ],
        [pltpu.VMEM] * (len(parts) + 3),
        "merge",
    )(first, second, stats, *parts)


def settle_kernel(plan, wide_ref, own_ref, other_ref, out_ref):
    stats = [ref[plan.share_rows :, :].astype(jnp.float32) for ref in (own_ref, other_ref)]
    high = lax.axis_index("ctx") // plan.half
    for piece in range(2 * plan.units):
        swapped = (piece + plan.units) % (2 * plan.units)
        _, scale, total = factors(stats, [piece, swapped])
        at, other_at = piece * plan.piece, swapped * plan.piece
        values = [wide_ref[at : at + plan.piece, :], other_ref[other_at : other_at + plan.piece, :]]
        done = mix(values, columns(plan, [f / total for f in scale])).astype(jnp.bfloat16)
        side, unit = piece // plan.units, piece % plan.units
        row_at = pl.multiple_of((high ^ side) * plan.side_rows, plan.side_rows)
        for head in range(plan.unit_heads):
            to = (unit * plan.unit_heads + head) * HD
            rows = done[head * plan.side_rows : (head + 1) * plan.side_rows, :]
            out_ref[pl.ds(row_at, plan.side_rows), to : to + HD] = rows


def settle(plan, wide, own, other):
    return local(
        functools.partial(settle_kernel, plan),
        jax.ShapeDtypeStruct((plan.rows, plan.heads * HD), jnp.bfloat16),
        [pltpu.VMEM] * 3,
        "settle",
    )(wide, own, other)


def project_kernel(plan, part, *refs):
    block_ref, weight_ref, *before, out_ref = refs
    depth = plan.heads * HD
    at = pl.multiple_of(plan.share(part) * depth, depth)
    total = jnp.dot(block_ref[...], weight_ref[pl.ds(at, depth), :], preferred_element_type=jnp.float32)
    for ref in before:
        total = total + ref[...]
    out_ref[...] = total.astype(out_ref.dtype)


def project(plan, part, block, weight, before, dtype):
    operands = [block, weight] + ([] if before is None else [before])
    return local(
        functools.partial(project_kernel, plan, part),
        jax.ShapeDtypeStruct((plan.rows, weight.shape[1]), dtype),
        [pltpu.VMEM] * len(operands),
        "project",
    )(*operands)


def per_device(queries, cache, out_weight, offsets, starts):
    plan = Plan(lax.axis_size("ctx"), queries.shape[0])
    half = plan.half
    out_weight = pltpu.with_memory_space_constraint(out_weight, pltpu.VMEM)

    own = queries.reshape(plan.rows_here, KVH, GROUP, HD)
    own = own.transpose(1, 2, 0, 3).reshape(KVH, GROUP * plan.rows_here, HD)
    far = swap(own, "ctx", half)
    sides = [[block] + [swap(block, "ctx", k) for k in range(1, half)] for block in (own, far)]
    order, one_hot, bias = ready(plan, cache.shape[0], offsets, starts, sides[0][-1])
    keys = pltpu.with_memory_space_constraint(turn(cache, sides[0][-1]), pltpu.VMEM)
    cache = pltpu.with_memory_space_constraint(cache, pltpu.VMEM)
    tables = (keys, cache, bias, order, one_hot)
    if own.shape[1] % 16 != 0:
        sides = [[jnp.concatenate(blocks, axis=1)] for blocks in sides]

    parts = list(reversed(range(half)))
    begun = {part: attend(plan, part, 0, sides[0], *tables) for part in parts}
    received = []
    for part in parts[:-1]:
        (piece,) = attend(plan, part, 1, sides[1], *tables, *begun[part])
        received.append(swap(piece, "ctx", part))
    first, stats = begun[0]
    second, stats = attend(plan, 0, 1, sides[1], *tables, stats)

    near, wide = merge(plan, first, second, stats, received)
    block = settle(plan, wide, near, swap(near, "ctx", plan.across))

    total = project(plan, 0, block, out_weight, None, jnp.float32)
    blocks = [swap(block, "ctx", k) for k in range(1, half)]
    for k in range(1, half):
        dtype = jnp.float32 if k < half - 1 else jnp.bfloat16
        total = project(plan, k, blocks[k - 1], out_weight, total, dtype)
    return from_behind(total, "segment", 1)


def solution(mesh):
    in_specs = (
        P(("segment", "ctx"), None),
        P(("segment", "ctx"), None),
        P("segment", "ctx"),
        P("segment"),
        P("segment"),
    )
    out_specs = P("segment", "ctx")
    return jax.shard_map(
        per_device, mesh=mesh, in_specs=in_specs, out_specs=out_specs, check_vma=False
    )
```

time: 51 us -> 52.5 us (1.029)
  Pallas kernels: 12.7 us -> 17.4 us
  waiting for transfers between devices: 15.2 us -> 12 us
    pallas_call x6 -> x11, Pallas kernels: 8.96 us -> 13.6 us  [the longest x8 10.3 us: attend(): local(functools.partial(attend_kernel, plan, part, side), out_shape, [plt...]
    ppermute x14, waiting for transfers between devices: 11.6 us -> 8.28 us  [swap(): return lax.ppermute(value, axis, [(i, i ^ bits) for i in range(devices)])]
  transfers between devices with their start and end apart: 15 -> 15, of which waited for: 9 -> 5; matrix products, arithmetic and copies ran while one was open for 0% -> 0% of each run, Pallas kernels for 18% -> 27%
where the time goes in v5:
time: 52.5 us; the launch traced here: 52.4 us
  starting transfers between devices  20.7 us (39%)
  Pallas kernels  17.4 us (33%)
  waiting for transfers between devices  12 us (23%)
  between operations  1.67 us (3%)
  local copies, waits for them, and re-layouts  0.67 us (1%)
    ppermute x14, starting transfers between devices, swap(): return lax.ppermute(value, axis, [(i, i ^ bits) for i in range(devices)])  20.7 us
    pallas_call x8, Pallas kernels, attend(): local(functools.partial(attend_kernel, plan, part, side), out_shape, [plt...  10.3 us
    ppermute x14, waiting for transfers between devices, swap(): return lax.ppermute(value, axis, [(i, i ^ bits) for i in range(devices)])  8.28 us
    ppermute x1, waiting for transfers between devices, from_behind(): lax.ppermute(value, axis, [(i, (i + by) % devices) for i in range(devices)])  3.69 us
    pallas_call x4, Pallas kernels, project(): local(functools.partial(project_kernel, plan, part), jax.ShapeDtypeStruct...  3.31 us
    pallas_call x1, Pallas kernels, turn(): local(turn_kernel, pltpu.VMEM((KVH, HD, span), cache.dtype), [pltpu.HBM,...  2.63 us
  transfers between devices with their start and end apart: 15, of which 5 were waited for; matrix products, arithmetic and copies ran while one was open for 0% of the time, Pallas kernels for 27%

profile of v5, /device:TPU:0, one launch (start us, length us, event | category | flops | bytes accessed | tf_op | source)
XLA Modules:
  0.0 52.4 jit_solution(9314725541224193002)
XLA Ops:
  0.0 4.0 %collective-permute-start.3 = (bf16[8,32,128]{2,1,0:T(8,128)(2,1)}, bf16[8,32,128]{2,1,0:T(8,128)(2,1)S(1)}, u32[]{:S(2)}, u32[]{:S(2)}) collective-permute-start(bf16[8,32,128]{2,1,0:T(8,128)(2,1)} %bitcast.13), channel_id=1, source_target_pairs={{0,4},{1,5},{2,6},{3,7},{4,0},{5,1},{6,2},{7,3},{8,12},{9,13},{10,... | collective-permute-start | bytes 196616 | tf_op jit(solution)/shard_map/ppermute | solution.py:25
  4.0 2.5 %collective-permute-start.2 = (bf16[8,32,128]{2,1,0:T(8,128)(2,1)}, bf16[8,32,128]{2,1,0:T(8,128)(2,1)S(1)}, u32[]{:S(2)}, u32[]{:S(2)}) collective-permute-start(bf16[8,32,128]{2,1,0:T(8,128)(2,1)} %bitcast.14), channel_id=1, source_target_pairs={{0,3},{1,2},{2,1},{3,0},{4,7},{5,6},{6,5},{7,4},{8,11},{9,10},{10,... | collective-permute-start | bytes 196616 | tf_op jit(solution)/shard_map/ppermute | solution.py:25
  6.5 0.4 collective-permute-start.1
  7.0 0.5 %collective-permute-start = (bf16[8,32,128]{2,1,0:T(8,128)(2,1)}, bf16[8,32,128]{2,1,0:T(8,128)(2,1)S(1)}, u32[]{:S(2)}, u32[]{:S(2)}) collective-permute-start(bf16[8,32,128]{2,1,0:T(8,128)(2,1)} %bitcast.16), channel_id=1, source_target_pairs={{0,1},{1,0},{2,3},{3,2},{4,5},{5,4},{6,7},{7,6},{8,9},{9,8},{10,11... | collective-permute-start | bytes 196616 | tf_op jit(solution)/shard_map/ppermute | solution.py:25
  8.2 0.0 slice-start
  9.0 0.0 slice-start.1
  9.0 0.0 collective-permute-done.3.refs_0_
  9.0 2.6 %collective-permute-start.6 = (bf16[8,32,128]{2,1,0:T(8,128)(2,1)S(1)}, bf16[8,32,128]{2,1,0:T(8,128)(2,1)S(1)}, u32[]{:S(2)}, u32[]{:S(2)}) collective-permute-start(bf16[8,32,128]{2,1,0:T(8,128)(2,1)S(1)} %collective-permute-done.3.refs_0_), channel_id=1, source_target_pairs={{0,3},{1,2},{2,1},{3,0},{4,7},{5,6},{6,5},{7,4},{8,11},{9,10},{10,... | collective-permute-start | bytes 196616 | tf_op jit(solution)/shard_map/ppermute | solution.py:25
  11.6 0.4 collective-permute-start.5
  12.0 0.0 collective-permute-done.2.after_ref.refs_3_
  12.0 0.5 %collective-permute-start.4 = (bf16[8,32,128]{2,1,0:T(8,128)(2,1)S(1)}, bf16[8,32,128]{2,1,0:T(8,128)(2,1)S(1)}, u32[]{:S(2)}, u32[]{:S(2)}) collective-permute-start(bf16[8,32,128]{2,1,0:T(8,128)(2,1)S(1)} %collective-permute-done.3.refs_0_), channel_id=1, source_target_pairs={{0,1},{1,0},{2,3},{3,2},{4,5},{5,4},{6,7},{7,6},{8,9},{9,8},{10,11... | collective-permute-start | bytes 196616 | tf_op jit(solution)/shard_map/ppermute | solution.py:25
  12.6 2.6 %turn.1.refs_4_ = bf16[8,128,2048]{2,1,0:T(8,128)(2,1)S(1)} custom-call(bf16[2048,2048]{1,0:T(8,128)(2,1)} %refs_5_.15, bf16[8,32,128]{2,1,0:T(8,128)(2,1)S(1)} %collective-permute-done.2.after_ref.refs_3_), custom_call_target="tpu_custom_call" | custom-call | flops 8000000000 | bytes 8388608 | tf_op jit(solution)/shard_map/turn/pallas_call | solution.py:125
  15.2 0.1 ready.1
  15.3 0.0 collective-permute-done.refs_1_
  15.4 1.3 %attend.14.refs_9_ = bf16[272,128]{1,0:T(8,128)(2,1)S(1)} custom-call(bf16[8,32,128]{2,1,0:T(8,128)(2,1)S(1)} %bitcast.17, bf16[8,32,128]{2,1,0:T(8,128)(2,1)S(1)} %collective-permute-done.refs_1_, bf16[8,32,128]{2,1,0:T(8,128)(2,1)S(1)} %collective-permute-done.1.refs_2_, bf16[8,32,128]{2,1,0:T(8,128)(2,1)S(1)} %collective-permute-done.2.after_ref.refs_3_, ...), custom_call_target="tpu_custom_call" | custom-call | flops 268435456 | bytes 2097152 | tf_op jit(solution)/shard_map/attend/pallas_call | solution.py:214
  16.7 1.3 %attend.12.refs_9_ = bf16[272,128]{1,0:T(8,128)(2,1)S(1)} custom-call(bf16[8,32,128]{2,1,0:T(8,128)(2,1)S(1)} %bitcast.18, bf16[8,32,128]{2,1,0:T(8,128)(2,1)S(1)} %collective-permute-done.refs_1_, bf16[8,32,128]{2,1,0:T(8,128)(2,1)S(1)} %collective-permute-done.1.refs_2_, bf16[8,32,128]{2,1,0:T(8,128)(2,1)S(1)} %collective-permute-done.2.after_ref.refs_3_, ...), custom_call_target="tpu_custom_call" | custom-call | flops 268435456 | bytes 2097152 | tf_op jit(solution)/shard_map/attend/pallas_call | solution.py:214
  18.0 1.3 %attend.10.refs_9_ = bf16[272,128]{1,0:T(8,128)(2,1)S(1)} custom-call(bf16[8,32,128]{2,1,0:T(8,128)(2,1)S(1)} %bitcast.19, bf16[8,32,128]{2,1,0:T(8,128)(2,1)S(1)} %collective-permute-done.refs_1_, bf16[8,32,128]{2,1,0:T(8,128)(2,1)S(1)} %collective-permute-done.1.refs_2_, bf16[8,32,128]{2,1,0:T(8,128)(2,1)S(1)} %collective-permute-done.2.after_ref.refs_3_, ...), custom_call_target="tpu_custom_call" | custom-call | flops 268435456 | bytes 2097152 | tf_op jit(solution)/shard_map/attend/pallas_call | solution.py:214
  19.3 0.0 collective-permute-done.6.refs_3_
  19.3 0.0 collective-permute-done.4.refs_1_
  19.3 1.3 %attend.11 = bf16[528,128]{1,0:T(8,128)(2,1)S(1)} custom-call(bf16[8,32,128]{2,1,0:T(8,128)(2,1)S(1)} %collective-permute-done.3.refs_0_, bf16[8,32,128]{2,1,0:T(8,128)(2,1)S(1)} %collective-permute-done.4.refs_1_, bf16[8,32,128]{2,1,0:T(8,128)(2,1)S(1)} %collective-permute-done.5.refs_2_, bf16[8,32,128]{2,1,0:T(8,128)(2,1)S(1)} %collective-permute-done.6.refs_3_, ...), custom_call_target="tpu_custom_call" | custom-call | flops 268435456 | bytes 2097152 | tf_op jit(solution)/shard_map/attend/pallas_call | solution.py:214
  20.6 2.6 %collective-permute-start.7 = (bf16[528,128]{1,0:T(8,128)(2,1)S(1)}, bf16[528,128]{1,0:T(8,128)(2,1)S(1)}, u32[]{:S(2)}, u32[]{:S(2)}) collective-permute-start(bf16[528,128]{1,0:T(8,128)(2,1)S(1)} %attend.11), channel_id=1, source_target_pairs={{0,3},{1,2},{2,1},{3,0},{4,7},{5,6},{6,5},{7,4},{8,11},{9,10},{10,... | collective-permute-start | bytes 405512 | tf_op jit(solution)/shard_map/ppermute | solution.py:25
  23.2 1.2 %attend.13 = bf16[528,128]{1,0:T(8,128)(2,1)S(1)} custom-call(bf16[8,32,128]{2,1,0:T(8,128)(2,1)S(1)} %collective-permute-done.3.refs_0_, bf16[8,32,128]{2,1,0:T(8,128)(2,1)S(1)} %collective-permute-done.4.refs_1_, bf16[8,32,128]{2,1,0:T(8,128)(2,1)S(1)} %collective-permute-done.5.refs_2_, bf16[8,32,128]{2,1,0:T(8,128)(2,1)S(1)} %collective-permute-done.6.refs_3_, ...), custom_call_target="tpu_custom_call" | custom-call | flops 268435456 | bytes 2097152 | tf_op jit(solution)/shard_map/attend/pallas_call | solution.py:214
  24.4 0.5 collective-permute-start.8
  25.0 1.3 %attend.15 = bf16[528,128]{1,0:T(8,128)(2,1)S(1)} custom-call(bf16[8,32,128]{2,1,0:T(8,128)(2,1)S(1)} %collective-permute-done.3.refs_0_, bf16[8,32,128]{2,1,0:T(8,128)(2,1)S(1)} %collective-permute-done.4.refs_1_, bf16[8,32,128]{2,1,0:T(8,128)(2,1)S(1)} %collective-permute-done.5.refs_2_, bf16[8,32,128]{2,1,0:T(8,128)(2,1)S(1)} %collective-permute-done.6.refs_3_, ...), custom_call_target="tpu_custom_call" | custom-call | flops 268435456 | bytes 2097152 | tf_op jit(solution)/shard_map/attend/pallas_call | solution.py:214
  26.2 0.0 slice-start.4
  26.3 0.7 %collective-permute-start.9 = (bf16[528,128]{1,0:T(8,128)(2,1)S(1)}, bf16[528,128]{1,0:T(8,128)(2,1)S(1)}, u32[]{:S(2)}, u32[]{:S(2)}) collective-permute-start(bf16[528,128]{1,0:T(8,128)(2,1)S(1)} %attend.15), channel_id=1, source_target_pairs={{0,1},{1,0},{2,3},{3,2},{4,5},{5,4},{6,7},{7,6},{8,9},{9,8},{10,11... | collective-permute-start | bytes 405512 | tf_op jit(solution)/shard_map/ppermute | solution.py:25
  26.9 1.3 %attend.8 = (f32[256,128]{1,0:T(8,128)S(1)}, bf16[16,128]{1,0:T(8,128)(2,1)S(1)}) custom-call(bf16[8,32,128]{2,1,0:T(8,128)(2,1)S(1)} %bitcast.20, bf16[8,32,128]{2,1,0:T(8,128)(2,1)S(1)} %collective-permute-done.refs_1_, bf16[8,32,128]{2,1,0:T(8,128)(2,1)S(1)} %collective-permute-done.1.refs_2_, ...), custom_call_target="tpu_custom_call" | custom-call | flops 268435456 | bytes 2097152 | tf_op jit(solution)/shard_map/attend/pallas_call | solution.py:214
  28.2 0.0 slice-start.5
  28.2 1.3 %attend.9 = (f32[256,128]{1,0:T(8,128)S(1)}, bf16[16,128]{1,0:T(8,128)(2,1)S(1)}) custom-call(bf16[8,32,128]{2,1,0:T(8,128)(2,1)S(1)} %collective-permute-done.3.refs_0_, bf16[8,32,128]{2,1,0:T(8,128)(2,1)S(1)} %collective-permute-done.4.refs_1_, bf16[8,32,128]{2,1,0:T(8,128)(2,1)S(1)} %collective-permute-done.5.refs_2_, ...), custom_call_target="tpu_custom_call" | custom-call | flops 268435456 | bytes 2097152 | tf_op jit(solution)/shard_map/attend/pallas_call | solution.py:214
  29.5 0.0 collective-permute-done.7.refs_0_
  29.6 1.8 %collective-permute-done.9.refs_2_ = bf16[528,128]{1,0:T(8,128)(2,1)S(1)} collective-permute-done((bf16[528,128]{1,0:T(8,128)(2,1)S(1)}, bf16[528,128]{1,0:T(8,128)(2,1)S(1)}, u32[]{:S(2)}, u32[]{:S(2)}) %collective-permute-start.9) | collective-permute-done | bytes 135200 | tf_op jit(solution)/shard_map/ppermute | solution.py:25
  31.3 0.6 %merge.1 = (bf16[528,128]{1,0:T(8,128)(2,1)S(1)}, f32[512,128]{1,0:T(8,128)S(1)}) custom-call(f32[256,128]{1,0:T(8,128)S(1)} %get-tuple-element.17.first_ref, f32[256,128]{1,0:T(8,128)S(1)} %get-tuple-element.19.second_ref, bf16[16,128]{1,0:T(8,128)(2,1)S(1)} %get-tuple-element.20.stat_ref, bf16[528,128]{1,0:T(8,128)(2,1)S(1)} %collective-permute-done.7.refs_0_, ...), custom_call_target="tpu_custom_call" | custom-call | tf_op jit(solution)/shard_map/merge/pallas_call | solution.py:269
  31.9 2.3 %collective-permute-start.10 = (bf16[528,128]{1,0:T(8,128)(2,1)S(1)}, bf16[528,128]{1,0:T(8,128)(2,1)S(1)}, u32[]{:S(2)}, u32[]{:S(2)}) collective-permute-start(bf16[528,128]{1,0:T(8,128)(2,1)S(1)} %get-tuple-element.22.own_ref), channel_id=1, source_target_pairs={{0,6},{1,7},{2,4},{3,5},{4,2},{5,3},{6,0},{7,1},{8,14},{9,15},{10,... | collective-permute-start | bytes 405512 | tf_op jit(solution)/shard_map/ppermute | solution.py:25
  34.2 4.7 %collective-permute-done.10.other_ref = bf16[528,128]{1,0:T(8,128)(2,1)S(1)} collective-permute-done((bf16[528,128]{1,0:T(8,128)(2,1)S(1)}, bf16[528,128]{1,0:T(8,128)(2,1)S(1)}, u32[]{:S(2)}, u32[]{:S(2)}) %collective-permute-start.10) | collective-permute-done | bytes 135200 | tf_op jit(solution)/shard_map/ppermute | solution.py:25
  38.9 0.4 settle.1.refs_0_
  39.3 0.7 %collective-permute-start.13 = (bf16[32,2048]{1,0:T(8,128)(2,1)S(1)}, bf16[32,2048]{1,0:T(8,128)(2,1)S(1)}, u32[]{:S(2)}, u32[]{:S(2)}) collective-permute-start(bf16[32,2048]{1,0:T(8,128)(2,1)S(1)} %settle.1.refs_0_), channel_id=1, source_target_pairs={{0,1},{1,0},{2,3},{3,2},{4,5},{5,4},{6,7},{7,6},{8,9},{9,8},{10,11... | collective-permute-start | bytes 393224 | tf_op jit(solution)/shard_map/ppermute | solution.py:25
  40.0 1.2 %collective-permute-start.12 = (bf16[32,2048]{1,0:T(8,128)(2,1)S(1)}, bf16[32,2048]{1,0:T(8,128)(2,1)S(1)}, u32[]{:S(2)}, u32[]{:S(2)}) collective-permute-start(bf16[32,2048]{1,0:T(8,128)(2,1)S(1)} %settle.1.refs_0_), channel_id=1, source_target_pairs={{0,2},{1,3},{2,0},{3,1},{4,6},{5,7},{6,4},{7,5},{8,10},{9,11},{10,... | collective-permute-start | bytes 393224 | tf_op jit(solution)/shard_map/ppermute | solution.py:25
  41.1 1.7 %collective-permute-start.11 = (bf16[32,2048]{1,0:T(8,128)(2,1)S(1)}, bf16[32,2048]{1,0:T(8,128)(2,1)S(1)}, u32[]{:S(2)}, u32[]{:S(2)}) collective-permute-start(bf16[32,2048]{1,0:T(8,128)(2,1)S(1)} %settle.1.refs_0_), channel_id=1, source_target_pairs={{0,3},{1,2},{2,1},{3,0},{4,7},{5,6},{6,5},{7,4},{8,11},{9,10},{10,... | collective-permute-start | bytes 393224 | tf_op jit(solution)/shard_map/ppermute | solution.py:25
  42.9 0.8 %project.4.refs_2_ = f32[32,1024]{1,0:T(8,128)S(1)} custom-call(bf16[32,2048]{1,0:T(8,128)(2,1)S(1)} %settle.1.refs_0_, bf16[8192,1024]{1,0:T(8,128)(2,1)S(1)} %bitcast.12), custom_call_target="tpu_custom_call" | custom-call | tf_op jit(solution)/shard_map/project/pallas_call | solution.py:318
  43.7 0.6 %collective-permute-done.13.refs_0_ = bf16[32,2048]{1,0:T(8,128)(2,1)S(1)} collective-permute-done((bf16[32,2048]{1,0:T(8,128)(2,1)S(1)}, bf16[32,2048]{1,0:T(8,128)(2,1)S(1)}, u32[]{:S(2)}, u32[]{:S(2)}) %collective-permute-start.13) | collective-permute-done | bytes 131104 | tf_op jit(solution)/shard_map/ppermute | solution.py:25
  44.4 0.8 %project.5.refs_2_ = f32[32,1024]{1,0:T(8,128)S(1)} custom-call(bf16[32,2048]{1,0:T(8,128)(2,1)S(1)} %collective-permute-done.13.refs_0_, bf16[8192,1024]{1,0:T(8,128)(2,1)S(1)} %bitcast.12, f32[32,1024]{1,0:T(8,128)S(1)} %project.4.refs_2_), custom_call_target="tpu_custom_call" | custom-call | tf_op jit(solution)/shard_map/project/pallas_call | solution.py:318
  45.2 0.0 collective-permute-done.12.refs_0_
  45.2 0.8 %project.6.refs_2_ = f32[32,1024]{1,0:T(8,128)S(1)} custom-call(bf16[32,2048]{1,0:T(8,128)(2,1)S(1)} %collective-permute-done.12.refs_0_, bf16[8192,1024]{1,0:T(8,128)(2,1)S(1)} %bitcast.12, f32[32,1024]{1,0:T(8,128)S(1)} %project.5.refs_2_), custom_call_target="tpu_custom_call" | custom-call | tf_op jit(solution)/shard_map/project/pallas_call | solution.py:318
  46.0 1.2 %collective-permute-done.11.refs_0_ = bf16[32,2048]{1,0:T(8,128)(2,1)S(1)} collective-permute-done((bf16[32,2048]{1,0:T(8,128)(2,1)S(1)}, bf16[32,2048]{1,0:T(8,128)(2,1)S(1)}, u32[]{:S(2)}, u32[]{:S(2)}) %collective-permute-start.11) | collective-permute-done | bytes 131104 | tf_op jit(solution)/shard_map/ppermute | solution.py:25
  47.2 0.8 %project.7 = bf16[32,1024]{1,0:T(8,128)(2,1)S(1)} custom-call(bf16[32,2048]{1,0:T(8,128)(2,1)S(1)} %collective-permute-done.11.refs_0_, bf16[8192,1024]{1,0:T(8,128)(2,1)S(1)} %bitcast.12, f32[32,1024]{1,0:T(8,128)S(1)} %project.6.refs_2_), custom_call_target="tpu_custom_call" | custom-call | tf_op jit(solution)/shard_map/project/pallas_call | solution.py:318
  48.0 0.0 collective-permute-start.14
  48.1 3.7 %collective-permute-done.14 = bf16[32,1024]{1,0:T(8,128)(2,1)S(1)} collective-permute-done((bf16[32,1024]{1,0:T(8,128)(2,1)S(1)}, bf16[32,1024]{1,0:T(8,128)(2,1)S(1)}, u32[]{:S(2)}, u32[]{:S(2)}) %collective-permute-start.14) | collective-permute-done | bytes 65568 | tf_op jit(solution)/shard_map/ppermute | solution.py:30
  51.8 0.6 %copy.10 = bf16[32,1024]{1,0:T(8,128)(2,1)} copy(bf16[32,1024]{1,0:T(8,128)(2,1)S(1)} %collective-permute-done.14) | data formatting | bytes 131072
  (15 shorter events, 0.0 us)
Async XLA Ops:
  0.0 9.0 %collective-permute-start.3 = (bf16[8,32,128]{2,1,0:T(8,128)(2,1)}, bf16[8,32,128]{2,1,0:T(8,128)(2,1)S(1)}, u32[]{:S(2)}, u32[]{:S(2)}) collective-permute-start(bf16[8,32,128]{2,1,0:T(8,128)(2,1)} %bitcast.13), channel_id=1, source_target_pairs={{0,4},{1,5},{2,6},{3,7},{4,0},{5,1},{6,2},{7,3},{8,12},{9,13},{10,... | collective-permute-start | bytes 196616 | tf_op jit(solution)/shard_map/ppermute | solution.py:25
  4.0 8.0 %collective-permute-start.2 = (bf16[8,32,128]{2,1,0:T(8,128)(2,1)}, bf16[8,32,128]{2,1,0:T(8,128)(2,1)S(1)}, u32[]{:S(2)}, u32[]{:S(2)}) collective-permute-start(bf16[8,32,128]{2,1,0:T(8,128)(2,1)} %bitcast.14), channel_id=1, source_target_pairs={{0,3},{1,2},{2,1},{3,0},{4,7},{5,6},{6,5},{7,4},{8,11},{9,10},{10,... | collective-permute-start | bytes 196616 | tf_op jit(solution)/shard_map/ppermute | solution.py:25
  6.5 8.8 %collective-permute-start.1 = (bf16[8,32,128]{2,1,0:T(8,128)(2,1)}, bf16[8,32,128]{2,1,0:T(8,128)(2,1)S(1)}, u32[]{:S(2)}, u32[]{:S(2)}) collective-permute-start(bf16[8,32,128]{2,1,0:T(8,128)(2,1)} %bitcast.15), channel_id=1, source_target_pairs={{0,2},{1,3},{2,0},{3,1},{4,6},{5,7},{6,4},{7,5},{8,10},{9,11},{10,... | collective-permute-start | bytes 196616 | tf_op jit(solution)/shard_map/ppermute | solution.py:25
  7.0 8.4 %collective-permute-start = (bf16[8,32,128]{2,1,0:T(8,128)(2,1)}, bf16[8,32,128]{2,1,0:T(8,128)(2,1)S(1)}, u32[]{:S(2)}, u32[]{:S(2)}) collective-permute-start(bf16[8,32,128]{2,1,0:T(8,128)(2,1)} %bitcast.16), channel_id=1, source_target_pairs={{0,1},{1,0},{2,3},{3,2},{4,5},{5,4},{6,7},{7,6},{8,9},{9,8},{10,11... | collective-permute-start | bytes 196616 | tf_op jit(solution)/shard_map/ppermute | solution.py:25
  8.2 7.2 %slice-start = ((s8[8388608]{0:T(1024)(128)(4,1)}), s8[4194304]{0:T(1024)(128)(4,1)S(1)}, s32[]{:S(2)}) async-start(s8[8388608]{0:T(1024)(128)(4,1)} %bitcast.9), calls=%async_computation | async-start | bytes 8388608
  9.0 6.4 %slice-start.1 = ((s8[8388608]{0:T(1024)(128)(4,1)}), s8[4194304]{0:T(1024)(128)(4,1)S(1)}, s32[]{:S(2)}) async-start(s8[8388608]{0:T(1024)(128)(4,1)} %bitcast.9), calls=%async_computation.1 | async-start | bytes 8388608
  9.0 6.4 %copy-start = (bf16[4,8192]{1,0:T(4,128)(2,1)S(1)}, bf16[4,8192]{1,0:T(4,128)(2,1)}, u32[]{:S(2)}) copy-start(bf16[4,8192]{1,0:T(4,128)(2,1)} %param.5) | copy-start | bytes 196612
  9.0 10.3 %collective-permute-start.6 = (bf16[8,32,128]{2,1,0:T(8,128)(2,1)S(1)}, bf16[8,32,128]{2,1,0:T(8,128)(2,1)S(1)}, u32[]{:S(2)}, u32[]{:S(2)}) collective-permute-start(bf16[8,32,128]{2,1,0:T(8,128)(2,1)S(1)} %collective-permute-done.3.refs_0_), channel_id=1, source_target_pairs={{0,3},{1,2},{2,1},{3,0},{4,7},{5,6},{6,5},{7,4},{8,11},{9,10},{10,... | collective-permute-start | bytes 196616 | tf_op jit(solution)/shard_map/ppermute | solution.py:25
  11.6 7.7 %collective-permute-start.5 = (bf16[8,32,128]{2,1,0:T(8,128)(2,1)S(1)}, bf16[8,32,128]{2,1,0:T(8,128)(2,1)S(1)}, u32[]{:S(2)}, u32[]{:S(2)}) collective-permute-start(bf16[8,32,128]{2,1,0:T(8,128)(2,1)S(1)} %collective-permute-done.3.refs_0_), channel_id=1, source_target_pairs={{0,2},{1,3},{2,0},{3,1},{4,6},{5,7},{6,4},{7,5},{8,10},{9,11},{10,... | collective-permute-start | bytes 196616 | tf_op jit(solution)/shard_map/ppermute | solution.py:25
  12.0 7.3 %collective-permute-start.4 = (bf16[8,32,128]{2,1,0:T(8,128)(2,1)S(1)}, bf16[8,32,128]{2,1,0:T(8,128)(2,1)S(1)}, u32[]{:S(2)}, u32[]{:S(2)}) collective-permute-start(bf16[8,32,128]{2,1,0:T(8,128)(2,1)S(1)} %collective-permute-done.3.refs_0_), channel_id=1, source_target_pairs={{0,1},{1,0},{2,3},{3,2},{4,5},{5,4},{6,7},{7,6},{8,9},{9,8},{10,11... | collective-permute-start | bytes 196616 | tf_op jit(solution)/shard_map/ppermute | solution.py:25
  20.6 8.9 %collective-permute-start.7 = (bf16[528,128]{1,0:T(8,128)(2,1)S(1)}, bf16[528,128]{1,0:T(8,128)(2,1)S(1)}, u32[]{:S(2)}, u32[]{:S(2)}) collective-permute-start(bf16[528,128]{1,0:T(8,128)(2,1)S(1)} %attend.11), channel_id=1, source_target_pairs={{0,3},{1,2},{2,1},{3,0},{4,7},{5,6},{6,5},{7,4},{8,11},{9,10},{10,... | collective-permute-start | bytes 405512 | tf_op jit(solution)/shard_map/ppermute | solution.py:25
  24.4 5.1 %collective-permute-start.8 = (bf16[528,128]{1,0:T(8,128)(2,1)S(1)}, bf16[528,128]{1,0:T(8,128)(2,1)S(1)}, u32[]{:S(2)}, u32[]{:S(2)}) collective-permute-start(bf16[528,128]{1,0:T(8,128)(2,1)S(1)} %attend.13), channel_id=1, source_target_pairs={{0,2},{1,3},{2,0},{3,1},{4,6},{5,7},{6,4},{7,5},{8,10},{9,11},{10,... | collective-permute-start | bytes 405512 | tf_op jit(solution)/shard_map/ppermute | solution.py:25
  25.0 17.9 %slice-start.2 = ((s8[16777216]{0:T(1024)(128)(4,1)}), s8[4194304]{0:T(1024)(128)(4,1)S(1)}, s32[]{:S(2)}) async-start(s8[16777216]{0:T(1024)(128)(4,1)} %bitcast.11), calls=%async_computation.2 | async-start | bytes 8388608
  25.0 17.9 %slice-start.3 = ((s8[16777216]{0:T(1024)(128)(4,1)}), s8[4194304]{0:T(1024)(128)(4,1)S(1)}, s32[]{:S(2)}) async-start(s8[16777216]{0:T(1024)(128)(4,1)} %bitcast.11), calls=%async_computation.3 | async-start | bytes 8388608
  26.2 16.6 %slice-start.4 = ((s8[16777216]{0:T(1024)(128)(4,1)}), s8[4194304]{0:T(1024)(128)(4,1)S(1)}, s32[]{:S(2)}) async-start(s8[16777216]{0:T(1024)(128)(4,1)} %bitcast.11), calls=%async_computation.4 | async-start | bytes 8388608
  26.3 5.1 %collective-permute-start.9 = (bf16[528,128]{1,0:T(8,128)(2,1)S(1)}, bf16[528,128]{1,0:T(8,128)(2,1)S(1)}, u32[]{:S(2)}, u32[]{:S(2)}) collective-permute-start(bf16[528,128]{1,0:T(8,128)(2,1)S(1)} %attend.15), channel_id=1, source_target_pairs={{0,1},{1,0},{2,3},{3,2},{4,5},{5,4},{6,7},{7,6},{8,9},{9,8},{10,11... | collective-permute-start | bytes 405512 | tf_op jit(solution)/shard_map/ppermute | solution.py:25
  28.2 14.7 %slice-start.5 = ((s8[16777216]{0:T(1024)(128)(4,1)}), s8[4194304]{0:T(1024)(128)(4,1)S(1)}, s32[]{:S(2)}) async-start(s8[16777216]{0:T(1024)(128)(4,1)} %bitcast.11), calls=%async_computation.5 | async-start | bytes 8388608
  31.9 7.0 %collective-permute-start.10 = (bf16[528,128]{1,0:T(8,128)(2,1)S(1)}, bf16[528,128]{1,0:T(8,128)(2,1)S(1)}, u32[]{:S(2)}, u32[]{:S(2)}) collective-permute-start(bf16[528,128]{1,0:T(8,128)(2,1)S(1)} %get-tuple-element.22.own_ref), channel_id=1, source_target_pairs={{0,6},{1,7},{2,4},{3,5},{4,2},{5,3},{6,0},{7,1},{8,14},{9,15},{10,... | collective-permute-start | bytes 405512 | tf_op jit(solution)/shard_map/ppermute | solution.py:25
  39.3 5.0 %collective-permute-start.13 = (bf16[32,2048]{1,0:T(8,128)(2,1)S(1)}, bf16[32,2048]{1,0:T(8,128)(2,1)S(1)}, u32[]{:S(2)}, u32[]{:S(2)}) collective-permute-start(bf16[32,2048]{1,0:T(8,128)(2,1)S(1)} %settle.1.refs_0_), channel_id=1, source_target_pairs={{0,1},{1,0},{2,3},{3,2},{4,5},{5,4},{6,7},{7,6},{8,9},{9,8},{10,11... | collective-permute-start | bytes 393224 | tf_op jit(solution)/shard_map/ppermute | solution.py:25
  40.0 5.2 %collective-permute-start.12 = (bf16[32,2048]{1,0:T(8,128)(2,1)S(1)}, bf16[32,2048]{1,0:T(8,128)(2,1)S(1)}, u32[]{:S(2)}, u32[]{:S(2)}) collective-permute-start(bf16[32,2048]{1,0:T(8,128)(2,1)S(1)} %settle.1.refs_0_), channel_id=1, source_target_pairs={{0,2},{1,3},{2,0},{3,1},{4,6},{5,7},{6,4},{7,5},{8,10},{9,11},{10,... | collective-permute-start | bytes 393224 | tf_op jit(solution)/shard_map/ppermute | solution.py:25
  41.1 6.1 %collective-permute-start.11 = (bf16[32,2048]{1,0:T(8,128)(2,1)S(1)}, bf16[32,2048]{1,0:T(8,128)(2,1)S(1)}, u32[]{:S(2)}, u32[]{:S(2)}) collective-permute-start(bf16[32,2048]{1,0:T(8,128)(2,1)S(1)} %settle.1.refs_0_), channel_id=1, source_target_pairs={{0,3},{1,2},{2,1},{3,0},{4,7},{5,6},{6,5},{7,4},{8,11},{9,10},{10,... | collective-permute-start | bytes 393224 | tf_op jit(solution)/shard_map/ppermute | solution.py:25
  48.0 3.7 %collective-permute-start.14 = (bf16[32,1024]{1,0:T(8,128)(2,1)S(1)}, bf16[32,1024]{1,0:T(8,128)(2,1)S(1)}, u32[]{:S(2)}, u32[]{:S(2)}) collective-permute-start(bf16[32,1024]{1,0:T(8,128)(2,1)S(1)} %project.7), channel_id=1, source_target_pairs={{0,8},{8,16},{16,24},{24,0},{1,9},{9,17},{17,25},{25,1},{2,10},{10... | collective-permute-start | bytes 196616 | tf_op jit(solution)/shard_map/ppermute | solution.py:30

commit v6 on v4

--- a/solution.py
+++ b/solution.py
@@ -45,6 +45,7 @@
         self.unit_rows = self.unit_heads * self.rows
         self.blocks = self.unit_rows // 128
         self.share_rows = self.units * self.unit_rows
+        self.by_device = self.unit_heads == GROUP and GROUP * rows_here % 16 == 0
 
     def share(self, part):
         me = lax.axis_index("ctx")
@@ -68,53 +69,42 @@
     )
 
 
-def ready_kernel(plan, offset_ref, start_ref, own_ref, held_ref, order_ref, one_hot_ref, bias_ref, sem):
-    copy = pltpu.make_async_copy(own_ref, held_ref, sem)
-    copy.start()
+def ready_kernel(plan, offset_ref, start_ref, after_ref, order_ref, one_hot_ref, bias_ref):
+    del after_ref
     me = lax.axis_index("ctx")
     low, high = me % plan.half, me // plan.half
     row = lax.broadcasted_iota(jnp.int32, (plan.group_rows, 128), 0)
     lane = lax.broadcasted_iota(jnp.int32, (plan.group_rows, 128), 1)
     query = lax.rem(row, plan.rows)
     device = lax.div(query, plan.rows_here)
-    block = 2 * (lax.rem(device, plan.half) ^ low) + (lax.div(device, plan.half) ^ high)
+    block = device
+    if not plan.by_device:
+        block = 2 * (lax.rem(device, plan.half) ^ low) + (lax.div(device, plan.half) ^ high)
     origin = (block * GROUP + lax.div(row, plan.rows)) * plan.rows_here + lax.rem(query, plan.rows_here)
     for at in range(0, plan.group_rows, 128):
         order_ref[:, at : at + 128] = jnp.where(lane + at == origin, 1.0, 0.0).astype(jnp.bfloat16)
+    if plan.by_device:
+        query = lax.div(row, GROUP * plan.rows_here) * plan.rows_here + lax.rem(row, plan.rows_here)
     one_hot_ref[...] = jnp.where(query == lane, 1.0, 0.0).astype(jnp.bfloat16)
     span = bias_ref.shape[0]
-    offset, start = offset_ref[0], start_ref[0]
-    first = me * span
-    every = (first >= start) & (first + span - 1 <= offset)
-
-    @pl.when(every)
-    def _():
-        bias_ref[...] = jnp.zeros_like(bias_ref)
-
-    @pl.when(jnp.logical_not(every))
-    def _():
-        position = first + lax.broadcasted_iota(jnp.int32, (span, 128), 0)
-        last = offset + lax.broadcasted_iota(jnp.int32, (span, 128), 1)
-        shown = (position >= start) & (position <= last)
-        bias_ref[...] = jnp.where(shown, 0.0, HIDDEN).astype(jnp.bfloat16)
-
-    copy.wait()
-
-
-def ready(plan, span, offsets, starts, own):
+    position = me * span + lax.broadcasted_iota(jnp.int32, (span, 128), 0)
+    asked = lax.broadcasted_iota(jnp.int32, (span, 128), 1)
+    shown = (position >= start_ref[0]) & (position <= offset_ref[0] + asked)
+    bias_ref[...] = jnp.where(shown, 0.0, HIDDEN).astype(jnp.bfloat16)
+
+
+def ready(plan, span, offsets, starts, after):
     return local(
         functools.partial(ready_kernel, plan),
         [
-            pltpu.VMEM(own.shape, own.dtype),
             jax.ShapeDtypeStruct((plan.group_rows, plan.group_rows), jnp.bfloat16),
             jax.ShapeDtypeStruct((plan.group_rows, 128), jnp.bfloat16),
             jax.ShapeDtypeStruct((span, 128), jnp.bfloat16),
         ],
-        [pltpu.SMEM, pltpu.SMEM, pltpu.HBM],
+        [pltpu.SMEM, pltpu.SMEM, pl.ANY],
         "ready",
-        [pltpu.SemaphoreType.DMA],
-        pl.CostEstimate(flops=8_000_000_000, bytes_accessed=4 * span * HD, transcendentals=0),
-    )(offsets, starts, pltpu.with_memory_space_constraint(own, pltpu.HBM))
+        cost=pl.CostEstimate(flops=8_000_000_000, bytes_accessed=4 * span * HD, transcendentals=0),
+    )(offsets, starts, after)
 
 
 def write_stats(ref, at, rows):
@@ -131,10 +121,16 @@
 
 
 def attend_kernel(plan, part, *refs):
-    *query_refs, cache_ref, bias_ref, order_ref, one_hot_ref, out_ref = refs[: -1 - (part == 0)]
-    score_ref = refs[-1]
-    value_ref, stat_ref, stat_at = (out_ref, refs[-2], 0) if part == 0 else (out_ref, out_ref, plan.share_rows)
+    *refs, score_ref, held_ref = refs
+    if part == 0:
+        *refs, value_ref, stat_ref = refs
+        stat_at = 0
+    else:
+        *refs, value_ref = refs
+        stat_ref, stat_at = value_ref, plan.share_rows
+    *query_refs, cache_ref, bias_ref, order_ref, one_hot_ref = refs
     span = cache_ref.shape[0]
+    me = lax.axis_index("ctx")
     mine = plan.share(part)
     row_at = pl.multiple_of((mine * plan.heads) % GROUP * plan.rows, plan.unit_rows)
     order = order_ref[pl.ds(row_at, plan.unit_rows), :]
@@ -143,9 +139,16 @@
     groups = [(mine * plan.heads + unit * plan.unit_heads) // GROUP for unit in range(plan.units)]
     peaks = []
     for unit, group in enumerate(groups):
-        stacked = jnp.concatenate([ref[group] for ref in query_refs], axis=0)
-        queries = jnp.dot(order, stacked, preferred_element_type=jnp.float32)
-        queries = jnp.concatenate([queries.astype(jnp.bfloat16), one_hot], axis=1)
+        if plan.by_device:
+            for block, ref in enumerate(query_refs):
+                device = me ^ (block // 2) ^ (block % 2 * plan.half)
+                to = pl.multiple_of(device * GROUP * plan.rows_here, GROUP * plan.rows_here)
+                held_ref[unit, pl.ds(to, GROUP * plan.rows_here), :] = ref[group]
+            queries = held_ref[unit]
+        else:
+            stacked = jnp.concatenate([ref[group] for ref in query_refs], axis=0)
+            queries = jnp.dot(order, stacked, preferred_element_type=jnp.float32).astype(jnp.bfloat16)
+        queries = jnp.concatenate([queries, one_hot], axis=1)
         key_at = pl.multiple_of(group * HD, HD)
         keys = jnp.concatenate([cache_ref[:, pl.ds(key_at, HD)], bias_ref[...]], axis=1)
         scores = lax.dot_general(queries, keys, (((1,), (1,)), ((), ())), preferred_element_type=jnp.float32)
@@ -190,7 +193,10 @@
         out_shape,
         [pltpu.VMEM] * (len(queries) + 1 + len(tables)),
         "attend",
-        [pltpu.VMEM((plan.units, plan.unit_rows, span), jnp.float32)],
+        [
+            pltpu.VMEM((plan.units, plan.unit_rows, span), jnp.float32),
+            pltpu.VMEM((plan.units, plan.unit_rows, HD), jnp.bfloat16),
+        ],
         pl.CostEstimate(
             flops=4 * plan.share_rows * span * HD,
             bytes_accessed=2 * plan.units * span * HD * 2,
@@ -253,24 +259,29 @@
     )(wide, stats, *parts)
 
 
-def settle_kernel(plan, wide_ref, own_ref, other_ref, out_ref):
+def settle_kernel(plan, wide_ref, own_ref, other_ref, order_ref, out_ref):
     stats = [(own_ref, plan.share_rows), (other_ref, plan.share_rows)]
-    for block in range(plan.units * plan.blocks):
-        _, scale, total = factors(stats, block)
-        done = mix([wide_ref, other_ref], block * 128, columns([f / total for f in scale]))
-        done = done.astype(jnp.bfloat16)
-        for row in range(0, 128, plan.rows):
-            to = (block * 128 + row) // plan.rows * HD
-            out_ref[:, to : to + HD] = done[row : row + plan.rows, :]
-
-
-def settle(plan, wide, own, other):
+    for unit in range(plan.units):
+        done = []
+        for block in range(unit * plan.blocks, (unit + 1) * plan.blocks):
+            _, scale, total = factors(stats, block)
+            mixed = mix([wide_ref, other_ref], block * 128, columns([f / total for f in scale]))
+            done.append(mixed.astype(jnp.bfloat16))
+        done = jnp.concatenate(done, axis=0)
+        if plan.by_device:
+            done = jnp.dot(order_ref[...], done, preferred_element_type=jnp.float32).astype(jnp.bfloat16)
+        for head in range(plan.unit_heads):
+            to = (unit * plan.unit_heads + head) * HD
+            out_ref[:, to : to + HD] = done[head * plan.rows : (head + 1) * plan.rows, :]
+
+
+def settle(plan, wide, own, other, order):
     return local(
         functools.partial(settle_kernel, plan),
         jax.ShapeDtypeStruct((plan.rows, plan.heads * HD), jnp.bfloat16),
-        [pltpu.VMEM] * 3,
+        [pltpu.VMEM] * 4,
         "settle",
-    )(wide, own, other)
+    )(wide, own, other, order)
 
 
 def project_kernel(plan, part, *refs):
@@ -301,11 +312,11 @@
 
     own = queries.reshape(plan.rows_here, KVH, GROUP, HD)
     own = own.transpose(1, 2, 0, 3).reshape(KVH, GROUP * plan.rows_here, HD)
-    held, order, one_hot, bias = ready(plan, cache.shape[0], offsets, starts, own)
     far = swap(own, "ctx", half)
-    if own.shape[1] % 16 == 0:
-        gathered = [held, far]
-        near = [swap(own, "ctx", k) for k in range(1, half)]
+    near = [swap(own, "ctx", k) for k in range(1, half)]
+    order, one_hot, bias = ready(plan, cache.shape[0], offsets, starts, near[-1])
+    if plan.by_device:
+        gathered = [own, far]
         for k in range(1, half):
             gathered += [near[k - 1], swap(far, "ctx", k)]
     else:
@@ -319,7 +330,7 @@
     wide, stats = attend(plan, 0, gathered, cache, bias, order, one_hot)
 
     near, near_wide = merge(plan, wide, stats, received)
-    block = settle(plan, near_wide, near, swap(near, "ctx", plan.across))
+    block = settle(plan, near_wide, near, swap(near, "ctx", plan.across), order)
 
     total = project(plan, 0, block, out_weight, None, jnp.float32)
     blocks = [swap(block, "ctx", k) for k in range(1, half)]

time: 51 us -> 50.5 us (level)
  Pallas kernels: 12.7 us -> 11.5 us
  waiting for transfers between devices: 15.2 us -> 16 us
    pallas_call x4, Pallas kernels: 7.56 us -> 6.74 us  [attend(): local(functools.partial(attend_kernel, plan, part), out_shape, [pltpu.VME...]
    ppermute x14, waiting for transfers between devices: 11.6 us -> 12.3 us  [swap(): return lax.ppermute(value, axis, [(i, i ^ bits) for i in range(devices)])]
    pallas_call x1, Pallas kernels: 0.85 us -> 0.32 us  [ready(): local(functools.partial(ready_kernel, plan), [jax.ShapeDtypeStruct((plan....]
  transfers between devices with their start and end apart: 15 -> 15, of which waited for: 9 -> 9; matrix products, arithmetic and copies ran while one was open for 0% -> 0% of each run, Pallas kernels for 18% -> 16%
where the time goes in v6:
time: 50.5 us; the launch traced here: 50.4 us
  starting transfers between devices  20.8 us (41%)
  waiting for transfers between devices  16 us (32%)
  Pallas kernels  11.5 us (23%)
  between operations  1.46 us (3%)
  local copies, waits for them, and re-layouts  0.67 us (1%)
    ppermute x14, starting transfers between devices, swap(): return lax.ppermute(value, axis, [(i, i ^ bits) for i in range(devices)])  20.8 us
    ppermute x14, waiting for transfers between devices, swap(): return lax.ppermute(value, axis, [(i, i ^ bits) for i in range(devices)])  12.3 us
    pallas_call x4, Pallas kernels, attend(): local(functools.partial(attend_kernel, plan, part), out_shape, [pltpu.VME...  6.74 us
    ppermute x1, waiting for transfers between devices, from_behind(): lax.ppermute(value, axis, [(i, (i + by) % devices) for i in range(devices)])  3.69 us
    pallas_call x4, Pallas kernels, project(): local(functools.partial(project_kernel, plan, part), jax.ShapeDtypeStruct...  3.29 us
  transfers between devices with their start and end apart: 15, of which 9 were waited for; matrix products, arithmetic and copies ran while one was open for 0% of the time, Pallas kernels for 16%

profile of v6, /device:TPU:0, one launch (start us, length us, event | category | flops | bytes accessed | tf_op | source)
XLA Modules:
  0.0 50.4 jit_solution(1168492560692663222)
XLA Ops:
  0.0 4.0 %collective-permute-start = (bf16[8,32,128]{2,1,0:T(8,128)(2,1)}, bf16[8,32,128]{2,1,0:T(8,128)(2,1)S(1)}, u32[]{:S(2)}, u32[]{:S(2)}) collective-permute-start(bf16[8,32,128]{2,1,0:T(8,128)(2,1)} %bitcast.9), channel_id=1, source_target_pairs={{0,4},{1,5},{2,6},{3,7},{4,0},{5,1},{6,2},{7,3},{8,12},{9,13},{10,... | collective-permute-start | bytes 196616 | tf_op jit(solution)/shard_map/ppermute | solution.py:25
  4.0 2.5 %collective-permute-start.5 = (bf16[8,32,128]{2,1,0:T(8,128)(2,1)}, bf16[8,32,128]{2,1,0:T(8,128)(2,1)S(1)}, u32[]{:S(2)}, u32[]{:S(2)}) collective-permute-start(bf16[8,32,128]{2,1,0:T(8,128)(2,1)} %bitcast.10), channel_id=1, source_target_pairs={{0,3},{1,2},{2,1},{3,0},{4,7},{5,6},{6,5},{7,4},{8,11},{9,10},{10,... | collective-permute-start | bytes 196616 | tf_op jit(solution)/shard_map/ppermute | solution.py:25
  6.5 0.4 collective-permute-start.3
  7.0 0.5 %collective-permute-start.1 = (bf16[8,32,128]{2,1,0:T(8,128)(2,1)}, bf16[8,32,128]{2,1,0:T(8,128)(2,1)S(1)}, u32[]{:S(2)}, u32[]{:S(2)}) collective-permute-start(bf16[8,32,128]{2,1,0:T(8,128)(2,1)} %bitcast.12), channel_id=1, source_target_pairs={{0,1},{1,0},{2,3},{3,2},{4,5},{5,4},{6,7},{7,6},{8,9},{9,8},{10,11... | collective-permute-start | bytes 196616 | tf_op jit(solution)/shard_map/ppermute | solution.py:25
  8.8 0.0 slice-start.5
  8.8 0.0 collective-permute-done.refs_1_
  8.8 2.6 %collective-permute-start.6 = (bf16[8,32,128]{2,1,0:T(8,128)(2,1)S(1)}, bf16[8,32,128]{2,1,0:T(8,128)(2,1)S(1)}, u32[]{:S(2)}, u32[]{:S(2)}) collective-permute-start(bf16[8,32,128]{2,1,0:T(8,128)(2,1)S(1)} %collective-permute-done.refs_1_), channel_id=1, source_target_pairs={{0,3},{1,2},{2,1},{3,0},{4,7},{5,6},{6,5},{7,4},{8,11},{9,10},{10,... | collective-permute-start | bytes 196616 | tf_op jit(solution)/shard_map/ppermute | solution.py:25
  11.4 0.4 collective-permute-start.4
  11.9 0.0 collective-permute-done.5.after_ref.refs_6_
  11.9 0.5 %collective-permute-start.2 = (bf16[8,32,128]{2,1,0:T(8,128)(2,1)S(1)}, bf16[8,32,128]{2,1,0:T(8,128)(2,1)S(1)}, u32[]{:S(2)}, u32[]{:S(2)}) collective-permute-start(bf16[8,32,128]{2,1,0:T(8,128)(2,1)S(1)} %collective-permute-done.refs_1_), channel_id=1, source_target_pairs={{0,1},{1,0},{2,3},{3,2},{4,5},{5,4},{6,7},{7,6},{8,9},{9,8},{10,11... | collective-permute-start | bytes 196616 | tf_op jit(solution)/shard_map/ppermute | solution.py:25
  12.4 0.3 ready.1
  12.7 0.0 collective-permute-done.3.refs_4_
  12.7 0.0 collective-permute-done.1.refs_2_
  12.8 1.3 %collective-permute-done.6.refs_7_ = bf16[8,32,128]{2,1,0:T(8,128)(2,1)S(1)} collective-permute-done((bf16[8,32,128]{2,1,0:T(8,128)(2,1)S(1)}, bf16[8,32,128]{2,1,0:T(8,128)(2,1)S(1)}, u32[]{:S(2)}, u32[]{:S(2)}) %collective-permute-start.6) | collective-permute-done | bytes 65568 | tf_op jit(solution)/shard_map/ppermute | solution.py:25
  14.1 1.6 %collective-permute-done.4.refs_5_ = bf16[8,32,128]{2,1,0:T(8,128)(2,1)S(1)} collective-permute-done((bf16[8,32,128]{2,1,0:T(8,128)(2,1)S(1)}, bf16[8,32,128]{2,1,0:T(8,128)(2,1)S(1)}, u32[]{:S(2)}, u32[]{:S(2)}) %collective-permute-start.4) | collective-permute-done | bytes 65568 | tf_op jit(solution)/shard_map/ppermute | solution.py:25
  15.7 0.5 collective-permute-done.2.refs_3_
  16.2 1.7 %attend.5 = bf16[528,128]{1,0:T(8,128)(2,1)S(1)} custom-call(bf16[8,32,128]{2,1,0:T(8,128)(2,1)S(1)} %bitcast.13, bf16[8,32,128]{2,1,0:T(8,128)(2,1)S(1)} %collective-permute-done.refs_1_, bf16[8,32,128]{2,1,0:T(8,128)(2,1)S(1)} %collective-permute-done.1.refs_2_, bf16[8,32,128]{2,1,0:T(8,128)(2,1)S(1)} %collective-permute-done.2.refs_3_, ...), custom_call_target="tpu_custom_call" | custom-call | flops 536870912 | bytes 2097152 | tf_op jit(solution)/shard_map/attend/pallas_call | solution.py:191
  17.9 0.0 slice-start
  17.9 0.0 slice-start.1
  17.9 1.6 %collective-permute-start.7 = (bf16[528,128]{1,0:T(8,128)(2,1)S(1)}, bf16[528,128]{1,0:T(8,128)(2,1)S(1)}, u32[]{:S(2)}, u32[]{:S(2)}) collective-permute-start(bf16[528,128]{1,0:T(8,128)(2,1)S(1)} %attend.5), channel_id=1, source_target_pairs={{0,3},{1,2},{2,1},{3,0},{4,7},{5,6},{6,5},{7,4},{8,11},{9,10},{10,... | collective-permute-start | bytes 405512 | tf_op jit(solution)/shard_map/ppermute | solution.py:25
  19.5 1.7 %attend.6 = bf16[528,128]{1,0:T(8,128)(2,1)S(1)} custom-call(bf16[8,32,128]{2,1,0:T(8,128)(2,1)S(1)} %bitcast.14, bf16[8,32,128]{2,1,0:T(8,128)(2,1)S(1)} %collective-permute-done.refs_1_, bf16[8,32,128]{2,1,0:T(8,128)(2,1)S(1)} %collective-permute-done.1.refs_2_, bf16[8,32,128]{2,1,0:T(8,128)(2,1)S(1)} %collective-permute-done.2.refs_3_, ...), custom_call_target="tpu_custom_call" | custom-call | flops 536870912 | bytes 2097152 | tf_op jit(solution)/shard_map/attend/pallas_call | solution.py:191
  21.2 0.0 slice-start.2
  21.2 0.5 %collective-permute-start.8 = (bf16[528,128]{1,0:T(8,128)(2,1)S(1)}, bf16[528,128]{1,0:T(8,128)(2,1)S(1)}, u32[]{:S(2)}, u32[]{:S(2)}) collective-permute-start(bf16[528,128]{1,0:T(8,128)(2,1)S(1)} %attend.6), channel_id=1, source_target_pairs={{0,2},{1,3},{2,0},{3,1},{4,6},{5,7},{6,4},{7,5},{8,10},{9,11},{10,... | collective-permute-start | bytes 405512 | tf_op jit(solution)/shard_map/ppermute | solution.py:25
  21.7 1.7 %attend.7 = bf16[528,128]{1,0:T(8,128)(2,1)S(1)} custom-call(bf16[8,32,128]{2,1,0:T(8,128)(2,1)S(1)} %bitcast.15, bf16[8,32,128]{2,1,0:T(8,128)(2,1)S(1)} %collective-permute-done.refs_1_, bf16[8,32,128]{2,1,0:T(8,128)(2,1)S(1)} %collective-permute-done.1.refs_2_, bf16[8,32,128]{2,1,0:T(8,128)(2,1)S(1)} %collective-permute-done.2.refs_3_, ...), custom_call_target="tpu_custom_call" | custom-call | flops 536870912 | bytes 2097152 | tf_op jit(solution)/shard_map/attend/pallas_call | solution.py:191
  23.4 0.0 slice-start.3
  23.4 1.5 %collective-permute-start.9 = (bf16[528,128]{1,0:T(8,128)(2,1)S(1)}, bf16[528,128]{1,0:T(8,128)(2,1)S(1)}, u32[]{:S(2)}, u32[]{:S(2)}) collective-permute-start(bf16[528,128]{1,0:T(8,128)(2,1)S(1)} %attend.7), channel_id=1, source_target_pairs={{0,1},{1,0},{2,3},{3,2},{4,5},{5,4},{6,7},{7,6},{8,9},{9,8},{10,11... | collective-permute-start | bytes 405512 | tf_op jit(solution)/shard_map/ppermute | solution.py:25
  24.9 1.6 %attend.4 = (f32[512,128]{1,0:T(8,128)S(1)}, bf16[16,128]{1,0:T(8,128)(2,1)S(1)}) custom-call(bf16[8,32,128]{2,1,0:T(8,128)(2,1)S(1)} %bitcast.16, bf16[8,32,128]{2,1,0:T(8,128)(2,1)S(1)} %collective-permute-done.refs_1_, bf16[8,32,128]{2,1,0:T(8,128)(2,1)S(1)} %collective-permute-done.1.refs_2_, bf16[8,32,128]{2,1,0:T(8,128)(2,1)S(1)} %collective-permute-done.2.refs_3_, ...), custom_call_target="tpu_custom_call" | custom-call | flops 536870912 | bytes 2097152 | tf_op jit(solution)/shard_map/attend/pallas_call | solution.py:191
  26.6 0.0 collective-permute-done.7.refs_0_
  26.6 0.0 collective-permute-done.8.refs_1_
  26.6 1.9 %collective-permute-done.9.refs_2_ = bf16[528,128]{1,0:T(8,128)(2,1)S(1)} collective-permute-done((bf16[528,128]{1,0:T(8,128)(2,1)S(1)}, bf16[528,128]{1,0:T(8,128)(2,1)S(1)}, u32[]{:S(2)}, u32[]{:S(2)}) %collective-permute-start.9) | collective-permute-done | bytes 135200 | tf_op jit(solution)/shard_map/ppermute | solution.py:25
  28.5 0.6 %merge.1 = (bf16[528,128]{1,0:T(8,128)(2,1)S(1)}, f32[512,128]{1,0:T(8,128)S(1)}) custom-call(f32[512,128]{1,0:T(8,128)S(1)} %get-tuple-element.15.wide_ref, bf16[16,128]{1,0:T(8,128)(2,1)S(1)} %get-tuple-element.16.stat_ref, bf16[528,128]{1,0:T(8,128)(2,1)S(1)} %collective-permute-done.7.refs_0_, bf16[528,128]{1,0:T(8,128)(2,1)S(1)} %collective-permute-done.8.refs_1_, ...), custom_call_target="tpu_custom_call" | custom-call | tf_op jit(solution)/shard_map/merge/pallas_call | solution.py:251
  29.0 2.5 %collective-permute-start.10 = (bf16[528,128]{1,0:T(8,128)(2,1)S(1)}, bf16[528,128]{1,0:T(8,128)(2,1)S(1)}, u32[]{:S(2)}, u32[]{:S(2)}) collective-permute-start(bf16[528,128]{1,0:T(8,128)(2,1)S(1)} %get-tuple-element.18.own_ref), channel_id=1, source_target_pairs={{0,6},{1,7},{2,4},{3,5},{4,2},{5,3},{6,0},{7,1},{8,14},{9,15},{10,... | collective-permute-start | bytes 405512 | tf_op jit(solution)/shard_map/ppermute | solution.py:25
  31.6 4.5 %collective-permute-done.10.other_ref = bf16[528,128]{1,0:T(8,128)(2,1)S(1)} collective-permute-done((bf16[528,128]{1,0:T(8,128)(2,1)S(1)}, bf16[528,128]{1,0:T(8,128)(2,1)S(1)}, u32[]{:S(2)}, u32[]{:S(2)}) %collective-permute-start.10) | collective-permute-done | bytes 135200 | tf_op jit(solution)/shard_map/ppermute | solution.py:25
  36.0 0.6 %settle.1.refs_0_ = bf16[32,2048]{1,0:T(8,128)(2,1)S(1)} custom-call(f32[512,128]{1,0:T(8,128)S(1)} %get-tuple-element.17.wide_ref, bf16[528,128]{1,0:T(8,128)(2,1)S(1)} %get-tuple-element.18.own_ref, bf16[528,128]{1,0:T(8,128)(2,1)S(1)} %collective-permute-done.10.other_ref, bf16[256,256]{1,0:T(8,128)(2,1)S(1)} %get-tuple-element.13.refs_10_.order_ref), custom_call_target="tpu_custom_call" | custom-call | tf_op jit(solution)/shard_map/settle/pallas_call | solution.py:279
  36.6 1.6 %collective-permute-start.13 = (bf16[32,2048]{1,0:T(8,128)(2,1)S(1)}, bf16[32,2048]{1,0:T(8,128)(2,1)S(1)}, u32[]{:S(2)}, u32[]{:S(2)}) collective-permute-start(bf16[32,2048]{1,0:T(8,128)(2,1)S(1)} %settle.1.refs_0_), channel_id=1, source_target_pairs={{0,1},{1,0},{2,3},{3,2},{4,5},{5,4},{6,7},{7,6},{8,9},{9,8},{10,11... | collective-permute-start | bytes 393224 | tf_op jit(solution)/shard_map/ppermute | solution.py:25
  38.2 1.1 %collective-permute-start.12 = (bf16[32,2048]{1,0:T(8,128)(2,1)S(1)}, bf16[32,2048]{1,0:T(8,128)(2,1)S(1)}, u32[]{:S(2)}, u32[]{:S(2)}) collective-permute-start(bf16[32,2048]{1,0:T(8,128)(2,1)S(1)} %settle.1.refs_0_), channel_id=1, source_target_pairs={{0,2},{1,3},{2,0},{3,1},{4,6},{5,7},{6,4},{7,5},{8,10},{9,11},{10,... | collective-permute-start | bytes 393224 | tf_op jit(solution)/shard_map/ppermute | solution.py:25
  39.3 0.8 %collective-permute-start.11 = (bf16[32,2048]{1,0:T(8,128)(2,1)S(1)}, bf16[32,2048]{1,0:T(8,128)(2,1)S(1)}, u32[]{:S(2)}, u32[]{:S(2)}) collective-permute-start(bf16[32,2048]{1,0:T(8,128)(2,1)S(1)} %settle.1.refs_0_), channel_id=1, source_target_pairs={{0,3},{1,2},{2,1},{3,0},{4,7},{5,6},{6,5},{7,4},{8,11},{9,10},{10,... | collective-permute-start | bytes 393224 | tf_op jit(solution)/shard_map/ppermute | solution.py:25
  40.2 0.0 slice-done
  40.2 0.8 %project.4.refs_2_ = f32[32,1024]{1,0:T(8,128)S(1)} custom-call(bf16[32,2048]{1,0:T(8,128)(2,1)S(1)} %settle.1.refs_0_, bf16[8192,1024]{1,0:T(8,128)(2,1)S(1)} %bitcast.6), custom_call_target="tpu_custom_call" | custom-call | tf_op jit(solution)/shard_map/project/pallas_call | solution.py:299
  41.0 0.6 %collective-permute-done.13.refs_0_ = bf16[32,2048]{1,0:T(8,128)(2,1)S(1)} collective-permute-done((bf16[32,2048]{1,0:T(8,128)(2,1)S(1)}, bf16[32,2048]{1,0:T(8,128)(2,1)S(1)}, u32[]{:S(2)}, u32[]{:S(2)}) %collective-permute-start.13) | collective-permute-done | bytes 131104 | tf_op jit(solution)/shard_map/ppermute | solution.py:25
  41.6 0.8 %project.5.refs_2_ = f32[32,1024]{1,0:T(8,128)S(1)} custom-call(bf16[32,2048]{1,0:T(8,128)(2,1)S(1)} %collective-permute-done.13.refs_0_, bf16[8192,1024]{1,0:T(8,128)(2,1)S(1)} %bitcast.6, f32[32,1024]{1,0:T(8,128)S(1)} %project.4.refs_2_), custom_call_target="tpu_custom_call" | custom-call | tf_op jit(solution)/shard_map/project/pallas_call | solution.py:299
  42.5 0.7 %collective-permute-done.12.refs_0_ = bf16[32,2048]{1,0:T(8,128)(2,1)S(1)} collective-permute-done((bf16[32,2048]{1,0:T(8,128)(2,1)S(1)}, bf16[32,2048]{1,0:T(8,128)(2,1)S(1)}, u32[]{:S(2)}, u32[]{:S(2)}) %collective-permute-start.12) | collective-permute-done | bytes 131104 | tf_op jit(solution)/shard_map/ppermute | solution.py:25
  43.2 0.8 %project.6.refs_2_ = f32[32,1024]{1,0:T(8,128)S(1)} custom-call(bf16[32,2048]{1,0:T(8,128)(2,1)S(1)} %collective-permute-done.12.refs_0_, bf16[8192,1024]{1,0:T(8,128)(2,1)S(1)} %bitcast.6, f32[32,1024]{1,0:T(8,128)S(1)} %project.5.refs_2_), custom_call_target="tpu_custom_call" | custom-call | tf_op jit(solution)/shard_map/project/pallas_call | solution.py:299
  44.0 1.2 %collective-permute-done.11.refs_0_ = bf16[32,2048]{1,0:T(8,128)(2,1)S(1)} collective-permute-done((bf16[32,2048]{1,0:T(8,128)(2,1)S(1)}, bf16[32,2048]{1,0:T(8,128)(2,1)S(1)}, u32[]{:S(2)}, u32[]{:S(2)}) %collective-permute-start.11) | collective-permute-done | bytes 131104 | tf_op jit(solution)/shard_map/ppermute | solution.py:25
  45.2 0.8 %project.7 = bf16[32,1024]{1,0:T(8,128)(2,1)S(1)} custom-call(bf16[32,2048]{1,0:T(8,128)(2,1)S(1)} %collective-permute-done.11.refs_0_, bf16[8192,1024]{1,0:T(8,128)(2,1)S(1)} %bitcast.6, f32[32,1024]{1,0:T(8,128)S(1)} %project.6.refs_2_), custom_call_target="tpu_custom_call" | custom-call | tf_op jit(solution)/shard_map/project/pallas_call | solution.py:299
  46.0 0.0 collective-permute-start.14
  46.0 3.7 %collective-permute-done.14 = bf16[32,1024]{1,0:T(8,128)(2,1)S(1)} collective-permute-done((bf16[32,1024]{1,0:T(8,128)(2,1)S(1)}, bf16[32,1024]{1,0:T(8,128)(2,1)S(1)}, u32[]{:S(2)}, u32[]{:S(2)}) %collective-permute-start.14) | collective-permute-done | bytes 65568 | tf_op jit(solution)/shard_map/ppermute | solution.py:30
  49.7 0.6 %copy.10 = bf16[32,1024]{1,0:T(8,128)(2,1)} copy(bf16[32,1024]{1,0:T(8,128)(2,1)S(1)} %collective-permute-done.14) | data formatting | bytes 131072
  (10 shorter events, 0.0 us)
Async XLA Ops:
  0.0 16.1 %copy-start = (bf16[4,8192]{1,0:T(4,128)(2,1)S(1)}, bf16[4,8192]{1,0:T(4,128)(2,1)}, u32[]{:S(2)}) copy-start(bf16[4,8192]{1,0:T(4,128)(2,1)} %param.5) | copy-start | bytes 196612
  0.0 16.1 %slice-start.4 = ((s8[8388608]{0:T(1024)(128)(4,1)}), s8[4194304]{0:T(1024)(128)(4,1)S(1)}, s32[]{:S(2)}) async-start(s8[8388608]{0:T(1024)(128)(4,1)} %bitcast.7), calls=%async_computation.4 | async-start | bytes 8388608
  0.0 8.8 %collective-permute-start = (bf16[8,32,128]{2,1,0:T(8,128)(2,1)}, bf16[8,32,128]{2,1,0:T(8,128)(2,1)S(1)}, u32[]{:S(2)}, u32[]{:S(2)}) collective-permute-start(bf16[8,32,128]{2,1,0:T(8,128)(2,1)} %bitcast.9), channel_id=1, source_target_pairs={{0,4},{1,5},{2,6},{3,7},{4,0},{5,1},{6,2},{7,3},{8,12},{9,13},{10,... | collective-permute-start | bytes 196616 | tf_op jit(solution)/shard_map/ppermute | solution.py:25
  4.0 7.8 %collective-permute-start.5 = (bf16[8,32,128]{2,1,0:T(8,128)(2,1)}, bf16[8,32,128]{2,1,0:T(8,128)(2,1)S(1)}, u32[]{:S(2)}, u32[]{:S(2)}) collective-permute-start(bf16[8,32,128]{2,1,0:T(8,128)(2,1)} %bitcast.10), channel_id=1, source_target_pairs={{0,3},{1,2},{2,1},{3,0},{4,7},{5,6},{6,5},{7,4},{8,11},{9,10},{10,... | collective-permute-start | bytes 196616 | tf_op jit(solution)/shard_map/ppermute | solution.py:25
  6.5 6.2 %collective-permute-start.3 = (bf16[8,32,128]{2,1,0:T(8,128)(2,1)}, bf16[8,32,128]{2,1,0:T(8,128)(2,1)S(1)}, u32[]{:S(2)}, u32[]{:S(2)}) collective-permute-start(bf16[8,32,128]{2,1,0:T(8,128)(2,1)} %bitcast.11), channel_id=1, source_target_pairs={{0,2},{1,3},{2,0},{3,1},{4,6},{5,7},{6,4},{7,5},{8,10},{9,11},{10,... | collective-permute-start | bytes 196616 | tf_op jit(solution)/shard_map/ppermute | solution.py:25
  7.0 5.7 %collective-permute-start.1 = (bf16[8,32,128]{2,1,0:T(8,128)(2,1)}, bf16[8,32,128]{2,1,0:T(8,128)(2,1)S(1)}, u32[]{:S(2)}, u32[]{:S(2)}) collective-permute-start(bf16[8,32,128]{2,1,0:T(8,128)(2,1)} %bitcast.12), channel_id=1, source_target_pairs={{0,1},{1,0},{2,3},{3,2},{4,5},{5,4},{6,7},{7,6},{8,9},{9,8},{10,11... | collective-permute-start | bytes 196616 | tf_op jit(solution)/shard_map/ppermute | solution.py:25
  8.8 7.3 %slice-start.5 = ((s8[8388608]{0:T(1024)(128)(4,1)}), s8[4194304]{0:T(1024)(128)(4,1)S(1)}, s32[]{:S(2)}) async-start(s8[8388608]{0:T(1024)(128)(4,1)} %bitcast.7), calls=%async_computation.5 | async-start | bytes 8388608
  8.8 5.2 %collective-permute-start.6 = (bf16[8,32,128]{2,1,0:T(8,128)(2,1)S(1)}, bf16[8,32,128]{2,1,0:T(8,128)(2,1)S(1)}, u32[]{:S(2)}, u32[]{:S(2)}) collective-permute-start(bf16[8,32,128]{2,1,0:T(8,128)(2,1)S(1)} %collective-permute-done.refs_1_), channel_id=1, source_target_pairs={{0,3},{1,2},{2,1},{3,0},{4,7},{5,6},{6,5},{7,4},{8,11},{9,10},{10,... | collective-permute-start | bytes 196616 | tf_op jit(solution)/shard_map/ppermute | solution.py:25
  11.4 4.3 %collective-permute-start.4 = (bf16[8,32,128]{2,1,0:T(8,128)(2,1)S(1)}, bf16[8,32,128]{2,1,0:T(8,128)(2,1)S(1)}, u32[]{:S(2)}, u32[]{:S(2)}) collective-permute-start(bf16[8,32,128]{2,1,0:T(8,128)(2,1)S(1)} %collective-permute-done.refs_1_), channel_id=1, source_target_pairs={{0,2},{1,3},{2,0},{3,1},{4,6},{5,7},{6,4},{7,5},{8,10},{9,11},{10,... | collective-permute-start | bytes 196616 | tf_op jit(solution)/shard_map/ppermute | solution.py:25
  11.9 4.3 %collective-permute-start.2 = (bf16[8,32,128]{2,1,0:T(8,128)(2,1)S(1)}, bf16[8,32,128]{2,1,0:T(8,128)(2,1)S(1)}, u32[]{:S(2)}, u32[]{:S(2)}) collective-permute-start(bf16[8,32,128]{2,1,0:T(8,128)(2,1)S(1)} %collective-permute-done.refs_1_), channel_id=1, source_target_pairs={{0,1},{1,0},{2,3},{3,2},{4,5},{5,4},{6,7},{7,6},{8,9},{9,8},{10,11... | collective-permute-start | bytes 196616 | tf_op jit(solution)/shard_map/ppermute | solution.py:25
  17.9 22.3 %slice-start = ((s8[16777216]{0:T(1024)(128)(4,1)}), s8[4194304]{0:T(1024)(128)(4,1)S(1)}, s32[]{:S(2)}) async-start(s8[16777216]{0:T(1024)(128)(4,1)} %bitcast.5), calls=%async_computation | async-start | bytes 8388608
  17.9 22.3 %slice-start.1 = ((s8[16777216]{0:T(1024)(128)(4,1)}), s8[4194304]{0:T(1024)(128)(4,1)S(1)}, s32[]{:S(2)}) async-start(s8[16777216]{0:T(1024)(128)(4,1)} %bitcast.5), calls=%async_computation.1 | async-start | bytes 8388608
  17.9 8.7 %collective-permute-start.7 = (bf16[528,128]{1,0:T(8,128)(2,1)S(1)}, bf16[528,128]{1,0:T(8,128)(2,1)S(1)}, u32[]{:S(2)}, u32[]{:S(2)}) collective-permute-start(bf16[528,128]{1,0:T(8,128)(2,1)S(1)} %attend.5), channel_id=1, source_target_pairs={{0,3},{1,2},{2,1},{3,0},{4,7},{5,6},{6,5},{7,4},{8,11},{9,10},{10,... | collective-permute-start | bytes 405512 | tf_op jit(solution)/shard_map/ppermute | solution.py:25
  21.2 19.0 %slice-start.2 = ((s8[16777216]{0:T(1024)(128)(4,1)}), s8[4194304]{0:T(1024)(128)(4,1)S(1)}, s32[]{:S(2)}) async-start(s8[16777216]{0:T(1024)(128)(4,1)} %bitcast.5), calls=%async_computation.2 | async-start | bytes 8388608
  21.2 5.4 %collective-permute-start.8 = (bf16[528,128]{1,0:T(8,128)(2,1)S(1)}, bf16[528,128]{1,0:T(8,128)(2,1)S(1)}, u32[]{:S(2)}, u32[]{:S(2)}) collective-permute-start(bf16[528,128]{1,0:T(8,128)(2,1)S(1)} %attend.6), channel_id=1, source_target_pairs={{0,2},{1,3},{2,0},{3,1},{4,6},{5,7},{6,4},{7,5},{8,10},{9,11},{10,... | collective-permute-start | bytes 405512 | tf_op jit(solution)/shard_map/ppermute | solution.py:25
  23.4 16.8 %slice-start.3 = ((s8[16777216]{0:T(1024)(128)(4,1)}), s8[4194304]{0:T(1024)(128)(4,1)S(1)}, s32[]{:S(2)}) async-start(s8[16777216]{0:T(1024)(128)(4,1)} %bitcast.5), calls=%async_computation.3 | async-start | bytes 8388608
  23.4 5.1 %collective-permute-start.9 = (bf16[528,128]{1,0:T(8,128)(2,1)S(1)}, bf16[528,128]{1,0:T(8,128)(2,1)S(1)}, u32[]{:S(2)}, u32[]{:S(2)}) collective-permute-start(bf16[528,128]{1,0:T(8,128)(2,1)S(1)} %attend.7), channel_id=1, source_target_pairs={{0,1},{1,0},{2,3},{3,2},{4,5},{5,4},{6,7},{7,6},{8,9},{9,8},{10,11... | collective-permute-start | bytes 405512 | tf_op jit(solution)/shard_map/ppermute | solution.py:25
  29.0 7.0 %collective-permute-start.10 = (bf16[528,128]{1,0:T(8,128)(2,1)S(1)}, bf16[528,128]{1,0:T(8,128)(2,1)S(1)}, u32[]{:S(2)}, u32[]{:S(2)}) collective-permute-start(bf16[528,128]{1,0:T(8,128)(2,1)S(1)} %get-tuple-element.18.own_ref), channel_id=1, source_target_pairs={{0,6},{1,7},{2,4},{3,5},{4,2},{5,3},{6,0},{7,1},{8,14},{9,15},{10,... | collective-permute-start | bytes 405512 | tf_op jit(solution)/shard_map/ppermute | solution.py:25
  36.6 5.0 %collective-permute-start.13 = (bf16[32,2048]{1,0:T(8,128)(2,1)S(1)}, bf16[32,2048]{1,0:T(8,128)(2,1)S(1)}, u32[]{:S(2)}, u32[]{:S(2)}) collective-permute-start(bf16[32,2048]{1,0:T(8,128)(2,1)S(1)} %settle.1.refs_0_), channel_id=1, source_target_pairs={{0,1},{1,0},{2,3},{3,2},{4,5},{5,4},{6,7},{7,6},{8,9},{9,8},{10,11... | collective-permute-start | bytes 393224 | tf_op jit(solution)/shard_map/ppermute | solution.py:25
  38.2 5.0 %collective-permute-start.12 = (bf16[32,2048]{1,0:T(8,128)(2,1)S(1)}, bf16[32,2048]{1,0:T(8,128)(2,1)S(1)}, u32[]{:S(2)}, u32[]{:S(2)}) collective-permute-start(bf16[32,2048]{1,0:T(8,128)(2,1)S(1)} %settle.1.refs_0_), channel_id=1, source_target_pairs={{0,2},{1,3},{2,0},{3,1},{4,6},{5,7},{6,4},{7,5},{8,10},{9,11},{10,... | collective-permute-start | bytes 393224 | tf_op jit(solution)/shard_map/ppermute | solution.py:25
  39.3 5.9 %collective-permute-start.11 = (bf16[32,2048]{1,0:T(8,128)(2,1)S(1)}, bf16[32,2048]{1,0:T(8,128)(2,1)S(1)}, u32[]{:S(2)}, u32[]{:S(2)}) collective-permute-start(bf16[32,2048]{1,0:T(8,128)(2,1)S(1)} %settle.1.refs_0_), channel_id=1, source_target_pairs={{0,3},{1,2},{2,1},{3,0},{4,7},{5,6},{6,5},{7,4},{8,11},{9,10},{10,... | collective-permute-start | bytes 393224 | tf_op jit(solution)/shard_map/ppermute | solution.py:25
  46.0 3.7 %collective-permute-start.14 = (bf16[32,1024]{1,0:T(8,128)(2,1)S(1)}, bf16[32,1024]{1,0:T(8,128)(2,1)S(1)}, u32[]{:S(2)}, u32[]{:S(2)}) collective-permute-start(bf16[32,1024]{1,0:T(8,128)(2,1)S(1)} %project.7), channel_id=1, source_target_pairs={{0,8},{8,16},{16,24},{24,0},{1,9},{9,17},{17,25},{25,1},{2,10},{10... | collective-permute-start | bytes 196616 | tf_op jit(solution)/shard_map/ppermute | solution.py:30

commit v7 on v6

--- a/solution.py
+++ b/solution.py
@@ -69,10 +69,9 @@
     )
 
 
-def ready_kernel(plan, offset_ref, start_ref, after_ref, order_ref, one_hot_ref, bias_ref):
-    del after_ref
-    me = lax.axis_index("ctx")
-    low, high = me % plan.half, me // plan.half
+def order_kernel(plan, order_ref, one_hot_ref):
+    low = lax.axis_index("ctx") % plan.half
+    high = lax.axis_index("ctx") // plan.half
     row = lax.broadcasted_iota(jnp.int32, (plan.group_rows, 128), 0)
     lane = lax.broadcasted_iota(jnp.int32, (plan.group_rows, 128), 1)
     query = lax.rem(row, plan.rows)
@@ -86,24 +85,37 @@
     if plan.by_device:
         query = lax.div(row, GROUP * plan.rows_here) * plan.rows_here + lax.rem(row, plan.rows_here)
     one_hot_ref[...] = jnp.where(query == lane, 1.0, 0.0).astype(jnp.bfloat16)
+
+
+def row_order(plan):
+    return local(
+        functools.partial(order_kernel, plan),
+        [
+            jax.ShapeDtypeStruct((plan.group_rows, plan.group_rows), jnp.bfloat16),
+            jax.ShapeDtypeStruct((plan.group_rows, 128), jnp.bfloat16),
+        ],
+        [],
+        "order",
+        cost=pl.CostEstimate(flops=8_000_000_000, bytes_accessed=0, transcendentals=0),
+    )()
+
+
+def mask_kernel(offset_ref, start_ref, after_ref, bias_ref):
+    del after_ref
     span = bias_ref.shape[0]
-    position = me * span + lax.broadcasted_iota(jnp.int32, (span, 128), 0)
+    position = lax.axis_index("ctx") * span + lax.broadcasted_iota(jnp.int32, (span, 128), 0)
     asked = lax.broadcasted_iota(jnp.int32, (span, 128), 1)
     shown = (position >= start_ref[0]) & (position <= offset_ref[0] + asked)
     bias_ref[...] = jnp.where(shown, 0.0, HIDDEN).astype(jnp.bfloat16)
 
 
-def ready(plan, span, offsets, starts, after):
-    return local(
-        functools.partial(ready_kernel, plan),
-        [
-            jax.ShapeDtypeStruct((plan.group_rows, plan.group_rows), jnp.bfloat16),
-            jax.ShapeDtypeStruct((plan.group_rows, 128), jnp.bfloat16),
-            jax.ShapeDtypeStruct((span, 128), jnp.bfloat16),
-        ],
+def mask(span, offsets, starts, after):
+    return local(
+        mask_kernel,
+        jax.ShapeDtypeStruct((span, 128), jnp.bfloat16),
         [pltpu.SMEM, pltpu.SMEM, pl.ANY],
-        "ready",
-        cost=pl.CostEstimate(flops=8_000_000_000, bytes_accessed=4 * span * HD, transcendentals=0),
+        "mask",
+        cost=pl.CostEstimate(flops=1_000_000, bytes_accessed=256 * span, transcendentals=0),
     )(offsets, starts, after)
 
 
@@ -314,7 +326,8 @@
     own = own.transpose(1, 2, 0, 3).reshape(KVH, GROUP * plan.rows_here, HD)
     far = swap(own, "ctx", half)
     near = [swap(own, "ctx", k) for k in range(1, half)]
-    order, one_hot, bias = ready(plan, cache.shape[0], offsets, starts, near[-1])
+    order, one_hot = row_order(plan)
+    bias = mask(cache.shape[0], offsets, starts, near[-1])
     if plan.by_device:
         gathered = [own, far]
         for k in range(1, half):

time: 50.5 us -> 49.3 us (0.976)
  waiting for transfers between devices: 16 us -> 13.3 us
  starting transfers between devices: 20.8 us -> 22.2 us
    ppermute x14, waiting for transfers between devices: 12.3 us -> 9.57 us  [swap(): return lax.ppermute(value, axis, [(i, i ^ bits) for i in range(devices)])]
    ppermute x14, starting transfers between devices: 20.8 us -> 22.2 us  [swap(): return lax.ppermute(value, axis, [(i, i ^ bits) for i in range(devices)])]
  transfers between devices with their start and end apart: 15 -> 15, of which waited for: 9 -> 8; matrix products, arithmetic and copies ran while one was open for 0% -> 0% of each run, Pallas kernels for 16% -> 16%
where the time goes in v7:
time: 49.3 us; the launch traced here: 49.1 us
  starting transfers between devices  22.2 us (45%)
  waiting for transfers between devices  13.3 us (27%)
  Pallas kernels  11.5 us (23%)
  between operations  1.47 us (3%)
  local copies, waits for them, and re-layouts  0.67 us (1%)
    ppermute x14, starting transfers between devices, swap(): return lax.ppermute(value, axis, [(i, i ^ bits) for i in range(devices)])  22.2 us
    ppermute x14, waiting for transfers between devices, swap(): return lax.ppermute(value, axis, [(i, i ^ bits) for i in range(devices)])  9.57 us
    pallas_call x4, Pallas kernels, attend(): local(functools.partial(attend_kernel, plan, part), out_shape, [pltpu.VME...  6.74 us
    ppermute x1, waiting for transfers between devices, from_behind(): lax.ppermute(value, axis, [(i, (i + by) % devices) for i in range(devices)])  3.69 us
    pallas_call x4, Pallas kernels, project(): local(functools.partial(project_kernel, plan, part), jax.ShapeDtypeStruct...  3.29 us
  transfers between devices with their start and end apart: 15, of which 8 were waited for; matrix products, arithmetic and copies ran while one was open for 0% of the time, Pallas kernels for 16%

profile of v7, /device:TPU:0, one launch (start us, length us, event | category | flops | bytes accessed | tf_op | source)
XLA Modules:
  0.0 49.1 jit_solution(9422598832754318381)
XLA Ops:
  0.0 4.1 %collective-permute-start = (bf16[8,32,128]{2,1,0:T(8,128)(2,1)}, bf16[8,32,128]{2,1,0:T(8,128)(2,1)S(1)}, u32[]{:S(2)}, u32[]{:S(2)}) collective-permute-start(bf16[8,32,128]{2,1,0:T(8,128)(2,1)} %bitcast.9), channel_id=1, source_target_pairs={{0,4},{1,5},{2,6},{3,7},{4,0},{5,1},{6,2},{7,3},{8,12},{9,13},{10,... | collective-permute-start | bytes 196616 | tf_op jit(solution)/shard_map/ppermute | solution.py:25
  4.1 2.5 %collective-permute-start.5 = (bf16[8,32,128]{2,1,0:T(8,128)(2,1)}, bf16[8,32,128]{2,1,0:T(8,128)(2,1)S(1)}, u32[]{:S(2)}, u32[]{:S(2)}) collective-permute-start(bf16[8,32,128]{2,1,0:T(8,128)(2,1)} %bitcast.10), channel_id=1, source_target_pairs={{0,3},{1,2},{2,1},{3,0},{4,7},{5,6},{6,5},{7,4},{8,11},{9,10},{10,... | collective-permute-start | bytes 196616 | tf_op jit(solution)/shard_map/ppermute | solution.py:25
  6.6 0.4 collective-permute-start.3
  7.1 0.5 %collective-permute-start.1 = (bf16[8,32,128]{2,1,0:T(8,128)(2,1)}, bf16[8,32,128]{2,1,0:T(8,128)(2,1)S(1)}, u32[]{:S(2)}, u32[]{:S(2)}) collective-permute-start(bf16[8,32,128]{2,1,0:T(8,128)(2,1)} %bitcast.12), channel_id=1, source_target_pairs={{0,1},{1,0},{2,3},{3,2},{4,5},{5,4},{6,7},{7,6},{8,9},{9,8},{10,11... | collective-permute-start | bytes 196616 | tf_op jit(solution)/shard_map/ppermute | solution.py:25
  7.6 0.0 collective-permute-done.refs_1_
  7.6 2.5 %collective-permute-start.6 = (bf16[8,32,128]{2,1,0:T(8,128)(2,1)S(1)}, bf16[8,32,128]{2,1,0:T(8,128)(2,1)S(1)}, u32[]{:S(2)}, u32[]{:S(2)}) collective-permute-start(bf16[8,32,128]{2,1,0:T(8,128)(2,1)S(1)} %collective-permute-done.refs_1_), channel_id=1, source_target_pairs={{0,3},{1,2},{2,1},{3,0},{4,7},{5,6},{6,5},{7,4},{8,11},{9,10},{10,... | collective-permute-start | bytes 196616 | tf_op jit(solution)/shard_map/ppermute | solution.py:25
  10.1 0.6 %collective-permute-start.4 = (bf16[8,32,128]{2,1,0:T(8,128)(2,1)S(1)}, bf16[8,32,128]{2,1,0:T(8,128)(2,1)S(1)}, u32[]{:S(2)}, u32[]{:S(2)}) collective-permute-start(bf16[8,32,128]{2,1,0:T(8,128)(2,1)S(1)} %collective-permute-done.refs_1_), channel_id=1, source_target_pairs={{0,2},{1,3},{2,0},{3,1},{4,6},{5,7},{6,4},{7,5},{8,10},{9,11},{10,... | collective-permute-start | bytes 196616 | tf_op jit(solution)/shard_map/ppermute | solution.py:25
  10.7 0.0 collective-permute-done.5.after_ref.refs_6_
  10.7 1.1 %collective-permute-start.2 = (bf16[8,32,128]{2,1,0:T(8,128)(2,1)S(1)}, bf16[8,32,128]{2,1,0:T(8,128)(2,1)S(1)}, u32[]{:S(2)}, u32[]{:S(2)}) collective-permute-start(bf16[8,32,128]{2,1,0:T(8,128)(2,1)S(1)} %collective-permute-done.refs_1_), channel_id=1, source_target_pairs={{0,1},{1,0},{2,3},{3,2},{4,5},{5,4},{6,7},{7,6},{8,9},{9,8},{10,11... | collective-permute-start | bytes 196616 | tf_op jit(solution)/shard_map/ppermute | solution.py:25
  11.8 0.1 order.1
  13.2 0.2 mask.1.refs_9_
  13.4 0.0 collective-permute-done.3.refs_4_
  13.4 0.0 collective-permute-done.1.refs_2_
  13.4 0.0 collective-permute-done.6.refs_7_
  13.4 0.9 %collective-permute-done.4.refs_5_ = bf16[8,32,128]{2,1,0:T(8,128)(2,1)S(1)} collective-permute-done((bf16[8,32,128]{2,1,0:T(8,128)(2,1)S(1)}, bf16[8,32,128]{2,1,0:T(8,128)(2,1)S(1)}, u32[]{:S(2)}, u32[]{:S(2)}) %collective-permute-start.4) | collective-permute-done | bytes 65568 | tf_op jit(solution)/shard_map/ppermute | solution.py:25
  14.4 0.6 %collective-permute-done.2.refs_3_ = bf16[8,32,128]{2,1,0:T(8,128)(2,1)S(1)} collective-permute-done((bf16[8,32,128]{2,1,0:T(8,128)(2,1)S(1)}, bf16[8,32,128]{2,1,0:T(8,128)(2,1)S(1)}, u32[]{:S(2)}, u32[]{:S(2)}) %collective-permute-start.2) | collective-permute-done | bytes 65568 | tf_op jit(solution)/shard_map/ppermute | solution.py:25
  15.0 0.0 copy-done
  15.0 1.7 %attend.5 = bf16[528,128]{1,0:T(8,128)(2,1)S(1)} custom-call(bf16[8,32,128]{2,1,0:T(8,128)(2,1)S(1)} %bitcast.13, bf16[8,32,128]{2,1,0:T(8,128)(2,1)S(1)} %collective-permute-done.refs_1_, bf16[8,32,128]{2,1,0:T(8,128)(2,1)S(1)} %collective-permute-done.1.refs_2_, bf16[8,32,128]{2,1,0:T(8,128)(2,1)S(1)} %collective-permute-done.2.refs_3_, ...), custom_call_target="tpu_custom_call" | custom-call | flops 536870912 | bytes 2097152 | tf_op jit(solution)/shard_map/attend/pallas_call | solution.py:203
  16.7 0.0 slice-start
  16.7 0.0 slice-start.1
  16.7 1.4 %collective-permute-start.7 = (bf16[528,128]{1,0:T(8,128)(2,1)S(1)}, bf16[528,128]{1,0:T(8,128)(2,1)S(1)}, u32[]{:S(2)}, u32[]{:S(2)}) collective-permute-start(bf16[528,128]{1,0:T(8,128)(2,1)S(1)} %attend.5), channel_id=1, source_target_pairs={{0,3},{1,2},{2,1},{3,0},{4,7},{5,6},{6,5},{7,4},{8,11},{9,10},{10,... | collective-permute-start | bytes 405512 | tf_op jit(solution)/shard_map/ppermute | solution.py:25
  18.2 1.7 %attend.6 = bf16[528,128]{1,0:T(8,128)(2,1)S(1)} custom-call(bf16[8,32,128]{2,1,0:T(8,128)(2,1)S(1)} %bitcast.14, bf16[8,32,128]{2,1,0:T(8,128)(2,1)S(1)} %collective-permute-done.refs_1_, bf16[8,32,128]{2,1,0:T(8,128)(2,1)S(1)} %collective-permute-done.1.refs_2_, bf16[8,32,128]{2,1,0:T(8,128)(2,1)S(1)} %collective-permute-done.2.refs_3_, ...), custom_call_target="tpu_custom_call" | custom-call | flops 536870912 | bytes 2097152 | tf_op jit(solution)/shard_map/attend/pallas_call | solution.py:203
  19.9 0.0 slice-start.2
  19.9 1.2 %collective-permute-start.8 = (bf16[528,128]{1,0:T(8,128)(2,1)S(1)}, bf16[528,128]{1,0:T(8,128)(2,1)S(1)}, u32[]{:S(2)}, u32[]{:S(2)}) collective-permute-start(bf16[528,128]{1,0:T(8,128)(2,1)S(1)} %attend.6), channel_id=1, source_target_pairs={{0,2},{1,3},{2,0},{3,1},{4,6},{5,7},{6,4},{7,5},{8,10},{9,11},{10,... | collective-permute-start | bytes 405512 | tf_op jit(solution)/shard_map/ppermute | solution.py:25
  21.1 1.7 %attend.7 = bf16[528,128]{1,0:T(8,128)(2,1)S(1)} custom-call(bf16[8,32,128]{2,1,0:T(8,128)(2,1)S(1)} %bitcast.15, bf16[8,32,128]{2,1,0:T(8,128)(2,1)S(1)} %collective-permute-done.refs_1_, bf16[8,32,128]{2,1,0:T(8,128)(2,1)S(1)} %collective-permute-done.1.refs_2_, bf16[8,32,128]{2,1,0:T(8,128)(2,1)S(1)} %collective-permute-done.2.refs_3_, ...), custom_call_target="tpu_custom_call" | custom-call | flops 536870912 | bytes 2097152 | tf_op jit(solution)/shard_map/attend/pallas_call | solution.py:203
  22.8 0.0 slice-start.3
  22.8 1.0 %collective-permute-start.9 = (bf16[528,128]{1,0:T(8,128)(2,1)S(1)}, bf16[528,128]{1,0:T(8,128)(2,1)S(1)}, u32[]{:S(2)}, u32[]{:S(2)}) collective-permute-start(bf16[528,128]{1,0:T(8,128)(2,1)S(1)} %attend.7), channel_id=1, source_target_pairs={{0,1},{1,0},{2,3},{3,2},{4,5},{5,4},{6,7},{7,6},{8,9},{9,8},{10,11... | collective-permute-start | bytes 405512 | tf_op jit(solution)/shard_map/ppermute | solution.py:25
  23.8 1.6 %attend.4 = (f32[512,128]{1,0:T(8,128)S(1)}, bf16[16,128]{1,0:T(8,128)(2,1)S(1)}) custom-call(bf16[8,32,128]{2,1,0:T(8,128)(2,1)S(1)} %bitcast.16, bf16[8,32,128]{2,1,0:T(8,128)(2,1)S(1)} %collective-permute-done.refs_1_, bf16[8,32,128]{2,1,0:T(8,128)(2,1)S(1)} %collective-permute-done.1.refs_2_, bf16[8,32,128]{2,1,0:T(8,128)(2,1)S(1)} %collective-permute-done.2.refs_3_, ...), custom_call_target="tpu_custom_call" | custom-call | flops 536870912 | bytes 2097152 | tf_op jit(solution)/shard_map/attend/pallas_call | solution.py:203
  25.4 0.0 collective-permute-done.7.refs_0_
  25.4 0.0 collective-permute-done.8.refs_1_
  25.4 2.4 %collective-permute-done.9.refs_2_ = bf16[528,128]{1,0:T(8,128)(2,1)S(1)} collective-permute-done((bf16[528,128]{1,0:T(8,128)(2,1)S(1)}, bf16[528,128]{1,0:T(8,128)(2,1)S(1)}, u32[]{:S(2)}, u32[]{:S(2)}) %collective-permute-start.9) | collective-permute-done | bytes 135200 | tf_op jit(solution)/shard_map/ppermute | solution.py:25
  27.9 0.6 %merge.1 = (bf16[528,128]{1,0:T(8,128)(2,1)S(1)}, f32[512,128]{1,0:T(8,128)S(1)}) custom-call(f32[512,128]{1,0:T(8,128)S(1)} %get-tuple-element.13.wide_ref, bf16[16,128]{1,0:T(8,128)(2,1)S(1)} %get-tuple-element.14.stat_ref, bf16[528,128]{1,0:T(8,128)(2,1)S(1)} %collective-permute-done.7.refs_0_, bf16[528,128]{1,0:T(8,128)(2,1)S(1)} %collective-permute-done.8.refs_1_, ...), custom_call_target="tpu_custom_call" | custom-call | tf_op jit(solution)/shard_map/merge/pallas_call | solution.py:263
  28.4 3.2 %collective-permute-start.10 = (bf16[528,128]{1,0:T(8,128)(2,1)S(1)}, bf16[528,128]{1,0:T(8,128)(2,1)S(1)}, u32[]{:S(2)}, u32[]{:S(2)}) collective-permute-start(bf16[528,128]{1,0:T(8,128)(2,1)S(1)} %get-tuple-element.16.own_ref), channel_id=1, source_target_pairs={{0,6},{1,7},{2,4},{3,5},{4,2},{5,3},{6,0},{7,1},{8,14},{9,15},{10,... | collective-permute-start | bytes 405512 | tf_op jit(solution)/shard_map/ppermute | solution.py:25
  31.7 3.6 %collective-permute-done.10.other_ref = bf16[528,128]{1,0:T(8,128)(2,1)S(1)} collective-permute-done((bf16[528,128]{1,0:T(8,128)(2,1)S(1)}, bf16[528,128]{1,0:T(8,128)(2,1)S(1)}, u32[]{:S(2)}, u32[]{:S(2)}) %collective-permute-start.10) | collective-permute-done | bytes 135200 | tf_op jit(solution)/shard_map/ppermute | solution.py:25
  35.3 0.6 %settle.1.refs_0_ = bf16[32,2048]{1,0:T(8,128)(2,1)S(1)} custom-call(f32[512,128]{1,0:T(8,128)S(1)} %get-tuple-element.15.wide_ref, bf16[528,128]{1,0:T(8,128)(2,1)S(1)} %get-tuple-element.16.own_ref, bf16[528,128]{1,0:T(8,128)(2,1)S(1)} %collective-permute-done.10.other_ref, bf16[256,256]{1,0:T(8,128)(2,1)S(1)} %get-tuple-element.11.refs_10_.order_ref), custom_call_target="tpu_custom_call" | custom-call | tf_op jit(solution)/shard_map/settle/pallas_call | solution.py:291
  35.9 1.4 %collective-permute-start.13 = (bf16[32,2048]{1,0:T(8,128)(2,1)S(1)}, bf16[32,2048]{1,0:T(8,128)(2,1)S(1)}, u32[]{:S(2)}, u32[]{:S(2)}) collective-permute-start(bf16[32,2048]{1,0:T(8,128)(2,1)S(1)} %settle.1.refs_0_), channel_id=1, source_target_pairs={{0,1},{1,0},{2,3},{3,2},{4,5},{5,4},{6,7},{7,6},{8,9},{9,8},{10,11... | collective-permute-start | bytes 393224 | tf_op jit(solution)/shard_map/ppermute | solution.py:25
  37.3 0.7 %collective-permute-start.12 = (bf16[32,2048]{1,0:T(8,128)(2,1)S(1)}, bf16[32,2048]{1,0:T(8,128)(2,1)S(1)}, u32[]{:S(2)}, u32[]{:S(2)}) collective-permute-start(bf16[32,2048]{1,0:T(8,128)(2,1)S(1)} %settle.1.refs_0_), channel_id=1, source_target_pairs={{0,2},{1,3},{2,0},{3,1},{4,6},{5,7},{6,4},{7,5},{8,10},{9,11},{10,... | collective-permute-start | bytes 393224 | tf_op jit(solution)/shard_map/ppermute | solution.py:25
  38.0 1.4 %collective-permute-start.11 = (bf16[32,2048]{1,0:T(8,128)(2,1)S(1)}, bf16[32,2048]{1,0:T(8,128)(2,1)S(1)}, u32[]{:S(2)}, u32[]{:S(2)}) collective-permute-start(bf16[32,2048]{1,0:T(8,128)(2,1)S(1)} %settle.1.refs_0_), channel_id=1, source_target_pairs={{0,3},{1,2},{2,1},{3,0},{4,7},{5,6},{6,5},{7,4},{8,11},{9,10},{10,... | collective-permute-start | bytes 393224 | tf_op jit(solution)/shard_map/ppermute | solution.py:25
  39.4 0.8 %project.4.refs_2_ = f32[32,1024]{1,0:T(8,128)S(1)} custom-call(bf16[32,2048]{1,0:T(8,128)(2,1)S(1)} %settle.1.refs_0_, bf16[8192,1024]{1,0:T(8,128)(2,1)S(1)} %bitcast.6), custom_call_target="tpu_custom_call" | custom-call | tf_op jit(solution)/shard_map/project/pallas_call | solution.py:311
  40.3 0.6 %collective-permute-done.13.refs_0_ = bf16[32,2048]{1,0:T(8,128)(2,1)S(1)} collective-permute-done((bf16[32,2048]{1,0:T(8,128)(2,1)S(1)}, bf16[32,2048]{1,0:T(8,128)(2,1)S(1)}, u32[]{:S(2)}, u32[]{:S(2)}) %collective-permute-start.13) | collective-permute-done | bytes 131104 | tf_op jit(solution)/shard_map/ppermute | solution.py:25
  40.9 0.8 %project.5.refs_2_ = f32[32,1024]{1,0:T(8,128)S(1)} custom-call(bf16[32,2048]{1,0:T(8,128)(2,1)S(1)} %collective-permute-done.13.refs_0_, bf16[8192,1024]{1,0:T(8,128)(2,1)S(1)} %bitcast.6, f32[32,1024]{1,0:T(8,128)S(1)} %project.4.refs_2_), custom_call_target="tpu_custom_call" | custom-call | tf_op jit(solution)/shard_map/project/pallas_call | solution.py:311
  41.7 0.6 %collective-permute-done.12.refs_0_ = bf16[32,2048]{1,0:T(8,128)(2,1)S(1)} collective-permute-done((bf16[32,2048]{1,0:T(8,128)(2,1)S(1)}, bf16[32,2048]{1,0:T(8,128)(2,1)S(1)}, u32[]{:S(2)}, u32[]{:S(2)}) %collective-permute-start.12) | collective-permute-done | bytes 131104 | tf_op jit(solution)/shard_map/ppermute | solution.py:25
  42.3 0.8 %project.6.refs_2_ = f32[32,1024]{1,0:T(8,128)S(1)} custom-call(bf16[32,2048]{1,0:T(8,128)(2,1)S(1)} %collective-permute-done.12.refs_0_, bf16[8192,1024]{1,0:T(8,128)(2,1)S(1)} %bitcast.6, f32[32,1024]{1,0:T(8,128)S(1)} %project.5.refs_2_), custom_call_target="tpu_custom_call" | custom-call | tf_op jit(solution)/shard_map/project/pallas_call | solution.py:311
  43.1 0.8 %collective-permute-done.11.refs_0_ = bf16[32,2048]{1,0:T(8,128)(2,1)S(1)} collective-permute-done((bf16[32,2048]{1,0:T(8,128)(2,1)S(1)}, bf16[32,2048]{1,0:T(8,128)(2,1)S(1)}, u32[]{:S(2)}, u32[]{:S(2)}) %collective-permute-start.11) | collective-permute-done | bytes 131104 | tf_op jit(solution)/shard_map/ppermute | solution.py:25
  43.9 0.8 %project.7 = bf16[32,1024]{1,0:T(8,128)(2,1)S(1)} custom-call(bf16[32,2048]{1,0:T(8,128)(2,1)S(1)} %collective-permute-done.11.refs_0_, bf16[8192,1024]{1,0:T(8,128)(2,1)S(1)} %bitcast.6, f32[32,1024]{1,0:T(8,128)S(1)} %project.6.refs_2_), custom_call_target="tpu_custom_call" | custom-call | tf_op jit(solution)/shard_map/project/pallas_call | solution.py:311
  44.7 0.0 collective-permute-start.14
  44.7 3.7 %collective-permute-done.14 = bf16[32,1024]{1,0:T(8,128)(2,1)S(1)} collective-permute-done((bf16[32,1024]{1,0:T(8,128)(2,1)S(1)}, bf16[32,1024]{1,0:T(8,128)(2,1)S(1)}, u32[]{:S(2)}, u32[]{:S(2)}) %collective-permute-start.14) | collective-permute-done | bytes 65568 | tf_op jit(solution)/shard_map/ppermute | solution.py:30
  48.4 0.6 %copy.10 = bf16[32,1024]{1,0:T(8,128)(2,1)} copy(bf16[32,1024]{1,0:T(8,128)(2,1)S(1)} %collective-permute-done.14) | data formatting | bytes 131072
  (11 shorter events, 0.0 us)
Async XLA Ops:
  0.0 15.0 %copy-start = (bf16[4,8192]{1,0:T(4,128)(2,1)S(1)}, bf16[4,8192]{1,0:T(4,128)(2,1)}, u32[]{:S(2)}) copy-start(bf16[4,8192]{1,0:T(4,128)(2,1)} %param.5) | copy-start | bytes 196612
  0.0 15.0 %slice-start.4 = ((s8[8388608]{0:T(1024)(128)(4,1)}), s8[4194304]{0:T(1024)(128)(4,1)S(1)}, s32[]{:S(2)}) async-start(s8[8388608]{0:T(1024)(128)(4,1)} %bitcast.7), calls=%async_computation.4 | async-start | bytes 8388608
  0.0 15.0 %slice-start.5 = ((s8[8388608]{0:T(1024)(128)(4,1)}), s8[4194304]{0:T(1024)(128)(4,1)S(1)}, s32[]{:S(2)}) async-start(s8[8388608]{0:T(1024)(128)(4,1)} %bitcast.7), calls=%async_computation.5 | async-start | bytes 8388608
  0.0 7.6 %collective-permute-start = (bf16[8,32,128]{2,1,0:T(8,128)(2,1)}, bf16[8,32,128]{2,1,0:T(8,128)(2,1)S(1)}, u32[]{:S(2)}, u32[]{:S(2)}) collective-permute-start(bf16[8,32,128]{2,1,0:T(8,128)(2,1)} %bitcast.9), channel_id=1, source_target_pairs={{0,4},{1,5},{2,6},{3,7},{4,0},{5,1},{6,2},{7,3},{8,12},{9,13},{10,... | collective-permute-start | bytes 196616 | tf_op jit(solution)/shard_map/ppermute | solution.py:25
  4.1 6.6 %collective-permute-start.5 = (bf16[8,32,128]{2,1,0:T(8,128)(2,1)}, bf16[8,32,128]{2,1,0:T(8,128)(2,1)S(1)}, u32[]{:S(2)}, u32[]{:S(2)}) collective-permute-start(bf16[8,32,128]{2,1,0:T(8,128)(2,1)} %bitcast.10), channel_id=1, source_target_pairs={{0,3},{1,2},{2,1},{3,0},{4,7},{5,6},{6,5},{7,4},{8,11},{9,10},{10,... | collective-permute-start | bytes 196616 | tf_op jit(solution)/shard_map/ppermute | solution.py:25
  6.6 6.8 %collective-permute-start.3 = (bf16[8,32,128]{2,1,0:T(8,128)(2,1)}, bf16[8,32,128]{2,1,0:T(8,128)(2,1)S(1)}, u32[]{:S(2)}, u32[]{:S(2)}) collective-permute-start(bf16[8,32,128]{2,1,0:T(8,128)(2,1)} %bitcast.11), channel_id=1, source_target_pairs={{0,2},{1,3},{2,0},{3,1},{4,6},{5,7},{6,4},{7,5},{8,10},{9,11},{10,... | collective-permute-start | bytes 196616 | tf_op jit(solution)/shard_map/ppermute | solution.py:25
  7.1 6.4 %collective-permute-start.1 = (bf16[8,32,128]{2,1,0:T(8,128)(2,1)}, bf16[8,32,128]{2,1,0:T(8,128)(2,1)S(1)}, u32[]{:S(2)}, u32[]{:S(2)}) collective-permute-start(bf16[8,32,128]{2,1,0:T(8,128)(2,1)} %bitcast.12), channel_id=1, source_target_pairs={{0,1},{1,0},{2,3},{3,2},{4,5},{5,4},{6,7},{7,6},{8,9},{9,8},{10,11... | collective-permute-start | bytes 196616 | tf_op jit(solution)/shard_map/ppermute | solution.py:25
  7.6 5.8 %collective-permute-start.6 = (bf16[8,32,128]{2,1,0:T(8,128)(2,1)S(1)}, bf16[8,32,128]{2,1,0:T(8,128)(2,1)S(1)}, u32[]{:S(2)}, u32[]{:S(2)}) collective-permute-start(bf16[8,32,128]{2,1,0:T(8,128)(2,1)S(1)} %collective-permute-done.refs_1_), channel_id=1, source_target_pairs={{0,3},{1,2},{2,1},{3,0},{4,7},{5,6},{6,5},{7,4},{8,11},{9,10},{10,... | collective-permute-start | bytes 196616 | tf_op jit(solution)/shard_map/ppermute | solution.py:25
  10.1 4.3 %collective-permute-start.4 = (bf16[8,32,128]{2,1,0:T(8,128)(2,1)S(1)}, bf16[8,32,128]{2,1,0:T(8,128)(2,1)S(1)}, u32[]{:S(2)}, u32[]{:S(2)}) collective-permute-start(bf16[8,32,128]{2,1,0:T(8,128)(2,1)S(1)} %collective-permute-done.refs_1_), channel_id=1, source_target_pairs={{0,2},{1,3},{2,0},{3,1},{4,6},{5,7},{6,4},{7,5},{8,10},{9,11},{10,... | collective-permute-start | bytes 196616 | tf_op jit(solution)/shard_map/ppermute | solution.py:25
  10.7 4.3 %collective-permute-start.2 = (bf16[8,32,128]{2,1,0:T(8,128)(2,1)S(1)}, bf16[8,32,128]{2,1,0:T(8,128)(2,1)S(1)}, u32[]{:S(2)}, u32[]{:S(2)}) collective-permute-start(bf16[8,32,128]{2,1,0:T(8,128)(2,1)S(1)} %collective-permute-done.refs_1_), channel_id=1, source_target_pairs={{0,1},{1,0},{2,3},{3,2},{4,5},{5,4},{6,7},{7,6},{8,9},{9,8},{10,11... | collective-permute-start | bytes 196616 | tf_op jit(solution)/shard_map/ppermute | solution.py:25
  16.7 22.7 %slice-start = ((s8[16777216]{0:T(1024)(128)(4,1)}), s8[4194304]{0:T(1024)(128)(4,1)S(1)}, s32[]{:S(2)}) async-start(s8[16777216]{0:T(1024)(128)(4,1)} %bitcast.5), calls=%async_computation | async-start | bytes 8388608
  16.7 22.7 %slice-start.1 = ((s8[16777216]{0:T(1024)(128)(4,1)}), s8[4194304]{0:T(1024)(128)(4,1)S(1)}, s32[]{:S(2)}) async-start(s8[16777216]{0:T(1024)(128)(4,1)} %bitcast.5), calls=%async_computation.1 | async-start | bytes 8388608
  16.7 8.7 %collective-permute-start.7 = (bf16[528,128]{1,0:T(8,128)(2,1)S(1)}, bf16[528,128]{1,0:T(8,128)(2,1)S(1)}, u32[]{:S(2)}, u32[]{:S(2)}) collective-permute-start(bf16[528,128]{1,0:T(8,128)(2,1)S(1)} %attend.5), channel_id=1, source_target_pairs={{0,3},{1,2},{2,1},{3,0},{4,7},{5,6},{6,5},{7,4},{8,11},{9,10},{10,... | collective-permute-start | bytes 405512 | tf_op jit(solution)/shard_map/ppermute | solution.py:25
  19.9 19.6 %slice-start.2 = ((s8[16777216]{0:T(1024)(128)(4,1)}), s8[4194304]{0:T(1024)(128)(4,1)S(1)}, s32[]{:S(2)}) async-start(s8[16777216]{0:T(1024)(128)(4,1)} %bitcast.5), calls=%async_computation.2 | async-start | bytes 8388608
  19.9 5.6 %collective-permute-start.8 = (bf16[528,128]{1,0:T(8,128)(2,1)S(1)}, bf16[528,128]{1,0:T(8,128)(2,1)S(1)}, u32[]{:S(2)}, u32[]{:S(2)}) collective-permute-start(bf16[528,128]{1,0:T(8,128)(2,1)S(1)} %attend.6), channel_id=1, source_target_pairs={{0,2},{1,3},{2,0},{3,1},{4,6},{5,7},{6,4},{7,5},{8,10},{9,11},{10,... | collective-permute-start | bytes 405512 | tf_op jit(solution)/shard_map/ppermute | solution.py:25
  22.8 16.7 %slice-start.3 = ((s8[16777216]{0:T(1024)(128)(4,1)}), s8[4194304]{0:T(1024)(128)(4,1)S(1)}, s32[]{:S(2)}) async-start(s8[16777216]{0:T(1024)(128)(4,1)} %bitcast.5), calls=%async_computation.3 | async-start | bytes 8388608
  22.8 5.1 %collective-permute-start.9 = (bf16[528,128]{1,0:T(8,128)(2,1)S(1)}, bf16[528,128]{1,0:T(8,128)(2,1)S(1)}, u32[]{:S(2)}, u32[]{:S(2)}) collective-permute-start(bf16[528,128]{1,0:T(8,128)(2,1)S(1)} %attend.7), channel_id=1, source_target_pairs={{0,1},{1,0},{2,3},{3,2},{4,5},{5,4},{6,7},{7,6},{8,9},{9,8},{10,11... | collective-permute-start | bytes 405512 | tf_op jit(solution)/shard_map/ppermute | solution.py:25
  28.4 6.9 %collective-permute-start.10 = (bf16[528,128]{1,0:T(8,128)(2,1)S(1)}, bf16[528,128]{1,0:T(8,128)(2,1)S(1)}, u32[]{:S(2)}, u32[]{:S(2)}) collective-permute-start(bf16[528,128]{1,0:T(8,128)(2,1)S(1)} %get-tuple-element.16.own_ref), channel_id=1, source_target_pairs={{0,6},{1,7},{2,4},{3,5},{4,2},{5,3},{6,0},{7,1},{8,14},{9,15},{10,... | collective-permute-start | bytes 405512 | tf_op jit(solution)/shard_map/ppermute | solution.py:25
  35.9 5.0 %collective-permute-start.13 = (bf16[32,2048]{1,0:T(8,128)(2,1)S(1)}, bf16[32,2048]{1,0:T(8,128)(2,1)S(1)}, u32[]{:S(2)}, u32[]{:S(2)}) collective-permute-start(bf16[32,2048]{1,0:T(8,128)(2,1)S(1)} %settle.1.refs_0_), channel_id=1, source_target_pairs={{0,1},{1,0},{2,3},{3,2},{4,5},{5,4},{6,7},{7,6},{8,9},{9,8},{10,11... | collective-permute-start | bytes 393224 | tf_op jit(solution)/shard_map/ppermute | solution.py:25
  37.3 5.0 %collective-permute-start.12 = (bf16[32,2048]{1,0:T(8,128)(2,1)S(1)}, bf16[32,2048]{1,0:T(8,128)(2,1)S(1)}, u32[]{:S(2)}, u32[]{:S(2)}) collective-permute-start(bf16[32,2048]{1,0:T(8,128)(2,1)S(1)} %settle.1.refs_0_), channel_id=1, source_target_pairs={{0,2},{1,3},{2,0},{3,1},{4,6},{5,7},{6,4},{7,5},{8,10},{9,11},{10,... | collective-permute-start | bytes 393224 | tf_op jit(solution)/shard_map/ppermute | solution.py:25
  38.0 5.9 %collective-permute-start.11 = (bf16[32,2048]{1,0:T(8,128)(2,1)S(1)}, bf16[32,2048]{1,0:T(8,128)(2,1)S(1)}, u32[]{:S(2)}, u32[]{:S(2)}) collective-permute-start(bf16[32,2048]{1,0:T(8,128)(2,1)S(1)} %settle.1.refs_0_), channel_id=1, source_target_pairs={{0,3},{1,2},{2,1},{3,0},{4,7},{5,6},{6,5},{7,4},{8,11},{9,10},{10,... | collective-permute-start | bytes 393224 | tf_op jit(solution)/shard_map/ppermute | solution.py:25
  44.7 3.7 %collective-permute-start.14 = (bf16[32,1024]{1,0:T(8,128)(2,1)S(1)}, bf16[32,1024]{1,0:T(8,128)(2,1)S(1)}, u32[]{:S(2)}, u32[]{:S(2)}) collective-permute-start(bf16[32,1024]{1,0:T(8,128)(2,1)S(1)} %project.7), channel_id=1, source_target_pairs={{0,8},{8,16},{16,24},{24,0},{1,9},{9,17},{17,25},{25,1},{2,10},{10... | collective-permute-start | bytes 196616 | tf_op jit(solution)/shard_map/ppermute | solution.py:30

commit v8 on v7

--- a/solution.py
+++ b/solution.py
@@ -218,11 +218,12 @@
 
 
 def columns(rows):
-    index = lax.broadcasted_iota(jnp.int32, (128, 128), 0)
-    table = jnp.zeros((128, 128), jnp.float32)
+    size = -(-len(rows) // 8) * 8
+    index = lax.broadcasted_iota(jnp.int32, (size, 128), 0)
+    table = jnp.zeros((size, 128), jnp.float32)
     for i, row in enumerate(rows):
         table = jnp.where(index == i, row, table)
-    turned = jnp.transpose(table)
+    turned = jnp.transpose(jnp.concatenate([table, jnp.zeros((128 - size, 128), jnp.float32)], axis=0))
     return [turned[:, i : i + 1] for i in range(len(rows))]
 
 
@@ -247,12 +248,15 @@
 def merge_kernel(plan, wide_ref, stat_ref, *refs):
     *parts, out_ref, wide_out_ref = refs
     stats = [(stat_ref, 0)] + [(ref, plan.share_rows) for ref in parts]
-    rows = []
+    rows, scales = [], []
     for block in range(plan.units * plan.blocks):
         joint, scale, total = factors(stats, block)
         rows += [joint, total]
+        scales += scale
+    scales = columns(scales)
+    for block in range(plan.units * plan.blocks):
         at = block * 128
-        mixed = mix([wide_ref] + parts, at, columns(scale))
+        mixed = mix([wide_ref] + parts, at, scales[block * len(stats) : (block + 1) * len(stats)])
         wide_out_ref[at : at + 128, :] = mixed
         out_ref[at : at + 128, :] = mixed.astype(jnp.bfloat16)
     write_stats(out_ref, plan.share_rows, rows)
@@ -273,11 +277,15 @@
 
 def settle_kernel(plan, wide_ref, own_ref, other_ref, order_ref, out_ref):
     stats = [(own_ref, plan.share_rows), (other_ref, plan.share_rows)]
+    scales = []
+    for block in range(plan.units * plan.blocks):
+        _, scale, total = factors(stats, block)
+        scales += [f / total for f in scale]
+    scales = columns(scales)
     for unit in range(plan.units):
         done = []
         for block in range(unit * plan.blocks, (unit + 1) * plan.blocks):
-            _, scale, total = factors(stats, block)
-            mixed = mix([wide_ref, other_ref], block * 128, columns([f / total for f in scale]))
+            mixed = mix([wide_ref, other_ref], block * 128, scales[2 * block : 2 * block + 2])
             done.append(mixed.astype(jnp.bfloat16))
         done = jnp.concatenate(done, axis=0)
         if plan.by_device:
@@ -314,6 +322,23 @@
         [pltpu.VMEM] * len(operands),
         "project",
     )(*operands)
+
+
+def deliver_kernel(value_ref, out_ref, sem):
+    copy = pltpu.make_async_copy(value_ref, out_ref, sem)
+    copy.start()
+    copy.wait()
+
+
+def deliver(value):
+    return pl.pallas_call(
+        deliver_kernel,
+        out_shape=pltpu.HBM(value.shape, value.dtype),
+        in_specs=[pl.BlockSpec(memory_space=pltpu.VMEM)],
+        out_specs=pl.BlockSpec(memory_space=pltpu.HBM),
+        scratch_shapes=[pltpu.SemaphoreType.DMA],
+        name="deliver",
+    )(value)
 
 
 def per_device(queries, cache, out_weight, offsets, starts):
@@ -350,7 +375,7 @@
     for k in range(1, half):
         dtype = jnp.float32 if k < half - 1 else jnp.bfloat16
         total = project(plan, k, blocks[k - 1], out_weight, total, dtype)
-    return from_behind(total, "segment", 1)
+    return deliver(from_behind(total, "segment", 1))
 
 
 def solution(mesh):

time: 49.3 us -> 50.7 us (1.028)
  Pallas kernels: 11.5 us -> 12.9 us
    pallas_call x0 -> x1, Pallas kernels: none -> 1.47 us  [deliver(): pl.pallas_call(deliver_kernel, out_shape=pltpu.HBM(value.shape, value.dty...]
  transfers between devices with their start and end apart: 15 -> 15, of which waited for: 8 -> 8; matrix products, arithmetic and copies ran while one was open for 0% -> 0% of each run, Pallas kernels for 16% -> 15%
where the time goes in v8:
time: 50.7 us; the launch traced here: 50.5 us
  starting transfers between devices  22.2 us (44%)
  waiting for transfers between devices  13.3 us (26%)
  Pallas kernels  12.9 us (25%)
  between operations  1.47 us (3%)
  local copies, waits for them, and re-layouts  0.66 us (1%)
    ppermute x14, starting transfers between devices, swap(): return lax.ppermute(value, axis, [(i, i ^ bits) for i in range(devices)])  22.2 us
    ppermute x14, waiting for transfers between devices, swap(): return lax.ppermute(value, axis, [(i, i ^ bits) for i in range(devices)])  9.57 us
    pallas_call x4, Pallas kernels, attend(): local(functools.partial(attend_kernel, plan, part), out_shape, [pltpu.VME...  6.74 us
    ppermute x1, waiting for transfers between devices, from_behind(): lax.ppermute(value, axis, [(i, (i + by) % devices) for i in range(devices)])  3.69 us
    pallas_call x4, Pallas kernels, project(): local(functools.partial(project_kernel, plan, part), jax.ShapeDtypeStruct...  3.29 us
    pallas_call x1, Pallas kernels, deliver(): pl.pallas_call(deliver_kernel, out_shape=pltpu.HBM(value.shape, value.dty...  1.47 us
  transfers between devices with their start and end apart: 15, of which 8 were waited for; matrix products, arithmetic and copies ran while one was open for 0% of the time, Pallas kernels for 15%

profile of v8, /device:TPU:0, one launch (start us, length us, event | category | flops | bytes accessed | tf_op | source)
XLA Modules:
  0.0 50.5 jit_solution(17248320325843430968)
XLA Ops:
  0.0 4.1 %collective-permute-start = (bf16[8,32,128]{2,1,0:T(8,128)(2,1)}, bf16[8,32,128]{2,1,0:T(8,128)(2,1)S(1)}, u32[]{:S(2)}, u32[]{:S(2)}) collective-permute-start(bf16[8,32,128]{2,1,0:T(8,128)(2,1)} %bitcast.9), channel_id=1, source_target_pairs={{0,4},{1,5},{2,6},{3,7},{4,0},{5,1},{6,2},{7,3},{8,12},{9,13},{10,... | collective-permute-start | bytes 196616 | tf_op jit(solution)/shard_map/ppermute | solution.py:25
  4.1 2.5 %collective-permute-start.5 = (bf16[8,32,128]{2,1,0:T(8,128)(2,1)}, bf16[8,32,128]{2,1,0:T(8,128)(2,1)S(1)}, u32[]{:S(2)}, u32[]{:S(2)}) collective-permute-start(bf16[8,32,128]{2,1,0:T(8,128)(2,1)} %bitcast.10), channel_id=1, source_target_pairs={{0,3},{1,2},{2,1},{3,0},{4,7},{5,6},{6,5},{7,4},{8,11},{9,10},{10,... | collective-permute-start | bytes 196616 | tf_op jit(solution)/shard_map/ppermute | solution.py:25
  6.6 0.4 collective-permute-start.3
  7.1 0.5 %collective-permute-start.1 = (bf16[8,32,128]{2,1,0:T(8,128)(2,1)}, bf16[8,32,128]{2,1,0:T(8,128)(2,1)S(1)}, u32[]{:S(2)}, u32[]{:S(2)}) collective-permute-start(bf16[8,32,128]{2,1,0:T(8,128)(2,1)} %bitcast.12), channel_id=1, source_target_pairs={{0,1},{1,0},{2,3},{3,2},{4,5},{5,4},{6,7},{7,6},{8,9},{9,8},{10,11... | collective-permute-start | bytes 196616 | tf_op jit(solution)/shard_map/ppermute | solution.py:25
  7.6 0.0 collective-permute-done.refs_1_
  7.6 2.5 %collective-permute-start.6 = (bf16[8,32,128]{2,1,0:T(8,128)(2,1)S(1)}, bf16[8,32,128]{2,1,0:T(8,128)(2,1)S(1)}, u32[]{:S(2)}, u32[]{:S(2)}) collective-permute-start(bf16[8,32,128]{2,1,0:T(8,128)(2,1)S(1)} %collective-permute-done.refs_1_), channel_id=1, source_target_pairs={{0,3},{1,2},{2,1},{3,0},{4,7},{5,6},{6,5},{7,4},{8,11},{9,10},{10,... | collective-permute-start | bytes 196616 | tf_op jit(solution)/shard_map/ppermute | solution.py:25
  10.1 0.6 %collective-permute-start.4 = (bf16[8,32,128]{2,1,0:T(8,128)(2,1)S(1)}, bf16[8,32,128]{2,1,0:T(8,128)(2,1)S(1)}, u32[]{:S(2)}, u32[]{:S(2)}) collective-permute-start(bf16[8,32,128]{2,1,0:T(8,128)(2,1)S(1)} %collective-permute-done.refs_1_), channel_id=1, source_target_pairs={{0,2},{1,3},{2,0},{3,1},{4,6},{5,7},{6,4},{7,5},{8,10},{9,11},{10,... | collective-permute-start | bytes 196616 | tf_op jit(solution)/shard_map/ppermute | solution.py:25
  10.7 0.0 collective-permute-done.5.after_ref.refs_6_
  10.7 1.1 %collective-permute-start.2 = (bf16[8,32,128]{2,1,0:T(8,128)(2,1)S(1)}, bf16[8,32,128]{2,1,0:T(8,128)(2,1)S(1)}, u32[]{:S(2)}, u32[]{:S(2)}) collective-permute-start(bf16[8,32,128]{2,1,0:T(8,128)(2,1)S(1)} %collective-permute-done.refs_1_), channel_id=1, source_target_pairs={{0,1},{1,0},{2,3},{3,2},{4,5},{5,4},{6,7},{7,6},{8,9},{9,8},{10,11... | collective-permute-start | bytes 196616 | tf_op jit(solution)/shard_map/ppermute | solution.py:25
  11.8 0.1 order.1
  13.2 0.2 mask.1.refs_9_
  13.4 0.0 collective-permute-done.3.refs_4_
  13.4 0.0 collective-permute-done.1.refs_2_
  13.4 0.0 collective-permute-done.6.refs_7_
  13.4 0.9 %collective-permute-done.4.refs_5_ = bf16[8,32,128]{2,1,0:T(8,128)(2,1)S(1)} collective-permute-done((bf16[8,32,128]{2,1,0:T(8,128)(2,1)S(1)}, bf16[8,32,128]{2,1,0:T(8,128)(2,1)S(1)}, u32[]{:S(2)}, u32[]{:S(2)}) %collective-permute-start.4) | collective-permute-done | bytes 65568 | tf_op jit(solution)/shard_map/ppermute | solution.py:25
  14.4 0.6 %collective-permute-done.2.refs_3_ = bf16[8,32,128]{2,1,0:T(8,128)(2,1)S(1)} collective-permute-done((bf16[8,32,128]{2,1,0:T(8,128)(2,1)S(1)}, bf16[8,32,128]{2,1,0:T(8,128)(2,1)S(1)}, u32[]{:S(2)}, u32[]{:S(2)}) %collective-permute-start.2) | collective-permute-done | bytes 65568 | tf_op jit(solution)/shard_map/ppermute | solution.py:25
  15.0 1.7 %attend.5 = bf16[528,128]{1,0:T(8,128)(2,1)S(1)} custom-call(bf16[8,32,128]{2,1,0:T(8,128)(2,1)S(1)} %bitcast.13, bf16[8,32,128]{2,1,0:T(8,128)(2,1)S(1)} %collective-permute-done.refs_1_, bf16[8,32,128]{2,1,0:T(8,128)(2,1)S(1)} %collective-permute-done.1.refs_2_, bf16[8,32,128]{2,1,0:T(8,128)(2,1)S(1)} %collective-permute-done.2.refs_3_, ...), custom_call_target="tpu_custom_call" | custom-call | flops 536870912 | bytes 2097152 | tf_op jit(solution)/shard_map/attend/pallas_call | solution.py:203
  16.7 0.0 slice-start
  16.7 0.0 slice-start.1
  16.7 1.4 %collective-permute-start.7 = (bf16[528,128]{1,0:T(8,128)(2,1)S(1)}, bf16[528,128]{1,0:T(8,128)(2,1)S(1)}, u32[]{:S(2)}, u32[]{:S(2)}) collective-permute-start(bf16[528,128]{1,0:T(8,128)(2,1)S(1)} %attend.5), channel_id=1, source_target_pairs={{0,3},{1,2},{2,1},{3,0},{4,7},{5,6},{6,5},{7,4},{8,11},{9,10},{10,... | collective-permute-start | bytes 405512 | tf_op jit(solution)/shard_map/ppermute | solution.py:25
  18.2 1.7 %attend.6 = bf16[528,128]{1,0:T(8,128)(2,1)S(1)} custom-call(bf16[8,32,128]{2,1,0:T(8,128)(2,1)S(1)} %bitcast.14, bf16[8,32,128]{2,1,0:T(8,128)(2,1)S(1)} %collective-permute-done.refs_1_, bf16[8,32,128]{2,1,0:T(8,128)(2,1)S(1)} %collective-permute-done.1.refs_2_, bf16[8,32,128]{2,1,0:T(8,128)(2,1)S(1)} %collective-permute-done.2.refs_3_, ...), custom_call_target="tpu_custom_call" | custom-call | flops 536870912 | bytes 2097152 | tf_op jit(solution)/shard_map/attend/pallas_call | solution.py:203
  19.9 0.0 slice-start.2
  19.9 1.2 %collective-permute-start.8 = (bf16[528,128]{1,0:T(8,128)(2,1)S(1)}, bf16[528,128]{1,0:T(8,128)(2,1)S(1)}, u32[]{:S(2)}, u32[]{:S(2)}) collective-permute-start(bf16[528,128]{1,0:T(8,128)(2,1)S(1)} %attend.6), channel_id=1, source_target_pairs={{0,2},{1,3},{2,0},{3,1},{4,6},{5,7},{6,4},{7,5},{8,10},{9,11},{10,... | collective-permute-start | bytes 405512 | tf_op jit(solution)/shard_map/ppermute | solution.py:25
  21.1 1.7 %attend.7 = bf16[528,128]{1,0:T(8,128)(2,1)S(1)} custom-call(bf16[8,32,128]{2,1,0:T(8,128)(2,1)S(1)} %bitcast.15, bf16[8,32,128]{2,1,0:T(8,128)(2,1)S(1)} %collective-permute-done.refs_1_, bf16[8,32,128]{2,1,0:T(8,128)(2,1)S(1)} %collective-permute-done.1.refs_2_, bf16[8,32,128]{2,1,0:T(8,128)(2,1)S(1)} %collective-permute-done.2.refs_3_, ...), custom_call_target="tpu_custom_call" | custom-call | flops 536870912 | bytes 2097152 | tf_op jit(solution)/shard_map/attend/pallas_call | solution.py:203
  22.8 0.0 slice-start.3
  22.8 1.0 %collective-permute-start.9 = (bf16[528,128]{1,0:T(8,128)(2,1)S(1)}, bf16[528,128]{1,0:T(8,128)(2,1)S(1)}, u32[]{:S(2)}, u32[]{:S(2)}) collective-permute-start(bf16[528,128]{1,0:T(8,128)(2,1)S(1)} %attend.7), channel_id=1, source_target_pairs={{0,1},{1,0},{2,3},{3,2},{4,5},{5,4},{6,7},{7,6},{8,9},{9,8},{10,11... | collective-permute-start | bytes 405512 | tf_op jit(solution)/shard_map/ppermute | solution.py:25
  23.8 1.6 %attend.4 = (f32[512,128]{1,0:T(8,128)S(1)}, bf16[16,128]{1,0:T(8,128)(2,1)S(1)}) custom-call(bf16[8,32,128]{2,1,0:T(8,128)(2,1)S(1)} %bitcast.16, bf16[8,32,128]{2,1,0:T(8,128)(2,1)S(1)} %collective-permute-done.refs_1_, bf16[8,32,128]{2,1,0:T(8,128)(2,1)S(1)} %collective-permute-done.1.refs_2_, bf16[8,32,128]{2,1,0:T(8,128)(2,1)S(1)} %collective-permute-done.2.refs_3_, ...), custom_call_target="tpu_custom_call" | custom-call | flops 536870912 | bytes 2097152 | tf_op jit(solution)/shard_map/attend/pallas_call | solution.py:203
  25.4 0.0 collective-permute-done.7.refs_0_
  25.4 0.0 collective-permute-done.8.refs_1_
  25.4 2.4 %collective-permute-done.9.refs_2_ = bf16[528,128]{1,0:T(8,128)(2,1)S(1)} collective-permute-done((bf16[528,128]{1,0:T(8,128)(2,1)S(1)}, bf16[528,128]{1,0:T(8,128)(2,1)S(1)}, u32[]{:S(2)}, u32[]{:S(2)}) %collective-permute-start.9) | collective-permute-done | bytes 135200 | tf_op jit(solution)/shard_map/ppermute | solution.py:25
  27.9 0.5 merge.1
  28.4 3.2 %collective-permute-start.10 = (bf16[528,128]{1,0:T(8,128)(2,1)S(1)}, bf16[528,128]{1,0:T(8,128)(2,1)S(1)}, u32[]{:S(2)}, u32[]{:S(2)}) collective-permute-start(bf16[528,128]{1,0:T(8,128)(2,1)S(1)} %get-tuple-element.16.own_ref), channel_id=1, source_target_pairs={{0,6},{1,7},{2,4},{3,5},{4,2},{5,3},{6,0},{7,1},{8,14},{9,15},{10,... | collective-permute-start | bytes 405512 | tf_op jit(solution)/shard_map/ppermute | solution.py:25
  31.6 3.6 %collective-permute-done.10.other_ref = bf16[528,128]{1,0:T(8,128)(2,1)S(1)} collective-permute-done((bf16[528,128]{1,0:T(8,128)(2,1)S(1)}, bf16[528,128]{1,0:T(8,128)(2,1)S(1)}, u32[]{:S(2)}, u32[]{:S(2)}) %collective-permute-start.10) | collective-permute-done | bytes 135200 | tf_op jit(solution)/shard_map/ppermute | solution.py:25
  35.2 0.6 %settle.1.refs_0_ = bf16[32,2048]{1,0:T(8,128)(2,1)S(1)} custom-call(f32[512,128]{1,0:T(8,128)S(1)} %get-tuple-element.15.wide_ref, bf16[528,128]{1,0:T(8,128)(2,1)S(1)} %get-tuple-element.16.own_ref, bf16[528,128]{1,0:T(8,128)(2,1)S(1)} %collective-permute-done.10.other_ref, bf16[256,256]{1,0:T(8,128)(2,1)S(1)} %get-tuple-element.11.refs_10_.order_ref), custom_call_target="tpu_custom_call" | custom-call | tf_op jit(solution)/shard_map/settle/pallas_call | solution.py:299
  35.8 1.4 %collective-permute-start.13 = (bf16[32,2048]{1,0:T(8,128)(2,1)S(1)}, bf16[32,2048]{1,0:T(8,128)(2,1)S(1)}, u32[]{:S(2)}, u32[]{:S(2)}) collective-permute-start(bf16[32,2048]{1,0:T(8,128)(2,1)S(1)} %settle.1.refs_0_), channel_id=1, source_target_pairs={{0,1},{1,0},{2,3},{3,2},{4,5},{5,4},{6,7},{7,6},{8,9},{9,8},{10,11... | collective-permute-start | bytes 393224 | tf_op jit(solution)/shard_map/ppermute | solution.py:25
  37.2 0.8 %collective-permute-start.12 = (bf16[32,2048]{1,0:T(8,128)(2,1)S(1)}, bf16[32,2048]{1,0:T(8,128)(2,1)S(1)}, u32[]{:S(2)}, u32[]{:S(2)}) collective-permute-start(bf16[32,2048]{1,0:T(8,128)(2,1)S(1)} %settle.1.refs_0_), channel_id=1, source_target_pairs={{0,2},{1,3},{2,0},{3,1},{4,6},{5,7},{6,4},{7,5},{8,10},{9,11},{10,... | collective-permute-start | bytes 393224 | tf_op jit(solution)/shard_map/ppermute | solution.py:25
  38.0 1.4 %collective-permute-start.11 = (bf16[32,2048]{1,0:T(8,128)(2,1)S(1)}, bf16[32,2048]{1,0:T(8,128)(2,1)S(1)}, u32[]{:S(2)}, u32[]{:S(2)}) collective-permute-start(bf16[32,2048]{1,0:T(8,128)(2,1)S(1)} %settle.1.refs_0_), channel_id=1, source_target_pairs={{0,3},{1,2},{2,1},{3,0},{4,7},{5,6},{6,5},{7,4},{8,11},{9,10},{10,... | collective-permute-start | bytes 393224 | tf_op jit(solution)/shard_map/ppermute | solution.py:25
  39.4 0.8 %project.4.refs_2_ = f32[32,1024]{1,0:T(8,128)S(1)} custom-call(bf16[32,2048]{1,0:T(8,128)(2,1)S(1)} %settle.1.refs_0_, bf16[8192,1024]{1,0:T(8,128)(2,1)S(1)} %bitcast.6), custom_call_target="tpu_custom_call" | custom-call | tf_op jit(solution)/shard_map/project/pallas_call | solution.py:319
  40.2 0.6 %collective-permute-done.13.refs_0_ = bf16[32,2048]{1,0:T(8,128)(2,1)S(1)} collective-permute-done((bf16[32,2048]{1,0:T(8,128)(2,1)S(1)}, bf16[32,2048]{1,0:T(8,128)(2,1)S(1)}, u32[]{:S(2)}, u32[]{:S(2)}) %collective-permute-start.13) | collective-permute-done | bytes 131104 | tf_op jit(solution)/shard_map/ppermute | solution.py:25
  40.9 0.8 %project.5.refs_2_ = f32[32,1024]{1,0:T(8,128)S(1)} custom-call(bf16[32,2048]{1,0:T(8,128)(2,1)S(1)} %collective-permute-done.13.refs_0_, bf16[8192,1024]{1,0:T(8,128)(2,1)S(1)} %bitcast.6, f32[32,1024]{1,0:T(8,128)S(1)} %project.4.refs_2_), custom_call_target="tpu_custom_call" | custom-call | tf_op jit(solution)/shard_map/project/pallas_call | solution.py:319
  41.7 0.5 %collective-permute-done.12.refs_0_ = bf16[32,2048]{1,0:T(8,128)(2,1)S(1)} collective-permute-done((bf16[32,2048]{1,0:T(8,128)(2,1)S(1)}, bf16[32,2048]{1,0:T(8,128)(2,1)S(1)}, u32[]{:S(2)}, u32[]{:S(2)}) %collective-permute-start.12) | collective-permute-done | bytes 131104 | tf_op jit(solution)/shard_map/ppermute | solution.py:25
  42.2 0.8 %project.6.refs_2_ = f32[32,1024]{1,0:T(8,128)S(1)} custom-call(bf16[32,2048]{1,0:T(8,128)(2,1)S(1)} %collective-permute-done.12.refs_0_, bf16[8192,1024]{1,0:T(8,128)(2,1)S(1)} %bitcast.6, f32[32,1024]{1,0:T(8,128)S(1)} %project.5.refs_2_), custom_call_target="tpu_custom_call" | custom-call | tf_op jit(solution)/shard_map/project/pallas_call | solution.py:319
  43.0 0.8 %collective-permute-done.11.refs_0_ = bf16[32,2048]{1,0:T(8,128)(2,1)S(1)} collective-permute-done((bf16[32,2048]{1,0:T(8,128)(2,1)S(1)}, bf16[32,2048]{1,0:T(8,128)(2,1)S(1)}, u32[]{:S(2)}, u32[]{:S(2)}) %collective-permute-start.11) | collective-permute-done | bytes 131104 | tf_op jit(solution)/shard_map/ppermute | solution.py:25
  43.9 0.8 %project.7 = bf16[32,1024]{1,0:T(8,128)(2,1)S(1)} custom-call(bf16[32,2048]{1,0:T(8,128)(2,1)S(1)} %collective-permute-done.11.refs_0_, bf16[8192,1024]{1,0:T(8,128)(2,1)S(1)} %bitcast.6, f32[32,1024]{1,0:T(8,128)S(1)} %project.6.refs_2_), custom_call_target="tpu_custom_call" | custom-call | tf_op jit(solution)/shard_map/project/pallas_call | solution.py:319
  44.7 0.0 collective-permute-start.14
  44.7 3.7 %collective-permute-done.14.value_ref = bf16[32,1024]{1,0:T(8,128)(2,1)S(1)} collective-permute-done((bf16[32,1024]{1,0:T(8,128)(2,1)S(1)}, bf16[32,1024]{1,0:T(8,128)(2,1)S(1)}, u32[]{:S(2)}, u32[]{:S(2)}) %collective-permute-start.14) | collective-permute-done | bytes 65568 | tf_op jit(solution)/shard_map/ppermute | solution.py:30
  48.4 0.6 %copy-done.1 = bf16[32,1024]{1,0:T(8,128)(2,1)} copy-done((bf16[32,1024]{1,0:T(8,128)(2,1)}, bf16[32,1024]{1,0:T(8,128)(2,1)S(1)}, u32[]{:S(2)}) %copy-start.1) | copy-done | bytes 65560
  49.0 1.5 %deliver.1 = bf16[32,1024]{1,0:T(8,128)(2,1)} custom-call(bf16[32,1024]{1,0:T(8,128)(2,1)} %copy-done.1), custom_call_target="tpu_custom_call" | custom-call | tf_op jit(solution)/shard_map/deliver/pallas_call | solution.py:334
  (13 shorter events, 0.0 us)
Async XLA Ops:
  0.0 15.0 %copy-start = (bf16[4,8192]{1,0:T(4,128)(2,1)S(1)}, bf16[4,8192]{1,0:T(4,128)(2,1)}, u32[]{:S(2)}) copy-start(bf16[4,8192]{1,0:T(4,128)(2,1)} %param.5) | copy-start | bytes 196612
  0.0 15.0 %slice-start.4 = ((s8[8388608]{0:T(1024)(128)(4,1)}), s8[4194304]{0:T(1024)(128)(4,1)S(1)}, s32[]{:S(2)}) async-start(s8[8388608]{0:T(1024)(128)(4,1)} %bitcast.7), calls=%async_computation.4 | async-start | bytes 8388608
  0.0 15.0 %slice-start.5 = ((s8[8388608]{0:T(1024)(128)(4,1)}), s8[4194304]{0:T(1024)(128)(4,1)S(1)}, s32[]{:S(2)}) async-start(s8[8388608]{0:T(1024)(128)(4,1)} %bitcast.7), calls=%async_computation.5 | async-start | bytes 8388608
  0.0 7.6 %collective-permute-start = (bf16[8,32,128]{2,1,0:T(8,128)(2,1)}, bf16[8,32,128]{2,1,0:T(8,128)(2,1)S(1)}, u32[]{:S(2)}, u32[]{:S(2)}) collective-permute-start(bf16[8,32,128]{2,1,0:T(8,128)(2,1)} %bitcast.9), channel_id=1, source_target_pairs={{0,4},{1,5},{2,6},{3,7},{4,0},{5,1},{6,2},{7,3},{8,12},{9,13},{10,... | collective-permute-start | bytes 196616 | tf_op jit(solution)/shard_map/ppermute | solution.py:25
  4.1 6.6 %collective-permute-start.5 = (bf16[8,32,128]{2,1,0:T(8,128)(2,1)}, bf16[8,32,128]{2,1,0:T(8,128)(2,1)S(1)}, u32[]{:S(2)}, u32[]{:S(2)}) collective-permute-start(bf16[8,32,128]{2,1,0:T(8,128)(2,1)} %bitcast.10), channel_id=1, source_target_pairs={{0,3},{1,2},{2,1},{3,0},{4,7},{5,6},{6,5},{7,4},{8,11},{9,10},{10,... | collective-permute-start | bytes 196616 | tf_op jit(solution)/shard_map/ppermute | solution.py:25
  6.6 6.8 %collective-permute-start.3 = (bf16[8,32,128]{2,1,0:T(8,128)(2,1)}, bf16[8,32,128]{2,1,0:T(8,128)(2,1)S(1)}, u32[]{:S(2)}, u32[]{:S(2)}) collective-permute-start(bf16[8,32,128]{2,1,0:T(8,128)(2,1)} %bitcast.11), channel_id=1, source_target_pairs={{0,2},{1,3},{2,0},{3,1},{4,6},{5,7},{6,4},{7,5},{8,10},{9,11},{10,... | collective-permute-start | bytes 196616 | tf_op jit(solution)/shard_map/ppermute | solution.py:25
  7.1 6.4 %collective-permute-start.1 = (bf16[8,32,128]{2,1,0:T(8,128)(2,1)}, bf16[8,32,128]{2,1,0:T(8,128)(2,1)S(1)}, u32[]{:S(2)}, u32[]{:S(2)}) collective-permute-start(bf16[8,32,128]{2,1,0:T(8,128)(2,1)} %bitcast.12), channel_id=1, source_target_pairs={{0,1},{1,0},{2,3},{3,2},{4,5},{5,4},{6,7},{7,6},{8,9},{9,8},{10,11... | collective-permute-start | bytes 196616 | tf_op jit(solution)/shard_map/ppermute | solution.py:25
  7.6 5.8 %collective-permute-start.6 = (bf16[8,32,128]{2,1,0:T(8,128)(2,1)S(1)}, bf16[8,32,128]{2,1,0:T(8,128)(2,1)S(1)}, u32[]{:S(2)}, u32[]{:S(2)}) collective-permute-start(bf16[8,32,128]{2,1,0:T(8,128)(2,1)S(1)} %collective-permute-done.refs_1_), channel_id=1, source_target_pairs={{0,3},{1,2},{2,1},{3,0},{4,7},{5,6},{6,5},{7,4},{8,11},{9,10},{10,... | collective-permute-start | bytes 196616 | tf_op jit(solution)/shard_map/ppermute | solution.py:25
  10.1 4.3 %collective-permute-start.4 = (bf16[8,32,128]{2,1,0:T(8,128)(2,1)S(1)}, bf16[8,32,128]{2,1,0:T(8,128)(2,1)S(1)}, u32[]{:S(2)}, u32[]{:S(2)}) collective-permute-start(bf16[8,32,128]{2,1,0:T(8,128)(2,1)S(1)} %collective-permute-done.refs_1_), channel_id=1, source_target_pairs={{0,2},{1,3},{2,0},{3,1},{4,6},{5,7},{6,4},{7,5},{8,10},{9,11},{10,... | collective-permute-start | bytes 196616 | tf_op jit(solution)/shard_map/ppermute | solution.py:25
  10.7 4.3 %collective-permute-start.2 = (bf16[8,32,128]{2,1,0:T(8,128)(2,1)S(1)}, bf16[8,32,128]{2,1,0:T(8,128)(2,1)S(1)}, u32[]{:S(2)}, u32[]{:S(2)}) collective-permute-start(bf16[8,32,128]{2,1,0:T(8,128)(2,1)S(1)} %collective-permute-done.refs_1_), channel_id=1, source_target_pairs={{0,1},{1,0},{2,3},{3,2},{4,5},{5,4},{6,7},{7,6},{8,9},{9,8},{10,11... | collective-permute-start | bytes 196616 | tf_op jit(solution)/shard_map/ppermute | solution.py:25
  16.7 22.7 %slice-start = ((s8[16777216]{0:T(1024)(128)(4,1)}), s8[4194304]{0:T(1024)(128)(4,1)S(1)}, s32[]{:S(2)}) async-start(s8[16777216]{0:T(1024)(128)(4,1)} %bitcast.5), calls=%async_computation | async-start | bytes 8388608
  16.7 22.7 %slice-start.1 = ((s8[16777216]{0:T(1024)(128)(4,1)}), s8[4194304]{0:T(1024)(128)(4,1)S(1)}, s32[]{:S(2)}) async-start(s8[16777216]{0:T(1024)(128)(4,1)} %bitcast.5), calls=%async_computation.1 | async-start | bytes 8388608
  16.7 8.7 %collective-permute-start.7 = (bf16[528,128]{1,0:T(8,128)(2,1)S(1)}, bf16[528,128]{1,0:T(8,128)(2,1)S(1)}, u32[]{:S(2)}, u32[]{:S(2)}) collective-permute-start(bf16[528,128]{1,0:T(8,128)(2,1)S(1)} %attend.5), channel_id=1, source_target_pairs={{0,3},{1,2},{2,1},{3,0},{4,7},{5,6},{6,5},{7,4},{8,11},{9,10},{10,... | collective-permute-start | bytes 405512 | tf_op jit(solution)/shard_map/ppermute | solution.py:25
  19.9 19.5 %slice-start.2 = ((s8[16777216]{0:T(1024)(128)(4,1)}), s8[4194304]{0:T(1024)(128)(4,1)S(1)}, s32[]{:S(2)}) async-start(s8[16777216]{0:T(1024)(128)(4,1)} %bitcast.5), calls=%async_computation.2 | async-start | bytes 8388608
  19.9 5.6 %collective-permute-start.8 = (bf16[528,128]{1,0:T(8,128)(2,1)S(1)}, bf16[528,128]{1,0:T(8,128)(2,1)S(1)}, u32[]{:S(2)}, u32[]{:S(2)}) collective-permute-start(bf16[528,128]{1,0:T(8,128)(2,1)S(1)} %attend.6), channel_id=1, source_target_pairs={{0,2},{1,3},{2,0},{3,1},{4,6},{5,7},{6,4},{7,5},{8,10},{9,11},{10,... | collective-permute-start | bytes 405512 | tf_op jit(solution)/shard_map/ppermute | solution.py:25
  22.8 16.6 %slice-start.3 = ((s8[16777216]{0:T(1024)(128)(4,1)}), s8[4194304]{0:T(1024)(128)(4,1)S(1)}, s32[]{:S(2)}) async-start(s8[16777216]{0:T(1024)(128)(4,1)} %bitcast.5), calls=%async_computation.3 | async-start | bytes 8388608
  22.8 5.1 %collective-permute-start.9 = (bf16[528,128]{1,0:T(8,128)(2,1)S(1)}, bf16[528,128]{1,0:T(8,128)(2,1)S(1)}, u32[]{:S(2)}, u32[]{:S(2)}) collective-permute-start(bf16[528,128]{1,0:T(8,128)(2,1)S(1)} %attend.7), channel_id=1, source_target_pairs={{0,1},{1,0},{2,3},{3,2},{4,5},{5,4},{6,7},{7,6},{8,9},{9,8},{10,11... | collective-permute-start | bytes 405512 | tf_op jit(solution)/shard_map/ppermute | solution.py:25
  28.4 6.9 %collective-permute-start.10 = (bf16[528,128]{1,0:T(8,128)(2,1)S(1)}, bf16[528,128]{1,0:T(8,128)(2,1)S(1)}, u32[]{:S(2)}, u32[]{:S(2)}) collective-permute-start(bf16[528,128]{1,0:T(8,128)(2,1)S(1)} %get-tuple-element.16.own_ref), channel_id=1, source_target_pairs={{0,6},{1,7},{2,4},{3,5},{4,2},{5,3},{6,0},{7,1},{8,14},{9,15},{10,... | collective-permute-start | bytes 405512 | tf_op jit(solution)/shard_map/ppermute | solution.py:25
  35.8 5.0 %collective-permute-start.13 = (bf16[32,2048]{1,0:T(8,128)(2,1)S(1)}, bf16[32,2048]{1,0:T(8,128)(2,1)S(1)}, u32[]{:S(2)}, u32[]{:S(2)}) collective-permute-start(bf16[32,2048]{1,0:T(8,128)(2,1)S(1)} %settle.1.refs_0_), channel_id=1, source_target_pairs={{0,1},{1,0},{2,3},{3,2},{4,5},{5,4},{6,7},{7,6},{8,9},{9,8},{10,11... | collective-permute-start | bytes 393224 | tf_op jit(solution)/shard_map/ppermute | solution.py:25
  37.2 5.0 %collective-permute-start.12 = (bf16[32,2048]{1,0:T(8,128)(2,1)S(1)}, bf16[32,2048]{1,0:T(8,128)(2,1)S(1)}, u32[]{:S(2)}, u32[]{:S(2)}) collective-permute-start(bf16[32,2048]{1,0:T(8,128)(2,1)S(1)} %settle.1.refs_0_), channel_id=1, source_target_pairs={{0,2},{1,3},{2,0},{3,1},{4,6},{5,7},{6,4},{7,5},{8,10},{9,11},{10,... | collective-permute-start | bytes 393224 | tf_op jit(solution)/shard_map/ppermute | solution.py:25
  38.0 5.9 %collective-permute-start.11 = (bf16[32,2048]{1,0:T(8,128)(2,1)S(1)}, bf16[32,2048]{1,0:T(8,128)(2,1)S(1)}, u32[]{:S(2)}, u32[]{:S(2)}) collective-permute-start(bf16[32,2048]{1,0:T(8,128)(2,1)S(1)} %settle.1.refs_0_), channel_id=1, source_target_pairs={{0,3},{1,2},{2,1},{3,0},{4,7},{5,6},{6,5},{7,4},{8,11},{9,10},{10,... | collective-permute-start | bytes 393224 | tf_op jit(solution)/shard_map/ppermute | solution.py:25
  44.7 3.7 %collective-permute-start.14 = (bf16[32,1024]{1,0:T(8,128)(2,1)S(1)}, bf16[32,1024]{1,0:T(8,128)(2,1)S(1)}, u32[]{:S(2)}, u32[]{:S(2)}) collective-permute-start(bf16[32,1024]{1,0:T(8,128)(2,1)S(1)} %project.7), channel_id=1, source_target_pairs={{0,8},{8,16},{16,24},{24,0},{1,9},{9,17},{17,25},{25,1},{2,10},{10... | collective-permute-start | bytes 196616 | tf_op jit(solution)/shard_map/ppermute | solution.py:30
  48.4 0.6 %copy-start.1 = (bf16[32,1024]{1,0:T(8,128)(2,1)}, bf16[32,1024]{1,0:T(8,128)(2,1)S(1)}, u32[]{:S(2)}) copy-start(bf16[32,1024]{1,0:T(8,128)(2,1)S(1)} %collective-permute-done.14.value_ref) | copy-start | bytes 196612

commit v9 on v8

--- a/solution.py
+++ b/solution.py
@@ -47,6 +47,9 @@
         self.share_rows = self.units * self.unit_rows
         self.by_device = self.unit_heads == GROUP and GROUP * rows_here % 16 == 0
 
+        far = [self.half ^ k for k in range(0, self.half, 2)]
+        self.sources = list(range(self.half)) + far + [k ^ 1 for k in far]
+
     def share(self, part):
         me = lax.axis_index("ctx")
         return (me % self.half) ^ (me // self.half * self.fold) ^ part
@@ -78,7 +81,9 @@
     device = lax.div(query, plan.rows_here)
     block = device
     if not plan.by_device:
-        block = 2 * (lax.rem(device, plan.half) ^ low) + (lax.div(device, plan.half) ^ high)
+        away = lax.rem(device, plan.half) ^ low
+        beyond = plan.half + lax.rem(away, 2) * (plan.half // 2) + lax.div(away, 2)
+        block = jnp.where(lax.div(device, plan.half) == high, away, beyond)
     origin = (block * GROUP + lax.div(row, plan.rows)) * plan.rows_here + lax.rem(query, plan.rows_here)
     for at in range(0, plan.group_rows, 128):
         order_ref[:, at : at + 128] = jnp.where(lane + at == origin, 1.0, 0.0).astype(jnp.bfloat16)
@@ -117,6 +122,23 @@
         "mask",
         cost=pl.CostEstimate(flops=1_000_000, bytes_accessed=256 * span, transcendentals=0),
     )(offsets, starts, after)
+
+
+def join_kernel(*refs):
+    *parts, out_ref = refs
+    rows = parts[0].shape[1]
+    for i, part in enumerate(parts):
+        out_ref[:, i * rows : (i + 1) * rows, :] = part[...]
+
+
+def join(blocks):
+    groups, rows, width = blocks[0].shape
+    return local(
+        join_kernel,
+        jax.ShapeDtypeStruct((groups, len(blocks) * rows, width), blocks[0].dtype),
+        [pltpu.VMEM] * len(blocks),
+        "join",
+    )(*blocks)
 
 
 def write_stats(ref, at, rows):
@@ -152,10 +174,12 @@
     peaks = []
     for unit, group in enumerate(groups):
         if plan.by_device:
-            for block, ref in enumerate(query_refs):
-                device = me ^ (block // 2) ^ (block % 2 * plan.half)
-                to = pl.multiple_of(device * GROUP * plan.rows_here, GROUP * plan.rows_here)
-                held_ref[unit, pl.ds(to, GROUP * plan.rows_here), :] = ref[group]
+            rows = GROUP * plan.rows_here
+            sources = [(ref, 0) for ref in query_refs[:-2]]
+            sources += [(ref, at) for ref in query_refs[-2:] for at in range(0, ref.shape[1], rows)]
+            for away, (ref, at) in zip(plan.sources, sources):
+                to = pl.multiple_of((me ^ away) * rows, rows)
+                held_ref[unit, pl.ds(to, rows), :] = ref[group, at : at + rows, :]
             queries = held_ref[unit]
         else:
             stacked = jnp.concatenate([ref[group] for ref in query_refs], axis=0)
@@ -324,23 +348,6 @@
     )(*operands)
 
 
-def deliver_kernel(value_ref, out_ref, sem):
-    copy = pltpu.make_async_copy(value_ref, out_ref, sem)
-    copy.start()
-    copy.wait()
-
-
-def deliver(value):
-    return pl.pallas_call(
-        deliver_kernel,
-        out_shape=pltpu.HBM(value.shape, value.dtype),
-        in_specs=[pl.BlockSpec(memory_space=pltpu.VMEM)],
-        out_specs=pl.BlockSpec(memory_space=pltpu.HBM),
-        scratch_shapes=[pltpu.SemaphoreType.DMA],
-        name="deliver",
-    )(value)
-
-
 def per_device(queries, cache, out_weight, offsets, starts):
     plan = Plan(lax.axis_size("ctx"), queries.shape[0])
     half = plan.half
@@ -349,17 +356,16 @@
 
     own = queries.reshape(plan.rows_here, KVH, GROUP, HD)
     own = own.transpose(1, 2, 0, 3).reshape(KVH, GROUP * plan.rows_here, HD)
-    far = swap(own, "ctx", half)
+    far = [swap(own, "ctx", k) for k in plan.sources[half : half + half // 2]]
     near = [swap(own, "ctx", k) for k in range(1, half)]
     order, one_hot = row_order(plan)
     bias = mask(cache.shape[0], offsets, starts, near[-1])
     if plan.by_device:
-        gathered = [own, far]
-        for k in range(1, half):
-            gathered += [near[k - 1], swap(far, "ctx", k)]
+        far = join(far)
+        gathered = [own] + near + [far, swap(far, "ctx", 1)]
     else:
-        pair = jnp.concatenate([own, far], axis=1)
-        gathered = [pair] + [swap(pair, "ctx", k) for k in range(1, half)]
+        far = jnp.concatenate(far, axis=1)
+        gathered = [jnp.concatenate([own] + near + [far, swap(far, "ctx", 1)], axis=1)]
 
     received = []
     for part in reversed(range(1, half)):
@@ -375,7 +381,7 @@
     for k in range(1, half):
         dtype = jnp.float32 if k < half - 1 else jnp.bfloat16
         total = project(plan, k, blocks[k - 1], out_weight, total, dtype)
-    return deliver(from_behind(total, "segment", 1))
+    return from_behind(total, "segment", 1)
 
 
 def solution(mesh):

time: 50.7 us -> 50.8 us (level)
  waiting for transfers between devices: 13.3 us -> 17.3 us
  starting transfers between devices: 22.2 us -> 19.7 us
  Pallas kernels: 12.9 us -> 11.5 us
    ppermute x14 -> x13, waiting for transfers between devices: 9.57 us -> 13.6 us  [swap(): return lax.ppermute(value, axis, [(i, i ^ bits) for i in range(devices)])]
    ppermute x14 -> x13, starting transfers between devices: 22.2 us -> 19.7 us  [swap(): return lax.ppermute(value, axis, [(i, i ^ bits) for i in range(devices)])]
    pallas_call x1, Pallas kernels: 1.47 us -> 0.01 us  [join(): local(join_kernel, jax.ShapeDtypeStruct((groups, len(blocks) * rows, widt...]
  transfers between devices with their start and end apart: 15 -> 14, of which waited for: 8 -> 7; matrix products, arithmetic and copies ran while one was open for 0% -> 0% of each run, Pallas kernels for 15% -> 16%
where the time goes in v9:
time: 50.8 us; the launch traced here: 50.6 us
  starting transfers between devices  19.7 us (39%)
  waiting for transfers between devices  17.3 us (34%)
  Pallas kernels  11.5 us (23%)
  between operations  1.48 us (3%)
  local copies, waits for them, and re-layouts  0.67 us (1%)
    ppermute x13, starting transfers between devices, swap(): return lax.ppermute(value, axis, [(i, i ^ bits) for i in range(devices)])  19.7 us
    ppermute x13, waiting for transfers between devices, swap(): return lax.ppermute(value, axis, [(i, i ^ bits) for i in range(devices)])  13.6 us
    pallas_call x4, Pallas kernels, attend(): local(functools.partial(attend_kernel, plan, part), out_shape, [pltpu.VME...  6.74 us
    ppermute x1, waiting for transfers between devices, from_behind(): lax.ppermute(value, axis, [(i, (i + by) % devices) for i in range(devices)])  3.69 us
    pallas_call x4, Pallas kernels, project(): local(functools.partial(project_kernel, plan, part), jax.ShapeDtypeStruct...  3.31 us
  transfers between devices with their start and end apart: 14, of which 7 were waited for; matrix products, arithmetic and copies ran while one was open for 0% of the time, Pallas kernels for 16%

profile of v9, /device:TPU:0, one launch (start us, length us, event | category | flops | bytes accessed | tf_op | source)
XLA Modules:
  0.0 50.6 jit_solution(7736028937087212104)
XLA Ops:
  0.0 5.0 %collective-permute-start.4 = (bf16[8,32,128]{2,1,0:T(8,128)(2,1)}, bf16[8,32,128]{2,1,0:T(8,128)(2,1)S(1)}, u32[]{:S(2)}, u32[]{:S(2)}) collective-permute-start(bf16[8,32,128]{2,1,0:T(8,128)(2,1)} %bitcast.9), channel_id=1, source_target_pairs={{0,6},{1,7},{2,4},{3,5},{4,2},{5,3},{6,0},{7,1},{8,14},{9,15},{10,... | collective-permute-start | bytes 196616 | tf_op jit(solution)/shard_map/ppermute | solution.py:25
  5.1 0.0 collective-permute-start.3
  5.1 1.7 %collective-permute-start.2 = (bf16[8,32,128]{2,1,0:T(8,128)(2,1)}, bf16[8,32,128]{2,1,0:T(8,128)(2,1)S(1)}, u32[]{:S(2)}, u32[]{:S(2)}) collective-permute-start(bf16[8,32,128]{2,1,0:T(8,128)(2,1)} %bitcast.11), channel_id=1, source_target_pairs={{0,3},{1,2},{2,1},{3,0},{4,7},{5,6},{6,5},{7,4},{8,11},{9,10},{10,... | collective-permute-start | bytes 196616 | tf_op jit(solution)/shard_map/ppermute | solution.py:25
  6.8 1.2 %collective-permute-start.1 = (bf16[8,32,128]{2,1,0:T(8,128)(2,1)}, bf16[8,32,128]{2,1,0:T(8,128)(2,1)S(1)}, u32[]{:S(2)}, u32[]{:S(2)}) collective-permute-start(bf16[8,32,128]{2,1,0:T(8,128)(2,1)} %bitcast.12), channel_id=1, source_target_pairs={{0,2},{1,3},{2,0},{3,1},{4,6},{5,7},{6,4},{7,5},{8,10},{9,11},{10,... | collective-permute-start | bytes 196616 | tf_op jit(solution)/shard_map/ppermute | solution.py:25
  8.0 0.5 %collective-permute-start = (bf16[8,32,128]{2,1,0:T(8,128)(2,1)}, bf16[8,32,128]{2,1,0:T(8,128)(2,1)S(1)}, u32[]{:S(2)}, u32[]{:S(2)}) collective-permute-start(bf16[8,32,128]{2,1,0:T(8,128)(2,1)} %bitcast.13), channel_id=1, source_target_pairs={{0,1},{1,0},{2,3},{3,2},{4,5},{5,4},{6,7},{7,6},{8,9},{9,8},{10,11... | collective-permute-start | bytes 196616 | tf_op jit(solution)/shard_map/ppermute | solution.py:25
  8.5 0.0 collective-permute-done.4.refs_1_
  8.6 2.5 %collective-permute-done.3.refs_0_ = bf16[8,32,128]{2,1,0:T(8,128)(2,1)S(1)} collective-permute-done((bf16[8,32,128]{2,1,0:T(8,128)(2,1)}, bf16[8,32,128]{2,1,0:T(8,128)(2,1)S(1)}, u32[]{:S(2)}, u32[]{:S(2)}) %collective-permute-start.3) | collective-permute-done | bytes 65568 | tf_op jit(solution)/shard_map/ppermute | solution.py:25
  11.0 0.0 slice-start.5
  11.1 1.6 %collective-permute-start.5 = (bf16[8,64,128]{2,1,0:T(8,128)(2,1)S(1)}, bf16[8,64,128]{2,1,0:T(8,128)(2,1)S(1)}, u32[]{:S(2)}, u32[]{:S(2)}) collective-permute-start(bf16[8,64,128]{2,1,0:T(8,128)(2,1)S(1)} %join.1.refs_4_), channel_id=1, source_target_pairs={{0,1},{1,0},{2,3},{3,2},{4,5},{5,4},{6,7},{7,6},{8,9},{9,8},{10,11... | collective-permute-start | bytes 393224 | tf_op jit(solution)/shard_map/ppermute | solution.py:25
  12.6 0.1 order.1
  14.0 0.0 collective-permute-done.2.after_ref.refs_3_
  14.0 0.2 mask.1.refs_7_
  14.3 0.0 collective-permute-done.1.refs_2_
  14.3 0.0 collective-permute-done.refs_1_
  14.3 1.8 %collective-permute-done.5.refs_5_ = bf16[8,64,128]{2,1,0:T(8,128)(2,1)S(1)} collective-permute-done((bf16[8,64,128]{2,1,0:T(8,128)(2,1)S(1)}, bf16[8,64,128]{2,1,0:T(8,128)(2,1)S(1)}, u32[]{:S(2)}, u32[]{:S(2)}) %collective-permute-start.5) | collective-permute-done | bytes 131104 | tf_op jit(solution)/shard_map/ppermute | solution.py:25
  16.1 0.0 slice-done.5
  16.1 1.7 %attend.5 = bf16[528,128]{1,0:T(8,128)(2,1)S(1)} custom-call(bf16[8,32,128]{2,1,0:T(8,128)(2,1)S(1)} %bitcast.14, bf16[8,32,128]{2,1,0:T(8,128)(2,1)S(1)} %collective-permute-done.refs_1_, bf16[8,32,128]{2,1,0:T(8,128)(2,1)S(1)} %collective-permute-done.1.refs_2_, bf16[8,32,128]{2,1,0:T(8,128)(2,1)S(1)} %collective-permute-done.2.after_ref.refs_3_, ...), custom_call_target="tpu_custom_call" | custom-call | flops 536870912 | bytes 2097152 | tf_op jit(solution)/shard_map/attend/pallas_call | solution.py:227
  17.8 0.0 slice-start
  17.9 0.0 slice-start.1
  17.9 0.8 %collective-permute-start.6 = (bf16[528,128]{1,0:T(8,128)(2,1)S(1)}, bf16[528,128]{1,0:T(8,128)(2,1)S(1)}, u32[]{:S(2)}, u32[]{:S(2)}) collective-permute-start(bf16[528,128]{1,0:T(8,128)(2,1)S(1)} %attend.5), channel_id=1, source_target_pairs={{0,3},{1,2},{2,1},{3,0},{4,7},{5,6},{6,5},{7,4},{8,11},{9,10},{10,... | collective-permute-start | bytes 405512 | tf_op jit(solution)/shard_map/ppermute | solution.py:25
  18.6 1.7 %attend.6 = bf16[528,128]{1,0:T(8,128)(2,1)S(1)} custom-call(bf16[8,32,128]{2,1,0:T(8,128)(2,1)S(1)} %bitcast.15, bf16[8,32,128]{2,1,0:T(8,128)(2,1)S(1)} %collective-permute-done.refs_1_, bf16[8,32,128]{2,1,0:T(8,128)(2,1)S(1)} %collective-permute-done.1.refs_2_, bf16[8,32,128]{2,1,0:T(8,128)(2,1)S(1)} %collective-permute-done.2.after_ref.refs_3_, ...), custom_call_target="tpu_custom_call" | custom-call | flops 536870912 | bytes 2097152 | tf_op jit(solution)/shard_map/attend/pallas_call | solution.py:227
  20.3 0.0 slice-start.2
  20.3 2.4 %collective-permute-start.7 = (bf16[528,128]{1,0:T(8,128)(2,1)S(1)}, bf16[528,128]{1,0:T(8,128)(2,1)S(1)}, u32[]{:S(2)}, u32[]{:S(2)}) collective-permute-start(bf16[528,128]{1,0:T(8,128)(2,1)S(1)} %attend.6), channel_id=1, source_target_pairs={{0,2},{1,3},{2,0},{3,1},{4,6},{5,7},{6,4},{7,5},{8,10},{9,11},{10,... | collective-permute-start | bytes 405512 | tf_op jit(solution)/shard_map/ppermute | solution.py:25
  22.8 1.7 %attend.7 = bf16[528,128]{1,0:T(8,128)(2,1)S(1)} custom-call(bf16[8,32,128]{2,1,0:T(8,128)(2,1)S(1)} %bitcast.16, bf16[8,32,128]{2,1,0:T(8,128)(2,1)S(1)} %collective-permute-done.refs_1_, bf16[8,32,128]{2,1,0:T(8,128)(2,1)S(1)} %collective-permute-done.1.refs_2_, bf16[8,32,128]{2,1,0:T(8,128)(2,1)S(1)} %collective-permute-done.2.after_ref.refs_3_, ...), custom_call_target="tpu_custom_call" | custom-call | flops 536870912 | bytes 2097152 | tf_op jit(solution)/shard_map/attend/pallas_call | solution.py:227
  24.5 0.0 slice-start.3
  24.5 0.4 collective-permute-start.8
  24.9 1.6 %attend.4 = (f32[512,128]{1,0:T(8,128)S(1)}, bf16[16,128]{1,0:T(8,128)(2,1)S(1)}) custom-call(bf16[8,32,128]{2,1,0:T(8,128)(2,1)S(1)} %bitcast.17, bf16[8,32,128]{2,1,0:T(8,128)(2,1)S(1)} %collective-permute-done.refs_1_, bf16[8,32,128]{2,1,0:T(8,128)(2,1)S(1)} %collective-permute-done.1.refs_2_, ...), custom_call_target="tpu_custom_call" | custom-call | flops 536870912 | bytes 2097152 | tf_op jit(solution)/shard_map/attend/pallas_call | solution.py:227
  26.5 0.0 collective-permute-done.6.refs_0_
  26.6 0.0 collective-permute-done.7.refs_1_
  26.6 3.0 %collective-permute-done.8.refs_2_ = bf16[528,128]{1,0:T(8,128)(2,1)S(1)} collective-permute-done((bf16[528,128]{1,0:T(8,128)(2,1)S(1)}, bf16[528,128]{1,0:T(8,128)(2,1)S(1)}, u32[]{:S(2)}, u32[]{:S(2)}) %collective-permute-start.8) | collective-permute-done | bytes 135200 | tf_op jit(solution)/shard_map/ppermute | solution.py:25
  29.6 0.5 merge.1
  30.1 2.4 %collective-permute-start.9 = (bf16[528,128]{1,0:T(8,128)(2,1)S(1)}, bf16[528,128]{1,0:T(8,128)(2,1)S(1)}, u32[]{:S(2)}, u32[]{:S(2)}) collective-permute-start(bf16[528,128]{1,0:T(8,128)(2,1)S(1)} %get-tuple-element.16.own_ref), channel_id=1, source_target_pairs={{0,6},{1,7},{2,4},{3,5},{4,2},{5,3},{6,0},{7,1},{8,14},{9,15},{10,... | collective-permute-start | bytes 405512 | tf_op jit(solution)/shard_map/ppermute | solution.py:25
  32.5 4.4 %collective-permute-done.9.other_ref = bf16[528,128]{1,0:T(8,128)(2,1)S(1)} collective-permute-done((bf16[528,128]{1,0:T(8,128)(2,1)S(1)}, bf16[528,128]{1,0:T(8,128)(2,1)S(1)}, u32[]{:S(2)}, u32[]{:S(2)}) %collective-permute-start.9) | collective-permute-done | bytes 135200 | tf_op jit(solution)/shard_map/ppermute | solution.py:25
  37.0 0.6 %settle.1.refs_0_ = bf16[32,2048]{1,0:T(8,128)(2,1)S(1)} custom-call(f32[512,128]{1,0:T(8,128)S(1)} %get-tuple-element.15.wide_ref, bf16[528,128]{1,0:T(8,128)(2,1)S(1)} %get-tuple-element.16.own_ref, bf16[528,128]{1,0:T(8,128)(2,1)S(1)} %collective-permute-done.9.other_ref, bf16[256,256]{1,0:T(8,128)(2,1)S(1)} %get-tuple-element.11.refs_8_.order_ref), custom_call_target="tpu_custom_call" | custom-call | tf_op jit(solution)/shard_map/settle/pallas_call | solution.py:323
  37.6 0.4 collective-permute-start.12
  38.0 0.0 collective-permute-start.11
  38.0 3.1 %collective-permute-start.10 = (bf16[32,2048]{1,0:T(8,128)(2,1)S(1)}, bf16[32,2048]{1,0:T(8,128)(2,1)S(1)}, u32[]{:S(2)}, u32[]{:S(2)}) collective-permute-start(bf16[32,2048]{1,0:T(8,128)(2,1)S(1)} %settle.1.refs_0_), channel_id=1, source_target_pairs={{0,3},{1,2},{2,1},{3,0},{4,7},{5,6},{6,5},{7,4},{8,11},{9,10},{10,... | collective-permute-start | bytes 393224 | tf_op jit(solution)/shard_map/ppermute | solution.py:25
  41.1 0.0 slice-done.2
  41.1 0.8 %project.4.refs_2_ = f32[32,1024]{1,0:T(8,128)S(1)} custom-call(bf16[32,2048]{1,0:T(8,128)(2,1)S(1)} %settle.1.refs_0_, bf16[8192,1024]{1,0:T(8,128)(2,1)S(1)} %bitcast.6), custom_call_target="tpu_custom_call" | custom-call | tf_op jit(solution)/shard_map/project/pallas_call | solution.py:343
  42.0 0.6 %collective-permute-done.12.refs_0_ = bf16[32,2048]{1,0:T(8,128)(2,1)S(1)} collective-permute-done((bf16[32,2048]{1,0:T(8,128)(2,1)S(1)}, bf16[32,2048]{1,0:T(8,128)(2,1)S(1)}, u32[]{:S(2)}, u32[]{:S(2)}) %collective-permute-start.12) | collective-permute-done | bytes 131104 | tf_op jit(solution)/shard_map/ppermute | solution.py:25
  42.6 0.8 %project.5.refs_2_ = f32[32,1024]{1,0:T(8,128)S(1)} custom-call(bf16[32,2048]{1,0:T(8,128)(2,1)S(1)} %collective-permute-done.12.refs_0_, bf16[8192,1024]{1,0:T(8,128)(2,1)S(1)} %bitcast.6, f32[32,1024]{1,0:T(8,128)S(1)} %project.4.refs_2_), custom_call_target="tpu_custom_call" | custom-call | tf_op jit(solution)/shard_map/project/pallas_call | solution.py:343
  43.4 0.0 collective-permute-done.11.refs_0_
  43.4 0.8 %project.6.refs_2_ = f32[32,1024]{1,0:T(8,128)S(1)} custom-call(bf16[32,2048]{1,0:T(8,128)(2,1)S(1)} %collective-permute-done.11.refs_0_, bf16[8192,1024]{1,0:T(8,128)(2,1)S(1)} %bitcast.6, f32[32,1024]{1,0:T(8,128)S(1)} %project.5.refs_2_), custom_call_target="tpu_custom_call" | custom-call | tf_op jit(solution)/shard_map/project/pallas_call | solution.py:343
  44.3 1.2 %collective-permute-done.10.refs_0_ = bf16[32,2048]{1,0:T(8,128)(2,1)S(1)} collective-permute-done((bf16[32,2048]{1,0:T(8,128)(2,1)S(1)}, bf16[32,2048]{1,0:T(8,128)(2,1)S(1)}, u32[]{:S(2)}, u32[]{:S(2)}) %collective-permute-start.10) | collective-permute-done | bytes 131104 | tf_op jit(solution)/shard_map/ppermute | solution.py:25
  45.5 0.8 %project.7 = bf16[32,1024]{1,0:T(8,128)(2,1)S(1)} custom-call(bf16[32,2048]{1,0:T(8,128)(2,1)S(1)} %collective-permute-done.10.refs_0_, bf16[8192,1024]{1,0:T(8,128)(2,1)S(1)} %bitcast.6, f32[32,1024]{1,0:T(8,128)S(1)} %project.6.refs_2_), custom_call_target="tpu_custom_call" | custom-call | tf_op jit(solution)/shard_map/project/pallas_call | solution.py:343
  46.3 0.0 collective-permute-start.13
  46.3 3.7 %collective-permute-done.13 = bf16[32,1024]{1,0:T(8,128)(2,1)S(1)} collective-permute-done((bf16[32,1024]{1,0:T(8,128)(2,1)S(1)}, bf16[32,1024]{1,0:T(8,128)(2,1)S(1)}, u32[]{:S(2)}, u32[]{:S(2)}) %collective-permute-start.13) | collective-permute-done | bytes 65568 | tf_op jit(solution)/shard_map/ppermute | solution.py:30
  50.0 0.6 %copy.10 = bf16[32,1024]{1,0:T(8,128)(2,1)} copy(bf16[32,1024]{1,0:T(8,128)(2,1)S(1)} %collective-permute-done.13) | data formatting | bytes 131072
  (10 shorter events, 0.0 us)
Async XLA Ops:
  0.0 16.1 %copy-start = (bf16[4,8192]{1,0:T(4,128)(2,1)S(1)}, bf16[4,8192]{1,0:T(4,128)(2,1)}, u32[]{:S(2)}) copy-start(bf16[4,8192]{1,0:T(4,128)(2,1)} %param.5) | copy-start | bytes 196612
  0.0 16.1 %slice-start.4 = ((s8[8388608]{0:T(1024)(128)(4,1)}), s8[4194304]{0:T(1024)(128)(4,1)S(1)}, s32[]{:S(2)}) async-start(s8[8388608]{0:T(1024)(128)(4,1)} %bitcast.7), calls=%async_computation.4 | async-start | bytes 8388608
  0.0 8.5 %collective-permute-start.4 = (bf16[8,32,128]{2,1,0:T(8,128)(2,1)}, bf16[8,32,128]{2,1,0:T(8,128)(2,1)S(1)}, u32[]{:S(2)}, u32[]{:S(2)}) collective-permute-start(bf16[8,32,128]{2,1,0:T(8,128)(2,1)} %bitcast.9), channel_id=1, source_target_pairs={{0,6},{1,7},{2,4},{3,5},{4,2},{5,3},{6,0},{7,1},{8,14},{9,15},{10,... | collective-permute-start | bytes 196616 | tf_op jit(solution)/shard_map/ppermute | solution.py:25
  5.1 6.0 %collective-permute-start.3 = (bf16[8,32,128]{2,1,0:T(8,128)(2,1)}, bf16[8,32,128]{2,1,0:T(8,128)(2,1)S(1)}, u32[]{:S(2)}, u32[]{:S(2)}) collective-permute-start(bf16[8,32,128]{2,1,0:T(8,128)(2,1)} %bitcast.10), channel_id=1, source_target_pairs={{0,4},{1,5},{2,6},{3,7},{4,0},{5,1},{6,2},{7,3},{8,12},{9,13},{10,... | collective-permute-start | bytes 196616 | tf_op jit(solution)/shard_map/ppermute | solution.py:25
  5.1 9.0 %collective-permute-start.2 = (bf16[8,32,128]{2,1,0:T(8,128)(2,1)}, bf16[8,32,128]{2,1,0:T(8,128)(2,1)S(1)}, u32[]{:S(2)}, u32[]{:S(2)}) collective-permute-start(bf16[8,32,128]{2,1,0:T(8,128)(2,1)} %bitcast.11), channel_id=1, source_target_pairs={{0,3},{1,2},{2,1},{3,0},{4,7},{5,6},{6,5},{7,4},{8,11},{9,10},{10,... | collective-permute-start | bytes 196616 | tf_op jit(solution)/shard_map/ppermute | solution.py:25
  6.8 7.5 %collective-permute-start.1 = (bf16[8,32,128]{2,1,0:T(8,128)(2,1)}, bf16[8,32,128]{2,1,0:T(8,128)(2,1)S(1)}, u32[]{:S(2)}, u32[]{:S(2)}) collective-permute-start(bf16[8,32,128]{2,1,0:T(8,128)(2,1)} %bitcast.12), channel_id=1, source_target_pairs={{0,2},{1,3},{2,0},{3,1},{4,6},{5,7},{6,4},{7,5},{8,10},{9,11},{10,... | collective-permute-start | bytes 196616 | tf_op jit(solution)/shard_map/ppermute | solution.py:25
  8.0 6.3 %collective-permute-start = (bf16[8,32,128]{2,1,0:T(8,128)(2,1)}, bf16[8,32,128]{2,1,0:T(8,128)(2,1)S(1)}, u32[]{:S(2)}, u32[]{:S(2)}) collective-permute-start(bf16[8,32,128]{2,1,0:T(8,128)(2,1)} %bitcast.13), channel_id=1, source_target_pairs={{0,1},{1,0},{2,3},{3,2},{4,5},{5,4},{6,7},{7,6},{8,9},{9,8},{10,11... | collective-permute-start | bytes 196616 | tf_op jit(solution)/shard_map/ppermute | solution.py:25
  11.0 5.1 %slice-start.5 = ((s8[8388608]{0:T(1024)(128)(4,1)}), s8[4194304]{0:T(1024)(128)(4,1)S(1)}, s32[]{:S(2)}) async-start(s8[8388608]{0:T(1024)(128)(4,1)} %bitcast.7), calls=%async_computation.5 | async-start | bytes 8388608
  11.1 5.0 %collective-permute-start.5 = (bf16[8,64,128]{2,1,0:T(8,128)(2,1)S(1)}, bf16[8,64,128]{2,1,0:T(8,128)(2,1)S(1)}, u32[]{:S(2)}, u32[]{:S(2)}) collective-permute-start(bf16[8,64,128]{2,1,0:T(8,128)(2,1)S(1)} %join.1.refs_4_), channel_id=1, source_target_pairs={{0,1},{1,0},{2,3},{3,2},{4,5},{5,4},{6,7},{7,6},{8,9},{9,8},{10,11... | collective-permute-start | bytes 393224 | tf_op jit(solution)/shard_map/ppermute | solution.py:25
  17.8 23.3 %slice-start = ((s8[16777216]{0:T(1024)(128)(4,1)}), s8[4194304]{0:T(1024)(128)(4,1)S(1)}, s32[]{:S(2)}) async-start(s8[16777216]{0:T(1024)(128)(4,1)} %bitcast.5), calls=%async_computation | async-start | bytes 8388608
  17.9 23.3 %slice-start.1 = ((s8[16777216]{0:T(1024)(128)(4,1)}), s8[4194304]{0:T(1024)(128)(4,1)S(1)}, s32[]{:S(2)}) async-start(s8[16777216]{0:T(1024)(128)(4,1)} %bitcast.5), calls=%async_computation.1 | async-start | bytes 8388608
  17.9 8.7 %collective-permute-start.6 = (bf16[528,128]{1,0:T(8,128)(2,1)S(1)}, bf16[528,128]{1,0:T(8,128)(2,1)S(1)}, u32[]{:S(2)}, u32[]{:S(2)}) collective-permute-start(bf16[528,128]{1,0:T(8,128)(2,1)S(1)} %attend.5), channel_id=1, source_target_pairs={{0,3},{1,2},{2,1},{3,0},{4,7},{5,6},{6,5},{7,4},{8,11},{9,10},{10,... | collective-permute-start | bytes 405512 | tf_op jit(solution)/shard_map/ppermute | solution.py:25
  20.3 20.8 %slice-start.2 = ((s8[16777216]{0:T(1024)(128)(4,1)}), s8[4194304]{0:T(1024)(128)(4,1)S(1)}, s32[]{:S(2)}) async-start(s8[16777216]{0:T(1024)(128)(4,1)} %bitcast.5), calls=%async_computation.2 | async-start | bytes 8388608
  20.3 6.2 %collective-permute-start.7 = (bf16[528,128]{1,0:T(8,128)(2,1)S(1)}, bf16[528,128]{1,0:T(8,128)(2,1)S(1)}, u32[]{:S(2)}, u32[]{:S(2)}) collective-permute-start(bf16[528,128]{1,0:T(8,128)(2,1)S(1)} %attend.6), channel_id=1, source_target_pairs={{0,2},{1,3},{2,0},{3,1},{4,6},{5,7},{6,4},{7,5},{8,10},{9,11},{10,... | collective-permute-start | bytes 405512 | tf_op jit(solution)/shard_map/ppermute | solution.py:25
  24.5 16.6 %slice-start.3 = ((s8[16777216]{0:T(1024)(128)(4,1)}), s8[4194304]{0:T(1024)(128)(4,1)S(1)}, s32[]{:S(2)}) async-start(s8[16777216]{0:T(1024)(128)(4,1)} %bitcast.5), calls=%async_computation.3 | async-start | bytes 8388608
  24.5 5.1 %collective-permute-start.8 = (bf16[528,128]{1,0:T(8,128)(2,1)S(1)}, bf16[528,128]{1,0:T(8,128)(2,1)S(1)}, u32[]{:S(2)}, u32[]{:S(2)}) collective-permute-start(bf16[528,128]{1,0:T(8,128)(2,1)S(1)} %attend.7), channel_id=1, source_target_pairs={{0,1},{1,0},{2,3},{3,2},{4,5},{5,4},{6,7},{7,6},{8,9},{9,8},{10,11... | collective-permute-start | bytes 405512 | tf_op jit(solution)/shard_map/ppermute | solution.py:25
  30.1 6.9 %collective-permute-start.9 = (bf16[528,128]{1,0:T(8,128)(2,1)S(1)}, bf16[528,128]{1,0:T(8,128)(2,1)S(1)}, u32[]{:S(2)}, u32[]{:S(2)}) collective-permute-start(bf16[528,128]{1,0:T(8,128)(2,1)S(1)} %get-tuple-element.16.own_ref), channel_id=1, source_target_pairs={{0,6},{1,7},{2,4},{3,5},{4,2},{5,3},{6,0},{7,1},{8,14},{9,15},{10,... | collective-permute-start | bytes 405512 | tf_op jit(solution)/shard_map/ppermute | solution.py:25
  37.6 5.0 %collective-permute-start.12 = (bf16[32,2048]{1,0:T(8,128)(2,1)S(1)}, bf16[32,2048]{1,0:T(8,128)(2,1)S(1)}, u32[]{:S(2)}, u32[]{:S(2)}) collective-permute-start(bf16[32,2048]{1,0:T(8,128)(2,1)S(1)} %settle.1.refs_0_), channel_id=1, source_target_pairs={{0,1},{1,0},{2,3},{3,2},{4,5},{5,4},{6,7},{7,6},{8,9},{9,8},{10,11... | collective-permute-start | bytes 393224 | tf_op jit(solution)/shard_map/ppermute | solution.py:25
  38.0 5.5 %collective-permute-start.11 = (bf16[32,2048]{1,0:T(8,128)(2,1)S(1)}, bf16[32,2048]{1,0:T(8,128)(2,1)S(1)}, u32[]{:S(2)}, u32[]{:S(2)}) collective-permute-start(bf16[32,2048]{1,0:T(8,128)(2,1)S(1)} %settle.1.refs_0_), channel_id=1, source_target_pairs={{0,2},{1,3},{2,0},{3,1},{4,6},{5,7},{6,4},{7,5},{8,10},{9,11},{10,... | collective-permute-start | bytes 393224 | tf_op jit(solution)/shard_map/ppermute | solution.py:25
  38.0 7.5 %collective-permute-start.10 = (bf16[32,2048]{1,0:T(8,128)(2,1)S(1)}, bf16[32,2048]{1,0:T(8,128)(2,1)S(1)}, u32[]{:S(2)}, u32[]{:S(2)}) collective-permute-start(bf16[32,2048]{1,0:T(8,128)(2,1)S(1)} %settle.1.refs_0_), channel_id=1, source_target_pairs={{0,3},{1,2},{2,1},{3,0},{4,7},{5,6},{6,5},{7,4},{8,11},{9,10},{10,... | collective-permute-start | bytes 393224 | tf_op jit(solution)/shard_map/ppermute | solution.py:25
  46.3 3.7 %collective-permute-start.13 = (bf16[32,1024]{1,0:T(8,128)(2,1)S(1)}, bf16[32,1024]{1,0:T(8,128)(2,1)S(1)}, u32[]{:S(2)}, u32[]{:S(2)}) collective-permute-start(bf16[32,1024]{1,0:T(8,128)(2,1)S(1)} %project.7), channel_id=1, source_target_pairs={{0,8},{8,16},{16,24},{24,0},{1,9},{9,17},{17,25},{25,1},{2,10},{10... | collective-permute-start | bytes 196616 | tf_op jit(solution)/shard_map/ppermute | solution.py:30

commit v10 on v8

--- a/solution.py
+++ b/solution.py
@@ -324,23 +324,6 @@
     )(*operands)
 
 
-def deliver_kernel(value_ref, out_ref, sem):
-    copy = pltpu.make_async_copy(value_ref, out_ref, sem)
-    copy.start()
-    copy.wait()
-
-
-def deliver(value):
-    return pl.pallas_call(
-        deliver_kernel,
-        out_shape=pltpu.HBM(value.shape, value.dtype),
-        in_specs=[pl.BlockSpec(memory_space=pltpu.VMEM)],
-        out_specs=pl.BlockSpec(memory_space=pltpu.HBM),
-        scratch_shapes=[pltpu.SemaphoreType.DMA],
-        name="deliver",
-    )(value)
-
-
 def per_device(queries, cache, out_weight, offsets, starts):
     plan = Plan(lax.axis_size("ctx"), queries.shape[0])
     half = plan.half
@@ -362,7 +345,7 @@
         gathered = [pair] + [swap(pair, "ctx", k) for k in range(1, half)]
 
     received = []
-    for part in reversed(range(1, half)):
+    for part in sorted(range(1, half), key=lambda k: (k % 2 == 0, -k)):
         (piece,) = attend(plan, part, gathered, cache, bias, order, one_hot)
         received.append(swap(piece, "ctx", part))
     wide, stats = attend(plan, 0, gathered, cache, bias, order, one_hot)
@@ -375,7 +358,7 @@
     for k in range(1, half):
         dtype = jnp.float32 if k < half - 1 else jnp.bfloat16
         total = project(plan, k, blocks[k - 1], out_weight, total, dtype)
-    return deliver(from_behind(total, "segment", 1))
+    return from_behind(total, "segment", 1)
 
 
 def solution(mesh):

time: 50.7 us -> 49.5 us (0.976)
  Pallas kernels: 12.9 us -> 11.5 us
  waiting for transfers between devices: 13.3 us -> 14.4 us
  starting transfers between devices: 22.2 us -> 21.4 us
    pallas_call x1 -> x0, Pallas kernels: 1.47 us -> none  [deliver(): pl.pallas_call(deliver_kernel, out_shape=pltpu.HBM(value.shape, value.dty...]
    ppermute x14, waiting for transfers between devices: 9.57 us -> 10.7 us  [swap(): return lax.ppermute(value, axis, [(i, i ^ bits) for i in range(devices)])]
    ppermute x14, starting transfers between devices: 22.2 us -> 21.3 us  [swap(): return lax.ppermute(value, axis, [(i, i ^ bits) for i in range(devices)])]
  transfers between devices with their start and end apart: 15 -> 15, of which waited for: 8 -> 7; matrix products, arithmetic and copies ran while one was open for 0% -> 0% of each run, Pallas kernels for 15% -> 16%
where the time goes in v10:
time: 49.5 us; the launch traced here: 49.4 us
  starting transfers between devices  21.4 us (43%)
  waiting for transfers between devices  14.4 us (29%)
  Pallas kernels  11.5 us (23%)
  between operations  1.47 us (3%)
  local copies, waits for them, and re-layouts  0.67 us (1%)
    ppermute x14, starting transfers between devices, swap(): return lax.ppermute(value, axis, [(i, i ^ bits) for i in range(devices)])  21.3 us
    ppermute x14, waiting for transfers between devices, swap(): return lax.ppermute(value, axis, [(i, i ^ bits) for i in range(devices)])  10.7 us
    pallas_call x4, Pallas kernels, attend(): local(functools.partial(attend_kernel, plan, part), out_shape, [pltpu.VME...  6.73 us
    ppermute x1, waiting for transfers between devices, from_behind(): lax.ppermute(value, axis, [(i, (i + by) % devices) for i in range(devices)])  3.69 us
    pallas_call x4, Pallas kernels, project(): local(functools.partial(project_kernel, plan, part), jax.ShapeDtypeStruct...  3.31 us
  transfers between devices with their start and end apart: 15, of which 7 were waited for; matrix products, arithmetic and copies ran while one was open for 0% of the time, Pallas kernels for 16%

profile of v10, /device:TPU:0, one launch (start us, length us, event | category | flops | bytes accessed | tf_op | source)
XLA Modules:
  0.0 49.4 jit_solution(10998295689905825750)
XLA Ops:
  0.0 4.1 %collective-permute-start = (bf16[8,32,128]{2,1,0:T(8,128)(2,1)}, bf16[8,32,128]{2,1,0:T(8,128)(2,1)S(1)}, u32[]{:S(2)}, u32[]{:S(2)}) collective-permute-start(bf16[8,32,128]{2,1,0:T(8,128)(2,1)} %bitcast.9), channel_id=1, source_target_pairs={{0,4},{1,5},{2,6},{3,7},{4,0},{5,1},{6,2},{7,3},{8,12},{9,13},{10,... | collective-permute-start | bytes 196616 | tf_op jit(solution)/shard_map/ppermute | solution.py:25
  4.1 2.5 %collective-permute-start.5 = (bf16[8,32,128]{2,1,0:T(8,128)(2,1)}, bf16[8,32,128]{2,1,0:T(8,128)(2,1)S(1)}, u32[]{:S(2)}, u32[]{:S(2)}) collective-permute-start(bf16[8,32,128]{2,1,0:T(8,128)(2,1)} %bitcast.10), channel_id=1, source_target_pairs={{0,3},{1,2},{2,1},{3,0},{4,7},{5,6},{6,5},{7,4},{8,11},{9,10},{10,... | collective-permute-start | bytes 196616 | tf_op jit(solution)/shard_map/ppermute | solution.py:25
  6.6 0.4 collective-permute-start.3
  7.1 0.5 %collective-permute-start.1 = (bf16[8,32,128]{2,1,0:T(8,128)(2,1)}, bf16[8,32,128]{2,1,0:T(8,128)(2,1)S(1)}, u32[]{:S(2)}, u32[]{:S(2)}) collective-permute-start(bf16[8,32,128]{2,1,0:T(8,128)(2,1)} %bitcast.12), channel_id=1, source_target_pairs={{0,1},{1,0},{2,3},{3,2},{4,5},{5,4},{6,7},{7,6},{8,9},{9,8},{10,11... | collective-permute-start | bytes 196616 | tf_op jit(solution)/shard_map/ppermute | solution.py:25
  7.6 0.0 collective-permute-done.refs_1_
  7.6 2.5 %collective-permute-start.6 = (bf16[8,32,128]{2,1,0:T(8,128)(2,1)S(1)}, bf16[8,32,128]{2,1,0:T(8,128)(2,1)S(1)}, u32[]{:S(2)}, u32[]{:S(2)}) collective-permute-start(bf16[8,32,128]{2,1,0:T(8,128)(2,1)S(1)} %collective-permute-done.refs_1_), channel_id=1, source_target_pairs={{0,3},{1,2},{2,1},{3,0},{4,7},{5,6},{6,5},{7,4},{8,11},{9,10},{10,... | collective-permute-start | bytes 196616 | tf_op jit(solution)/shard_map/ppermute | solution.py:25
  10.1 0.6 %collective-permute-start.4 = (bf16[8,32,128]{2,1,0:T(8,128)(2,1)S(1)}, bf16[8,32,128]{2,1,0:T(8,128)(2,1)S(1)}, u32[]{:S(2)}, u32[]{:S(2)}) collective-permute-start(bf16[8,32,128]{2,1,0:T(8,128)(2,1)S(1)} %collective-permute-done.refs_1_), channel_id=1, source_target_pairs={{0,2},{1,3},{2,0},{3,1},{4,6},{5,7},{6,4},{7,5},{8,10},{9,11},{10,... | collective-permute-start | bytes 196616 | tf_op jit(solution)/shard_map/ppermute | solution.py:25
  10.7 0.0 collective-permute-done.5.after_ref.refs_6_
  10.7 1.1 %collective-permute-start.2 = (bf16[8,32,128]{2,1,0:T(8,128)(2,1)S(1)}, bf16[8,32,128]{2,1,0:T(8,128)(2,1)S(1)}, u32[]{:S(2)}, u32[]{:S(2)}) collective-permute-start(bf16[8,32,128]{2,1,0:T(8,128)(2,1)S(1)} %collective-permute-done.refs_1_), channel_id=1, source_target_pairs={{0,1},{1,0},{2,3},{3,2},{4,5},{5,4},{6,7},{7,6},{8,9},{9,8},{10,11... | collective-permute-start | bytes 196616 | tf_op jit(solution)/shard_map/ppermute | solution.py:25
  11.8 0.1 order.1
  13.2 0.2 mask.1.refs_9_
  13.4 0.0 collective-permute-done.3.refs_4_
  13.4 0.0 collective-permute-done.1.refs_2_
  13.4 0.0 collective-permute-done.6.refs_7_
  13.4 0.9 %collective-permute-done.4.refs_5_ = bf16[8,32,128]{2,1,0:T(8,128)(2,1)S(1)} collective-permute-done((bf16[8,32,128]{2,1,0:T(8,128)(2,1)S(1)}, bf16[8,32,128]{2,1,0:T(8,128)(2,1)S(1)}, u32[]{:S(2)}, u32[]{:S(2)}) %collective-permute-start.4) | collective-permute-done | bytes 65568 | tf_op jit(solution)/shard_map/ppermute | solution.py:25
  14.4 0.6 %collective-permute-done.2.refs_3_ = bf16[8,32,128]{2,1,0:T(8,128)(2,1)S(1)} collective-permute-done((bf16[8,32,128]{2,1,0:T(8,128)(2,1)S(1)}, bf16[8,32,128]{2,1,0:T(8,128)(2,1)S(1)}, u32[]{:S(2)}, u32[]{:S(2)}) %collective-permute-start.2) | collective-permute-done | bytes 65568 | tf_op jit(solution)/shard_map/ppermute | solution.py:25
  15.0 1.7 %attend.5 = bf16[528,128]{1,0:T(8,128)(2,1)S(1)} custom-call(bf16[8,32,128]{2,1,0:T(8,128)(2,1)S(1)} %bitcast.13, bf16[8,32,128]{2,1,0:T(8,128)(2,1)S(1)} %collective-permute-done.refs_1_, bf16[8,32,128]{2,1,0:T(8,128)(2,1)S(1)} %collective-permute-done.1.refs_2_, bf16[8,32,128]{2,1,0:T(8,128)(2,1)S(1)} %collective-permute-done.2.refs_3_, ...), custom_call_target="tpu_custom_call" | custom-call | flops 536870912 | bytes 2097152 | tf_op jit(solution)/shard_map/attend/pallas_call | solution.py:203
  16.7 0.0 slice-start
  16.7 0.0 slice-start.1
  16.7 1.4 %collective-permute-start.7 = (bf16[528,128]{1,0:T(8,128)(2,1)S(1)}, bf16[528,128]{1,0:T(8,128)(2,1)S(1)}, u32[]{:S(2)}, u32[]{:S(2)}) collective-permute-start(bf16[528,128]{1,0:T(8,128)(2,1)S(1)} %attend.5), channel_id=1, source_target_pairs={{0,3},{1,2},{2,1},{3,0},{4,7},{5,6},{6,5},{7,4},{8,11},{9,10},{10,... | collective-permute-start | bytes 405512 | tf_op jit(solution)/shard_map/ppermute | solution.py:25
  18.2 1.7 %attend.6 = bf16[528,128]{1,0:T(8,128)(2,1)S(1)} custom-call(bf16[8,32,128]{2,1,0:T(8,128)(2,1)S(1)} %bitcast.14, bf16[8,32,128]{2,1,0:T(8,128)(2,1)S(1)} %collective-permute-done.refs_1_, bf16[8,32,128]{2,1,0:T(8,128)(2,1)S(1)} %collective-permute-done.1.refs_2_, bf16[8,32,128]{2,1,0:T(8,128)(2,1)S(1)} %collective-permute-done.2.refs_3_, ...), custom_call_target="tpu_custom_call" | custom-call | flops 536870912 | bytes 2097152 | tf_op jit(solution)/shard_map/attend/pallas_call | solution.py:203
  19.8 0.0 slice-start.2
  19.9 1.6 %collective-permute-start.8 = (bf16[528,128]{1,0:T(8,128)(2,1)S(1)}, bf16[528,128]{1,0:T(8,128)(2,1)S(1)}, u32[]{:S(2)}, u32[]{:S(2)}) collective-permute-start(bf16[528,128]{1,0:T(8,128)(2,1)S(1)} %attend.6), channel_id=1, source_target_pairs={{0,1},{1,0},{2,3},{3,2},{4,5},{5,4},{6,7},{7,6},{8,9},{9,8},{10,11... | collective-permute-start | bytes 405512 | tf_op jit(solution)/shard_map/ppermute | solution.py:25
  21.4 1.7 %attend.7 = bf16[528,128]{1,0:T(8,128)(2,1)S(1)} custom-call(bf16[8,32,128]{2,1,0:T(8,128)(2,1)S(1)} %bitcast.15, bf16[8,32,128]{2,1,0:T(8,128)(2,1)S(1)} %collective-permute-done.refs_1_, bf16[8,32,128]{2,1,0:T(8,128)(2,1)S(1)} %collective-permute-done.1.refs_2_, bf16[8,32,128]{2,1,0:T(8,128)(2,1)S(1)} %collective-permute-done.2.refs_3_, ...), custom_call_target="tpu_custom_call" | custom-call | flops 536870912 | bytes 2097152 | tf_op jit(solution)/shard_map/attend/pallas_call | solution.py:203
  23.1 0.0 slice-start.3
  23.1 0.6 %collective-permute-start.9 = (bf16[528,128]{1,0:T(8,128)(2,1)S(1)}, bf16[528,128]{1,0:T(8,128)(2,1)S(1)}, u32[]{:S(2)}, u32[]{:S(2)}) collective-permute-start(bf16[528,128]{1,0:T(8,128)(2,1)S(1)} %attend.7), channel_id=1, source_target_pairs={{0,2},{1,3},{2,0},{3,1},{4,6},{5,7},{6,4},{7,5},{8,10},{9,11},{10,... | collective-permute-start | bytes 405512 | tf_op jit(solution)/shard_map/ppermute | solution.py:25
  23.8 1.6 %attend.4 = (f32[512,128]{1,0:T(8,128)S(1)}, bf16[16,128]{1,0:T(8,128)(2,1)S(1)}) custom-call(bf16[8,32,128]{2,1,0:T(8,128)(2,1)S(1)} %bitcast.16, bf16[8,32,128]{2,1,0:T(8,128)(2,1)S(1)} %collective-permute-done.refs_1_, bf16[8,32,128]{2,1,0:T(8,128)(2,1)S(1)} %collective-permute-done.1.refs_2_, bf16[8,32,128]{2,1,0:T(8,128)(2,1)S(1)} %collective-permute-done.2.refs_3_, ...), custom_call_target="tpu_custom_call" | custom-call | flops 536870912 | bytes 2097152 | tf_op jit(solution)/shard_map/attend/pallas_call | solution.py:203
  25.4 0.0 collective-permute-done.7.refs_0_
  25.4 0.0 collective-permute-done.8.refs_1_
  25.4 2.8 %collective-permute-done.9.refs_2_ = bf16[528,128]{1,0:T(8,128)(2,1)S(1)} collective-permute-done((bf16[528,128]{1,0:T(8,128)(2,1)S(1)}, bf16[528,128]{1,0:T(8,128)(2,1)S(1)}, u32[]{:S(2)}, u32[]{:S(2)}) %collective-permute-start.9) | collective-permute-done | bytes 135200 | tf_op jit(solution)/shard_map/ppermute | solution.py:25
  28.2 0.5 %merge.1 = (bf16[528,128]{1,0:T(8,128)(2,1)S(1)}, f32[512,128]{1,0:T(8,128)S(1)}) custom-call(f32[512,128]{1,0:T(8,128)S(1)} %get-tuple-element.13.wide_ref, bf16[16,128]{1,0:T(8,128)(2,1)S(1)} %get-tuple-element.14.stat_ref, bf16[528,128]{1,0:T(8,128)(2,1)S(1)} %collective-permute-done.7.refs_0_, bf16[528,128]{1,0:T(8,128)(2,1)S(1)} %collective-permute-done.8.refs_1_, ...), custom_call_target="tpu_custom_call" | custom-call | tf_op jit(solution)/shard_map/merge/pallas_call | solution.py:267
  28.7 2.4 %collective-permute-start.10 = (bf16[528,128]{1,0:T(8,128)(2,1)S(1)}, bf16[528,128]{1,0:T(8,128)(2,1)S(1)}, u32[]{:S(2)}, u32[]{:S(2)}) collective-permute-start(bf16[528,128]{1,0:T(8,128)(2,1)S(1)} %get-tuple-element.16.own_ref), channel_id=1, source_target_pairs={{0,6},{1,7},{2,4},{3,5},{4,2},{5,3},{6,0},{7,1},{8,14},{9,15},{10,... | collective-permute-start | bytes 405512 | tf_op jit(solution)/shard_map/ppermute | solution.py:25
  31.1 4.6 %collective-permute-done.10.other_ref = bf16[528,128]{1,0:T(8,128)(2,1)S(1)} collective-permute-done((bf16[528,128]{1,0:T(8,128)(2,1)S(1)}, bf16[528,128]{1,0:T(8,128)(2,1)S(1)}, u32[]{:S(2)}, u32[]{:S(2)}) %collective-permute-start.10) | collective-permute-done | bytes 135200 | tf_op jit(solution)/shard_map/ppermute | solution.py:25
  35.7 0.6 %settle.1.refs_0_ = bf16[32,2048]{1,0:T(8,128)(2,1)S(1)} custom-call(f32[512,128]{1,0:T(8,128)S(1)} %get-tuple-element.15.wide_ref, bf16[528,128]{1,0:T(8,128)(2,1)S(1)} %get-tuple-element.16.own_ref, bf16[528,128]{1,0:T(8,128)(2,1)S(1)} %collective-permute-done.10.other_ref, bf16[256,256]{1,0:T(8,128)(2,1)S(1)} %get-tuple-element.11.refs_10_.order_ref), custom_call_target="tpu_custom_call" | custom-call | tf_op jit(solution)/shard_map/settle/pallas_call | solution.py:299
  36.3 0.6 %collective-permute-start.13 = (bf16[32,2048]{1,0:T(8,128)(2,1)S(1)}, bf16[32,2048]{1,0:T(8,128)(2,1)S(1)}, u32[]{:S(2)}, u32[]{:S(2)}) collective-permute-start(bf16[32,2048]{1,0:T(8,128)(2,1)S(1)} %settle.1.refs_0_), channel_id=1, source_target_pairs={{0,1},{1,0},{2,3},{3,2},{4,5},{5,4},{6,7},{7,6},{8,9},{9,8},{10,11... | collective-permute-start | bytes 393224 | tf_op jit(solution)/shard_map/ppermute | solution.py:25
  36.9 1.4 %collective-permute-start.12 = (bf16[32,2048]{1,0:T(8,128)(2,1)S(1)}, bf16[32,2048]{1,0:T(8,128)(2,1)S(1)}, u32[]{:S(2)}, u32[]{:S(2)}) collective-permute-start(bf16[32,2048]{1,0:T(8,128)(2,1)S(1)} %settle.1.refs_0_), channel_id=1, source_target_pairs={{0,2},{1,3},{2,0},{3,1},{4,6},{5,7},{6,4},{7,5},{8,10},{9,11},{10,... | collective-permute-start | bytes 393224 | tf_op jit(solution)/shard_map/ppermute | solution.py:25
  38.3 1.6 %collective-permute-start.11 = (bf16[32,2048]{1,0:T(8,128)(2,1)S(1)}, bf16[32,2048]{1,0:T(8,128)(2,1)S(1)}, u32[]{:S(2)}, u32[]{:S(2)}) collective-permute-start(bf16[32,2048]{1,0:T(8,128)(2,1)S(1)} %settle.1.refs_0_), channel_id=1, source_target_pairs={{0,3},{1,2},{2,1},{3,0},{4,7},{5,6},{6,5},{7,4},{8,11},{9,10},{10,... | collective-permute-start | bytes 393224 | tf_op jit(solution)/shard_map/ppermute | solution.py:25
  39.9 0.0 slice-done.2
  39.9 0.8 %project.4.refs_2_ = f32[32,1024]{1,0:T(8,128)S(1)} custom-call(bf16[32,2048]{1,0:T(8,128)(2,1)S(1)} %settle.1.refs_0_, bf16[8192,1024]{1,0:T(8,128)(2,1)S(1)} %bitcast.6), custom_call_target="tpu_custom_call" | custom-call | tf_op jit(solution)/shard_map/project/pallas_call | solution.py:319
  40.7 0.6 %collective-permute-done.13.refs_0_ = bf16[32,2048]{1,0:T(8,128)(2,1)S(1)} collective-permute-done((bf16[32,2048]{1,0:T(8,128)(2,1)S(1)}, bf16[32,2048]{1,0:T(8,128)(2,1)S(1)}, u32[]{:S(2)}, u32[]{:S(2)}) %collective-permute-start.13) | collective-permute-done | bytes 131104 | tf_op jit(solution)/shard_map/ppermute | solution.py:25
  41.4 0.8 %project.5.refs_2_ = f32[32,1024]{1,0:T(8,128)S(1)} custom-call(bf16[32,2048]{1,0:T(8,128)(2,1)S(1)} %collective-permute-done.13.refs_0_, bf16[8192,1024]{1,0:T(8,128)(2,1)S(1)} %bitcast.6, f32[32,1024]{1,0:T(8,128)S(1)} %project.4.refs_2_), custom_call_target="tpu_custom_call" | custom-call | tf_op jit(solution)/shard_map/project/pallas_call | solution.py:319
  42.2 0.0 collective-permute-done.12.refs_0_
  42.2 0.8 %project.6.refs_2_ = f32[32,1024]{1,0:T(8,128)S(1)} custom-call(bf16[32,2048]{1,0:T(8,128)(2,1)S(1)} %collective-permute-done.12.refs_0_, bf16[8192,1024]{1,0:T(8,128)(2,1)S(1)} %bitcast.6, f32[32,1024]{1,0:T(8,128)S(1)} %project.5.refs_2_), custom_call_target="tpu_custom_call" | custom-call | tf_op jit(solution)/shard_map/project/pallas_call | solution.py:319
  43.0 1.2 %collective-permute-done.11.refs_0_ = bf16[32,2048]{1,0:T(8,128)(2,1)S(1)} collective-permute-done((bf16[32,2048]{1,0:T(8,128)(2,1)S(1)}, bf16[32,2048]{1,0:T(8,128)(2,1)S(1)}, u32[]{:S(2)}, u32[]{:S(2)}) %collective-permute-start.11) | collective-permute-done | bytes 131104 | tf_op jit(solution)/shard_map/ppermute | solution.py:25
  44.2 0.8 %project.7 = bf16[32,1024]{1,0:T(8,128)(2,1)S(1)} custom-call(bf16[32,2048]{1,0:T(8,128)(2,1)S(1)} %collective-permute-done.11.refs_0_, bf16[8192,1024]{1,0:T(8,128)(2,1)S(1)} %bitcast.6, f32[32,1024]{1,0:T(8,128)S(1)} %project.6.refs_2_), custom_call_target="tpu_custom_call" | custom-call | tf_op jit(solution)/shard_map/project/pallas_call | solution.py:319
  45.0 0.0 collective-permute-start.14
  45.1 3.7 %collective-permute-done.14 = bf16[32,1024]{1,0:T(8,128)(2,1)S(1)} collective-permute-done((bf16[32,1024]{1,0:T(8,128)(2,1)S(1)}, bf16[32,1024]{1,0:T(8,128)(2,1)S(1)}, u32[]{:S(2)}, u32[]{:S(2)}) %collective-permute-start.14) | collective-permute-done | bytes 65568 | tf_op jit(solution)/shard_map/ppermute | solution.py:30
  48.7 0.6 %copy.10 = bf16[32,1024]{1,0:T(8,128)(2,1)} copy(bf16[32,1024]{1,0:T(8,128)(2,1)S(1)} %collective-permute-done.14) | data formatting | bytes 131072
  (11 shorter events, 0.0 us)
Async XLA Ops:
  0.0 15.0 %copy-start = (bf16[4,8192]{1,0:T(4,128)(2,1)S(1)}, bf16[4,8192]{1,0:T(4,128)(2,1)}, u32[]{:S(2)}) copy-start(bf16[4,8192]{1,0:T(4,128)(2,1)} %param.5) | copy-start | bytes 196612
  0.0 15.0 %slice-start.4 = ((s8[8388608]{0:T(1024)(128)(4,1)}), s8[4194304]{0:T(1024)(128)(4,1)S(1)}, s32[]{:S(2)}) async-start(s8[8388608]{0:T(1024)(128)(4,1)} %bitcast.7), calls=%async_computation.4 | async-start | bytes 8388608
  0.0 15.0 %slice-start.5 = ((s8[8388608]{0:T(1024)(128)(4,1)}), s8[4194304]{0:T(1024)(128)(4,1)S(1)}, s32[]{:S(2)}) async-start(s8[8388608]{0:T(1024)(128)(4,1)} %bitcast.7), calls=%async_computation.5 | async-start | bytes 8388608
  0.0 7.6 %collective-permute-start = (bf16[8,32,128]{2,1,0:T(8,128)(2,1)}, bf16[8,32,128]{2,1,0:T(8,128)(2,1)S(1)}, u32[]{:S(2)}, u32[]{:S(2)}) collective-permute-start(bf16[8,32,128]{2,1,0:T(8,128)(2,1)} %bitcast.9), channel_id=1, source_target_pairs={{0,4},{1,5},{2,6},{3,7},{4,0},{5,1},{6,2},{7,3},{8,12},{9,13},{10,... | collective-permute-start | bytes 196616 | tf_op jit(solution)/shard_map/ppermute | solution.py:25
  4.1 6.6 %collective-permute-start.5 = (bf16[8,32,128]{2,1,0:T(8,128)(2,1)}, bf16[8,32,128]{2,1,0:T(8,128)(2,1)S(1)}, u32[]{:S(2)}, u32[]{:S(2)}) collective-permute-start(bf16[8,32,128]{2,1,0:T(8,128)(2,1)} %bitcast.10), channel_id=1, source_target_pairs={{0,3},{1,2},{2,1},{3,0},{4,7},{5,6},{6,5},{7,4},{8,11},{9,10},{10,... | collective-permute-start | bytes 196616 | tf_op jit(solution)/shard_map/ppermute | solution.py:25
  6.6 6.8 %collective-permute-start.3 = (bf16[8,32,128]{2,1,0:T(8,128)(2,1)}, bf16[8,32,128]{2,1,0:T(8,128)(2,1)S(1)}, u32[]{:S(2)}, u32[]{:S(2)}) collective-permute-start(bf16[8,32,128]{2,1,0:T(8,128)(2,1)} %bitcast.11), channel_id=1, source_target_pairs={{0,2},{1,3},{2,0},{3,1},{4,6},{5,7},{6,4},{7,5},{8,10},{9,11},{10,... | collective-permute-start | bytes 196616 | tf_op jit(solution)/shard_map/ppermute | solution.py:25
  7.1 6.4 %collective-permute-start.1 = (bf16[8,32,128]{2,1,0:T(8,128)(2,1)}, bf16[8,32,128]{2,1,0:T(8,128)(2,1)S(1)}, u32[]{:S(2)}, u32[]{:S(2)}) collective-permute-start(bf16[8,32,128]{2,1,0:T(8,128)(2,1)} %bitcast.12), channel_id=1, source_target_pairs={{0,1},{1,0},{2,3},{3,2},{4,5},{5,4},{6,7},{7,6},{8,9},{9,8},{10,11... | collective-permute-start | bytes 196616 | tf_op jit(solution)/shard_map/ppermute | solution.py:25
  7.6 5.8 %collective-permute-start.6 = (bf16[8,32,128]{2,1,0:T(8,128)(2,1)S(1)}, bf16[8,32,128]{2,1,0:T(8,128)(2,1)S(1)}, u32[]{:S(2)}, u32[]{:S(2)}) collective-permute-start(bf16[8,32,128]{2,1,0:T(8,128)(2,1)S(1)} %collective-permute-done.refs_1_), channel_id=1, source_target_pairs={{0,3},{1,2},{2,1},{3,0},{4,7},{5,6},{6,5},{7,4},{8,11},{9,10},{10,... | collective-permute-start | bytes 196616 | tf_op jit(solution)/shard_map/ppermute | solution.py:25
  10.1 4.3 %collective-permute-start.4 = (bf16[8,32,128]{2,1,0:T(8,128)(2,1)S(1)}, bf16[8,32,128]{2,1,0:T(8,128)(2,1)S(1)}, u32[]{:S(2)}, u32[]{:S(2)}) collective-permute-start(bf16[8,32,128]{2,1,0:T(8,128)(2,1)S(1)} %collective-permute-done.refs_1_), channel_id=1, source_target_pairs={{0,2},{1,3},{2,0},{3,1},{4,6},{5,7},{6,4},{7,5},{8,10},{9,11},{10,... | collective-permute-start | bytes 196616 | tf_op jit(solution)/shard_map/ppermute | solution.py:25
  10.7 4.3 %collective-permute-start.2 = (bf16[8,32,128]{2,1,0:T(8,128)(2,1)S(1)}, bf16[8,32,128]{2,1,0:T(8,128)(2,1)S(1)}, u32[]{:S(2)}, u32[]{:S(2)}) collective-permute-start(bf16[8,32,128]{2,1,0:T(8,128)(2,1)S(1)} %collective-permute-done.refs_1_), channel_id=1, source_target_pairs={{0,1},{1,0},{2,3},{3,2},{4,5},{5,4},{6,7},{7,6},{8,9},{9,8},{10,11... | collective-permute-start | bytes 196616 | tf_op jit(solution)/shard_map/ppermute | solution.py:25
  16.7 23.2 %slice-start = ((s8[16777216]{0:T(1024)(128)(4,1)}), s8[4194304]{0:T(1024)(128)(4,1)S(1)}, s32[]{:S(2)}) async-start(s8[16777216]{0:T(1024)(128)(4,1)} %bitcast.5), calls=%async_computation | async-start | bytes 8388608
  16.7 23.2 %slice-start.1 = ((s8[16777216]{0:T(1024)(128)(4,1)}), s8[4194304]{0:T(1024)(128)(4,1)S(1)}, s32[]{:S(2)}) async-start(s8[16777216]{0:T(1024)(128)(4,1)} %bitcast.5), calls=%async_computation.1 | async-start | bytes 8388608
  16.7 8.7 %collective-permute-start.7 = (bf16[528,128]{1,0:T(8,128)(2,1)S(1)}, bf16[528,128]{1,0:T(8,128)(2,1)S(1)}, u32[]{:S(2)}, u32[]{:S(2)}) collective-permute-start(bf16[528,128]{1,0:T(8,128)(2,1)S(1)} %attend.5), channel_id=1, source_target_pairs={{0,3},{1,2},{2,1},{3,0},{4,7},{5,6},{6,5},{7,4},{8,11},{9,10},{10,... | collective-permute-start | bytes 405512 | tf_op jit(solution)/shard_map/ppermute | solution.py:25
  19.8 20.0 %slice-start.2 = ((s8[16777216]{0:T(1024)(128)(4,1)}), s8[4194304]{0:T(1024)(128)(4,1)S(1)}, s32[]{:S(2)}) async-start(s8[16777216]{0:T(1024)(128)(4,1)} %bitcast.5), calls=%async_computation.2 | async-start | bytes 8388608
  19.9 5.6 %collective-permute-start.8 = (bf16[528,128]{1,0:T(8,128)(2,1)S(1)}, bf16[528,128]{1,0:T(8,128)(2,1)S(1)}, u32[]{:S(2)}, u32[]{:S(2)}) collective-permute-start(bf16[528,128]{1,0:T(8,128)(2,1)S(1)} %attend.6), channel_id=1, source_target_pairs={{0,1},{1,0},{2,3},{3,2},{4,5},{5,4},{6,7},{7,6},{8,9},{9,8},{10,11... | collective-permute-start | bytes 405512 | tf_op jit(solution)/shard_map/ppermute | solution.py:25
  23.1 16.8 %slice-start.3 = ((s8[16777216]{0:T(1024)(128)(4,1)}), s8[4194304]{0:T(1024)(128)(4,1)S(1)}, s32[]{:S(2)}) async-start(s8[16777216]{0:T(1024)(128)(4,1)} %bitcast.5), calls=%async_computation.3 | async-start | bytes 8388608
  23.1 5.1 %collective-permute-start.9 = (bf16[528,128]{1,0:T(8,128)(2,1)S(1)}, bf16[528,128]{1,0:T(8,128)(2,1)S(1)}, u32[]{:S(2)}, u32[]{:S(2)}) collective-permute-start(bf16[528,128]{1,0:T(8,128)(2,1)S(1)} %attend.7), channel_id=1, source_target_pairs={{0,2},{1,3},{2,0},{3,1},{4,6},{5,7},{6,4},{7,5},{8,10},{9,11},{10,... | collective-permute-start | bytes 405512 | tf_op jit(solution)/shard_map/ppermute | solution.py:25
  28.7 7.0 %collective-permute-start.10 = (bf16[528,128]{1,0:T(8,128)(2,1)S(1)}, bf16[528,128]{1,0:T(8,128)(2,1)S(1)}, u32[]{:S(2)}, u32[]{:S(2)}) collective-permute-start(bf16[528,128]{1,0:T(8,128)(2,1)S(1)} %get-tuple-element.16.own_ref), channel_id=1, source_target_pairs={{0,6},{1,7},{2,4},{3,5},{4,2},{5,3},{6,0},{7,1},{8,14},{9,15},{10,... | collective-permute-start | bytes 405512 | tf_op jit(solution)/shard_map/ppermute | solution.py:25
  36.3 5.0 %collective-permute-start.13 = (bf16[32,2048]{1,0:T(8,128)(2,1)S(1)}, bf16[32,2048]{1,0:T(8,128)(2,1)S(1)}, u32[]{:S(2)}, u32[]{:S(2)}) collective-permute-start(bf16[32,2048]{1,0:T(8,128)(2,1)S(1)} %settle.1.refs_0_), channel_id=1, source_target_pairs={{0,1},{1,0},{2,3},{3,2},{4,5},{5,4},{6,7},{7,6},{8,9},{9,8},{10,11... | collective-permute-start | bytes 393224 | tf_op jit(solution)/shard_map/ppermute | solution.py:25
  36.9 5.3 %collective-permute-start.12 = (bf16[32,2048]{1,0:T(8,128)(2,1)S(1)}, bf16[32,2048]{1,0:T(8,128)(2,1)S(1)}, u32[]{:S(2)}, u32[]{:S(2)}) collective-permute-start(bf16[32,2048]{1,0:T(8,128)(2,1)S(1)} %settle.1.refs_0_), channel_id=1, source_target_pairs={{0,2},{1,3},{2,0},{3,1},{4,6},{5,7},{6,4},{7,5},{8,10},{9,11},{10,... | collective-permute-start | bytes 393224 | tf_op jit(solution)/shard_map/ppermute | solution.py:25
  38.3 5.9 %collective-permute-start.11 = (bf16[32,2048]{1,0:T(8,128)(2,1)S(1)}, bf16[32,2048]{1,0:T(8,128)(2,1)S(1)}, u32[]{:S(2)}, u32[]{:S(2)}) collective-permute-start(bf16[32,2048]{1,0:T(8,128)(2,1)S(1)} %settle.1.refs_0_), channel_id=1, source_target_pairs={{0,3},{1,2},{2,1},{3,0},{4,7},{5,6},{6,5},{7,4},{8,11},{9,10},{10,... | collective-permute-start | bytes 393224 | tf_op jit(solution)/shard_map/ppermute | solution.py:25
  45.0 3.7 %collective-permute-start.14 = (bf16[32,1024]{1,0:T(8,128)(2,1)S(1)}, bf16[32,1024]{1,0:T(8,128)(2,1)S(1)}, u32[]{:S(2)}, u32[]{:S(2)}) collective-permute-start(bf16[32,1024]{1,0:T(8,128)(2,1)S(1)} %project.7), channel_id=1, source_target_pairs={{0,8},{8,16},{16,24},{24,0},{1,9},{9,17},{17,25},{25,1},{2,10},{10... | collective-permute-start | bytes 196616 | tf_op jit(solution)/shard_map/ppermute | solution.py:30

commit v11 on v10

--- a/solution.py
+++ b/solution.py
@@ -247,7 +247,8 @@
 
 def merge_kernel(plan, wide_ref, stat_ref, *refs):
     *parts, out_ref, wide_out_ref = refs
-    stats = [(stat_ref, 0)] + [(ref, plan.share_rows) for ref in parts]
+    size = stat_rows(plan.units * plan.blocks)
+    stats = [(stat_ref, stat_ref.shape[0] - size)] + [(ref, plan.share_rows) for ref in parts]
     rows, scales = [], []
     for block in range(plan.units * plan.blocks):
         joint, scale, total = factors(stats, block)
@@ -282,17 +283,19 @@
         _, scale, total = factors(stats, block)
         scales += [f / total for f in scale]
     scales = columns(scales)
+    done = []
+    for block in range(plan.units * plan.blocks):
+        mixed = mix([wide_ref, other_ref], block * 128, scales[2 * block : 2 * block + 2])
+        done.append(mixed.astype(jnp.bfloat16))
+    done = [done[unit * plan.blocks : (unit + 1) * plan.blocks] for unit in range(plan.units)]
+    done = jnp.concatenate([jnp.concatenate(blocks, axis=0) for blocks in done], axis=1)
+    if plan.by_device:
+        done = jnp.dot(order_ref[...], done, preferred_element_type=jnp.float32).astype(jnp.bfloat16)
     for unit in range(plan.units):
-        done = []
-        for block in range(unit * plan.blocks, (unit + 1) * plan.blocks):
-            mixed = mix([wide_ref, other_ref], block * 128, scales[2 * block : 2 * block + 2])
-            done.append(mixed.astype(jnp.bfloat16))
-        done = jnp.concatenate(done, axis=0)
-        if plan.by_device:
-            done = jnp.dot(order_ref[...], done, preferred_element_type=jnp.float32).astype(jnp.bfloat16)
         for head in range(plan.unit_heads):
             to = (unit * plan.unit_heads + head) * HD
-            out_ref[:, to : to + HD] = done[head * plan.rows : (head + 1) * plan.rows, :]
+            rows = slice(head * plan.rows, (head + 1) * plan.rows)
+            out_ref[:, to : to + HD] = done[rows, unit * HD : (unit + 1) * HD]
 
 
 def settle(plan, wide, own, other, order):
@@ -345,13 +348,14 @@
         gathered = [pair] + [swap(pair, "ctx", k) for k in range(1, half)]
 
     received = []
-    for part in sorted(range(1, half), key=lambda k: (k % 2 == 0, -k)):
+    for part in reversed(range(1, half)):
         (piece,) = attend(plan, part, gathered, cache, bias, order, one_hot)
         received.append(swap(piece, "ctx", part))
     wide, stats = attend(plan, 0, gathered, cache, bias, order, one_hot)
 
-    near, near_wide = merge(plan, wide, stats, received)
-    block = settle(plan, near_wide, near, swap(near, "ctx", plan.across), order)
+    near, wide = merge(plan, wide, stats, received[:-1])
+    near, wide = merge(plan, wide, near, received[-1:])
+    block = settle(plan, wide, near, swap(near, "ctx", plan.across), order)
 
     total = project(plan, 0, block, out_weight, None, jnp.float32)
     blocks = [swap(block, "ctx", k) for k in range(1, half)]

time: 49.5 us -> 49.1 us (level)
  waiting for transfers between devices: 14.4 us -> 12.8 us
  starting transfers between devices: 21.4 us -> 22.2 us
    ppermute x14, waiting for transfers between devices: 10.7 us -> 9.14 us  [swap(): return lax.ppermute(value, axis, [(i, i ^ bits) for i in range(devices)])]
    ppermute x14, starting transfers between devices: 21.3 us -> 22.2 us  [swap(): return lax.ppermute(value, axis, [(i, i ^ bits) for i in range(devices)])]
  transfers between devices with their start and end apart: 15 -> 15, of which waited for: 7 -> 8; matrix products, arithmetic and copies ran while one was open for 0% -> 0% of each run, Pallas kernels for 16% -> 17%
where the time goes in v11:
time: 49.1 us; the launch traced here: 48.8 us
  starting transfers between devices  22.2 us (45%)
  waiting for transfers between devices  12.8 us (26%)
  Pallas kernels  11.7 us (24%)
  between operations  1.47 us (3%)
  local copies, waits for them, and re-layouts  0.67 us (1%)
    ppermute x14, starting transfers between devices, swap(): return lax.ppermute(value, axis, [(i, i ^ bits) for i in range(devices)])  22.2 us
    ppermute x14, waiting for transfers between devices, swap(): return lax.ppermute(value, axis, [(i, i ^ bits) for i in range(devices)])  9.14 us
    pallas_call x4, Pallas kernels, attend(): local(functools.partial(attend_kernel, plan, part), out_shape, [pltpu.VME...  6.74 us
    ppermute x1, waiting for transfers between devices, from_behind(): lax.ppermute(value, axis, [(i, (i + by) % devices) for i in range(devices)])  3.69 us
    pallas_call x4, Pallas kernels, project(): local(functools.partial(project_kernel, plan, part), jax.ShapeDtypeStruct...  3.29 us
  transfers between devices with their start and end apart: 15, of which 8 were waited for; matrix products, arithmetic and copies ran while one was open for 0% of the time, Pallas kernels for 17%

profile of v11, /device:TPU:0, one launch (start us, length us, event | category | flops | bytes accessed | tf_op | source)
XLA Modules:
  0.0 48.8 jit_solution(13476253970842463488)
XLA Ops:
  0.0 4.1 %collective-permute-start = (bf16[8,32,128]{2,1,0:T(8,128)(2,1)}, bf16[8,32,128]{2,1,0:T(8,128)(2,1)S(1)}, u32[]{:S(2)}, u32[]{:S(2)}) collective-permute-start(bf16[8,32,128]{2,1,0:T(8,128)(2,1)} %bitcast.9), channel_id=1, source_target_pairs={{0,4},{1,5},{2,6},{3,7},{4,0},{5,1},{6,2},{7,3},{8,12},{9,13},{10,... | collective-permute-start | bytes 196616 | tf_op jit(solution)/shard_map/ppermute | solution.py:25
  4.1 2.5 %collective-permute-start.5 = (bf16[8,32,128]{2,1,0:T(8,128)(2,1)}, bf16[8,32,128]{2,1,0:T(8,128)(2,1)S(1)}, u32[]{:S(2)}, u32[]{:S(2)}) collective-permute-start(bf16[8,32,128]{2,1,0:T(8,128)(2,1)} %bitcast.10), channel_id=1, source_target_pairs={{0,3},{1,2},{2,1},{3,0},{4,7},{5,6},{6,5},{7,4},{8,11},{9,10},{10,... | collective-permute-start | bytes 196616 | tf_op jit(solution)/shard_map/ppermute | solution.py:25
  6.6 0.4 collective-permute-start.3
  7.1 0.5 %collective-permute-start.1 = (bf16[8,32,128]{2,1,0:T(8,128)(2,1)}, bf16[8,32,128]{2,1,0:T(8,128)(2,1)S(1)}, u32[]{:S(2)}, u32[]{:S(2)}) collective-permute-start(bf16[8,32,128]{2,1,0:T(8,128)(2,1)} %bitcast.12), channel_id=1, source_target_pairs={{0,1},{1,0},{2,3},{3,2},{4,5},{5,4},{6,7},{7,6},{8,9},{9,8},{10,11... | collective-permute-start | bytes 196616 | tf_op jit(solution)/shard_map/ppermute | solution.py:25
  7.6 0.0 collective-permute-done.refs_1_
  7.6 2.5 %collective-permute-start.6 = (bf16[8,32,128]{2,1,0:T(8,128)(2,1)S(1)}, bf16[8,32,128]{2,1,0:T(8,128)(2,1)S(1)}, u32[]{:S(2)}, u32[]{:S(2)}) collective-permute-start(bf16[8,32,128]{2,1,0:T(8,128)(2,1)S(1)} %collective-permute-done.refs_1_), channel_id=1, source_target_pairs={{0,3},{1,2},{2,1},{3,0},{4,7},{5,6},{6,5},{7,4},{8,11},{9,10},{10,... | collective-permute-start | bytes 196616 | tf_op jit(solution)/shard_map/ppermute | solution.py:25
  10.1 0.6 %collective-permute-start.4 = (bf16[8,32,128]{2,1,0:T(8,128)(2,1)S(1)}, bf16[8,32,128]{2,1,0:T(8,128)(2,1)S(1)}, u32[]{:S(2)}, u32[]{:S(2)}) collective-permute-start(bf16[8,32,128]{2,1,0:T(8,128)(2,1)S(1)} %collective-permute-done.refs_1_), channel_id=1, source_target_pairs={{0,2},{1,3},{2,0},{3,1},{4,6},{5,7},{6,4},{7,5},{8,10},{9,11},{10,... | collective-permute-start | bytes 196616 | tf_op jit(solution)/shard_map/ppermute | solution.py:25
  10.7 0.0 collective-permute-done.5.after_ref.refs_6_
  10.7 1.1 %collective-permute-start.2 = (bf16[8,32,128]{2,1,0:T(8,128)(2,1)S(1)}, bf16[8,32,128]{2,1,0:T(8,128)(2,1)S(1)}, u32[]{:S(2)}, u32[]{:S(2)}) collective-permute-start(bf16[8,32,128]{2,1,0:T(8,128)(2,1)S(1)} %collective-permute-done.refs_1_), channel_id=1, source_target_pairs={{0,1},{1,0},{2,3},{3,2},{4,5},{5,4},{6,7},{7,6},{8,9},{9,8},{10,11... | collective-permute-start | bytes 196616 | tf_op jit(solution)/shard_map/ppermute | solution.py:25
  11.8 0.1 order.1
  13.2 0.2 mask.1.refs_9_
  13.4 0.0 collective-permute-done.3.refs_4_
  13.4 0.0 collective-permute-done.1.refs_2_
  13.4 0.0 collective-permute-done.6.refs_7_
  13.4 0.9 %collective-permute-done.4.refs_5_ = bf16[8,32,128]{2,1,0:T(8,128)(2,1)S(1)} collective-permute-done((bf16[8,32,128]{2,1,0:T(8,128)(2,1)S(1)}, bf16[8,32,128]{2,1,0:T(8,128)(2,1)S(1)}, u32[]{:S(2)}, u32[]{:S(2)}) %collective-permute-start.4) | collective-permute-done | bytes 65568 | tf_op jit(solution)/shard_map/ppermute | solution.py:25
  14.4 0.6 %collective-permute-done.2.refs_3_ = bf16[8,32,128]{2,1,0:T(8,128)(2,1)S(1)} collective-permute-done((bf16[8,32,128]{2,1,0:T(8,128)(2,1)S(1)}, bf16[8,32,128]{2,1,0:T(8,128)(2,1)S(1)}, u32[]{:S(2)}, u32[]{:S(2)}) %collective-permute-start.2) | collective-permute-done | bytes 65568 | tf_op jit(solution)/shard_map/ppermute | solution.py:25
  15.0 1.7 %attend.5 = bf16[528,128]{1,0:T(8,128)(2,1)S(1)} custom-call(bf16[8,32,128]{2,1,0:T(8,128)(2,1)S(1)} %bitcast.13, bf16[8,32,128]{2,1,0:T(8,128)(2,1)S(1)} %collective-permute-done.refs_1_, bf16[8,32,128]{2,1,0:T(8,128)(2,1)S(1)} %collective-permute-done.1.refs_2_, bf16[8,32,128]{2,1,0:T(8,128)(2,1)S(1)} %collective-permute-done.2.refs_3_, ...), custom_call_target="tpu_custom_call" | custom-call | flops 536870912 | bytes 2097152 | tf_op jit(solution)/shard_map/attend/pallas_call | solution.py:203
  16.7 0.0 slice-start
  16.7 0.0 slice-start.1
  16.7 1.4 %collective-permute-start.7 = (bf16[528,128]{1,0:T(8,128)(2,1)S(1)}, bf16[528,128]{1,0:T(8,128)(2,1)S(1)}, u32[]{:S(2)}, u32[]{:S(2)}) collective-permute-start(bf16[528,128]{1,0:T(8,128)(2,1)S(1)} %attend.5), channel_id=1, source_target_pairs={{0,3},{1,2},{2,1},{3,0},{4,7},{5,6},{6,5},{7,4},{8,11},{9,10},{10,... | collective-permute-start | bytes 405512 | tf_op jit(solution)/shard_map/ppermute | solution.py:25
  18.2 1.7 %attend.6 = bf16[528,128]{1,0:T(8,128)(2,1)S(1)} custom-call(bf16[8,32,128]{2,1,0:T(8,128)(2,1)S(1)} %bitcast.14, bf16[8,32,128]{2,1,0:T(8,128)(2,1)S(1)} %collective-permute-done.refs_1_, bf16[8,32,128]{2,1,0:T(8,128)(2,1)S(1)} %collective-permute-done.1.refs_2_, bf16[8,32,128]{2,1,0:T(8,128)(2,1)S(1)} %collective-permute-done.2.refs_3_, ...), custom_call_target="tpu_custom_call" | custom-call | flops 536870912 | bytes 2097152 | tf_op jit(solution)/shard_map/attend/pallas_call | solution.py:203
  19.9 0.0 slice-start.2
  19.9 1.2 %collective-permute-start.8 = (bf16[528,128]{1,0:T(8,128)(2,1)S(1)}, bf16[528,128]{1,0:T(8,128)(2,1)S(1)}, u32[]{:S(2)}, u32[]{:S(2)}) collective-permute-start(bf16[528,128]{1,0:T(8,128)(2,1)S(1)} %attend.6), channel_id=1, source_target_pairs={{0,2},{1,3},{2,0},{3,1},{4,6},{5,7},{6,4},{7,5},{8,10},{9,11},{10,... | collective-permute-start | bytes 405512 | tf_op jit(solution)/shard_map/ppermute | solution.py:25
  21.1 1.7 %attend.7 = bf16[528,128]{1,0:T(8,128)(2,1)S(1)} custom-call(bf16[8,32,128]{2,1,0:T(8,128)(2,1)S(1)} %bitcast.15, bf16[8,32,128]{2,1,0:T(8,128)(2,1)S(1)} %collective-permute-done.refs_1_, bf16[8,32,128]{2,1,0:T(8,128)(2,1)S(1)} %collective-permute-done.1.refs_2_, bf16[8,32,128]{2,1,0:T(8,128)(2,1)S(1)} %collective-permute-done.2.refs_3_, ...), custom_call_target="tpu_custom_call" | custom-call | flops 536870912 | bytes 2097152 | tf_op jit(solution)/shard_map/attend/pallas_call | solution.py:203
  22.8 0.0 slice-start.3
  22.8 1.0 %collective-permute-start.9 = (bf16[528,128]{1,0:T(8,128)(2,1)S(1)}, bf16[528,128]{1,0:T(8,128)(2,1)S(1)}, u32[]{:S(2)}, u32[]{:S(2)}) collective-permute-start(bf16[528,128]{1,0:T(8,128)(2,1)S(1)} %attend.7), channel_id=1, source_target_pairs={{0,1},{1,0},{2,3},{3,2},{4,5},{5,4},{6,7},{7,6},{8,9},{9,8},{10,11... | collective-permute-start | bytes 405512 | tf_op jit(solution)/shard_map/ppermute | solution.py:25
  23.8 1.6 %attend.4 = (f32[512,128]{1,0:T(8,128)S(1)}, bf16[16,128]{1,0:T(8,128)(2,1)S(1)}) custom-call(bf16[8,32,128]{2,1,0:T(8,128)(2,1)S(1)} %bitcast.16, bf16[8,32,128]{2,1,0:T(8,128)(2,1)S(1)} %collective-permute-done.refs_1_, bf16[8,32,128]{2,1,0:T(8,128)(2,1)S(1)} %collective-permute-done.1.refs_2_, bf16[8,32,128]{2,1,0:T(8,128)(2,1)S(1)} %collective-permute-done.2.refs_3_, ...), custom_call_target="tpu_custom_call" | custom-call | flops 536870912 | bytes 2097152 | tf_op jit(solution)/shard_map/attend/pallas_call | solution.py:203
  25.4 0.0 collective-permute-done.7.refs_0_
  25.4 0.0 collective-permute-done.8.refs_1_
  25.4 0.4 merge.2
  25.9 2.0 %collective-permute-done.9.refs_0_ = bf16[528,128]{1,0:T(8,128)(2,1)S(1)} collective-permute-done((bf16[528,128]{1,0:T(8,128)(2,1)S(1)}, bf16[528,128]{1,0:T(8,128)(2,1)S(1)}, u32[]{:S(2)}, u32[]{:S(2)}) %collective-permute-start.9) | collective-permute-done | bytes 135200 | tf_op jit(solution)/shard_map/ppermute | solution.py:25
  27.9 0.3 merge.3
  28.2 3.2 %collective-permute-start.10 = (bf16[528,128]{1,0:T(8,128)(2,1)S(1)}, bf16[528,128]{1,0:T(8,128)(2,1)S(1)}, u32[]{:S(2)}, u32[]{:S(2)}) collective-permute-start(bf16[528,128]{1,0:T(8,128)(2,1)S(1)} %get-tuple-element.20.own_ref), channel_id=1, source_target_pairs={{0,6},{1,7},{2,4},{3,5},{4,2},{5,3},{6,0},{7,1},{8,14},{9,15},{10,... | collective-permute-start | bytes 405512 | tf_op jit(solution)/shard_map/ppermute | solution.py:25
  31.4 3.6 %collective-permute-done.10.other_ref = bf16[528,128]{1,0:T(8,128)(2,1)S(1)} collective-permute-done((bf16[528,128]{1,0:T(8,128)(2,1)S(1)}, bf16[528,128]{1,0:T(8,128)(2,1)S(1)}, u32[]{:S(2)}, u32[]{:S(2)}) %collective-permute-start.10) | collective-permute-done | bytes 135200 | tf_op jit(solution)/shard_map/ppermute | solution.py:25
  35.1 0.6 %settle.1.refs_0_ = bf16[32,2048]{1,0:T(8,128)(2,1)S(1)} custom-call(f32[512,128]{1,0:T(8,128)S(1)} %get-tuple-element.19.wide_ref, bf16[528,128]{1,0:T(8,128)(2,1)S(1)} %get-tuple-element.20.own_ref, bf16[528,128]{1,0:T(8,128)(2,1)S(1)} %collective-permute-done.10.other_ref, bf16[256,256]{1,0:T(8,128)(2,1)S(1)} %get-tuple-element.13.refs_10_.order_ref), custom_call_target="tpu_custom_call" | custom-call | tf_op jit(solution)/shard_map/settle/pallas_call | solution.py:302
  35.6 1.4 %collective-permute-start.13 = (bf16[32,2048]{1,0:T(8,128)(2,1)S(1)}, bf16[32,2048]{1,0:T(8,128)(2,1)S(1)}, u32[]{:S(2)}, u32[]{:S(2)}) collective-permute-start(bf16[32,2048]{1,0:T(8,128)(2,1)S(1)} %settle.1.refs_0_), channel_id=1, source_target_pairs={{0,1},{1,0},{2,3},{3,2},{4,5},{5,4},{6,7},{7,6},{8,9},{9,8},{10,11... | collective-permute-start | bytes 393224 | tf_op jit(solution)/shard_map/ppermute | solution.py:25
  37.1 0.7 %collective-permute-start.12 = (bf16[32,2048]{1,0:T(8,128)(2,1)S(1)}, bf16[32,2048]{1,0:T(8,128)(2,1)S(1)}, u32[]{:S(2)}, u32[]{:S(2)}) collective-permute-start(bf16[32,2048]{1,0:T(8,128)(2,1)S(1)} %settle.1.refs_0_), channel_id=1, source_target_pairs={{0,2},{1,3},{2,0},{3,1},{4,6},{5,7},{6,4},{7,5},{8,10},{9,11},{10,... | collective-permute-start | bytes 393224 | tf_op jit(solution)/shard_map/ppermute | solution.py:25
  37.8 1.4 %collective-permute-start.11 = (bf16[32,2048]{1,0:T(8,128)(2,1)S(1)}, bf16[32,2048]{1,0:T(8,128)(2,1)S(1)}, u32[]{:S(2)}, u32[]{:S(2)}) collective-permute-start(bf16[32,2048]{1,0:T(8,128)(2,1)S(1)} %settle.1.refs_0_), channel_id=1, source_target_pairs={{0,3},{1,2},{2,1},{3,0},{4,7},{5,6},{6,5},{7,4},{8,11},{9,10},{10,... | collective-permute-start | bytes 393224 | tf_op jit(solution)/shard_map/ppermute | solution.py:25
  39.2 0.8 %project.4.refs_2_ = f32[32,1024]{1,0:T(8,128)S(1)} custom-call(bf16[32,2048]{1,0:T(8,128)(2,1)S(1)} %settle.1.refs_0_, bf16[8192,1024]{1,0:T(8,128)(2,1)S(1)} %bitcast.6), custom_call_target="tpu_custom_call" | custom-call | tf_op jit(solution)/shard_map/project/pallas_call | solution.py:322
  40.0 0.6 %collective-permute-done.13.refs_0_ = bf16[32,2048]{1,0:T(8,128)(2,1)S(1)} collective-permute-done((bf16[32,2048]{1,0:T(8,128)(2,1)S(1)}, bf16[32,2048]{1,0:T(8,128)(2,1)S(1)}, u32[]{:S(2)}, u32[]{:S(2)}) %collective-permute-start.13) | collective-permute-done | bytes 131104 | tf_op jit(solution)/shard_map/ppermute | solution.py:25
  40.7 0.8 %project.5.refs_2_ = f32[32,1024]{1,0:T(8,128)S(1)} custom-call(bf16[32,2048]{1,0:T(8,128)(2,1)S(1)} %collective-permute-done.13.refs_0_, bf16[8192,1024]{1,0:T(8,128)(2,1)S(1)} %bitcast.6, f32[32,1024]{1,0:T(8,128)S(1)} %project.4.refs_2_), custom_call_target="tpu_custom_call" | custom-call | tf_op jit(solution)/shard_map/project/pallas_call | solution.py:322
  41.5 0.6 %collective-permute-done.12.refs_0_ = bf16[32,2048]{1,0:T(8,128)(2,1)S(1)} collective-permute-done((bf16[32,2048]{1,0:T(8,128)(2,1)S(1)}, bf16[32,2048]{1,0:T(8,128)(2,1)S(1)}, u32[]{:S(2)}, u32[]{:S(2)}) %collective-permute-start.12) | collective-permute-done | bytes 131104 | tf_op jit(solution)/shard_map/ppermute | solution.py:25
  42.0 0.8 %project.6.refs_2_ = f32[32,1024]{1,0:T(8,128)S(1)} custom-call(bf16[32,2048]{1,0:T(8,128)(2,1)S(1)} %collective-permute-done.12.refs_0_, bf16[8192,1024]{1,0:T(8,128)(2,1)S(1)} %bitcast.6, f32[32,1024]{1,0:T(8,128)S(1)} %project.5.refs_2_), custom_call_target="tpu_custom_call" | custom-call | tf_op jit(solution)/shard_map/project/pallas_call | solution.py:322
  42.9 0.8 %collective-permute-done.11.refs_0_ = bf16[32,2048]{1,0:T(8,128)(2,1)S(1)} collective-permute-done((bf16[32,2048]{1,0:T(8,128)(2,1)S(1)}, bf16[32,2048]{1,0:T(8,128)(2,1)S(1)}, u32[]{:S(2)}, u32[]{:S(2)}) %collective-permute-start.11) | collective-permute-done | bytes 131104 | tf_op jit(solution)/shard_map/ppermute | solution.py:25
  43.7 0.8 %project.7 = bf16[32,1024]{1,0:T(8,128)(2,1)S(1)} custom-call(bf16[32,2048]{1,0:T(8,128)(2,1)S(1)} %collective-permute-done.11.refs_0_, bf16[8192,1024]{1,0:T(8,128)(2,1)S(1)} %bitcast.6, f32[32,1024]{1,0:T(8,128)S(1)} %project.6.refs_2_), custom_call_target="tpu_custom_call" | custom-call | tf_op jit(solution)/shard_map/project/pallas_call | solution.py:322
  44.5 0.0 collective-permute-start.14
  44.5 3.7 %collective-permute-done.14 = bf16[32,1024]{1,0:T(8,128)(2,1)S(1)} collective-permute-done((bf16[32,1024]{1,0:T(8,128)(2,1)S(1)}, bf16[32,1024]{1,0:T(8,128)(2,1)S(1)}, u32[]{:S(2)}, u32[]{:S(2)}) %collective-permute-start.14) | collective-permute-done | bytes 65568 | tf_op jit(solution)/shard_map/ppermute | solution.py:30
  48.2 0.6 %copy.10 = bf16[32,1024]{1,0:T(8,128)(2,1)} copy(bf16[32,1024]{1,0:T(8,128)(2,1)S(1)} %collective-permute-done.14) | data formatting | bytes 131072
  (12 shorter events, 0.0 us)
Async XLA Ops:
  0.0 15.0 %copy-start = (bf16[4,8192]{1,0:T(4,128)(2,1)S(1)}, bf16[4,8192]{1,0:T(4,128)(2,1)}, u32[]{:S(2)}) copy-start(bf16[4,8192]{1,0:T(4,128)(2,1)} %param.5) | copy-start | bytes 196612
  0.0 15.0 %slice-start.4 = ((s8[8388608]{0:T(1024)(128)(4,1)}), s8[4194304]{0:T(1024)(128)(4,1)S(1)}, s32[]{:S(2)}) async-start(s8[8388608]{0:T(1024)(128)(4,1)} %bitcast.7), calls=%async_computation.4 | async-start | bytes 8388608
  0.0 15.0 %slice-start.5 = ((s8[8388608]{0:T(1024)(128)(4,1)}), s8[4194304]{0:T(1024)(128)(4,1)S(1)}, s32[]{:S(2)}) async-start(s8[8388608]{0:T(1024)(128)(4,1)} %bitcast.7), calls=%async_computation.5 | async-start | bytes 8388608
  0.0 7.6 %collective-permute-start = (bf16[8,32,128]{2,1,0:T(8,128)(2,1)}, bf16[8,32,128]{2,1,0:T(8,128)(2,1)S(1)}, u32[]{:S(2)}, u32[]{:S(2)}) collective-permute-start(bf16[8,32,128]{2,1,0:T(8,128)(2,1)} %bitcast.9), channel_id=1, source_target_pairs={{0,4},{1,5},{2,6},{3,7},{4,0},{5,1},{6,2},{7,3},{8,12},{9,13},{10,... | collective-permute-start | bytes 196616 | tf_op jit(solution)/shard_map/ppermute | solution.py:25
  4.1 6.6 %collective-permute-start.5 = (bf16[8,32,128]{2,1,0:T(8,128)(2,1)}, bf16[8,32,128]{2,1,0:T(8,128)(2,1)S(1)}, u32[]{:S(2)}, u32[]{:S(2)}) collective-permute-start(bf16[8,32,128]{2,1,0:T(8,128)(2,1)} %bitcast.10), channel_id=1, source_target_pairs={{0,3},{1,2},{2,1},{3,0},{4,7},{5,6},{6,5},{7,4},{8,11},{9,10},{10,... | collective-permute-start | bytes 196616 | tf_op jit(solution)/shard_map/ppermute | solution.py:25
  6.6 6.8 %collective-permute-start.3 = (bf16[8,32,128]{2,1,0:T(8,128)(2,1)}, bf16[8,32,128]{2,1,0:T(8,128)(2,1)S(1)}, u32[]{:S(2)}, u32[]{:S(2)}) collective-permute-start(bf16[8,32,128]{2,1,0:T(8,128)(2,1)} %bitcast.11), channel_id=1, source_target_pairs={{0,2},{1,3},{2,0},{3,1},{4,6},{5,7},{6,4},{7,5},{8,10},{9,11},{10,... | collective-permute-start | bytes 196616 | tf_op jit(solution)/shard_map/ppermute | solution.py:25
  7.1 6.4 %collective-permute-start.1 = (bf16[8,32,128]{2,1,0:T(8,128)(2,1)}, bf16[8,32,128]{2,1,0:T(8,128)(2,1)S(1)}, u32[]{:S(2)}, u32[]{:S(2)}) collective-permute-start(bf16[8,32,128]{2,1,0:T(8,128)(2,1)} %bitcast.12), channel_id=1, source_target_pairs={{0,1},{1,0},{2,3},{3,2},{4,5},{5,4},{6,7},{7,6},{8,9},{9,8},{10,11... | collective-permute-start | bytes 196616 | tf_op jit(solution)/shard_map/ppermute | solution.py:25
  7.6 5.8 %collective-permute-start.6 = (bf16[8,32,128]{2,1,0:T(8,128)(2,1)S(1)}, bf16[8,32,128]{2,1,0:T(8,128)(2,1)S(1)}, u32[]{:S(2)}, u32[]{:S(2)}) collective-permute-start(bf16[8,32,128]{2,1,0:T(8,128)(2,1)S(1)} %collective-permute-done.refs_1_), channel_id=1, source_target_pairs={{0,3},{1,2},{2,1},{3,0},{4,7},{5,6},{6,5},{7,4},{8,11},{9,10},{10,... | collective-permute-start | bytes 196616 | tf_op jit(solution)/shard_map/ppermute | solution.py:25
  10.1 4.3 %collective-permute-start.4 = (bf16[8,32,128]{2,1,0:T(8,128)(2,1)S(1)}, bf16[8,32,128]{2,1,0:T(8,128)(2,1)S(1)}, u32[]{:S(2)}, u32[]{:S(2)}) collective-permute-start(bf16[8,32,128]{2,1,0:T(8,128)(2,1)S(1)} %collective-permute-done.refs_1_), channel_id=1, source_target_pairs={{0,2},{1,3},{2,0},{3,1},{4,6},{5,7},{6,4},{7,5},{8,10},{9,11},{10,... | collective-permute-start | bytes 196616 | tf_op jit(solution)/shard_map/ppermute | solution.py:25
  10.7 4.3 %collective-permute-start.2 = (bf16[8,32,128]{2,1,0:T(8,128)(2,1)S(1)}, bf16[8,32,128]{2,1,0:T(8,128)(2,1)S(1)}, u32[]{:S(2)}, u32[]{:S(2)}) collective-permute-start(bf16[8,32,128]{2,1,0:T(8,128)(2,1)S(1)} %collective-permute-done.refs_1_), channel_id=1, source_target_pairs={{0,1},{1,0},{2,3},{3,2},{4,5},{5,4},{6,7},{7,6},{8,9},{9,8},{10,11... | collective-permute-start | bytes 196616 | tf_op jit(solution)/shard_map/ppermute | solution.py:25
  16.7 22.5 %slice-start = ((s8[16777216]{0:T(1024)(128)(4,1)}), s8[4194304]{0:T(1024)(128)(4,1)S(1)}, s32[]{:S(2)}) async-start(s8[16777216]{0:T(1024)(128)(4,1)} %bitcast.5), calls=%async_computation | async-start | bytes 8388608
  16.7 22.5 %slice-start.1 = ((s8[16777216]{0:T(1024)(128)(4,1)}), s8[4194304]{0:T(1024)(128)(4,1)S(1)}, s32[]{:S(2)}) async-start(s8[16777216]{0:T(1024)(128)(4,1)} %bitcast.5), calls=%async_computation.1 | async-start | bytes 8388608
  16.7 8.7 %collective-permute-start.7 = (bf16[528,128]{1,0:T(8,128)(2,1)S(1)}, bf16[528,128]{1,0:T(8,128)(2,1)S(1)}, u32[]{:S(2)}, u32[]{:S(2)}) collective-permute-start(bf16[528,128]{1,0:T(8,128)(2,1)S(1)} %attend.5), channel_id=1, source_target_pairs={{0,3},{1,2},{2,1},{3,0},{4,7},{5,6},{6,5},{7,4},{8,11},{9,10},{10,... | collective-permute-start | bytes 405512 | tf_op jit(solution)/shard_map/ppermute | solution.py:25
  19.9 19.3 %slice-start.2 = ((s8[16777216]{0:T(1024)(128)(4,1)}), s8[4194304]{0:T(1024)(128)(4,1)S(1)}, s32[]{:S(2)}) async-start(s8[16777216]{0:T(1024)(128)(4,1)} %bitcast.5), calls=%async_computation.2 | async-start | bytes 8388608
  19.9 5.6 %collective-permute-start.8 = (bf16[528,128]{1,0:T(8,128)(2,1)S(1)}, bf16[528,128]{1,0:T(8,128)(2,1)S(1)}, u32[]{:S(2)}, u32[]{:S(2)}) collective-permute-start(bf16[528,128]{1,0:T(8,128)(2,1)S(1)} %attend.6), channel_id=1, source_target_pairs={{0,2},{1,3},{2,0},{3,1},{4,6},{5,7},{6,4},{7,5},{8,10},{9,11},{10,... | collective-permute-start | bytes 405512 | tf_op jit(solution)/shard_map/ppermute | solution.py:25
  22.8 16.4 %slice-start.3 = ((s8[16777216]{0:T(1024)(128)(4,1)}), s8[4194304]{0:T(1024)(128)(4,1)S(1)}, s32[]{:S(2)}) async-start(s8[16777216]{0:T(1024)(128)(4,1)} %bitcast.5), calls=%async_computation.3 | async-start | bytes 8388608
  22.8 5.1 %collective-permute-start.9 = (bf16[528,128]{1,0:T(8,128)(2,1)S(1)}, bf16[528,128]{1,0:T(8,128)(2,1)S(1)}, u32[]{:S(2)}, u32[]{:S(2)}) collective-permute-start(bf16[528,128]{1,0:T(8,128)(2,1)S(1)} %attend.7), channel_id=1, source_target_pairs={{0,1},{1,0},{2,3},{3,2},{4,5},{5,4},{6,7},{7,6},{8,9},{9,8},{10,11... | collective-permute-start | bytes 405512 | tf_op jit(solution)/shard_map/ppermute | solution.py:25
  28.2 6.9 %collective-permute-start.10 = (bf16[528,128]{1,0:T(8,128)(2,1)S(1)}, bf16[528,128]{1,0:T(8,128)(2,1)S(1)}, u32[]{:S(2)}, u32[]{:S(2)}) collective-permute-start(bf16[528,128]{1,0:T(8,128)(2,1)S(1)} %get-tuple-element.20.own_ref), channel_id=1, source_target_pairs={{0,6},{1,7},{2,4},{3,5},{4,2},{5,3},{6,0},{7,1},{8,14},{9,15},{10,... | collective-permute-start | bytes 405512 | tf_op jit(solution)/shard_map/ppermute | solution.py:25
  35.6 5.0 %collective-permute-start.13 = (bf16[32,2048]{1,0:T(8,128)(2,1)S(1)}, bf16[32,2048]{1,0:T(8,128)(2,1)S(1)}, u32[]{:S(2)}, u32[]{:S(2)}) collective-permute-start(bf16[32,2048]{1,0:T(8,128)(2,1)S(1)} %settle.1.refs_0_), channel_id=1, source_target_pairs={{0,1},{1,0},{2,3},{3,2},{4,5},{5,4},{6,7},{7,6},{8,9},{9,8},{10,11... | collective-permute-start | bytes 393224 | tf_op jit(solution)/shard_map/ppermute | solution.py:25
  37.1 5.0 %collective-permute-start.12 = (bf16[32,2048]{1,0:T(8,128)(2,1)S(1)}, bf16[32,2048]{1,0:T(8,128)(2,1)S(1)}, u32[]{:S(2)}, u32[]{:S(2)}) collective-permute-start(bf16[32,2048]{1,0:T(8,128)(2,1)S(1)} %settle.1.refs_0_), channel_id=1, source_target_pairs={{0,2},{1,3},{2,0},{3,1},{4,6},{5,7},{6,4},{7,5},{8,10},{9,11},{10,... | collective-permute-start | bytes 393224 | tf_op jit(solution)/shard_map/ppermute | solution.py:25
  37.8 5.9 %collective-permute-start.11 = (bf16[32,2048]{1,0:T(8,128)(2,1)S(1)}, bf16[32,2048]{1,0:T(8,128)(2,1)S(1)}, u32[]{:S(2)}, u32[]{:S(2)}) collective-permute-start(bf16[32,2048]{1,0:T(8,128)(2,1)S(1)} %settle.1.refs_0_), channel_id=1, source_target_pairs={{0,3},{1,2},{2,1},{3,0},{4,7},{5,6},{6,5},{7,4},{8,11},{9,10},{10,... | collective-permute-start | bytes 393224 | tf_op jit(solution)/shard_map/ppermute | solution.py:25
  44.5 3.7 %collective-permute-start.14 = (bf16[32,1024]{1,0:T(8,128)(2,1)S(1)}, bf16[32,1024]{1,0:T(8,128)(2,1)S(1)}, u32[]{:S(2)}, u32[]{:S(2)}) collective-permute-start(bf16[32,1024]{1,0:T(8,128)(2,1)S(1)} %project.7), channel_id=1, source_target_pairs={{0,8},{8,16},{16,24},{24,0},{1,9},{9,17},{17,25},{25,1},{2,10},{10... | collective-permute-start | bytes 196616 | tf_op jit(solution)/shard_map/ppermute | solution.py:30

commit v12 on v11

--- a/solution.py
+++ b/solution.py
@@ -34,8 +34,7 @@
     def __init__(self, ctx, rows_here):
         self.ctx = ctx
         self.half = ctx // 2
-        self.fold = self.half // 2
-        self.across = self.half | self.fold
+        self.across = self.half
         self.rows_here = rows_here
         self.rows = ctx * rows_here
         self.group_rows = GROUP * self.rows
@@ -49,7 +48,7 @@
 
     def share(self, part):
         me = lax.axis_index("ctx")
-        return (me % self.half) ^ (me // self.half * self.fold) ^ part
+        return (me % self.half) ^ part
 
 
 def stat_rows(blocks):

time: 49.1 us -> 49.4 us (level)
  waiting for transfers between devices: 12.8 us -> 14.7 us
  starting transfers between devices: 22.2 us -> 20.8 us
    ppermute x14, waiting for transfers between devices: 9.14 us -> 11 us  [swap(): return lax.ppermute(value, axis, [(i, i ^ bits) for i in range(devices)])]
    ppermute x14, starting transfers between devices: 22.2 us -> 20.8 us  [swap(): return lax.ppermute(value, axis, [(i, i ^ bits) for i in range(devices)])]
where the time goes in v12:
time: 49.4 us; the launch traced here: 49.2 us
  starting transfers between devices  20.8 us (42%)
  waiting for transfers between devices  14.7 us (30%)
  Pallas kernels  11.6 us (23%)
  between operations  1.47 us (3%)
  local copies, waits for them, and re-layouts  0.67 us (1%)
    ppermute x14, starting transfers between devices, swap(): return lax.ppermute(value, axis, [(i, i ^ bits) for i in range(devices)])  20.8 us
    ppermute x14, waiting for transfers between devices, swap(): return lax.ppermute(value, axis, [(i, i ^ bits) for i in range(devices)])  11 us
    pallas_call x4, Pallas kernels, attend(): local(functools.partial(attend_kernel, plan, part), out_shape, [pltpu.VME...  6.72 us
    ppermute x1, waiting for transfers between devices, from_behind(): lax.ppermute(value, axis, [(i, (i + by) % devices) for i in range(devices)])  3.69 us
    pallas_call x4, Pallas kernels, project(): local(functools.partial(project_kernel, plan, part), jax.ShapeDtypeStruct...  3.29 us
  transfers between devices with their start and end apart: 15, of which 8 were waited for; matrix products, arithmetic and copies ran while one was open for 0% of the time, Pallas kernels for 17%

profile of v12, /device:TPU:0, one launch (start us, length us, event | category | flops | bytes accessed | tf_op | source)
XLA Modules:
  0.0 49.2 jit_solution(13259629279590286110)
XLA Ops:
  0.0 4.1 %collective-permute-start = (bf16[8,32,128]{2,1,0:T(8,128)(2,1)}, bf16[8,32,128]{2,1,0:T(8,128)(2,1)S(1)}, u32[]{:S(2)}, u32[]{:S(2)}) collective-permute-start(bf16[8,32,128]{2,1,0:T(8,128)(2,1)} %bitcast.9), channel_id=1, source_target_pairs={{0,4},{1,5},{2,6},{3,7},{4,0},{5,1},{6,2},{7,3},{8,12},{9,13},{10,... | collective-permute-start | bytes 196616 | tf_op jit(solution)/shard_map/ppermute | solution.py:25
  4.1 2.5 %collective-permute-start.5 = (bf16[8,32,128]{2,1,0:T(8,128)(2,1)}, bf16[8,32,128]{2,1,0:T(8,128)(2,1)S(1)}, u32[]{:S(2)}, u32[]{:S(2)}) collective-permute-start(bf16[8,32,128]{2,1,0:T(8,128)(2,1)} %bitcast.10), channel_id=1, source_target_pairs={{0,3},{1,2},{2,1},{3,0},{4,7},{5,6},{6,5},{7,4},{8,11},{9,10},{10,... | collective-permute-start | bytes 196616 | tf_op jit(solution)/shard_map/ppermute | solution.py:25
  6.6 0.4 collective-permute-start.3
  7.1 0.5 %collective-permute-start.1 = (bf16[8,32,128]{2,1,0:T(8,128)(2,1)}, bf16[8,32,128]{2,1,0:T(8,128)(2,1)S(1)}, u32[]{:S(2)}, u32[]{:S(2)}) collective-permute-start(bf16[8,32,128]{2,1,0:T(8,128)(2,1)} %bitcast.12), channel_id=1, source_target_pairs={{0,1},{1,0},{2,3},{3,2},{4,5},{5,4},{6,7},{7,6},{8,9},{9,8},{10,11... | collective-permute-start | bytes 196616 | tf_op jit(solution)/shard_map/ppermute | solution.py:25
  7.6 0.0 collective-permute-done.refs_1_
  7.6 2.5 %collective-permute-start.6 = (bf16[8,32,128]{2,1,0:T(8,128)(2,1)S(1)}, bf16[8,32,128]{2,1,0:T(8,128)(2,1)S(1)}, u32[]{:S(2)}, u32[]{:S(2)}) collective-permute-start(bf16[8,32,128]{2,1,0:T(8,128)(2,1)S(1)} %collective-permute-done.refs_1_), channel_id=1, source_target_pairs={{0,3},{1,2},{2,1},{3,0},{4,7},{5,6},{6,5},{7,4},{8,11},{9,10},{10,... | collective-permute-start | bytes 196616 | tf_op jit(solution)/shard_map/ppermute | solution.py:25
  10.1 0.6 %collective-permute-start.4 = (bf16[8,32,128]{2,1,0:T(8,128)(2,1)S(1)}, bf16[8,32,128]{2,1,0:T(8,128)(2,1)S(1)}, u32[]{:S(2)}, u32[]{:S(2)}) collective-permute-start(bf16[8,32,128]{2,1,0:T(8,128)(2,1)S(1)} %collective-permute-done.refs_1_), channel_id=1, source_target_pairs={{0,2},{1,3},{2,0},{3,1},{4,6},{5,7},{6,4},{7,5},{8,10},{9,11},{10,... | collective-permute-start | bytes 196616 | tf_op jit(solution)/shard_map/ppermute | solution.py:25
  10.7 0.0 collective-permute-done.5.after_ref.refs_6_
  10.7 1.1 %collective-permute-start.2 = (bf16[8,32,128]{2,1,0:T(8,128)(2,1)S(1)}, bf16[8,32,128]{2,1,0:T(8,128)(2,1)S(1)}, u32[]{:S(2)}, u32[]{:S(2)}) collective-permute-start(bf16[8,32,128]{2,1,0:T(8,128)(2,1)S(1)} %collective-permute-done.refs_1_), channel_id=1, source_target_pairs={{0,1},{1,0},{2,3},{3,2},{4,5},{5,4},{6,7},{7,6},{8,9},{9,8},{10,11... | collective-permute-start | bytes 196616 | tf_op jit(solution)/shard_map/ppermute | solution.py:25
  11.8 0.1 order.1
  13.2 0.2 mask.1.refs_9_
  13.4 0.0 collective-permute-done.3.refs_4_
  13.4 0.0 collective-permute-done.1.refs_2_
  13.4 0.0 collective-permute-done.6.refs_7_
  13.4 0.9 %collective-permute-done.4.refs_5_ = bf16[8,32,128]{2,1,0:T(8,128)(2,1)S(1)} collective-permute-done((bf16[8,32,128]{2,1,0:T(8,128)(2,1)S(1)}, bf16[8,32,128]{2,1,0:T(8,128)(2,1)S(1)}, u32[]{:S(2)}, u32[]{:S(2)}) %collective-permute-start.4) | collective-permute-done | bytes 65568 | tf_op jit(solution)/shard_map/ppermute | solution.py:25
  14.4 0.6 %collective-permute-done.2.refs_3_ = bf16[8,32,128]{2,1,0:T(8,128)(2,1)S(1)} collective-permute-done((bf16[8,32,128]{2,1,0:T(8,128)(2,1)S(1)}, bf16[8,32,128]{2,1,0:T(8,128)(2,1)S(1)}, u32[]{:S(2)}, u32[]{:S(2)}) %collective-permute-start.2) | collective-permute-done | bytes 65568 | tf_op jit(solution)/shard_map/ppermute | solution.py:25
  15.0 1.7 %attend.5 = bf16[528,128]{1,0:T(8,128)(2,1)S(1)} custom-call(bf16[8,32,128]{2,1,0:T(8,128)(2,1)S(1)} %bitcast.13, bf16[8,32,128]{2,1,0:T(8,128)(2,1)S(1)} %collective-permute-done.refs_1_, bf16[8,32,128]{2,1,0:T(8,128)(2,1)S(1)} %collective-permute-done.1.refs_2_, bf16[8,32,128]{2,1,0:T(8,128)(2,1)S(1)} %collective-permute-done.2.refs_3_, ...), custom_call_target="tpu_custom_call" | custom-call | flops 536870912 | bytes 2097152 | tf_op jit(solution)/shard_map/attend/pallas_call | solution.py:202
  16.7 0.0 slice-start
  16.7 0.0 slice-start.1
  16.7 1.4 %collective-permute-start.7 = (bf16[528,128]{1,0:T(8,128)(2,1)S(1)}, bf16[528,128]{1,0:T(8,128)(2,1)S(1)}, u32[]{:S(2)}, u32[]{:S(2)}) collective-permute-start(bf16[528,128]{1,0:T(8,128)(2,1)S(1)} %attend.5), channel_id=1, source_target_pairs={{0,3},{1,2},{2,1},{3,0},{4,7},{5,6},{6,5},{7,4},{8,11},{9,10},{10,... | collective-permute-start | bytes 405512 | tf_op jit(solution)/shard_map/ppermute | solution.py:25
  18.1 1.7 %attend.6 = bf16[528,128]{1,0:T(8,128)(2,1)S(1)} custom-call(bf16[8,32,128]{2,1,0:T(8,128)(2,1)S(1)} %bitcast.14, bf16[8,32,128]{2,1,0:T(8,128)(2,1)S(1)} %collective-permute-done.refs_1_, bf16[8,32,128]{2,1,0:T(8,128)(2,1)S(1)} %collective-permute-done.1.refs_2_, bf16[8,32,128]{2,1,0:T(8,128)(2,1)S(1)} %collective-permute-done.2.refs_3_, ...), custom_call_target="tpu_custom_call" | custom-call | flops 536870912 | bytes 2097152 | tf_op jit(solution)/shard_map/attend/pallas_call | solution.py:202
  19.8 0.0 slice-start.2
  19.9 1.2 %collective-permute-start.8 = (bf16[528,128]{1,0:T(8,128)(2,1)S(1)}, bf16[528,128]{1,0:T(8,128)(2,1)S(1)}, u32[]{:S(2)}, u32[]{:S(2)}) collective-permute-start(bf16[528,128]{1,0:T(8,128)(2,1)S(1)} %attend.6), channel_id=1, source_target_pairs={{0,2},{1,3},{2,0},{3,1},{4,6},{5,7},{6,4},{7,5},{8,10},{9,11},{10,... | collective-permute-start | bytes 405512 | tf_op jit(solution)/shard_map/ppermute | solution.py:25
  21.1 1.7 %attend.7 = bf16[528,128]{1,0:T(8,128)(2,1)S(1)} custom-call(bf16[8,32,128]{2,1,0:T(8,128)(2,1)S(1)} %bitcast.15, bf16[8,32,128]{2,1,0:T(8,128)(2,1)S(1)} %collective-permute-done.refs_1_, bf16[8,32,128]{2,1,0:T(8,128)(2,1)S(1)} %collective-permute-done.1.refs_2_, bf16[8,32,128]{2,1,0:T(8,128)(2,1)S(1)} %collective-permute-done.2.refs_3_, ...), custom_call_target="tpu_custom_call" | custom-call | flops 536870912 | bytes 2097152 | tf_op jit(solution)/shard_map/attend/pallas_call | solution.py:202
  22.8 0.0 slice-start.3
  22.8 1.0 %collective-permute-start.9 = (bf16[528,128]{1,0:T(8,128)(2,1)S(1)}, bf16[528,128]{1,0:T(8,128)(2,1)S(1)}, u32[]{:S(2)}, u32[]{:S(2)}) collective-permute-start(bf16[528,128]{1,0:T(8,128)(2,1)S(1)} %attend.7), channel_id=1, source_target_pairs={{0,1},{1,0},{2,3},{3,2},{4,5},{5,4},{6,7},{7,6},{8,9},{9,8},{10,11... | collective-permute-start | bytes 405512 | tf_op jit(solution)/shard_map/ppermute | solution.py:25
  23.8 1.6 %attend.4 = (f32[512,128]{1,0:T(8,128)S(1)}, bf16[16,128]{1,0:T(8,128)(2,1)S(1)}) custom-call(bf16[8,32,128]{2,1,0:T(8,128)(2,1)S(1)} %bitcast.16, bf16[8,32,128]{2,1,0:T(8,128)(2,1)S(1)} %collective-permute-done.refs_1_, bf16[8,32,128]{2,1,0:T(8,128)(2,1)S(1)} %collective-permute-done.1.refs_2_, bf16[8,32,128]{2,1,0:T(8,128)(2,1)S(1)} %collective-permute-done.2.refs_3_, ...), custom_call_target="tpu_custom_call" | custom-call | flops 536870912 | bytes 2097152 | tf_op jit(solution)/shard_map/attend/pallas_call | solution.py:202
  25.4 0.0 collective-permute-done.7.refs_0_
  25.4 0.0 collective-permute-done.8.refs_1_
  25.4 0.4 merge.2
  25.8 2.0 %collective-permute-done.9.refs_0_ = bf16[528,128]{1,0:T(8,128)(2,1)S(1)} collective-permute-done((bf16[528,128]{1,0:T(8,128)(2,1)S(1)}, bf16[528,128]{1,0:T(8,128)(2,1)S(1)}, u32[]{:S(2)}, u32[]{:S(2)}) %collective-permute-start.9) | collective-permute-done | bytes 135200 | tf_op jit(solution)/shard_map/ppermute | solution.py:25
  27.8 0.3 merge.3
  28.2 1.8 %collective-permute-start.10 = (bf16[528,128]{1,0:T(8,128)(2,1)S(1)}, bf16[528,128]{1,0:T(8,128)(2,1)S(1)}, u32[]{:S(2)}, u32[]{:S(2)}) collective-permute-start(bf16[528,128]{1,0:T(8,128)(2,1)S(1)} %get-tuple-element.20.own_ref), channel_id=1, source_target_pairs={{0,4},{1,5},{2,6},{3,7},{4,0},{5,1},{6,2},{7,3},{8,12},{9,13},{10,... | collective-permute-start | bytes 405512 | tf_op jit(solution)/shard_map/ppermute | solution.py:25
  30.0 5.6 %collective-permute-done.10.other_ref = bf16[528,128]{1,0:T(8,128)(2,1)S(1)} collective-permute-done((bf16[528,128]{1,0:T(8,128)(2,1)S(1)}, bf16[528,128]{1,0:T(8,128)(2,1)S(1)}, u32[]{:S(2)}, u32[]{:S(2)}) %collective-permute-start.10) | collective-permute-done | bytes 135200 | tf_op jit(solution)/shard_map/ppermute | solution.py:25
  35.6 0.6 %settle.1.refs_0_ = bf16[32,2048]{1,0:T(8,128)(2,1)S(1)} custom-call(f32[512,128]{1,0:T(8,128)S(1)} %get-tuple-element.19.wide_ref, bf16[528,128]{1,0:T(8,128)(2,1)S(1)} %get-tuple-element.20.own_ref, bf16[528,128]{1,0:T(8,128)(2,1)S(1)} %collective-permute-done.10.other_ref, bf16[256,256]{1,0:T(8,128)(2,1)S(1)} %get-tuple-element.13.refs_10_.order_ref), custom_call_target="tpu_custom_call" | custom-call | tf_op jit(solution)/shard_map/settle/pallas_call | solution.py:301
  36.2 1.0 %collective-permute-start.13 = (bf16[32,2048]{1,0:T(8,128)(2,1)S(1)}, bf16[32,2048]{1,0:T(8,128)(2,1)S(1)}, u32[]{:S(2)}, u32[]{:S(2)}) collective-permute-start(bf16[32,2048]{1,0:T(8,128)(2,1)S(1)} %settle.1.refs_0_), channel_id=1, source_target_pairs={{0,1},{1,0},{2,3},{3,2},{4,5},{5,4},{6,7},{7,6},{8,9},{9,8},{10,11... | collective-permute-start | bytes 393224 | tf_op jit(solution)/shard_map/ppermute | solution.py:25
  37.2 0.4 collective-permute-start.12
  37.6 2.2 %collective-permute-start.11 = (bf16[32,2048]{1,0:T(8,128)(2,1)S(1)}, bf16[32,2048]{1,0:T(8,128)(2,1)S(1)}, u32[]{:S(2)}, u32[]{:S(2)}) collective-permute-start(bf16[32,2048]{1,0:T(8,128)(2,1)S(1)} %settle.1.refs_0_), channel_id=1, source_target_pairs={{0,3},{1,2},{2,1},{3,0},{4,7},{5,6},{6,5},{7,4},{8,11},{9,10},{10,... | collective-permute-start | bytes 393224 | tf_op jit(solution)/shard_map/ppermute | solution.py:25
  39.8 0.8 %project.4.refs_2_ = f32[32,1024]{1,0:T(8,128)S(1)} custom-call(bf16[32,2048]{1,0:T(8,128)(2,1)S(1)} %settle.1.refs_0_, bf16[8192,1024]{1,0:T(8,128)(2,1)S(1)} %bitcast.6), custom_call_target="tpu_custom_call" | custom-call | tf_op jit(solution)/shard_map/project/pallas_call | solution.py:321
  40.6 0.6 %collective-permute-done.13.refs_0_ = bf16[32,2048]{1,0:T(8,128)(2,1)S(1)} collective-permute-done((bf16[32,2048]{1,0:T(8,128)(2,1)S(1)}, bf16[32,2048]{1,0:T(8,128)(2,1)S(1)}, u32[]{:S(2)}, u32[]{:S(2)}) %collective-permute-start.13) | collective-permute-done | bytes 131104 | tf_op jit(solution)/shard_map/ppermute | solution.py:25
  41.2 0.8 %project.5.refs_2_ = f32[32,1024]{1,0:T(8,128)S(1)} custom-call(bf16[32,2048]{1,0:T(8,128)(2,1)S(1)} %collective-permute-done.13.refs_0_, bf16[8192,1024]{1,0:T(8,128)(2,1)S(1)} %bitcast.6, f32[32,1024]{1,0:T(8,128)S(1)} %project.4.refs_2_), custom_call_target="tpu_custom_call" | custom-call | tf_op jit(solution)/shard_map/project/pallas_call | solution.py:321
  42.0 0.1 collective-permute-done.12.refs_0_
  42.2 0.8 %project.6.refs_2_ = f32[32,1024]{1,0:T(8,128)S(1)} custom-call(bf16[32,2048]{1,0:T(8,128)(2,1)S(1)} %collective-permute-done.12.refs_0_, bf16[8192,1024]{1,0:T(8,128)(2,1)S(1)} %bitcast.6, f32[32,1024]{1,0:T(8,128)S(1)} %project.5.refs_2_), custom_call_target="tpu_custom_call" | custom-call | tf_op jit(solution)/shard_map/project/pallas_call | solution.py:321
  43.0 1.1 %collective-permute-done.11.refs_0_ = bf16[32,2048]{1,0:T(8,128)(2,1)S(1)} collective-permute-done((bf16[32,2048]{1,0:T(8,128)(2,1)S(1)}, bf16[32,2048]{1,0:T(8,128)(2,1)S(1)}, u32[]{:S(2)}, u32[]{:S(2)}) %collective-permute-start.11) | collective-permute-done | bytes 131104 | tf_op jit(solution)/shard_map/ppermute | solution.py:25
  44.1 0.8 %project.7 = bf16[32,1024]{1,0:T(8,128)(2,1)S(1)} custom-call(bf16[32,2048]{1,0:T(8,128)(2,1)S(1)} %collective-permute-done.11.refs_0_, bf16[8192,1024]{1,0:T(8,128)(2,1)S(1)} %bitcast.6, f32[32,1024]{1,0:T(8,128)S(1)} %project.6.refs_2_), custom_call_target="tpu_custom_call" | custom-call | tf_op jit(solution)/shard_map/project/pallas_call | solution.py:321
  44.9 0.0 collective-permute-start.14
  44.9 3.7 %collective-permute-done.14 = bf16[32,1024]{1,0:T(8,128)(2,1)S(1)} collective-permute-done((bf16[32,1024]{1,0:T(8,128)(2,1)S(1)}, bf16[32,1024]{1,0:T(8,128)(2,1)S(1)}, u32[]{:S(2)}, u32[]{:S(2)}) %collective-permute-start.14) | collective-permute-done | bytes 65568 | tf_op jit(solution)/shard_map/ppermute | solution.py:30
  48.6 0.6 %copy.10 = bf16[32,1024]{1,0:T(8,128)(2,1)} copy(bf16[32,1024]{1,0:T(8,128)(2,1)S(1)} %collective-permute-done.14) | data formatting | bytes 131072
  (12 shorter events, 0.0 us)
Async XLA Ops:
  0.0 15.0 %copy-start = (bf16[4,8192]{1,0:T(4,128)(2,1)S(1)}, bf16[4,8192]{1,0:T(4,128)(2,1)}, u32[]{:S(2)}) copy-start(bf16[4,8192]{1,0:T(4,128)(2,1)} %param.5) | copy-start | bytes 196612
  0.0 15.0 %slice-start.4 = ((s8[8388608]{0:T(1024)(128)(4,1)}), s8[4194304]{0:T(1024)(128)(4,1)S(1)}, s32[]{:S(2)}) async-start(s8[8388608]{0:T(1024)(128)(4,1)} %bitcast.7), calls=%async_computation.4 | async-start | bytes 8388608
  0.0 15.0 %slice-start.5 = ((s8[8388608]{0:T(1024)(128)(4,1)}), s8[4194304]{0:T(1024)(128)(4,1)S(1)}, s32[]{:S(2)}) async-start(s8[8388608]{0:T(1024)(128)(4,1)} %bitcast.7), calls=%async_computation.5 | async-start | bytes 8388608
  0.0 7.6 %collective-permute-start = (bf16[8,32,128]{2,1,0:T(8,128)(2,1)}, bf16[8,32,128]{2,1,0:T(8,128)(2,1)S(1)}, u32[]{:S(2)}, u32[]{:S(2)}) collective-permute-start(bf16[8,32,128]{2,1,0:T(8,128)(2,1)} %bitcast.9), channel_id=1, source_target_pairs={{0,4},{1,5},{2,6},{3,7},{4,0},{5,1},{6,2},{7,3},{8,12},{9,13},{10,... | collective-permute-start | bytes 196616 | tf_op jit(solution)/shard_map/ppermute | solution.py:25
  4.1 6.6 %collective-permute-start.5 = (bf16[8,32,128]{2,1,0:T(8,128)(2,1)}, bf16[8,32,128]{2,1,0:T(8,128)(2,1)S(1)}, u32[]{:S(2)}, u32[]{:S(2)}) collective-permute-start(bf16[8,32,128]{2,1,0:T(8,128)(2,1)} %bitcast.10), channel_id=1, source_target_pairs={{0,3},{1,2},{2,1},{3,0},{4,7},{5,6},{6,5},{7,4},{8,11},{9,10},{10,... | collective-permute-start | bytes 196616 | tf_op jit(solution)/shard_map/ppermute | solution.py:25
  6.6 6.8 %collective-permute-start.3 = (bf16[8,32,128]{2,1,0:T(8,128)(2,1)}, bf16[8,32,128]{2,1,0:T(8,128)(2,1)S(1)}, u32[]{:S(2)}, u32[]{:S(2)}) collective-permute-start(bf16[8,32,128]{2,1,0:T(8,128)(2,1)} %bitcast.11), channel_id=1, source_target_pairs={{0,2},{1,3},{2,0},{3,1},{4,6},{5,7},{6,4},{7,5},{8,10},{9,11},{10,... | collective-permute-start | bytes 196616 | tf_op jit(solution)/shard_map/ppermute | solution.py:25
  7.1 6.4 %collective-permute-start.1 = (bf16[8,32,128]{2,1,0:T(8,128)(2,1)}, bf16[8,32,128]{2,1,0:T(8,128)(2,1)S(1)}, u32[]{:S(2)}, u32[]{:S(2)}) collective-permute-start(bf16[8,32,128]{2,1,0:T(8,128)(2,1)} %bitcast.12), channel_id=1, source_target_pairs={{0,1},{1,0},{2,3},{3,2},{4,5},{5,4},{6,7},{7,6},{8,9},{9,8},{10,11... | collective-permute-start | bytes 196616 | tf_op jit(solution)/shard_map/ppermute | solution.py:25
  7.6 5.8 %collective-permute-start.6 = (bf16[8,32,128]{2,1,0:T(8,128)(2,1)S(1)}, bf16[8,32,128]{2,1,0:T(8,128)(2,1)S(1)}, u32[]{:S(2)}, u32[]{:S(2)}) collective-permute-start(bf16[8,32,128]{2,1,0:T(8,128)(2,1)S(1)} %collective-permute-done.refs_1_), channel_id=1, source_target_pairs={{0,3},{1,2},{2,1},{3,0},{4,7},{5,6},{6,5},{7,4},{8,11},{9,10},{10,... | collective-permute-start | bytes 196616 | tf_op jit(solution)/shard_map/ppermute | solution.py:25
  10.1 4.3 %collective-permute-start.4 = (bf16[8,32,128]{2,1,0:T(8,128)(2,1)S(1)}, bf16[8,32,128]{2,1,0:T(8,128)(2,1)S(1)}, u32[]{:S(2)}, u32[]{:S(2)}) collective-permute-start(bf16[8,32,128]{2,1,0:T(8,128)(2,1)S(1)} %collective-permute-done.refs_1_), channel_id=1, source_target_pairs={{0,2},{1,3},{2,0},{3,1},{4,6},{5,7},{6,4},{7,5},{8,10},{9,11},{10,... | collective-permute-start | bytes 196616 | tf_op jit(solution)/shard_map/ppermute | solution.py:25
  10.7 4.3 %collective-permute-start.2 = (bf16[8,32,128]{2,1,0:T(8,128)(2,1)S(1)}, bf16[8,32,128]{2,1,0:T(8,128)(2,1)S(1)}, u32[]{:S(2)}, u32[]{:S(2)}) collective-permute-start(bf16[8,32,128]{2,1,0:T(8,128)(2,1)S(1)} %collective-permute-done.refs_1_), channel_id=1, source_target_pairs={{0,1},{1,0},{2,3},{3,2},{4,5},{5,4},{6,7},{7,6},{8,9},{9,8},{10,11... | collective-permute-start | bytes 196616 | tf_op jit(solution)/shard_map/ppermute | solution.py:25
  16.7 23.0 %slice-start = ((s8[16777216]{0:T(1024)(128)(4,1)}), s8[4194304]{0:T(1024)(128)(4,1)S(1)}, s32[]{:S(2)}) async-start(s8[16777216]{0:T(1024)(128)(4,1)} %bitcast.5), calls=%async_computation | async-start | bytes 8388608
  16.7 23.0 %slice-start.1 = ((s8[16777216]{0:T(1024)(128)(4,1)}), s8[4194304]{0:T(1024)(128)(4,1)S(1)}, s32[]{:S(2)}) async-start(s8[16777216]{0:T(1024)(128)(4,1)} %bitcast.5), calls=%async_computation.1 | async-start | bytes 8388608
  16.7 8.7 %collective-permute-start.7 = (bf16[528,128]{1,0:T(8,128)(2,1)S(1)}, bf16[528,128]{1,0:T(8,128)(2,1)S(1)}, u32[]{:S(2)}, u32[]{:S(2)}) collective-permute-start(bf16[528,128]{1,0:T(8,128)(2,1)S(1)} %attend.5), channel_id=1, source_target_pairs={{0,3},{1,2},{2,1},{3,0},{4,7},{5,6},{6,5},{7,4},{8,11},{9,10},{10,... | collective-permute-start | bytes 405512 | tf_op jit(solution)/shard_map/ppermute | solution.py:25
  19.8 19.9 %slice-start.2 = ((s8[16777216]{0:T(1024)(128)(4,1)}), s8[4194304]{0:T(1024)(128)(4,1)S(1)}, s32[]{:S(2)}) async-start(s8[16777216]{0:T(1024)(128)(4,1)} %bitcast.5), calls=%async_computation.2 | async-start | bytes 8388608
  19.9 5.6 %collective-permute-start.8 = (bf16[528,128]{1,0:T(8,128)(2,1)S(1)}, bf16[528,128]{1,0:T(8,128)(2,1)S(1)}, u32[]{:S(2)}, u32[]{:S(2)}) collective-permute-start(bf16[528,128]{1,0:T(8,128)(2,1)S(1)} %attend.6), channel_id=1, source_target_pairs={{0,2},{1,3},{2,0},{3,1},{4,6},{5,7},{6,4},{7,5},{8,10},{9,11},{10,... | collective-permute-start | bytes 405512 | tf_op jit(solution)/shard_map/ppermute | solution.py:25
  22.8 17.0 %slice-start.3 = ((s8[16777216]{0:T(1024)(128)(4,1)}), s8[4194304]{0:T(1024)(128)(4,1)S(1)}, s32[]{:S(2)}) async-start(s8[16777216]{0:T(1024)(128)(4,1)} %bitcast.5), calls=%async_computation.3 | async-start | bytes 8388608
  22.8 5.1 %collective-permute-start.9 = (bf16[528,128]{1,0:T(8,128)(2,1)S(1)}, bf16[528,128]{1,0:T(8,128)(2,1)S(1)}, u32[]{:S(2)}, u32[]{:S(2)}) collective-permute-start(bf16[528,128]{1,0:T(8,128)(2,1)S(1)} %attend.7), channel_id=1, source_target_pairs={{0,1},{1,0},{2,3},{3,2},{4,5},{5,4},{6,7},{7,6},{8,9},{9,8},{10,11... | collective-permute-start | bytes 405512 | tf_op jit(solution)/shard_map/ppermute | solution.py:25
  28.2 7.4 %collective-permute-start.10 = (bf16[528,128]{1,0:T(8,128)(2,1)S(1)}, bf16[528,128]{1,0:T(8,128)(2,1)S(1)}, u32[]{:S(2)}, u32[]{:S(2)}) collective-permute-start(bf16[528,128]{1,0:T(8,128)(2,1)S(1)} %get-tuple-element.20.own_ref), channel_id=1, source_target_pairs={{0,4},{1,5},{2,6},{3,7},{4,0},{5,1},{6,2},{7,3},{8,12},{9,13},{10,... | collective-permute-start | bytes 405512 | tf_op jit(solution)/shard_map/ppermute | solution.py:25
  36.2 5.0 %collective-permute-start.13 = (bf16[32,2048]{1,0:T(8,128)(2,1)S(1)}, bf16[32,2048]{1,0:T(8,128)(2,1)S(1)}, u32[]{:S(2)}, u32[]{:S(2)}) collective-permute-start(bf16[32,2048]{1,0:T(8,128)(2,1)S(1)} %settle.1.refs_0_), channel_id=1, source_target_pairs={{0,1},{1,0},{2,3},{3,2},{4,5},{5,4},{6,7},{7,6},{8,9},{9,8},{10,11... | collective-permute-start | bytes 393224 | tf_op jit(solution)/shard_map/ppermute | solution.py:25
  37.2 5.0 %collective-permute-start.12 = (bf16[32,2048]{1,0:T(8,128)(2,1)S(1)}, bf16[32,2048]{1,0:T(8,128)(2,1)S(1)}, u32[]{:S(2)}, u32[]{:S(2)}) collective-permute-start(bf16[32,2048]{1,0:T(8,128)(2,1)S(1)} %settle.1.refs_0_), channel_id=1, source_target_pairs={{0,2},{1,3},{2,0},{3,1},{4,6},{5,7},{6,4},{7,5},{8,10},{9,11},{10,... | collective-permute-start | bytes 393224 | tf_op jit(solution)/shard_map/ppermute | solution.py:25
  37.6 6.5 %collective-permute-start.11 = (bf16[32,2048]{1,0:T(8,128)(2,1)S(1)}, bf16[32,2048]{1,0:T(8,128)(2,1)S(1)}, u32[]{:S(2)}, u32[]{:S(2)}) collective-permute-start(bf16[32,2048]{1,0:T(8,128)(2,1)S(1)} %settle.1.refs_0_), channel_id=1, source_target_pairs={{0,3},{1,2},{2,1},{3,0},{4,7},{5,6},{6,5},{7,4},{8,11},{9,10},{10,... | collective-permute-start | bytes 393224 | tf_op jit(solution)/shard_map/ppermute | solution.py:25
  44.9 3.7 %collective-permute-start.14 = (bf16[32,1024]{1,0:T(8,128)(2,1)S(1)}, bf16[32,1024]{1,0:T(8,128)(2,1)S(1)}, u32[]{:S(2)}, u32[]{:S(2)}) collective-permute-start(bf16[32,1024]{1,0:T(8,128)(2,1)S(1)} %project.7), channel_id=1, source_target_pairs={{0,8},{8,16},{16,24},{24,0},{1,9},{9,17},{17,25},{25,1},{2,10},{10... | collective-permute-start | bytes 196616 | tf_op jit(solution)/shard_map/ppermute | solution.py:30

commit v13 on v11

--- a/solution.py
+++ b/solution.py
@@ -358,10 +358,9 @@
     block = settle(plan, wide, near, swap(near, "ctx", plan.across), order)
 
     total = project(plan, 0, block, out_weight, None, jnp.float32)
-    blocks = [swap(block, "ctx", k) for k in range(1, half)]
-    for k in range(1, half):
-        dtype = jnp.float32 if k < half - 1 else jnp.bfloat16
-        total = project(plan, k, blocks[k - 1], out_weight, total, dtype)
+    for k in reversed(range(1, half)):
+        dtype = jnp.float32 if k > 1 else jnp.bfloat16
+        total = project(plan, k, swap(block, "ctx", k), out_weight, total, dtype)
     return from_behind(total, "segment", 1)
 
 

time: 49.1 us -> 49.3 us (level)
  transfers between devices with their start and end apart: 15 -> 15, of which waited for: 8 -> 7; matrix products, arithmetic and copies ran while one was open for 0% -> 0% of each run, Pallas kernels for 17% -> 17%
where the time goes in v13:
time: 49.3 us; the launch traced here: 49.1 us
  starting transfers between devices  22.2 us (45%)
  waiting for transfers between devices  13.1 us (27%)
  Pallas kernels  11.7 us (24%)
  between operations  1.48 us (3%)
  local copies, waits for them, and re-layouts  0.67 us (1%)
    ppermute x14, starting transfers between devices, swap(): return lax.ppermute(value, axis, [(i, i ^ bits) for i in range(devices)])  22.2 us
    ppermute x14, waiting for transfers between devices, swap(): return lax.ppermute(value, axis, [(i, i ^ bits) for i in range(devices)])  9.41 us
    pallas_call x4, Pallas kernels, attend(): local(functools.partial(attend_kernel, plan, part), out_shape, [pltpu.VME...  6.74 us
    ppermute x1, waiting for transfers between devices, from_behind(): lax.ppermute(value, axis, [(i, (i + by) % devices) for i in range(devices)])  3.69 us
    pallas_call x4, Pallas kernels, project(): local(functools.partial(project_kernel, plan, part), jax.ShapeDtypeStruct...  3.31 us
  transfers between devices with their start and end apart: 15, of which 7 were waited for; matrix products, arithmetic and copies ran while one was open for 0% of the time, Pallas kernels for 17%

profile of v13, /device:TPU:0, one launch (start us, length us, event | category | flops | bytes accessed | tf_op | source)
XLA Modules:
  0.0 49.1 jit_solution(6780608213167409832)
XLA Ops:
  0.0 4.1 %collective-permute-start = (bf16[8,32,128]{2,1,0:T(8,128)(2,1)}, bf16[8,32,128]{2,1,0:T(8,128)(2,1)S(1)}, u32[]{:S(2)}, u32[]{:S(2)}) collective-permute-start(bf16[8,32,128]{2,1,0:T(8,128)(2,1)} %bitcast.9), channel_id=1, source_target_pairs={{0,4},{1,5},{2,6},{3,7},{4,0},{5,1},{6,2},{7,3},{8,12},{9,13},{10,... | collective-permute-start | bytes 196616 | tf_op jit(solution)/shard_map/ppermute | solution.py:25
  4.1 2.5 %collective-permute-start.5 = (bf16[8,32,128]{2,1,0:T(8,128)(2,1)}, bf16[8,32,128]{2,1,0:T(8,128)(2,1)S(1)}, u32[]{:S(2)}, u32[]{:S(2)}) collective-permute-start(bf16[8,32,128]{2,1,0:T(8,128)(2,1)} %bitcast.10), channel_id=1, source_target_pairs={{0,3},{1,2},{2,1},{3,0},{4,7},{5,6},{6,5},{7,4},{8,11},{9,10},{10,... | collective-permute-start | bytes 196616 | tf_op jit(solution)/shard_map/ppermute | solution.py:25
  6.6 0.4 collective-permute-start.3
  7.1 0.5 %collective-permute-start.1 = (bf16[8,32,128]{2,1,0:T(8,128)(2,1)}, bf16[8,32,128]{2,1,0:T(8,128)(2,1)S(1)}, u32[]{:S(2)}, u32[]{:S(2)}) collective-permute-start(bf16[8,32,128]{2,1,0:T(8,128)(2,1)} %bitcast.12), channel_id=1, source_target_pairs={{0,1},{1,0},{2,3},{3,2},{4,5},{5,4},{6,7},{7,6},{8,9},{9,8},{10,11... | collective-permute-start | bytes 196616 | tf_op jit(solution)/shard_map/ppermute | solution.py:25
  7.6 0.0 collective-permute-done.refs_1_
  7.6 2.5 %collective-permute-start.6 = (bf16[8,32,128]{2,1,0:T(8,128)(2,1)S(1)}, bf16[8,32,128]{2,1,0:T(8,128)(2,1)S(1)}, u32[]{:S(2)}, u32[]{:S(2)}) collective-permute-start(bf16[8,32,128]{2,1,0:T(8,128)(2,1)S(1)} %collective-permute-done.refs_1_), channel_id=1, source_target_pairs={{0,3},{1,2},{2,1},{3,0},{4,7},{5,6},{6,5},{7,4},{8,11},{9,10},{10,... | collective-permute-start | bytes 196616 | tf_op jit(solution)/shard_map/ppermute | solution.py:25
  10.1 0.6 %collective-permute-start.4 = (bf16[8,32,128]{2,1,0:T(8,128)(2,1)S(1)}, bf16[8,32,128]{2,1,0:T(8,128)(2,1)S(1)}, u32[]{:S(2)}, u32[]{:S(2)}) collective-permute-start(bf16[8,32,128]{2,1,0:T(8,128)(2,1)S(1)} %collective-permute-done.refs_1_), channel_id=1, source_target_pairs={{0,2},{1,3},{2,0},{3,1},{4,6},{5,7},{6,4},{7,5},{8,10},{9,11},{10,... | collective-permute-start | bytes 196616 | tf_op jit(solution)/shard_map/ppermute | solution.py:25
  10.7 0.0 collective-permute-done.5.after_ref.refs_6_
  10.7 1.1 %collective-permute-start.2 = (bf16[8,32,128]{2,1,0:T(8,128)(2,1)S(1)}, bf16[8,32,128]{2,1,0:T(8,128)(2,1)S(1)}, u32[]{:S(2)}, u32[]{:S(2)}) collective-permute-start(bf16[8,32,128]{2,1,0:T(8,128)(2,1)S(1)} %collective-permute-done.refs_1_), channel_id=1, source_target_pairs={{0,1},{1,0},{2,3},{3,2},{4,5},{5,4},{6,7},{7,6},{8,9},{9,8},{10,11... | collective-permute-start | bytes 196616 | tf_op jit(solution)/shard_map/ppermute | solution.py:25
  11.8 0.1 order.1
  13.2 0.2 mask.1.refs_9_
  13.4 0.0 collective-permute-done.3.refs_4_
  13.4 0.0 collective-permute-done.1.refs_2_
  13.4 0.0 collective-permute-done.6.refs_7_
  13.4 0.9 %collective-permute-done.4.refs_5_ = bf16[8,32,128]{2,1,0:T(8,128)(2,1)S(1)} collective-permute-done((bf16[8,32,128]{2,1,0:T(8,128)(2,1)S(1)}, bf16[8,32,128]{2,1,0:T(8,128)(2,1)S(1)}, u32[]{:S(2)}, u32[]{:S(2)}) %collective-permute-start.4) | collective-permute-done | bytes 65568 | tf_op jit(solution)/shard_map/ppermute | solution.py:25
  14.4 0.6 %collective-permute-done.2.refs_3_ = bf16[8,32,128]{2,1,0:T(8,128)(2,1)S(1)} collective-permute-done((bf16[8,32,128]{2,1,0:T(8,128)(2,1)S(1)}, bf16[8,32,128]{2,1,0:T(8,128)(2,1)S(1)}, u32[]{:S(2)}, u32[]{:S(2)}) %collective-permute-start.2) | collective-permute-done | bytes 65568 | tf_op jit(solution)/shard_map/ppermute | solution.py:25
  15.0 1.7 %attend.5 = bf16[528,128]{1,0:T(8,128)(2,1)S(1)} custom-call(bf16[8,32,128]{2,1,0:T(8,128)(2,1)S(1)} %bitcast.13, bf16[8,32,128]{2,1,0:T(8,128)(2,1)S(1)} %collective-permute-done.refs_1_, bf16[8,32,128]{2,1,0:T(8,128)(2,1)S(1)} %collective-permute-done.1.refs_2_, bf16[8,32,128]{2,1,0:T(8,128)(2,1)S(1)} %collective-permute-done.2.refs_3_, ...), custom_call_target="tpu_custom_call" | custom-call | flops 536870912 | bytes 2097152 | tf_op jit(solution)/shard_map/attend/pallas_call | solution.py:203
  16.7 0.0 slice-start
  16.7 0.0 slice-start.1
  16.7 1.4 %collective-permute-start.7 = (bf16[528,128]{1,0:T(8,128)(2,1)S(1)}, bf16[528,128]{1,0:T(8,128)(2,1)S(1)}, u32[]{:S(2)}, u32[]{:S(2)}) collective-permute-start(bf16[528,128]{1,0:T(8,128)(2,1)S(1)} %attend.5), channel_id=1, source_target_pairs={{0,3},{1,2},{2,1},{3,0},{4,7},{5,6},{6,5},{7,4},{8,11},{9,10},{10,... | collective-permute-start | bytes 405512 | tf_op jit(solution)/shard_map/ppermute | solution.py:25
  18.2 1.7 %attend.6 = bf16[528,128]{1,0:T(8,128)(2,1)S(1)} custom-call(bf16[8,32,128]{2,1,0:T(8,128)(2,1)S(1)} %bitcast.14, bf16[8,32,128]{2,1,0:T(8,128)(2,1)S(1)} %collective-permute-done.refs_1_, bf16[8,32,128]{2,1,0:T(8,128)(2,1)S(1)} %collective-permute-done.1.refs_2_, bf16[8,32,128]{2,1,0:T(8,128)(2,1)S(1)} %collective-permute-done.2.refs_3_, ...), custom_call_target="tpu_custom_call" | custom-call | flops 536870912 | bytes 2097152 | tf_op jit(solution)/shard_map/attend/pallas_call | solution.py:203
  19.9 0.0 slice-start.2
  19.9 1.2 %collective-permute-start.8 = (bf16[528,128]{1,0:T(8,128)(2,1)S(1)}, bf16[528,128]{1,0:T(8,128)(2,1)S(1)}, u32[]{:S(2)}, u32[]{:S(2)}) collective-permute-start(bf16[528,128]{1,0:T(8,128)(2,1)S(1)} %attend.6), channel_id=1, source_target_pairs={{0,2},{1,3},{2,0},{3,1},{4,6},{5,7},{6,4},{7,5},{8,10},{9,11},{10,... | collective-permute-start | bytes 405512 | tf_op jit(solution)/shard_map/ppermute | solution.py:25
  21.1 1.7 %attend.7 = bf16[528,128]{1,0:T(8,128)(2,1)S(1)} custom-call(bf16[8,32,128]{2,1,0:T(8,128)(2,1)S(1)} %bitcast.15, bf16[8,32,128]{2,1,0:T(8,128)(2,1)S(1)} %collective-permute-done.refs_1_, bf16[8,32,128]{2,1,0:T(8,128)(2,1)S(1)} %collective-permute-done.1.refs_2_, bf16[8,32,128]{2,1,0:T(8,128)(2,1)S(1)} %collective-permute-done.2.refs_3_, ...), custom_call_target="tpu_custom_call" | custom-call | flops 536870912 | bytes 2097152 | tf_op jit(solution)/shard_map/attend/pallas_call | solution.py:203
  22.8 0.0 slice-start.3
  22.8 1.0 %collective-permute-start.9 = (bf16[528,128]{1,0:T(8,128)(2,1)S(1)}, bf16[528,128]{1,0:T(8,128)(2,1)S(1)}, u32[]{:S(2)}, u32[]{:S(2)}) collective-permute-start(bf16[528,128]{1,0:T(8,128)(2,1)S(1)} %attend.7), channel_id=1, source_target_pairs={{0,1},{1,0},{2,3},{3,2},{4,5},{5,4},{6,7},{7,6},{8,9},{9,8},{10,11... | collective-permute-start | bytes 405512 | tf_op jit(solution)/shard_map/ppermute | solution.py:25
  23.8 1.6 %attend.4 = (f32[512,128]{1,0:T(8,128)S(1)}, bf16[16,128]{1,0:T(8,128)(2,1)S(1)}) custom-call(bf16[8,32,128]{2,1,0:T(8,128)(2,1)S(1)} %bitcast.16, bf16[8,32,128]{2,1,0:T(8,128)(2,1)S(1)} %collective-permute-done.refs_1_, bf16[8,32,128]{2,1,0:T(8,128)(2,1)S(1)} %collective-permute-done.1.refs_2_, bf16[8,32,128]{2,1,0:T(8,128)(2,1)S(1)} %collective-permute-done.2.refs_3_, ...), custom_call_target="tpu_custom_call" | custom-call | flops 536870912 | bytes 2097152 | tf_op jit(solution)/shard_map/attend/pallas_call | solution.py:203
  25.4 0.0 collective-permute-done.7.refs_0_
  25.4 0.0 collective-permute-done.8.refs_1_
  25.4 0.4 merge.2
  25.9 2.0 %collective-permute-done.9.refs_0_ = bf16[528,128]{1,0:T(8,128)(2,1)S(1)} collective-permute-done((bf16[528,128]{1,0:T(8,128)(2,1)S(1)}, bf16[528,128]{1,0:T(8,128)(2,1)S(1)}, u32[]{:S(2)}, u32[]{:S(2)}) %collective-permute-start.9) | collective-permute-done | bytes 135200 | tf_op jit(solution)/shard_map/ppermute | solution.py:25
  27.9 0.3 merge.3
  28.2 3.2 %collective-permute-start.10 = (bf16[528,128]{1,0:T(8,128)(2,1)S(1)}, bf16[528,128]{1,0:T(8,128)(2,1)S(1)}, u32[]{:S(2)}, u32[]{:S(2)}) collective-permute-start(bf16[528,128]{1,0:T(8,128)(2,1)S(1)} %get-tuple-element.20.own_ref), channel_id=1, source_target_pairs={{0,6},{1,7},{2,4},{3,5},{4,2},{5,3},{6,0},{7,1},{8,14},{9,15},{10,... | collective-permute-start | bytes 405512 | tf_op jit(solution)/shard_map/ppermute | solution.py:25
  31.4 3.6 %collective-permute-done.10.other_ref = bf16[528,128]{1,0:T(8,128)(2,1)S(1)} collective-permute-done((bf16[528,128]{1,0:T(8,128)(2,1)S(1)}, bf16[528,128]{1,0:T(8,128)(2,1)S(1)}, u32[]{:S(2)}, u32[]{:S(2)}) %collective-permute-start.10) | collective-permute-done | bytes 135200 | tf_op jit(solution)/shard_map/ppermute | solution.py:25
  35.1 0.6 %settle.1.refs_0_ = bf16[32,2048]{1,0:T(8,128)(2,1)S(1)} custom-call(f32[512,128]{1,0:T(8,128)S(1)} %get-tuple-element.19.wide_ref, bf16[528,128]{1,0:T(8,128)(2,1)S(1)} %get-tuple-element.20.own_ref, bf16[528,128]{1,0:T(8,128)(2,1)S(1)} %collective-permute-done.10.other_ref, bf16[256,256]{1,0:T(8,128)(2,1)S(1)} %get-tuple-element.13.refs_10_.order_ref), custom_call_target="tpu_custom_call" | custom-call | tf_op jit(solution)/shard_map/settle/pallas_call | solution.py:302
  35.6 1.6 %collective-permute-start.13 = (bf16[32,2048]{1,0:T(8,128)(2,1)S(1)}, bf16[32,2048]{1,0:T(8,128)(2,1)S(1)}, u32[]{:S(2)}, u32[]{:S(2)}) collective-permute-start(bf16[32,2048]{1,0:T(8,128)(2,1)S(1)} %settle.1.refs_0_), channel_id=1, source_target_pairs={{0,3},{1,2},{2,1},{3,0},{4,7},{5,6},{6,5},{7,4},{8,11},{9,10},{10,... | collective-permute-start | bytes 393224 | tf_op jit(solution)/shard_map/ppermute | solution.py:25
  37.2 1.5 %collective-permute-start.12 = (bf16[32,2048]{1,0:T(8,128)(2,1)S(1)}, bf16[32,2048]{1,0:T(8,128)(2,1)S(1)}, u32[]{:S(2)}, u32[]{:S(2)}) collective-permute-start(bf16[32,2048]{1,0:T(8,128)(2,1)S(1)} %settle.1.refs_0_), channel_id=1, source_target_pairs={{0,2},{1,3},{2,0},{3,1},{4,6},{5,7},{6,4},{7,5},{8,10},{9,11},{10,... | collective-permute-start | bytes 393224 | tf_op jit(solution)/shard_map/ppermute | solution.py:25
  38.8 0.4 collective-permute-start.11
  39.2 0.8 %project.4.refs_2_ = f32[32,1024]{1,0:T(8,128)S(1)} custom-call(bf16[32,2048]{1,0:T(8,128)(2,1)S(1)} %settle.1.refs_0_, bf16[8192,1024]{1,0:T(8,128)(2,1)S(1)} %bitcast.6), custom_call_target="tpu_custom_call" | custom-call | tf_op jit(solution)/shard_map/project/pallas_call | solution.py:322
  40.0 1.5 %collective-permute-done.13.refs_0_ = bf16[32,2048]{1,0:T(8,128)(2,1)S(1)} collective-permute-done((bf16[32,2048]{1,0:T(8,128)(2,1)S(1)}, bf16[32,2048]{1,0:T(8,128)(2,1)S(1)}, u32[]{:S(2)}, u32[]{:S(2)}) %collective-permute-start.13) | collective-permute-done | bytes 131104 | tf_op jit(solution)/shard_map/ppermute | solution.py:25
  41.6 0.8 %project.5.refs_2_ = f32[32,1024]{1,0:T(8,128)S(1)} custom-call(bf16[32,2048]{1,0:T(8,128)(2,1)S(1)} %collective-permute-done.13.refs_0_, bf16[8192,1024]{1,0:T(8,128)(2,1)S(1)} %bitcast.6, f32[32,1024]{1,0:T(8,128)S(1)} %project.4.refs_2_), custom_call_target="tpu_custom_call" | custom-call | tf_op jit(solution)/shard_map/project/pallas_call | solution.py:322
  42.4 0.7 %collective-permute-done.12.refs_0_ = bf16[32,2048]{1,0:T(8,128)(2,1)S(1)} collective-permute-done((bf16[32,2048]{1,0:T(8,128)(2,1)S(1)}, bf16[32,2048]{1,0:T(8,128)(2,1)S(1)}, u32[]{:S(2)}, u32[]{:S(2)}) %collective-permute-start.12) | collective-permute-done | bytes 131104 | tf_op jit(solution)/shard_map/ppermute | solution.py:25
  43.1 0.8 %project.6.refs_2_ = f32[32,1024]{1,0:T(8,128)S(1)} custom-call(bf16[32,2048]{1,0:T(8,128)(2,1)S(1)} %collective-permute-done.12.refs_0_, bf16[8192,1024]{1,0:T(8,128)(2,1)S(1)} %bitcast.6, f32[32,1024]{1,0:T(8,128)S(1)} %project.5.refs_2_), custom_call_target="tpu_custom_call" | custom-call | tf_op jit(solution)/shard_map/project/pallas_call | solution.py:322
  43.9 0.0 collective-permute-done.11.refs_0_
  43.9 0.8 %project.7 = bf16[32,1024]{1,0:T(8,128)(2,1)S(1)} custom-call(bf16[32,2048]{1,0:T(8,128)(2,1)S(1)} %collective-permute-done.11.refs_0_, bf16[8192,1024]{1,0:T(8,128)(2,1)S(1)} %bitcast.6, f32[32,1024]{1,0:T(8,128)S(1)} %project.6.refs_2_), custom_call_target="tpu_custom_call" | custom-call | tf_op jit(solution)/shard_map/project/pallas_call | solution.py:322
  44.8 0.0 collective-permute-start.14
  44.8 3.7 %collective-permute-done.14 = bf16[32,1024]{1,0:T(8,128)(2,1)S(1)} collective-permute-done((bf16[32,1024]{1,0:T(8,128)(2,1)S(1)}, bf16[32,1024]{1,0:T(8,128)(2,1)S(1)}, u32[]{:S(2)}, u32[]{:S(2)}) %collective-permute-start.14) | collective-permute-done | bytes 65568 | tf_op jit(solution)/shard_map/ppermute | solution.py:30
  48.5 0.6 %copy.10 = bf16[32,1024]{1,0:T(8,128)(2,1)} copy(bf16[32,1024]{1,0:T(8,128)(2,1)S(1)} %collective-permute-done.14) | data formatting | bytes 131072
  (12 shorter events, 0.0 us)
Async XLA Ops:
  0.0 15.0 %copy-start = (bf16[4,8192]{1,0:T(4,128)(2,1)S(1)}, bf16[4,8192]{1,0:T(4,128)(2,1)}, u32[]{:S(2)}) copy-start(bf16[4,8192]{1,0:T(4,128)(2,1)} %param.5) | copy-start | bytes 196612
  0.0 15.0 %slice-start.4 = ((s8[8388608]{0:T(1024)(128)(4,1)}), s8[4194304]{0:T(1024)(128)(4,1)S(1)}, s32[]{:S(2)}) async-start(s8[8388608]{0:T(1024)(128)(4,1)} %bitcast.7), calls=%async_computation.4 | async-start | bytes 8388608
  0.0 15.0 %slice-start.5 = ((s8[8388608]{0:T(1024)(128)(4,1)}), s8[4194304]{0:T(1024)(128)(4,1)S(1)}, s32[]{:S(2)}) async-start(s8[8388608]{0:T(1024)(128)(4,1)} %bitcast.7), calls=%async_computation.5 | async-start | bytes 8388608
  0.0 7.6 %collective-permute-start = (bf16[8,32,128]{2,1,0:T(8,128)(2,1)}, bf16[8,32,128]{2,1,0:T(8,128)(2,1)S(1)}, u32[]{:S(2)}, u32[]{:S(2)}) collective-permute-start(bf16[8,32,128]{2,1,0:T(8,128)(2,1)} %bitcast.9), channel_id=1, source_target_pairs={{0,4},{1,5},{2,6},{3,7},{4,0},{5,1},{6,2},{7,3},{8,12},{9,13},{10,... | collective-permute-start | bytes 196616 | tf_op jit(solution)/shard_map/ppermute | solution.py:25
  4.1 6.6 %collective-permute-start.5 = (bf16[8,32,128]{2,1,0:T(8,128)(2,1)}, bf16[8,32,128]{2,1,0:T(8,128)(2,1)S(1)}, u32[]{:S(2)}, u32[]{:S(2)}) collective-permute-start(bf16[8,32,128]{2,1,0:T(8,128)(2,1)} %bitcast.10), channel_id=1, source_target_pairs={{0,3},{1,2},{2,1},{3,0},{4,7},{5,6},{6,5},{7,4},{8,11},{9,10},{10,... | collective-permute-start | bytes 196616 | tf_op jit(solution)/shard_map/ppermute | solution.py:25
  6.6 6.8 %collective-permute-start.3 = (bf16[8,32,128]{2,1,0:T(8,128)(2,1)}, bf16[8,32,128]{2,1,0:T(8,128)(2,1)S(1)}, u32[]{:S(2)}, u32[]{:S(2)}) collective-permute-start(bf16[8,32,128]{2,1,0:T(8,128)(2,1)} %bitcast.11), channel_id=1, source_target_pairs={{0,2},{1,3},{2,0},{3,1},{4,6},{5,7},{6,4},{7,5},{8,10},{9,11},{10,... | collective-permute-start | bytes 196616 | tf_op jit(solution)/shard_map/ppermute | solution.py:25
  7.1 6.4 %collective-permute-start.1 = (bf16[8,32,128]{2,1,0:T(8,128)(2,1)}, bf16[8,32,128]{2,1,0:T(8,128)(2,1)S(1)}, u32[]{:S(2)}, u32[]{:S(2)}) collective-permute-start(bf16[8,32,128]{2,1,0:T(8,128)(2,1)} %bitcast.12), channel_id=1, source_target_pairs={{0,1},{1,0},{2,3},{3,2},{4,5},{5,4},{6,7},{7,6},{8,9},{9,8},{10,11... | collective-permute-start | bytes 196616 | tf_op jit(solution)/shard_map/ppermute | solution.py:25
  7.6 5.8 %collective-permute-start.6 = (bf16[8,32,128]{2,1,0:T(8,128)(2,1)S(1)}, bf16[8,32,128]{2,1,0:T(8,128)(2,1)S(1)}, u32[]{:S(2)}, u32[]{:S(2)}) collective-permute-start(bf16[8,32,128]{2,1,0:T(8,128)(2,1)S(1)} %collective-permute-done.refs_1_), channel_id=1, source_target_pairs={{0,3},{1,2},{2,1},{3,0},{4,7},{5,6},{6,5},{7,4},{8,11},{9,10},{10,... | collective-permute-start | bytes 196616 | tf_op jit(solution)/shard_map/ppermute | solution.py:25
  10.1 4.3 %collective-permute-start.4 = (bf16[8,32,128]{2,1,0:T(8,128)(2,1)S(1)}, bf16[8,32,128]{2,1,0:T(8,128)(2,1)S(1)}, u32[]{:S(2)}, u32[]{:S(2)}) collective-permute-start(bf16[8,32,128]{2,1,0:T(8,128)(2,1)S(1)} %collective-permute-done.refs_1_), channel_id=1, source_target_pairs={{0,2},{1,3},{2,0},{3,1},{4,6},{5,7},{6,4},{7,5},{8,10},{9,11},{10,... | collective-permute-start | bytes 196616 | tf_op jit(solution)/shard_map/ppermute | solution.py:25
  10.7 4.3 %collective-permute-start.2 = (bf16[8,32,128]{2,1,0:T(8,128)(2,1)S(1)}, bf16[8,32,128]{2,1,0:T(8,128)(2,1)S(1)}, u32[]{:S(2)}, u32[]{:S(2)}) collective-permute-start(bf16[8,32,128]{2,1,0:T(8,128)(2,1)S(1)} %collective-permute-done.refs_1_), channel_id=1, source_target_pairs={{0,1},{1,0},{2,3},{3,2},{4,5},{5,4},{6,7},{7,6},{8,9},{9,8},{10,11... | collective-permute-start | bytes 196616 | tf_op jit(solution)/shard_map/ppermute | solution.py:25
  16.7 22.5 %slice-start = ((s8[16777216]{0:T(1024)(128)(4,1)}), s8[4194304]{0:T(1024)(128)(4,1)S(1)}, s32[]{:S(2)}) async-start(s8[16777216]{0:T(1024)(128)(4,1)} %bitcast.5), calls=%async_computation | async-start | bytes 8388608
  16.7 22.5 %slice-start.1 = ((s8[16777216]{0:T(1024)(128)(4,1)}), s8[4194304]{0:T(1024)(128)(4,1)S(1)}, s32[]{:S(2)}) async-start(s8[16777216]{0:T(1024)(128)(4,1)} %bitcast.5), calls=%async_computation.1 | async-start | bytes 8388608
  16.7 8.7 %collective-permute-start.7 = (bf16[528,128]{1,0:T(8,128)(2,1)S(1)}, bf16[528,128]{1,0:T(8,128)(2,1)S(1)}, u32[]{:S(2)}, u32[]{:S(2)}) collective-permute-start(bf16[528,128]{1,0:T(8,128)(2,1)S(1)} %attend.5), channel_id=1, source_target_pairs={{0,3},{1,2},{2,1},{3,0},{4,7},{5,6},{6,5},{7,4},{8,11},{9,10},{10,... | collective-permute-start | bytes 405512 | tf_op jit(solution)/shard_map/ppermute | solution.py:25
  19.9 19.3 %slice-start.2 = ((s8[16777216]{0:T(1024)(128)(4,1)}), s8[4194304]{0:T(1024)(128)(4,1)S(1)}, s32[]{:S(2)}) async-start(s8[16777216]{0:T(1024)(128)(4,1)} %bitcast.5), calls=%async_computation.2 | async-start | bytes 8388608
  19.9 5.6 %collective-permute-start.8 = (bf16[528,128]{1,0:T(8,128)(2,1)S(1)}, bf16[528,128]{1,0:T(8,128)(2,1)S(1)}, u32[]{:S(2)}, u32[]{:S(2)}) collective-permute-start(bf16[528,128]{1,0:T(8,128)(2,1)S(1)} %attend.6), channel_id=1, source_target_pairs={{0,2},{1,3},{2,0},{3,1},{4,6},{5,7},{6,4},{7,5},{8,10},{9,11},{10,... | collective-permute-start | bytes 405512 | tf_op jit(solution)/shard_map/ppermute | solution.py:25
  22.8 16.4 %slice-start.3 = ((s8[16777216]{0:T(1024)(128)(4,1)}), s8[4194304]{0:T(1024)(128)(4,1)S(1)}, s32[]{:S(2)}) async-start(s8[16777216]{0:T(1024)(128)(4,1)} %bitcast.5), calls=%async_computation.3 | async-start | bytes 8388608
  22.8 5.1 %collective-permute-start.9 = (bf16[528,128]{1,0:T(8,128)(2,1)S(1)}, bf16[528,128]{1,0:T(8,128)(2,1)S(1)}, u32[]{:S(2)}, u32[]{:S(2)}) collective-permute-start(bf16[528,128]{1,0:T(8,128)(2,1)S(1)} %attend.7), channel_id=1, source_target_pairs={{0,1},{1,0},{2,3},{3,2},{4,5},{5,4},{6,7},{7,6},{8,9},{9,8},{10,11... | collective-permute-start | bytes 405512 | tf_op jit(solution)/shard_map/ppermute | solution.py:25
  28.2 6.9 %collective-permute-start.10 = (bf16[528,128]{1,0:T(8,128)(2,1)S(1)}, bf16[528,128]{1,0:T(8,128)(2,1)S(1)}, u32[]{:S(2)}, u32[]{:S(2)}) collective-permute-start(bf16[528,128]{1,0:T(8,128)(2,1)S(1)} %get-tuple-element.20.own_ref), channel_id=1, source_target_pairs={{0,6},{1,7},{2,4},{3,5},{4,2},{5,3},{6,0},{7,1},{8,14},{9,15},{10,... | collective-permute-start | bytes 405512 | tf_op jit(solution)/shard_map/ppermute | solution.py:25
  35.6 5.9 %collective-permute-start.13 = (bf16[32,2048]{1,0:T(8,128)(2,1)S(1)}, bf16[32,2048]{1,0:T(8,128)(2,1)S(1)}, u32[]{:S(2)}, u32[]{:S(2)}) collective-permute-start(bf16[32,2048]{1,0:T(8,128)(2,1)S(1)} %settle.1.refs_0_), channel_id=1, source_target_pairs={{0,3},{1,2},{2,1},{3,0},{4,7},{5,6},{6,5},{7,4},{8,11},{9,10},{10,... | collective-permute-start | bytes 393224 | tf_op jit(solution)/shard_map/ppermute | solution.py:25
  37.2 5.9 %collective-permute-start.12 = (bf16[32,2048]{1,0:T(8,128)(2,1)S(1)}, bf16[32,2048]{1,0:T(8,128)(2,1)S(1)}, u32[]{:S(2)}, u32[]{:S(2)}) collective-permute-start(bf16[32,2048]{1,0:T(8,128)(2,1)S(1)} %settle.1.refs_0_), channel_id=1, source_target_pairs={{0,2},{1,3},{2,0},{3,1},{4,6},{5,7},{6,4},{7,5},{8,10},{9,11},{10,... | collective-permute-start | bytes 393224 | tf_op jit(solution)/shard_map/ppermute | solution.py:25
  38.8 5.2 %collective-permute-start.11 = (bf16[32,2048]{1,0:T(8,128)(2,1)S(1)}, bf16[32,2048]{1,0:T(8,128)(2,1)S(1)}, u32[]{:S(2)}, u32[]{:S(2)}) collective-permute-start(bf16[32,2048]{1,0:T(8,128)(2,1)S(1)} %settle.1.refs_0_), channel_id=1, source_target_pairs={{0,1},{1,0},{2,3},{3,2},{4,5},{5,4},{6,7},{7,6},{8,9},{9,8},{10,11... | collective-permute-start | bytes 393224 | tf_op jit(solution)/shard_map/ppermute | solution.py:25
  44.8 3.7 %collective-permute-start.14 = (bf16[32,1024]{1,0:T(8,128)(2,1)S(1)}, bf16[32,1024]{1,0:T(8,128)(2,1)S(1)}, u32[]{:S(2)}, u32[]{:S(2)}) collective-permute-start(bf16[32,1024]{1,0:T(8,128)(2,1)S(1)} %project.7), channel_id=1, source_target_pairs={{0,8},{8,16},{16,24},{24,0},{1,9},{9,17},{17,25},{25,1},{2,10},{10... | collective-permute-start | bytes 196616 | tf_op jit(solution)/shard_map/ppermute | solution.py:30

commit v14 on v11

--- a/solution.py
+++ b/solution.py
@@ -132,39 +132,44 @@
     ref[at : at + size, :] = table.astype(jnp.bfloat16)
 
 
-def attend_kernel(plan, part, *refs):
+def attend_kernel(plan, part, given, onward, *refs):
     *refs, score_ref, held_ref = refs
+    if onward is not None:
+        *refs, next_score_ref, next_peak_ref = refs
     if part == 0:
         *refs, value_ref, stat_ref = refs
         stat_at = 0
     else:
         *refs, value_ref = refs
         stat_ref, stat_at = value_ref, plan.share_rows
+    if given:
+        *refs, given_score_ref, given_peak_ref = refs
     *query_refs, cache_ref, bias_ref, order_ref, one_hot_ref = refs
     span = cache_ref.shape[0]
     me = lax.axis_index("ctx")
-    mine = plan.share(part)
-    row_at = pl.multiple_of((mine * plan.heads) % GROUP * plan.rows, plan.unit_rows)
-    order = order_ref[pl.ds(row_at, plan.unit_rows), :]
-    one_hot = one_hot_ref[pl.ds(row_at, plan.unit_rows), :]
     ones = jnp.ones((span, HD), jnp.bfloat16)
-    groups = [(mine * plan.heads + unit * plan.unit_heads) // GROUP for unit in range(plan.units)]
-    peaks = []
-    for unit, group in enumerate(groups):
+
+    def group_of(share, unit):
+        return (share * plan.heads + unit * plan.unit_heads) // GROUP
+
+    def first(share, unit, slot, to_ref):
+        group = group_of(share, unit)
+        row_at = pl.multiple_of((share * plan.heads) % GROUP * plan.rows, plan.unit_rows)
         if plan.by_device:
             for block, ref in enumerate(query_refs):
                 device = me ^ (block // 2) ^ (block % 2 * plan.half)
                 to = pl.multiple_of(device * GROUP * plan.rows_here, GROUP * plan.rows_here)
-                held_ref[unit, pl.ds(to, GROUP * plan.rows_here), :] = ref[group]
-            queries = held_ref[unit]
+                held_ref[slot, pl.ds(to, GROUP * plan.rows_here), :] = ref[group]
+            queries = held_ref[slot]
         else:
             stacked = jnp.concatenate([ref[group] for ref in query_refs], axis=0)
+            order = order_ref[pl.ds(row_at, plan.unit_rows), :]
             queries = jnp.dot(order, stacked, preferred_element_type=jnp.float32).astype(jnp.bfloat16)
-        queries = jnp.concatenate([queries, one_hot], axis=1)
+        queries = jnp.concatenate([queries, one_hot_ref[pl.ds(row_at, plan.unit_rows), :]], axis=1)
         key_at = pl.multiple_of(group * HD, HD)
         keys = jnp.concatenate([cache_ref[:, pl.ds(key_at, HD)], bias_ref[...]], axis=1)
         scores = lax.dot_general(queries, keys, (((1,), (1,)), ((), ())), preferred_element_type=jnp.float32)
-        score_ref[unit] = scores
+        to_ref[...] = scores
         peak = [scores[:, at : at + 128] for at in range(0, span, 128)]
         while len(peak) > 1:
             peak = [jnp.maximum(*peak[i : i + 2]) for i in range(0, len(peak) - 1, 2)] + (
@@ -172,13 +177,25 @@
             )
         peak = jnp.max(peak[0], axis=1, keepdims=True) * LOG2_SCALE
         peak = jnp.maximum(jnp.ceil(peak * (1.0 / STEP)), FLOOR / STEP)
-        peaks.append(jnp.broadcast_to(peak, (plan.unit_rows, 128)))
+        return jnp.broadcast_to(peak, (plan.unit_rows, 128))
+
+    mine = plan.share(part)
+    scores, peaks = [], []
+    for unit in range(plan.units):
+        if unit == 0 and given:
+            scores.append(given_score_ref)
+            peaks.append(given_peak_ref[...])
+        else:
+            scores.append(score_ref.at[unit])
+            peaks.append(first(mine, unit, unit, score_ref.at[unit]))
     same = lax.broadcasted_iota(jnp.int32, (128, 128), 0) == lax.broadcasted_iota(jnp.int32, (128, 128), 1)
     stats = []
-    for unit, group in enumerate(groups):
+    for unit in range(plan.units):
+        if unit == plan.units - 1 and onward is not None:
+            next_peak_ref[...] = first(plan.share(onward), 0, plan.units, next_score_ref)
         shift = jnp.concatenate([peaks[unit] * STEP] * (span // 128), axis=1)
-        weights = jnp.exp2(score_ref[unit] * LOG2_SCALE - shift)
-        value_at = pl.multiple_of((KVH + group) * HD, HD)
+        weights = jnp.exp2(scores[unit][...] * LOG2_SCALE - shift)
+        value_at = pl.multiple_of((KVH + group_of(mine, unit)) * HD, HD)
         values = jnp.concatenate([cache_ref[:, pl.ds(value_at, HD)], ones], axis=1)
         both = jnp.dot(weights.astype(jnp.bfloat16), values, preferred_element_type=jnp.float32)
         at = unit * plan.unit_rows
@@ -190,7 +207,7 @@
     write_stats(stat_ref, stat_at, stats)
 
 
-def attend(plan, part, queries, cache, *tables):
+def attend(plan, part, onward, queries, cache, tables, given):
     span = cache.shape[0]
     size = stat_rows(plan.units * plan.blocks)
     if part == 0:
@@ -200,21 +217,27 @@
         ]
     else:
         out_shape = [jax.ShapeDtypeStruct((plan.share_rows + size, HD), jnp.bfloat16)]
-    return local(
-        functools.partial(attend_kernel, plan, part),
+    if onward is not None:
+        out_shape += [
+            pltpu.VMEM((plan.unit_rows, span), jnp.float32),
+            pltpu.VMEM((plan.unit_rows, 128), jnp.float32),
+        ]
+    given = [pltpu.with_memory_space_constraint(value, pltpu.VMEM) for value in given]
+    return local(
+        functools.partial(attend_kernel, plan, part, bool(given), onward),
         out_shape,
-        [pltpu.VMEM] * (len(queries) + 1 + len(tables)),
+        [pltpu.VMEM] * (len(queries) + 1 + len(tables) + len(given)),
         "attend",
         [
             pltpu.VMEM((plan.units, plan.unit_rows, span), jnp.float32),
-            pltpu.VMEM((plan.units, plan.unit_rows, HD), jnp.bfloat16),
+            pltpu.VMEM((plan.units + 1, plan.unit_rows, HD), jnp.bfloat16),
         ],
         pl.CostEstimate(
             flops=4 * plan.share_rows * span * HD,
             bytes_accessed=2 * plan.units * span * HD * 2,
             transcendentals=plan.share_rows * span,
         ),
-    )(*queries, cache, *tables)
+    )(*queries, cache, *tables, *given)
 
 
 def columns(rows):
@@ -347,11 +370,11 @@
         pair = jnp.concatenate([own, far], axis=1)
         gathered = [pair] + [swap(pair, "ctx", k) for k in range(1, half)]
 
-    received = []
+    received, given = [], []
     for part in reversed(range(1, half)):
-        (piece,) = attend(plan, part, gathered, cache, bias, order, one_hot)
+        piece, *given = attend(plan, part, part - 1, gathered, cache, (bias, order, one_hot), given)
         received.append(swap(piece, "ctx", part))
-    wide, stats = attend(plan, 0, gathered, cache, bias, order, one_hot)
+    wide, stats = attend(plan, 0, None, gathered, cache, (bias, order, one_hot), given)
 
     near, wide = merge(plan, wide, stats, received[:-1])
     near, wide = merge(plan, wide, near, received[-1:])

time: 49.1 us -> 52.2 us (1.063)
  starting transfers between devices: 22.2 us -> 23.7 us
  waiting for transfers between devices: 12.8 us -> 13.7 us
    ppermute x14, starting transfers between devices: 22.2 us -> 23.6 us  [swap(): return lax.ppermute(value, axis, [(i, i ^ bits) for i in range(devices)])]
    ppermute x14, waiting for transfers between devices: 9.14 us -> 9.96 us  [swap(): return lax.ppermute(value, axis, [(i, i ^ bits) for i in range(devices)])]
  transfers between devices with their start and end apart: 15 -> 15, of which waited for: 8 -> 8; matrix products, arithmetic and copies ran while one was open for 0% -> 0% of each run, Pallas kernels for 17% -> 12%
where the time goes in v14:
time: 52.2 us; the launch traced here: 52.1 us
  starting transfers between devices  23.7 us (45%)
  waiting for transfers between devices  13.7 us (26%)
  Pallas kernels  12.2 us (23%)
  between operations  1.72 us (3%)
  local copies, waits for them, and re-layouts  0.85 us (2%)
    ppermute x14, starting transfers between devices, swap(): return lax.ppermute(value, axis, [(i, i ^ bits) for i in range(devices)])  23.6 us
    ppermute x14, waiting for transfers between devices, swap(): return lax.ppermute(value, axis, [(i, i ^ bits) for i in range(devices)])  9.96 us
    pallas_call x4, Pallas kernels, attend(): local(functools.partial(attend_kernel, plan, part, bool(given), onward),...  7.24 us
    ppermute x1, waiting for transfers between devices, from_behind(): lax.ppermute(value, axis, [(i, (i + by) % devices) for i in range(devices)])  3.69 us
    pallas_call x4, Pallas kernels, project(): local(functools.partial(project_kernel, plan, part), jax.ShapeDtypeStruct...  3.32 us
  transfers between devices with their start and end apart: 15, of which 8 were waited for; matrix products, arithmetic and copies ran while one was open for 0% of the time, Pallas kernels for 12%

profile of v14, /device:TPU:0, one launch (start us, length us, event | category | flops | bytes accessed | tf_op | source)
XLA Modules:
  0.0 52.1 jit_solution(12850794099384818338)
XLA Ops:
  0.0 4.0 %collective-permute-start = (bf16[8,32,128]{2,1,0:T(8,128)(2,1)}, bf16[8,32,128]{2,1,0:T(8,128)(2,1)S(1)}, u32[]{:S(2)}, u32[]{:S(2)}) collective-permute-start(bf16[8,32,128]{2,1,0:T(8,128)(2,1)} %bitcast.7), channel_id=1, source_target_pairs={{0,4},{1,5},{2,6},{3,7},{4,0},{5,1},{6,2},{7,3},{8,12},{9,13},{10,... | collective-permute-start | bytes 196616 | tf_op jit(solution)/shard_map/ppermute | solution.py:25
  4.0 2.5 %collective-permute-start.5 = (bf16[8,32,128]{2,1,0:T(8,128)(2,1)}, bf16[8,32,128]{2,1,0:T(8,128)(2,1)S(1)}, u32[]{:S(2)}, u32[]{:S(2)}) collective-permute-start(bf16[8,32,128]{2,1,0:T(8,128)(2,1)} %bitcast.8), channel_id=1, source_target_pairs={{0,3},{1,2},{2,1},{3,0},{4,7},{5,6},{6,5},{7,4},{8,11},{9,10},{10,... | collective-permute-start | bytes 196616 | tf_op jit(solution)/shard_map/ppermute | solution.py:25
  6.5 0.4 collective-permute-start.3
  7.0 0.5 %collective-permute-start.1 = (bf16[8,32,128]{2,1,0:T(8,128)(2,1)}, bf16[8,32,128]{2,1,0:T(8,128)(2,1)S(1)}, u32[]{:S(2)}, u32[]{:S(2)}) collective-permute-start(bf16[8,32,128]{2,1,0:T(8,128)(2,1)} %bitcast.10), channel_id=1, source_target_pairs={{0,1},{1,0},{2,3},{3,2},{4,5},{5,4},{6,7},{7,6},{8,9},{9,8},{10,11... | collective-permute-start | bytes 196616 | tf_op jit(solution)/shard_map/ppermute | solution.py:25
  7.5 0.0 collective-permute-done.refs_1_
  7.5 2.5 %collective-permute-start.6 = (bf16[8,32,128]{2,1,0:T(8,128)(2,1)S(1)}, bf16[8,32,128]{2,1,0:T(8,128)(2,1)S(1)}, u32[]{:S(2)}, u32[]{:S(2)}) collective-permute-start(bf16[8,32,128]{2,1,0:T(8,128)(2,1)S(1)} %collective-permute-done.refs_1_), channel_id=1, source_target_pairs={{0,3},{1,2},{2,1},{3,0},{4,7},{5,6},{6,5},{7,4},{8,11},{9,10},{10,... | collective-permute-start | bytes 196616 | tf_op jit(solution)/shard_map/ppermute | solution.py:25
  10.0 0.6 %collective-permute-start.4 = (bf16[8,32,128]{2,1,0:T(8,128)(2,1)S(1)}, bf16[8,32,128]{2,1,0:T(8,128)(2,1)S(1)}, u32[]{:S(2)}, u32[]{:S(2)}) collective-permute-start(bf16[8,32,128]{2,1,0:T(8,128)(2,1)S(1)} %collective-permute-done.refs_1_), channel_id=1, source_target_pairs={{0,2},{1,3},{2,0},{3,1},{4,6},{5,7},{6,4},{7,5},{8,10},{9,11},{10,... | collective-permute-start | bytes 196616 | tf_op jit(solution)/shard_map/ppermute | solution.py:25
  10.6 0.0 collective-permute-done.5.after_ref.refs_6_
  10.7 1.1 %collective-permute-start.2 = (bf16[8,32,128]{2,1,0:T(8,128)(2,1)S(1)}, bf16[8,32,128]{2,1,0:T(8,128)(2,1)S(1)}, u32[]{:S(2)}, u32[]{:S(2)}) collective-permute-start(bf16[8,32,128]{2,1,0:T(8,128)(2,1)S(1)} %collective-permute-done.refs_1_), channel_id=1, source_target_pairs={{0,1},{1,0},{2,3},{3,2},{4,5},{5,4},{6,7},{7,6},{8,9},{9,8},{10,11... | collective-permute-start | bytes 196616 | tf_op jit(solution)/shard_map/ppermute | solution.py:25
  11.7 0.1 order.1
  13.4 0.2 mask.1.refs_9_
  13.6 0.0 collective-permute-done.3.refs_4_
  13.7 0.0 collective-permute-done.1.refs_2_
  13.7 0.0 collective-permute-done.6.refs_7_
  13.7 0.6 %collective-permute-done.4.refs_5_ = bf16[8,32,128]{2,1,0:T(8,128)(2,1)S(1)} collective-permute-done((bf16[8,32,128]{2,1,0:T(8,128)(2,1)S(1)}, bf16[8,32,128]{2,1,0:T(8,128)(2,1)S(1)}, u32[]{:S(2)}, u32[]{:S(2)}) %collective-permute-start.4) | collective-permute-done | bytes 65568 | tf_op jit(solution)/shard_map/ppermute | solution.py:25
  14.3 0.6 %collective-permute-done.2.refs_3_ = bf16[8,32,128]{2,1,0:T(8,128)(2,1)S(1)} collective-permute-done((bf16[8,32,128]{2,1,0:T(8,128)(2,1)S(1)}, bf16[8,32,128]{2,1,0:T(8,128)(2,1)S(1)}, u32[]{:S(2)}, u32[]{:S(2)}) %collective-permute-start.2) | collective-permute-done | bytes 65568 | tf_op jit(solution)/shard_map/ppermute | solution.py:25
  14.9 0.2 copy-done
  15.1 2.5 %attend.4 = (bf16[528,128]{1,0:T(8,128)(2,1)S(1)}, f32[256,2048]{1,0:T(8,128)S(1)}, f32[256,128]{1,0:T(8,128)S(1)}) custom-call(bf16[8,32,128]{2,1,0:T(8,128)(2,1)S(1)} %bitcast.11, bf16[8,32,128]{2,1,0:T(8,128)(2,1)S(1)} %collective-permute-done.refs_1_, bf16[8,32,128]{2,1,0:T(8,128)(2,1)S(1)} %collective-permute-done.1.refs_2_, ...), custom_call_target="tpu_custom_call" | custom-call | flops 536870912 | bytes 2097152 | tf_op jit(solution)/shard_map/attend/pallas_call | solution.py:226
  17.6 0.0 slice-start
  17.6 0.0 slice-start.1
  17.6 1.8 %attend.5 = (bf16[528,128]{1,0:T(8,128)(2,1)S(1)}, f32[256,2048]{1,0:T(8,128)S(1)}, f32[256,128]{1,0:T(8,128)S(1)}) custom-call(bf16[8,32,128]{2,1,0:T(8,128)(2,1)S(1)} %bitcast.12, bf16[8,32,128]{2,1,0:T(8,128)(2,1)S(1)} %collective-permute-done.refs_1_, bf16[8,32,128]{2,1,0:T(8,128)(2,1)S(1)} %collective-permute-done.1.refs_2_, ...), custom_call_target="tpu_custom_call" | custom-call | flops 536870912 | bytes 2097152 | tf_op jit(solution)/shard_map/attend/pallas_call | solution.py:226
  19.4 1.2 %collective-permute-start.8 = (bf16[528,128]{1,0:T(8,128)(2,1)S(1)}, bf16[528,128]{1,0:T(8,128)(2,1)S(1)}, u32[]{:S(2)}, u32[]{:S(2)}) collective-permute-start(bf16[528,128]{1,0:T(8,128)(2,1)S(1)} %get-tuple-element.33), channel_id=1, source_target_pairs={{0,2},{1,3},{2,0},{3,1},{4,6},{5,7},{6,4},{7,5},{8,10},{9,11},{10,... | collective-permute-start | bytes 405512 | tf_op jit(solution)/shard_map/ppermute | solution.py:25
  20.6 1.2 %collective-permute-start.7 = (bf16[528,128]{1,0:T(8,128)(2,1)S(1)}, bf16[528,128]{1,0:T(8,128)(2,1)S(1)}, u32[]{:S(2)}, u32[]{:S(2)}) collective-permute-start(bf16[528,128]{1,0:T(8,128)(2,1)S(1)} %get-tuple-element.32), channel_id=1, source_target_pairs={{0,3},{1,2},{2,1},{3,0},{4,7},{5,6},{6,5},{7,4},{8,11},{9,10},{10,... | collective-permute-start | bytes 405512 | tf_op jit(solution)/shard_map/ppermute | solution.py:25
  21.8 1.7 %attend.6 = (bf16[528,128]{1,0:T(8,128)(2,1)S(1)}, f32[256,2048]{1,0:T(8,128)S(1)}, f32[256,128]{1,0:T(8,128)S(1)}) custom-call(bf16[8,32,128]{2,1,0:T(8,128)(2,1)S(1)} %bitcast.13, bf16[8,32,128]{2,1,0:T(8,128)(2,1)S(1)} %collective-permute-done.refs_1_, bf16[8,32,128]{2,1,0:T(8,128)(2,1)S(1)} %collective-permute-done.1.refs_2_, ...), custom_call_target="tpu_custom_call" | custom-call | flops 536870912 | bytes 2097152 | tf_op jit(solution)/shard_map/attend/pallas_call | solution.py:226
  23.5 1.2 %collective-permute-start.9 = (bf16[528,128]{1,0:T(8,128)(2,1)S(1)}, bf16[528,128]{1,0:T(8,128)(2,1)S(1)}, u32[]{:S(2)}, u32[]{:S(2)}) collective-permute-start(bf16[528,128]{1,0:T(8,128)(2,1)S(1)} %get-tuple-element.36), channel_id=1, source_target_pairs={{0,1},{1,0},{2,3},{3,2},{4,5},{5,4},{6,7},{7,6},{8,9},{9,8},{10,11... | collective-permute-start | bytes 405512 | tf_op jit(solution)/shard_map/ppermute | solution.py:25
  24.7 1.3 %attend.7 = (f32[512,128]{1,0:T(8,128)S(1)}, bf16[16,128]{1,0:T(8,128)(2,1)S(1)}) custom-call(bf16[8,32,128]{2,1,0:T(8,128)(2,1)S(1)} %bitcast.14, bf16[8,32,128]{2,1,0:T(8,128)(2,1)S(1)} %collective-permute-done.refs_1_, bf16[8,32,128]{2,1,0:T(8,128)(2,1)S(1)} %collective-permute-done.1.refs_2_, bf16[8,32,128]{2,1,0:T(8,128)(2,1)S(1)} %collective-permute-done.2.refs_3_, ...), custom_call_target="tpu_custom_call" | custom-call | flops 536870912 | bytes 2097152 | tf_op jit(solution)/shard_map/attend/pallas_call | solution.py:226
  26.0 0.0 collective-permute-done.8.refs_1_
  26.0 0.7 %collective-permute-done.7.refs_0_ = bf16[528,128]{1,0:T(8,128)(2,1)S(1)} collective-permute-done((bf16[528,128]{1,0:T(8,128)(2,1)S(1)}, bf16[528,128]{1,0:T(8,128)(2,1)S(1)}, u32[]{:S(2)}, u32[]{:S(2)}) %collective-permute-start.7) | collective-permute-done | bytes 135200 | tf_op jit(solution)/shard_map/ppermute | solution.py:25
  26.7 0.4 merge.2
  27.1 1.5 %collective-permute-done.9.refs_0_ = bf16[528,128]{1,0:T(8,128)(2,1)S(1)} collective-permute-done((bf16[528,128]{1,0:T(8,128)(2,1)S(1)}, bf16[528,128]{1,0:T(8,128)(2,1)S(1)}, u32[]{:S(2)}, u32[]{:S(2)}) %collective-permute-start.9) | collective-permute-done | bytes 135200 | tf_op jit(solution)/shard_map/ppermute | solution.py:25
  28.6 0.3 merge.3
  28.9 3.9 %collective-permute-start.10 = (bf16[528,128]{1,0:T(8,128)(2,1)S(1)}, bf16[528,128]{1,0:T(8,128)(2,1)S(1)}, u32[]{:S(2)}, u32[]{:S(2)}) collective-permute-start(bf16[528,128]{1,0:T(8,128)(2,1)S(1)} %get-tuple-element.38.own_ref), channel_id=1, source_target_pairs={{0,6},{1,7},{2,4},{3,5},{4,2},{5,3},{6,0},{7,1},{8,14},{9,15},{10,... | collective-permute-start | bytes 405512 | tf_op jit(solution)/shard_map/ppermute | solution.py:25
  32.9 3.0 %collective-permute-done.10.other_ref = bf16[528,128]{1,0:T(8,128)(2,1)S(1)} collective-permute-done((bf16[528,128]{1,0:T(8,128)(2,1)S(1)}, bf16[528,128]{1,0:T(8,128)(2,1)S(1)}, u32[]{:S(2)}, u32[]{:S(2)}) %collective-permute-start.10) | collective-permute-done | bytes 135200 | tf_op jit(solution)/shard_map/ppermute | solution.py:25
  35.9 0.6 %settle.1.refs_0_ = bf16[32,2048]{1,0:T(8,128)(2,1)S(1)} custom-call(f32[512,128]{1,0:T(8,128)S(1)} %get-tuple-element.37.wide_ref, bf16[528,128]{1,0:T(8,128)(2,1)S(1)} %get-tuple-element.38.own_ref, bf16[528,128]{1,0:T(8,128)(2,1)S(1)} %collective-permute-done.10.other_ref, bf16[256,256]{1,0:T(8,128)(2,1)S(1)} %get-tuple-element.22.refs_10_.order_ref), custom_call_target="tpu_custom_call" | custom-call | tf_op jit(solution)/shard_map/settle/pallas_call | solution.py:325
  36.5 1.1 %collective-permute-start.13 = (bf16[32,2048]{1,0:T(8,128)(2,1)S(1)}, bf16[32,2048]{1,0:T(8,128)(2,1)S(1)}, u32[]{:S(2)}, u32[]{:S(2)}) collective-permute-start(bf16[32,2048]{1,0:T(8,128)(2,1)S(1)} %settle.1.refs_0_), channel_id=1, source_target_pairs={{0,1},{1,0},{2,3},{3,2},{4,5},{5,4},{6,7},{7,6},{8,9},{9,8},{10,11... | collective-permute-start | bytes 393224 | tf_op jit(solution)/shard_map/ppermute | solution.py:25
  37.6 2.9 %collective-permute-start.12 = (bf16[32,2048]{1,0:T(8,128)(2,1)S(1)}, bf16[32,2048]{1,0:T(8,128)(2,1)S(1)}, u32[]{:S(2)}, u32[]{:S(2)}) collective-permute-start(bf16[32,2048]{1,0:T(8,128)(2,1)S(1)} %settle.1.refs_0_), channel_id=1, source_target_pairs={{0,2},{1,3},{2,0},{3,1},{4,6},{5,7},{6,4},{7,5},{8,10},{9,11},{10,... | collective-permute-start | bytes 393224 | tf_op jit(solution)/shard_map/ppermute | solution.py:25
  40.5 0.4 collective-permute-start.11
  40.9 0.0 slice-done
  40.9 0.8 %project.4.refs_2_ = f32[32,1024]{1,0:T(8,128)S(1)} custom-call(bf16[32,2048]{1,0:T(8,128)(2,1)S(1)} %settle.1.refs_0_, bf16[8192,1024]{1,0:T(8,128)(2,1)S(1)} %bitcast.6), custom_call_target="tpu_custom_call" | custom-call | tf_op jit(solution)/shard_map/project/pallas_call | solution.py:345
  41.7 0.0 collective-permute-done.13.refs_0_
  41.7 0.8 %project.5.refs_2_ = f32[32,1024]{1,0:T(8,128)S(1)} custom-call(bf16[32,2048]{1,0:T(8,128)(2,1)S(1)} %collective-permute-done.13.refs_0_, bf16[8192,1024]{1,0:T(8,128)(2,1)S(1)} %bitcast.6, f32[32,1024]{1,0:T(8,128)S(1)} %project.4.refs_2_), custom_call_target="tpu_custom_call" | custom-call | tf_op jit(solution)/shard_map/project/pallas_call | solution.py:345
  42.6 2.2 %collective-permute-done.12.refs_0_ = bf16[32,2048]{1,0:T(8,128)(2,1)S(1)} collective-permute-done((bf16[32,2048]{1,0:T(8,128)(2,1)S(1)}, bf16[32,2048]{1,0:T(8,128)(2,1)S(1)}, u32[]{:S(2)}, u32[]{:S(2)}) %collective-permute-start.12) | collective-permute-done | bytes 131104 | tf_op jit(solution)/shard_map/ppermute | solution.py:25
  44.8 0.8 %project.6.refs_2_ = f32[32,1024]{1,0:T(8,128)S(1)} custom-call(bf16[32,2048]{1,0:T(8,128)(2,1)S(1)} %collective-permute-done.12.refs_0_, bf16[8192,1024]{1,0:T(8,128)(2,1)S(1)} %bitcast.6, f32[32,1024]{1,0:T(8,128)S(1)} %project.5.refs_2_), custom_call_target="tpu_custom_call" | custom-call | tf_op jit(solution)/shard_map/project/pallas_call | solution.py:345
  45.6 1.3 %collective-permute-done.11.refs_0_ = bf16[32,2048]{1,0:T(8,128)(2,1)S(1)} collective-permute-done((bf16[32,2048]{1,0:T(8,128)(2,1)S(1)}, bf16[32,2048]{1,0:T(8,128)(2,1)S(1)}, u32[]{:S(2)}, u32[]{:S(2)}) %collective-permute-start.11) | collective-permute-done | bytes 131104 | tf_op jit(solution)/shard_map/ppermute | solution.py:25
  46.9 0.8 %project.7 = bf16[32,1024]{1,0:T(8,128)(2,1)S(1)} custom-call(bf16[32,2048]{1,0:T(8,128)(2,1)S(1)} %collective-permute-done.11.refs_0_, bf16[8192,1024]{1,0:T(8,128)(2,1)S(1)} %bitcast.6, f32[32,1024]{1,0:T(8,128)S(1)} %project.6.refs_2_), custom_call_target="tpu_custom_call" | custom-call | tf_op jit(solution)/shard_map/project/pallas_call | solution.py:345
  47.7 0.0 collective-permute-start.14
  47.8 3.7 %collective-permute-done.14 = bf16[32,1024]{1,0:T(8,128)(2,1)S(1)} collective-permute-done((bf16[32,1024]{1,0:T(8,128)(2,1)S(1)}, bf16[32,1024]{1,0:T(8,128)(2,1)S(1)}, u32[]{:S(2)}, u32[]{:S(2)}) %collective-permute-start.14) | collective-permute-done | bytes 65568 | tf_op jit(solution)/shard_map/ppermute | solution.py:30
  51.4 0.6 %copy.10 = bf16[32,1024]{1,0:T(8,128)(2,1)} copy(bf16[32,1024]{1,0:T(8,128)(2,1)S(1)} %collective-permute-done.14) | data formatting | bytes 131072
  (9 shorter events, 0.0 us)
Async XLA Ops:
  0.0 14.9 %copy-start.1 = (bf16[4,8192]{1,0:T(4,128)(2,1)S(1)}, bf16[4,8192]{1,0:T(4,128)(2,1)}, u32[]{:S(2)}) copy-start(bf16[4,8192]{1,0:T(4,128)(2,1)} %param.5) | copy-start | bytes 196612
  0.0 7.5 %collective-permute-start = (bf16[8,32,128]{2,1,0:T(8,128)(2,1)}, bf16[8,32,128]{2,1,0:T(8,128)(2,1)S(1)}, u32[]{:S(2)}, u32[]{:S(2)}) collective-permute-start(bf16[8,32,128]{2,1,0:T(8,128)(2,1)} %bitcast.7), channel_id=1, source_target_pairs={{0,4},{1,5},{2,6},{3,7},{4,0},{5,1},{6,2},{7,3},{8,12},{9,13},{10,... | collective-permute-start | bytes 196616 | tf_op jit(solution)/shard_map/ppermute | solution.py:25
  4.0 6.6 %collective-permute-start.5 = (bf16[8,32,128]{2,1,0:T(8,128)(2,1)}, bf16[8,32,128]{2,1,0:T(8,128)(2,1)S(1)}, u32[]{:S(2)}, u32[]{:S(2)}) collective-permute-start(bf16[8,32,128]{2,1,0:T(8,128)(2,1)} %bitcast.8), channel_id=1, source_target_pairs={{0,3},{1,2},{2,1},{3,0},{4,7},{5,6},{6,5},{7,4},{8,11},{9,10},{10,... | collective-permute-start | bytes 196616 | tf_op jit(solution)/shard_map/ppermute | solution.py:25
  6.5 7.1 %collective-permute-start.3 = (bf16[8,32,128]{2,1,0:T(8,128)(2,1)}, bf16[8,32,128]{2,1,0:T(8,128)(2,1)S(1)}, u32[]{:S(2)}, u32[]{:S(2)}) collective-permute-start(bf16[8,32,128]{2,1,0:T(8,128)(2,1)} %bitcast.9), channel_id=1, source_target_pairs={{0,2},{1,3},{2,0},{3,1},{4,6},{5,7},{6,4},{7,5},{8,10},{9,11},{10,... | collective-permute-start | bytes 196616 | tf_op jit(solution)/shard_map/ppermute | solution.py:25
  7.0 6.7 %collective-permute-start.1 = (bf16[8,32,128]{2,1,0:T(8,128)(2,1)}, bf16[8,32,128]{2,1,0:T(8,128)(2,1)S(1)}, u32[]{:S(2)}, u32[]{:S(2)}) collective-permute-start(bf16[8,32,128]{2,1,0:T(8,128)(2,1)} %bitcast.10), channel_id=1, source_target_pairs={{0,1},{1,0},{2,3},{3,2},{4,5},{5,4},{6,7},{7,6},{8,9},{9,8},{10,11... | collective-permute-start | bytes 196616 | tf_op jit(solution)/shard_map/ppermute | solution.py:25
  7.5 6.1 %collective-permute-start.6 = (bf16[8,32,128]{2,1,0:T(8,128)(2,1)S(1)}, bf16[8,32,128]{2,1,0:T(8,128)(2,1)S(1)}, u32[]{:S(2)}, u32[]{:S(2)}) collective-permute-start(bf16[8,32,128]{2,1,0:T(8,128)(2,1)S(1)} %collective-permute-done.refs_1_), channel_id=1, source_target_pairs={{0,3},{1,2},{2,1},{3,0},{4,7},{5,6},{6,5},{7,4},{8,11},{9,10},{10,... | collective-permute-start | bytes 196616 | tf_op jit(solution)/shard_map/ppermute | solution.py:25
  10.0 4.3 %collective-permute-start.4 = (bf16[8,32,128]{2,1,0:T(8,128)(2,1)S(1)}, bf16[8,32,128]{2,1,0:T(8,128)(2,1)S(1)}, u32[]{:S(2)}, u32[]{:S(2)}) collective-permute-start(bf16[8,32,128]{2,1,0:T(8,128)(2,1)S(1)} %collective-permute-done.refs_1_), channel_id=1, source_target_pairs={{0,2},{1,3},{2,0},{3,1},{4,6},{5,7},{6,4},{7,5},{8,10},{9,11},{10,... | collective-permute-start | bytes 196616 | tf_op jit(solution)/shard_map/ppermute | solution.py:25
  10.7 4.3 %collective-permute-start.2 = (bf16[8,32,128]{2,1,0:T(8,128)(2,1)S(1)}, bf16[8,32,128]{2,1,0:T(8,128)(2,1)S(1)}, u32[]{:S(2)}, u32[]{:S(2)}) collective-permute-start(bf16[8,32,128]{2,1,0:T(8,128)(2,1)S(1)} %collective-permute-done.refs_1_), channel_id=1, source_target_pairs={{0,1},{1,0},{2,3},{3,2},{4,5},{5,4},{6,7},{7,6},{8,9},{9,8},{10,11... | collective-permute-start | bytes 196616 | tf_op jit(solution)/shard_map/ppermute | solution.py:25
  11.7 3.4 %copy-start = (bf16[2048,2048]{1,0:T(8,128)(2,1)S(1)}, bf16[2048,2048]{1,0:T(8,128)(2,1)}, u32[]{:S(2)}) copy-start(bf16[2048,2048]{1,0:T(8,128)(2,1)} %refs_8_.7) | copy-start | bytes 25165828
  17.6 23.3 %slice-start = ((s8[16777216]{0:T(1024)(128)(4,1)}), s8[4194304]{0:T(1024)(128)(4,1)S(1)}, s32[]{:S(2)}) async-start(s8[16777216]{0:T(1024)(128)(4,1)} %bitcast.5), calls=%async_computation | async-start | bytes 8388608
  17.6 23.3 %slice-start.1 = ((s8[16777216]{0:T(1024)(128)(4,1)}), s8[4194304]{0:T(1024)(128)(4,1)S(1)}, s32[]{:S(2)}) async-start(s8[16777216]{0:T(1024)(128)(4,1)} %bitcast.5), calls=%async_computation.1 | async-start | bytes 8388608
  19.4 6.7 %collective-permute-start.8 = (bf16[528,128]{1,0:T(8,128)(2,1)S(1)}, bf16[528,128]{1,0:T(8,128)(2,1)S(1)}, u32[]{:S(2)}, u32[]{:S(2)}) collective-permute-start(bf16[528,128]{1,0:T(8,128)(2,1)S(1)} %get-tuple-element.33), channel_id=1, source_target_pairs={{0,2},{1,3},{2,0},{3,1},{4,6},{5,7},{6,4},{7,5},{8,10},{9,11},{10,... | collective-permute-start | bytes 405512 | tf_op jit(solution)/shard_map/ppermute | solution.py:25
  20.6 6.1 %collective-permute-start.7 = (bf16[528,128]{1,0:T(8,128)(2,1)S(1)}, bf16[528,128]{1,0:T(8,128)(2,1)S(1)}, u32[]{:S(2)}, u32[]{:S(2)}) collective-permute-start(bf16[528,128]{1,0:T(8,128)(2,1)S(1)} %get-tuple-element.32), channel_id=1, source_target_pairs={{0,3},{1,2},{2,1},{3,0},{4,7},{5,6},{6,5},{7,4},{8,11},{9,10},{10,... | collective-permute-start | bytes 405512 | tf_op jit(solution)/shard_map/ppermute | solution.py:25
  21.8 19.0 %slice-start.2 = ((s8[16777216]{0:T(1024)(128)(4,1)}), s8[4194304]{0:T(1024)(128)(4,1)S(1)}, s32[]{:S(2)}) async-start(s8[16777216]{0:T(1024)(128)(4,1)} %bitcast.5), calls=%async_computation.2 | async-start | bytes 8388608
  23.5 5.1 %collective-permute-start.9 = (bf16[528,128]{1,0:T(8,128)(2,1)S(1)}, bf16[528,128]{1,0:T(8,128)(2,1)S(1)}, u32[]{:S(2)}, u32[]{:S(2)}) collective-permute-start(bf16[528,128]{1,0:T(8,128)(2,1)S(1)} %get-tuple-element.36), channel_id=1, source_target_pairs={{0,1},{1,0},{2,3},{3,2},{4,5},{5,4},{6,7},{7,6},{8,9},{9,8},{10,11... | collective-permute-start | bytes 405512 | tf_op jit(solution)/shard_map/ppermute | solution.py:25
  24.7 16.2 %slice-start.3 = ((s8[16777216]{0:T(1024)(128)(4,1)}), s8[4194304]{0:T(1024)(128)(4,1)S(1)}, s32[]{:S(2)}) async-start(s8[16777216]{0:T(1024)(128)(4,1)} %bitcast.5), calls=%async_computation.3 | async-start | bytes 8388608
  28.9 7.0 %collective-permute-start.10 = (bf16[528,128]{1,0:T(8,128)(2,1)S(1)}, bf16[528,128]{1,0:T(8,128)(2,1)S(1)}, u32[]{:S(2)}, u32[]{:S(2)}) collective-permute-start(bf16[528,128]{1,0:T(8,128)(2,1)S(1)} %get-tuple-element.38.own_ref), channel_id=1, source_target_pairs={{0,6},{1,7},{2,4},{3,5},{4,2},{5,3},{6,0},{7,1},{8,14},{9,15},{10,... | collective-permute-start | bytes 405512 | tf_op jit(solution)/shard_map/ppermute | solution.py:25
  36.5 5.2 %collective-permute-start.13 = (bf16[32,2048]{1,0:T(8,128)(2,1)S(1)}, bf16[32,2048]{1,0:T(8,128)(2,1)S(1)}, u32[]{:S(2)}, u32[]{:S(2)}) collective-permute-start(bf16[32,2048]{1,0:T(8,128)(2,1)S(1)} %settle.1.refs_0_), channel_id=1, source_target_pairs={{0,1},{1,0},{2,3},{3,2},{4,5},{5,4},{6,7},{7,6},{8,9},{9,8},{10,11... | collective-permute-start | bytes 393224 | tf_op jit(solution)/shard_map/ppermute | solution.py:25
  37.6 7.2 %collective-permute-start.12 = (bf16[32,2048]{1,0:T(8,128)(2,1)S(1)}, bf16[32,2048]{1,0:T(8,128)(2,1)S(1)}, u32[]{:S(2)}, u32[]{:S(2)}) collective-permute-start(bf16[32,2048]{1,0:T(8,128)(2,1)S(1)} %settle.1.refs_0_), channel_id=1, source_target_pairs={{0,2},{1,3},{2,0},{3,1},{4,6},{5,7},{6,4},{7,5},{8,10},{9,11},{10,... | collective-permute-start | bytes 393224 | tf_op jit(solution)/shard_map/ppermute | solution.py:25
  40.5 6.4 %collective-permute-start.11 = (bf16[32,2048]{1,0:T(8,128)(2,1)S(1)}, bf16[32,2048]{1,0:T(8,128)(2,1)S(1)}, u32[]{:S(2)}, u32[]{:S(2)}) collective-permute-start(bf16[32,2048]{1,0:T(8,128)(2,1)S(1)} %settle.1.refs_0_), channel_id=1, source_target_pairs={{0,3},{1,2},{2,1},{3,0},{4,7},{5,6},{6,5},{7,4},{8,11},{9,10},{10,... | collective-permute-start | bytes 393224 | tf_op jit(solution)/shard_map/ppermute | solution.py:25
  47.7 3.7 %collective-permute-start.14 = (bf16[32,1024]{1,0:T(8,128)(2,1)S(1)}, bf16[32,1024]{1,0:T(8,128)(2,1)S(1)}, u32[]{:S(2)}, u32[]{:S(2)}) collective-permute-start(bf16[32,1024]{1,0:T(8,128)(2,1)S(1)} %project.7), channel_id=1, source_target_pairs={{0,8},{8,16},{16,24},{24,0},{1,9},{9,17},{17,25},{25,1},{2,10},{10... | collective-permute-start | bytes 196616 | tf_op jit(solution)/shard_map/ppermute | solution.py:30

commit v15 on v13

--- a/solution.py
+++ b/solution.py
@@ -358,7 +358,7 @@
     block = settle(plan, wide, near, swap(near, "ctx", plan.across), order)
 
     total = project(plan, 0, block, out_weight, None, jnp.float32)
-    for k in reversed(range(1, half)):
+    for k in list(range(2, half)) + [1]:
         dtype = jnp.float32 if k > 1 else jnp.bfloat16
         total = project(plan, k, swap(block, "ctx", k), out_weight, total, dtype)
     return from_behind(total, "segment", 1)

time: 49.3 us -> 49.9 us (1.012)
  waiting for transfers between devices: 13.1 us -> 13.7 us
    ppermute x14, waiting for transfers between devices: 9.41 us -> 10.1 us  [swap(): return lax.ppermute(value, axis, [(i, i ^ bits) for i in range(devices)])]
  transfers between devices with their start and end apart: 15 -> 15, of which waited for: 7 -> 8; matrix products, arithmetic and copies ran while one was open for 0% -> 0% of each run, Pallas kernels for 17% -> 17%
where the time goes in v15:
time: 49.9 us; the launch traced here: 49.7 us
  starting transfers between devices  22.2 us (44%)
  waiting for transfers between devices  13.7 us (27%)
  Pallas kernels  11.7 us (23%)
  between operations  1.48 us (3%)
  local copies, waits for them, and re-layouts  0.67 us (1%)
    ppermute x14, starting transfers between devices, swap(): return lax.ppermute(value, axis, [(i, i ^ bits) for i in range(devices)])  22.2 us
    ppermute x14, waiting for transfers between devices, swap(): return lax.ppermute(value, axis, [(i, i ^ bits) for i in range(devices)])  10.1 us
    pallas_call x4, Pallas kernels, attend(): local(functools.partial(attend_kernel, plan, part), out_shape, [pltpu.VME...  6.74 us
    ppermute x1, waiting for transfers between devices, from_behind(): lax.ppermute(value, axis, [(i, (i + by) % devices) for i in range(devices)])  3.69 us
    pallas_call x4, Pallas kernels, project(): local(functools.partial(project_kernel, plan, part), jax.ShapeDtypeStruct...  3.29 us
  transfers between devices with their start and end apart: 15, of which 8 were waited for; matrix products, arithmetic and copies ran while one was open for 0% of the time, Pallas kernels for 17%

profile of v15, /device:TPU:0, one launch (start us, length us, event | category | flops | bytes accessed | tf_op | source)
XLA Modules:
  0.0 49.7 jit_solution(555175999336071602)
XLA Ops:
  0.0 4.1 %collective-permute-start = (bf16[8,32,128]{2,1,0:T(8,128)(2,1)}, bf16[8,32,128]{2,1,0:T(8,128)(2,1)S(1)}, u32[]{:S(2)}, u32[]{:S(2)}) collective-permute-start(bf16[8,32,128]{2,1,0:T(8,128)(2,1)} %bitcast.9), channel_id=1, source_target_pairs={{0,4},{1,5},{2,6},{3,7},{4,0},{5,1},{6,2},{7,3},{8,12},{9,13},{10,... | collective-permute-start | bytes 196616 | tf_op jit(solution)/shard_map/ppermute | solution.py:25
  4.1 2.5 %collective-permute-start.5 = (bf16[8,32,128]{2,1,0:T(8,128)(2,1)}, bf16[8,32,128]{2,1,0:T(8,128)(2,1)S(1)}, u32[]{:S(2)}, u32[]{:S(2)}) collective-permute-start(bf16[8,32,128]{2,1,0:T(8,128)(2,1)} %bitcast.10), channel_id=1, source_target_pairs={{0,3},{1,2},{2,1},{3,0},{4,7},{5,6},{6,5},{7,4},{8,11},{9,10},{10,... | collective-permute-start | bytes 196616 | tf_op jit(solution)/shard_map/ppermute | solution.py:25
  6.6 0.4 collective-permute-start.3
  7.1 0.5 %collective-permute-start.1 = (bf16[8,32,128]{2,1,0:T(8,128)(2,1)}, bf16[8,32,128]{2,1,0:T(8,128)(2,1)S(1)}, u32[]{:S(2)}, u32[]{:S(2)}) collective-permute-start(bf16[8,32,128]{2,1,0:T(8,128)(2,1)} %bitcast.12), channel_id=1, source_target_pairs={{0,1},{1,0},{2,3},{3,2},{4,5},{5,4},{6,7},{7,6},{8,9},{9,8},{10,11... | collective-permute-start | bytes 196616 | tf_op jit(solution)/shard_map/ppermute | solution.py:25
  7.6 0.0 collective-permute-done.refs_1_
  7.6 2.5 %collective-permute-start.6 = (bf16[8,32,128]{2,1,0:T(8,128)(2,1)S(1)}, bf16[8,32,128]{2,1,0:T(8,128)(2,1)S(1)}, u32[]{:S(2)}, u32[]{:S(2)}) collective-permute-start(bf16[8,32,128]{2,1,0:T(8,128)(2,1)S(1)} %collective-permute-done.refs_1_), channel_id=1, source_target_pairs={{0,3},{1,2},{2,1},{3,0},{4,7},{5,6},{6,5},{7,4},{8,11},{9,10},{10,... | collective-permute-start | bytes 196616 | tf_op jit(solution)/shard_map/ppermute | solution.py:25
  10.1 0.6 %collective-permute-start.4 = (bf16[8,32,128]{2,1,0:T(8,128)(2,1)S(1)}, bf16[8,32,128]{2,1,0:T(8,128)(2,1)S(1)}, u32[]{:S(2)}, u32[]{:S(2)}) collective-permute-start(bf16[8,32,128]{2,1,0:T(8,128)(2,1)S(1)} %collective-permute-done.refs_1_), channel_id=1, source_target_pairs={{0,2},{1,3},{2,0},{3,1},{4,6},{5,7},{6,4},{7,5},{8,10},{9,11},{10,... | collective-permute-start | bytes 196616 | tf_op jit(solution)/shard_map/ppermute | solution.py:25
  10.7 0.0 collective-permute-done.5.after_ref.refs_6_
  10.7 1.1 %collective-permute-start.2 = (bf16[8,32,128]{2,1,0:T(8,128)(2,1)S(1)}, bf16[8,32,128]{2,1,0:T(8,128)(2,1)S(1)}, u32[]{:S(2)}, u32[]{:S(2)}) collective-permute-start(bf16[8,32,128]{2,1,0:T(8,128)(2,1)S(1)} %collective-permute-done.refs_1_), channel_id=1, source_target_pairs={{0,1},{1,0},{2,3},{3,2},{4,5},{5,4},{6,7},{7,6},{8,9},{9,8},{10,11... | collective-permute-start | bytes 196616 | tf_op jit(solution)/shard_map/ppermute | solution.py:25
  11.8 0.1 order.1
  13.2 0.2 mask.1.refs_9_
  13.4 0.0 collective-permute-done.3.refs_4_
  13.4 0.0 collective-permute-done.1.refs_2_
  13.4 0.0 collective-permute-done.6.refs_7_
  13.4 0.9 %collective-permute-done.4.refs_5_ = bf16[8,32,128]{2,1,0:T(8,128)(2,1)S(1)} collective-permute-done((bf16[8,32,128]{2,1,0:T(8,128)(2,1)S(1)}, bf16[8,32,128]{2,1,0:T(8,128)(2,1)S(1)}, u32[]{:S(2)}, u32[]{:S(2)}) %collective-permute-start.4) | collective-permute-done | bytes 65568 | tf_op jit(solution)/shard_map/ppermute | solution.py:25
  14.4 0.6 %collective-permute-done.2.refs_3_ = bf16[8,32,128]{2,1,0:T(8,128)(2,1)S(1)} collective-permute-done((bf16[8,32,128]{2,1,0:T(8,128)(2,1)S(1)}, bf16[8,32,128]{2,1,0:T(8,128)(2,1)S(1)}, u32[]{:S(2)}, u32[]{:S(2)}) %collective-permute-start.2) | collective-permute-done | bytes 65568 | tf_op jit(solution)/shard_map/ppermute | solution.py:25
  15.0 1.7 %attend.5 = bf16[528,128]{1,0:T(8,128)(2,1)S(1)} custom-call(bf16[8,32,128]{2,1,0:T(8,128)(2,1)S(1)} %bitcast.13, bf16[8,32,128]{2,1,0:T(8,128)(2,1)S(1)} %collective-permute-done.refs_1_, bf16[8,32,128]{2,1,0:T(8,128)(2,1)S(1)} %collective-permute-done.1.refs_2_, bf16[8,32,128]{2,1,0:T(8,128)(2,1)S(1)} %collective-permute-done.2.refs_3_, ...), custom_call_target="tpu_custom_call" | custom-call | flops 536870912 | bytes 2097152 | tf_op jit(solution)/shard_map/attend/pallas_call | solution.py:203
  16.7 0.0 slice-start
  16.7 0.0 slice-start.1
  16.7 1.4 %collective-permute-start.7 = (bf16[528,128]{1,0:T(8,128)(2,1)S(1)}, bf16[528,128]{1,0:T(8,128)(2,1)S(1)}, u32[]{:S(2)}, u32[]{:S(2)}) collective-permute-start(bf16[528,128]{1,0:T(8,128)(2,1)S(1)} %attend.5), channel_id=1, source_target_pairs={{0,3},{1,2},{2,1},{3,0},{4,7},{5,6},{6,5},{7,4},{8,11},{9,10},{10,... | collective-permute-start | bytes 405512 | tf_op jit(solution)/shard_map/ppermute | solution.py:25
  18.2 1.7 %attend.6 = bf16[528,128]{1,0:T(8,128)(2,1)S(1)} custom-call(bf16[8,32,128]{2,1,0:T(8,128)(2,1)S(1)} %bitcast.14, bf16[8,32,128]{2,1,0:T(8,128)(2,1)S(1)} %collective-permute-done.refs_1_, bf16[8,32,128]{2,1,0:T(8,128)(2,1)S(1)} %collective-permute-done.1.refs_2_, bf16[8,32,128]{2,1,0:T(8,128)(2,1)S(1)} %collective-permute-done.2.refs_3_, ...), custom_call_target="tpu_custom_call" | custom-call | flops 536870912 | bytes 2097152 | tf_op jit(solution)/shard_map/attend/pallas_call | solution.py:203
  19.9 0.0 slice-start.2
  19.9 1.2 %collective-permute-start.8 = (bf16[528,128]{1,0:T(8,128)(2,1)S(1)}, bf16[528,128]{1,0:T(8,128)(2,1)S(1)}, u32[]{:S(2)}, u32[]{:S(2)}) collective-permute-start(bf16[528,128]{1,0:T(8,128)(2,1)S(1)} %attend.6), channel_id=1, source_target_pairs={{0,2},{1,3},{2,0},{3,1},{4,6},{5,7},{6,4},{7,5},{8,10},{9,11},{10,... | collective-permute-start | bytes 405512 | tf_op jit(solution)/shard_map/ppermute | solution.py:25
  21.1 1.7 %attend.7 = bf16[528,128]{1,0:T(8,128)(2,1)S(1)} custom-call(bf16[8,32,128]{2,1,0:T(8,128)(2,1)S(1)} %bitcast.15, bf16[8,32,128]{2,1,0:T(8,128)(2,1)S(1)} %collective-permute-done.refs_1_, bf16[8,32,128]{2,1,0:T(8,128)(2,1)S(1)} %collective-permute-done.1.refs_2_, bf16[8,32,128]{2,1,0:T(8,128)(2,1)S(1)} %collective-permute-done.2.refs_3_, ...), custom_call_target="tpu_custom_call" | custom-call | flops 536870912 | bytes 2097152 | tf_op jit(solution)/shard_map/attend/pallas_call | solution.py:203
  22.8 0.0 slice-start.3
  22.8 1.0 %collective-permute-start.9 = (bf16[528,128]{1,0:T(8,128)(2,1)S(1)}, bf16[528,128]{1,0:T(8,128)(2,1)S(1)}, u32[]{:S(2)}, u32[]{:S(2)}) collective-permute-start(bf16[528,128]{1,0:T(8,128)(2,1)S(1)} %attend.7), channel_id=1, source_target_pairs={{0,1},{1,0},{2,3},{3,2},{4,5},{5,4},{6,7},{7,6},{8,9},{9,8},{10,11... | collective-permute-start | bytes 405512 | tf_op jit(solution)/shard_map/ppermute | solution.py:25
  23.8 1.6 %attend.4 = (f32[512,128]{1,0:T(8,128)S(1)}, bf16[16,128]{1,0:T(8,128)(2,1)S(1)}) custom-call(bf16[8,32,128]{2,1,0:T(8,128)(2,1)S(1)} %bitcast.16, bf16[8,32,128]{2,1,0:T(8,128)(2,1)S(1)} %collective-permute-done.refs_1_, bf16[8,32,128]{2,1,0:T(8,128)(2,1)S(1)} %collective-permute-done.1.refs_2_, bf16[8,32,128]{2,1,0:T(8,128)(2,1)S(1)} %collective-permute-done.2.refs_3_, ...), custom_call_target="tpu_custom_call" | custom-call | flops 536870912 | bytes 2097152 | tf_op jit(solution)/shard_map/attend/pallas_call | solution.py:203
  25.4 0.0 collective-permute-done.7.refs_0_
  25.4 0.0 collective-permute-done.8.refs_1_
  25.4 0.4 merge.2
  25.9 2.0 %collective-permute-done.9.refs_0_ = bf16[528,128]{1,0:T(8,128)(2,1)S(1)} collective-permute-done((bf16[528,128]{1,0:T(8,128)(2,1)S(1)}, bf16[528,128]{1,0:T(8,128)(2,1)S(1)}, u32[]{:S(2)}, u32[]{:S(2)}) %collective-permute-start.9) | collective-permute-done | bytes 135200 | tf_op jit(solution)/shard_map/ppermute | solution.py:25
  27.9 0.3 merge.3
  28.2 3.2 %collective-permute-start.10 = (bf16[528,128]{1,0:T(8,128)(2,1)S(1)}, bf16[528,128]{1,0:T(8,128)(2,1)S(1)}, u32[]{:S(2)}, u32[]{:S(2)}) collective-permute-start(bf16[528,128]{1,0:T(8,128)(2,1)S(1)} %get-tuple-element.20.own_ref), channel_id=1, source_target_pairs={{0,6},{1,7},{2,4},{3,5},{4,2},{5,3},{6,0},{7,1},{8,14},{9,15},{10,... | collective-permute-start | bytes 405512 | tf_op jit(solution)/shard_map/ppermute | solution.py:25
  31.4 3.8 %collective-permute-done.10.other_ref = bf16[528,128]{1,0:T(8,128)(2,1)S(1)} collective-permute-done((bf16[528,128]{1,0:T(8,128)(2,1)S(1)}, bf16[528,128]{1,0:T(8,128)(2,1)S(1)}, u32[]{:S(2)}, u32[]{:S(2)}) %collective-permute-start.10) | collective-permute-done | bytes 135200 | tf_op jit(solution)/shard_map/ppermute | solution.py:25
  35.3 0.5 %settle.1.refs_0_ = bf16[32,2048]{1,0:T(8,128)(2,1)S(1)} custom-call(f32[512,128]{1,0:T(8,128)S(1)} %get-tuple-element.19.wide_ref, bf16[528,128]{1,0:T(8,128)(2,1)S(1)} %get-tuple-element.20.own_ref, bf16[528,128]{1,0:T(8,128)(2,1)S(1)} %collective-permute-done.10.other_ref, bf16[256,256]{1,0:T(8,128)(2,1)S(1)} %get-tuple-element.13.refs_10_.order_ref), custom_call_target="tpu_custom_call" | custom-call | tf_op jit(solution)/shard_map/settle/pallas_call | solution.py:302
  35.8 0.1 collective-permute-start.13
  35.9 2.9 %collective-permute-start.12 = (bf16[32,2048]{1,0:T(8,128)(2,1)S(1)}, bf16[32,2048]{1,0:T(8,128)(2,1)S(1)}, u32[]{:S(2)}, u32[]{:S(2)}) collective-permute-start(bf16[32,2048]{1,0:T(8,128)(2,1)S(1)} %settle.1.refs_0_), channel_id=1, source_target_pairs={{0,3},{1,2},{2,1},{3,0},{4,7},{5,6},{6,5},{7,4},{8,11},{9,10},{10,... | collective-permute-start | bytes 393224 | tf_op jit(solution)/shard_map/ppermute | solution.py:25
  38.8 0.6 %collective-permute-start.11 = (bf16[32,2048]{1,0:T(8,128)(2,1)S(1)}, bf16[32,2048]{1,0:T(8,128)(2,1)S(1)}, u32[]{:S(2)}, u32[]{:S(2)}) collective-permute-start(bf16[32,2048]{1,0:T(8,128)(2,1)S(1)} %settle.1.refs_0_), channel_id=1, source_target_pairs={{0,1},{1,0},{2,3},{3,2},{4,5},{5,4},{6,7},{7,6},{8,9},{9,8},{10,11... | collective-permute-start | bytes 393224 | tf_op jit(solution)/shard_map/ppermute | solution.py:25
  39.4 0.8 %project.4.refs_2_ = f32[32,1024]{1,0:T(8,128)S(1)} custom-call(bf16[32,2048]{1,0:T(8,128)(2,1)S(1)} %settle.1.refs_0_, bf16[8192,1024]{1,0:T(8,128)(2,1)S(1)} %bitcast.6), custom_call_target="tpu_custom_call" | custom-call | tf_op jit(solution)/shard_map/project/pallas_call | solution.py:322
  40.2 0.6 %collective-permute-done.13.refs_0_ = bf16[32,2048]{1,0:T(8,128)(2,1)S(1)} collective-permute-done((bf16[32,2048]{1,0:T(8,128)(2,1)S(1)}, bf16[32,2048]{1,0:T(8,128)(2,1)S(1)}, u32[]{:S(2)}, u32[]{:S(2)}) %collective-permute-start.13) | collective-permute-done | bytes 131104 | tf_op jit(solution)/shard_map/ppermute | solution.py:25
  40.9 0.8 %project.5.refs_2_ = f32[32,1024]{1,0:T(8,128)S(1)} custom-call(bf16[32,2048]{1,0:T(8,128)(2,1)S(1)} %collective-permute-done.13.refs_0_, bf16[8192,1024]{1,0:T(8,128)(2,1)S(1)} %bitcast.6, f32[32,1024]{1,0:T(8,128)S(1)} %project.4.refs_2_), custom_call_target="tpu_custom_call" | custom-call | tf_op jit(solution)/shard_map/project/pallas_call | solution.py:322
  41.7 1.6 %collective-permute-done.12.refs_0_ = bf16[32,2048]{1,0:T(8,128)(2,1)S(1)} collective-permute-done((bf16[32,2048]{1,0:T(8,128)(2,1)S(1)}, bf16[32,2048]{1,0:T(8,128)(2,1)S(1)}, u32[]{:S(2)}, u32[]{:S(2)}) %collective-permute-start.12) | collective-permute-done | bytes 131104 | tf_op jit(solution)/shard_map/ppermute | solution.py:25
  43.3 0.8 %project.6.refs_2_ = f32[32,1024]{1,0:T(8,128)S(1)} custom-call(bf16[32,2048]{1,0:T(8,128)(2,1)S(1)} %collective-permute-done.12.refs_0_, bf16[8192,1024]{1,0:T(8,128)(2,1)S(1)} %bitcast.6, f32[32,1024]{1,0:T(8,128)S(1)} %project.5.refs_2_), custom_call_target="tpu_custom_call" | custom-call | tf_op jit(solution)/shard_map/project/pallas_call | solution.py:322
  44.1 0.5 %collective-permute-done.11.refs_0_ = bf16[32,2048]{1,0:T(8,128)(2,1)S(1)} collective-permute-done((bf16[32,2048]{1,0:T(8,128)(2,1)S(1)}, bf16[32,2048]{1,0:T(8,128)(2,1)S(1)}, u32[]{:S(2)}, u32[]{:S(2)}) %collective-permute-start.11) | collective-permute-done | bytes 131104 | tf_op jit(solution)/shard_map/ppermute | solution.py:25
  44.6 0.8 %project.7 = bf16[32,1024]{1,0:T(8,128)(2,1)S(1)} custom-call(bf16[32,2048]{1,0:T(8,128)(2,1)S(1)} %collective-permute-done.11.refs_0_, bf16[8192,1024]{1,0:T(8,128)(2,1)S(1)} %bitcast.6, f32[32,1024]{1,0:T(8,128)S(1)} %project.6.refs_2_), custom_call_target="tpu_custom_call" | custom-call | tf_op jit(solution)/shard_map/project/pallas_call | solution.py:322
  45.4 0.0 collective-permute-start.14
  45.4 3.7 %collective-permute-done.14 = bf16[32,1024]{1,0:T(8,128)(2,1)S(1)} collective-permute-done((bf16[32,1024]{1,0:T(8,128)(2,1)S(1)}, bf16[32,1024]{1,0:T(8,128)(2,1)S(1)}, u32[]{:S(2)}, u32[]{:S(2)}) %collective-permute-start.14) | collective-permute-done | bytes 65568 | tf_op jit(solution)/shard_map/ppermute | solution.py:30
  49.1 0.6 %copy.10 = bf16[32,1024]{1,0:T(8,128)(2,1)} copy(bf16[32,1024]{1,0:T(8,128)(2,1)S(1)} %collective-permute-done.14) | data formatting | bytes 131072
  (12 shorter events, 0.0 us)
Async XLA Ops:
  0.0 15.0 %copy-start = (bf16[4,8192]{1,0:T(4,128)(2,1)S(1)}, bf16[4,8192]{1,0:T(4,128)(2,1)}, u32[]{:S(2)}) copy-start(bf16[4,8192]{1,0:T(4,128)(2,1)} %param.5) | copy-start | bytes 196612
  0.0 15.0 %slice-start.4 = ((s8[8388608]{0:T(1024)(128)(4,1)}), s8[4194304]{0:T(1024)(128)(4,1)S(1)}, s32[]{:S(2)}) async-start(s8[8388608]{0:T(1024)(128)(4,1)} %bitcast.7), calls=%async_computation.4 | async-start | bytes 8388608
  0.0 15.0 %slice-start.5 = ((s8[8388608]{0:T(1024)(128)(4,1)}), s8[4194304]{0:T(1024)(128)(4,1)S(1)}, s32[]{:S(2)}) async-start(s8[8388608]{0:T(1024)(128)(4,1)} %bitcast.7), calls=%async_computation.5 | async-start | bytes 8388608
  0.0 7.6 %collective-permute-start = (bf16[8,32,128]{2,1,0:T(8,128)(2,1)}, bf16[8,32,128]{2,1,0:T(8,128)(2,1)S(1)}, u32[]{:S(2)}, u32[]{:S(2)}) collective-permute-start(bf16[8,32,128]{2,1,0:T(8,128)(2,1)} %bitcast.9), channel_id=1, source_target_pairs={{0,4},{1,5},{2,6},{3,7},{4,0},{5,1},{6,2},{7,3},{8,12},{9,13},{10,... | collective-permute-start | bytes 196616 | tf_op jit(solution)/shard_map/ppermute | solution.py:25
  4.1 6.6 %collective-permute-start.5 = (bf16[8,32,128]{2,1,0:T(8,128)(2,1)}, bf16[8,32,128]{2,1,0:T(8,128)(2,1)S(1)}, u32[]{:S(2)}, u32[]{:S(2)}) collective-permute-start(bf16[8,32,128]{2,1,0:T(8,128)(2,1)} %bitcast.10), channel_id=1, source_target_pairs={{0,3},{1,2},{2,1},{3,0},{4,7},{5,6},{6,5},{7,4},{8,11},{9,10},{10,... | collective-permute-start | bytes 196616 | tf_op jit(solution)/shard_map/ppermute | solution.py:25
  6.6 6.8 %collective-permute-start.3 = (bf16[8,32,128]{2,1,0:T(8,128)(2,1)}, bf16[8,32,128]{2,1,0:T(8,128)(2,1)S(1)}, u32[]{:S(2)}, u32[]{:S(2)}) collective-permute-start(bf16[8,32,128]{2,1,0:T(8,128)(2,1)} %bitcast.11), channel_id=1, source_target_pairs={{0,2},{1,3},{2,0},{3,1},{4,6},{5,7},{6,4},{7,5},{8,10},{9,11},{10,... | collective-permute-start | bytes 196616 | tf_op jit(solution)/shard_map/ppermute | solution.py:25
  7.1 6.4 %collective-permute-start.1 = (bf16[8,32,128]{2,1,0:T(8,128)(2,1)}, bf16[8,32,128]{2,1,0:T(8,128)(2,1)S(1)}, u32[]{:S(2)}, u32[]{:S(2)}) collective-permute-start(bf16[8,32,128]{2,1,0:T(8,128)(2,1)} %bitcast.12), channel_id=1, source_target_pairs={{0,1},{1,0},{2,3},{3,2},{4,5},{5,4},{6,7},{7,6},{8,9},{9,8},{10,11... | collective-permute-start | bytes 196616 | tf_op jit(solution)/shard_map/ppermute | solution.py:25
  7.6 5.8 %collective-permute-start.6 = (bf16[8,32,128]{2,1,0:T(8,128)(2,1)S(1)}, bf16[8,32,128]{2,1,0:T(8,128)(2,1)S(1)}, u32[]{:S(2)}, u32[]{:S(2)}) collective-permute-start(bf16[8,32,128]{2,1,0:T(8,128)(2,1)S(1)} %collective-permute-done.refs_1_), channel_id=1, source_target_pairs={{0,3},{1,2},{2,1},{3,0},{4,7},{5,6},{6,5},{7,4},{8,11},{9,10},{10,... | collective-permute-start | bytes 196616 | tf_op jit(solution)/shard_map/ppermute | solution.py:25
  10.1 4.3 %collective-permute-start.4 = (bf16[8,32,128]{2,1,0:T(8,128)(2,1)S(1)}, bf16[8,32,128]{2,1,0:T(8,128)(2,1)S(1)}, u32[]{:S(2)}, u32[]{:S(2)}) collective-permute-start(bf16[8,32,128]{2,1,0:T(8,128)(2,1)S(1)} %collective-permute-done.refs_1_), channel_id=1, source_target_pairs={{0,2},{1,3},{2,0},{3,1},{4,6},{5,7},{6,4},{7,5},{8,10},{9,11},{10,... | collective-permute-start | bytes 196616 | tf_op jit(solution)/shard_map/ppermute | solution.py:25
  10.7 4.3 %collective-permute-start.2 = (bf16[8,32,128]{2,1,0:T(8,128)(2,1)S(1)}, bf16[8,32,128]{2,1,0:T(8,128)(2,1)S(1)}, u32[]{:S(2)}, u32[]{:S(2)}) collective-permute-start(bf16[8,32,128]{2,1,0:T(8,128)(2,1)S(1)} %collective-permute-done.refs_1_), channel_id=1, source_target_pairs={{0,1},{1,0},{2,3},{3,2},{4,5},{5,4},{6,7},{7,6},{8,9},{9,8},{10,11... | collective-permute-start | bytes 196616 | tf_op jit(solution)/shard_map/ppermute | solution.py:25
  16.7 22.7 %slice-start = ((s8[16777216]{0:T(1024)(128)(4,1)}), s8[4194304]{0:T(1024)(128)(4,1)S(1)}, s32[]{:S(2)}) async-start(s8[16777216]{0:T(1024)(128)(4,1)} %bitcast.5), calls=%async_computation | async-start | bytes 8388608
  16.7 22.7 %slice-start.1 = ((s8[16777216]{0:T(1024)(128)(4,1)}), s8[4194304]{0:T(1024)(128)(4,1)S(1)}, s32[]{:S(2)}) async-start(s8[16777216]{0:T(1024)(128)(4,1)} %bitcast.5), calls=%async_computation.1 | async-start | bytes 8388608
  16.7 8.7 %collective-permute-start.7 = (bf16[528,128]{1,0:T(8,128)(2,1)S(1)}, bf16[528,128]{1,0:T(8,128)(2,1)S(1)}, u32[]{:S(2)}, u32[]{:S(2)}) collective-permute-start(bf16[528,128]{1,0:T(8,128)(2,1)S(1)} %attend.5), channel_id=1, source_target_pairs={{0,3},{1,2},{2,1},{3,0},{4,7},{5,6},{6,5},{7,4},{8,11},{9,10},{10,... | collective-permute-start | bytes 405512 | tf_op jit(solution)/shard_map/ppermute | solution.py:25
  19.9 19.5 %slice-start.2 = ((s8[16777216]{0:T(1024)(128)(4,1)}), s8[4194304]{0:T(1024)(128)(4,1)S(1)}, s32[]{:S(2)}) async-start(s8[16777216]{0:T(1024)(128)(4,1)} %bitcast.5), calls=%async_computation.2 | async-start | bytes 8388608
  19.9 5.6 %collective-permute-start.8 = (bf16[528,128]{1,0:T(8,128)(2,1)S(1)}, bf16[528,128]{1,0:T(8,128)(2,1)S(1)}, u32[]{:S(2)}, u32[]{:S(2)}) collective-permute-start(bf16[528,128]{1,0:T(8,128)(2,1)S(1)} %attend.6), channel_id=1, source_target_pairs={{0,2},{1,3},{2,0},{3,1},{4,6},{5,7},{6,4},{7,5},{8,10},{9,11},{10,... | collective-permute-start | bytes 405512 | tf_op jit(solution)/shard_map/ppermute | solution.py:25
  22.8 16.6 %slice-start.3 = ((s8[16777216]{0:T(1024)(128)(4,1)}), s8[4194304]{0:T(1024)(128)(4,1)S(1)}, s32[]{:S(2)}) async-start(s8[16777216]{0:T(1024)(128)(4,1)} %bitcast.5), calls=%async_computation.3 | async-start | bytes 8388608
  22.8 5.1 %collective-permute-start.9 = (bf16[528,128]{1,0:T(8,128)(2,1)S(1)}, bf16[528,128]{1,0:T(8,128)(2,1)S(1)}, u32[]{:S(2)}, u32[]{:S(2)}) collective-permute-start(bf16[528,128]{1,0:T(8,128)(2,1)S(1)} %attend.7), channel_id=1, source_target_pairs={{0,1},{1,0},{2,3},{3,2},{4,5},{5,4},{6,7},{7,6},{8,9},{9,8},{10,11... | collective-permute-start | bytes 405512 | tf_op jit(solution)/shard_map/ppermute | solution.py:25
  28.2 7.1 %collective-permute-start.10 = (bf16[528,128]{1,0:T(8,128)(2,1)S(1)}, bf16[528,128]{1,0:T(8,128)(2,1)S(1)}, u32[]{:S(2)}, u32[]{:S(2)}) collective-permute-start(bf16[528,128]{1,0:T(8,128)(2,1)S(1)} %get-tuple-element.20.own_ref), channel_id=1, source_target_pairs={{0,6},{1,7},{2,4},{3,5},{4,2},{5,3},{6,0},{7,1},{8,14},{9,15},{10,... | collective-permute-start | bytes 405512 | tf_op jit(solution)/shard_map/ppermute | solution.py:25
  35.8 5.0 %collective-permute-start.13 = (bf16[32,2048]{1,0:T(8,128)(2,1)S(1)}, bf16[32,2048]{1,0:T(8,128)(2,1)S(1)}, u32[]{:S(2)}, u32[]{:S(2)}) collective-permute-start(bf16[32,2048]{1,0:T(8,128)(2,1)S(1)} %settle.1.refs_0_), channel_id=1, source_target_pairs={{0,2},{1,3},{2,0},{3,1},{4,6},{5,7},{6,4},{7,5},{8,10},{9,11},{10,... | collective-permute-start | bytes 393224 | tf_op jit(solution)/shard_map/ppermute | solution.py:25
  35.9 7.3 %collective-permute-start.12 = (bf16[32,2048]{1,0:T(8,128)(2,1)S(1)}, bf16[32,2048]{1,0:T(8,128)(2,1)S(1)}, u32[]{:S(2)}, u32[]{:S(2)}) collective-permute-start(bf16[32,2048]{1,0:T(8,128)(2,1)S(1)} %settle.1.refs_0_), channel_id=1, source_target_pairs={{0,3},{1,2},{2,1},{3,0},{4,7},{5,6},{6,5},{7,4},{8,11},{9,10},{10,... | collective-permute-start | bytes 393224 | tf_op jit(solution)/shard_map/ppermute | solution.py:25
  38.8 5.8 %collective-permute-start.11 = (bf16[32,2048]{1,0:T(8,128)(2,1)S(1)}, bf16[32,2048]{1,0:T(8,128)(2,1)S(1)}, u32[]{:S(2)}, u32[]{:S(2)}) collective-permute-start(bf16[32,2048]{1,0:T(8,128)(2,1)S(1)} %settle.1.refs_0_), channel_id=1, source_target_pairs={{0,1},{1,0},{2,3},{3,2},{4,5},{5,4},{6,7},{7,6},{8,9},{9,8},{10,11... | collective-permute-start | bytes 393224 | tf_op jit(solution)/shard_map/ppermute | solution.py:25
  45.4 3.7 %collective-permute-start.14 = (bf16[32,1024]{1,0:T(8,128)(2,1)S(1)}, bf16[32,1024]{1,0:T(8,128)(2,1)S(1)}, u32[]{:S(2)}, u32[]{:S(2)}) collective-permute-start(bf16[32,1024]{1,0:T(8,128)(2,1)S(1)} %project.7), channel_id=1, source_target_pairs={{0,8},{8,16},{16,24},{24,0},{1,9},{9,17},{17,25},{25,1},{2,10},{10... | collective-permute-start | bytes 196616 | tf_op jit(solution)/shard_map/ppermute | solution.py:30

commit v16 on v11

--- a/solution.py
+++ b/solution.py
@@ -153,7 +153,7 @@
     for unit, group in enumerate(groups):
         if plan.by_device:
             for block, ref in enumerate(query_refs):
-                device = me ^ (block // 2) ^ (block % 2 * plan.half)
+                device = me ^ (-(block // 2) % plan.half) ^ (block % 2 * plan.half)
                 to = pl.multiple_of(device * GROUP * plan.rows_here, GROUP * plan.rows_here)
                 held_ref[unit, pl.ds(to, GROUP * plan.rows_here), :] = ref[group]
             queries = held_ref[unit]
@@ -338,10 +338,10 @@
     far = swap(own, "ctx", half)
     near = [swap(own, "ctx", k) for k in range(1, half)]
     order, one_hot = row_order(plan)
-    bias = mask(cache.shape[0], offsets, starts, near[-1])
+    bias = mask(cache.shape[0], offsets, starts, near[0])
     if plan.by_device:
         gathered = [own, far]
-        for k in range(1, half):
+        for k in reversed(range(1, half)):
             gathered += [near[k - 1], swap(far, "ctx", k)]
     else:
         pair = jnp.concatenate([own, far], axis=1)

time: 49.1 us -> 49.7 us (1.012)
  waiting for transfers between devices: 12.8 us -> 13.7 us
    ppermute x14, waiting for transfers between devices: 9.14 us -> 10 us  [swap(): return lax.ppermute(value, axis, [(i, i ^ bits) for i in range(devices)])]
  transfers between devices with their start and end apart: 15 -> 15, of which waited for: 8 -> 7; matrix products, arithmetic and copies ran while one was open for 0% -> 0% of each run, Pallas kernels for 17% -> 17%
where the time goes in v16:
time: 49.7 us; the launch traced here: 49.5 us
  starting transfers between devices  22 us (44%)
  waiting for transfers between devices  13.7 us (28%)
  Pallas kernels  11.7 us (24%)
  between operations  1.48 us (3%)
  local copies, waits for them, and re-layouts  0.67 us (1%)
    ppermute x14, starting transfers between devices, swap(): return lax.ppermute(value, axis, [(i, i ^ bits) for i in range(devices)])  22 us
    ppermute x14, waiting for transfers between devices, swap(): return lax.ppermute(value, axis, [(i, i ^ bits) for i in range(devices)])  10 us
    pallas_call x4, Pallas kernels, attend(): local(functools.partial(attend_kernel, plan, part), out_shape, [pltpu.VME...  6.74 us
    ppermute x1, waiting for transfers between devices, from_behind(): lax.ppermute(value, axis, [(i, (i + by) % devices) for i in range(devices)])  3.69 us
    pallas_call x4, Pallas kernels, project(): local(functools.partial(project_kernel, plan, part), jax.ShapeDtypeStruct...  3.29 us
  transfers between devices with their start and end apart: 15, of which 7 were waited for; matrix products, arithmetic and copies ran while one was open for 0% of the time, Pallas kernels for 17%

profile of v16, /device:TPU:0, one launch (start us, length us, event | category | flops | bytes accessed | tf_op | source)
XLA Modules:
  0.0 49.5 jit_solution(17150716393748819147)
XLA Ops:
  0.0 4.1 %collective-permute-start = (bf16[8,32,128]{2,1,0:T(8,128)(2,1)}, bf16[8,32,128]{2,1,0:T(8,128)(2,1)S(1)}, u32[]{:S(2)}, u32[]{:S(2)}) collective-permute-start(bf16[8,32,128]{2,1,0:T(8,128)(2,1)} %bitcast.9), channel_id=1, source_target_pairs={{0,4},{1,5},{2,6},{3,7},{4,0},{5,1},{6,2},{7,3},{8,12},{9,13},{10,... | collective-permute-start | bytes 196616 | tf_op jit(solution)/shard_map/ppermute | solution.py:25
  4.1 1.5 %collective-permute-start.5 = (bf16[8,32,128]{2,1,0:T(8,128)(2,1)}, bf16[8,32,128]{2,1,0:T(8,128)(2,1)S(1)}, u32[]{:S(2)}, u32[]{:S(2)}) collective-permute-start(bf16[8,32,128]{2,1,0:T(8,128)(2,1)} %bitcast.10), channel_id=1, source_target_pairs={{0,1},{1,0},{2,3},{3,2},{4,5},{5,4},{6,7},{7,6},{8,9},{9,8},{10,11... | collective-permute-start | bytes 196616 | tf_op jit(solution)/shard_map/ppermute | solution.py:25
  5.6 1.6 %collective-permute-start.3 = (bf16[8,32,128]{2,1,0:T(8,128)(2,1)}, bf16[8,32,128]{2,1,0:T(8,128)(2,1)S(1)}, u32[]{:S(2)}, u32[]{:S(2)}) collective-permute-start(bf16[8,32,128]{2,1,0:T(8,128)(2,1)} %bitcast.11), channel_id=1, source_target_pairs={{0,2},{1,3},{2,0},{3,1},{4,6},{5,7},{6,4},{7,5},{8,10},{9,11},{10,... | collective-permute-start | bytes 196616 | tf_op jit(solution)/shard_map/ppermute | solution.py:25
  7.2 0.4 collective-permute-start.1
  7.6 0.0 collective-permute-done.refs_1_
  7.6 1.6 %collective-permute-start.6 = (bf16[8,32,128]{2,1,0:T(8,128)(2,1)S(1)}, bf16[8,32,128]{2,1,0:T(8,128)(2,1)S(1)}, u32[]{:S(2)}, u32[]{:S(2)}) collective-permute-start(bf16[8,32,128]{2,1,0:T(8,128)(2,1)S(1)} %collective-permute-done.refs_1_), channel_id=1, source_target_pairs={{0,1},{1,0},{2,3},{3,2},{4,5},{5,4},{6,7},{7,6},{8,9},{9,8},{10,11... | collective-permute-start | bytes 196616 | tf_op jit(solution)/shard_map/ppermute | solution.py:25
  9.2 1.5 %collective-permute-start.4 = (bf16[8,32,128]{2,1,0:T(8,128)(2,1)S(1)}, bf16[8,32,128]{2,1,0:T(8,128)(2,1)S(1)}, u32[]{:S(2)}, u32[]{:S(2)}) collective-permute-start(bf16[8,32,128]{2,1,0:T(8,128)(2,1)S(1)} %collective-permute-done.refs_1_), channel_id=1, source_target_pairs={{0,2},{1,3},{2,0},{3,1},{4,6},{5,7},{6,4},{7,5},{8,10},{9,11},{10,... | collective-permute-start | bytes 196616 | tf_op jit(solution)/shard_map/ppermute | solution.py:25
  10.7 0.0 collective-permute-done.5.after_ref.refs_6_
  10.7 1.2 %collective-permute-start.2 = (bf16[8,32,128]{2,1,0:T(8,128)(2,1)S(1)}, bf16[8,32,128]{2,1,0:T(8,128)(2,1)S(1)}, u32[]{:S(2)}, u32[]{:S(2)}) collective-permute-start(bf16[8,32,128]{2,1,0:T(8,128)(2,1)S(1)} %collective-permute-done.refs_1_), channel_id=1, source_target_pairs={{0,3},{1,2},{2,1},{3,0},{4,7},{5,6},{6,5},{7,4},{8,11},{9,10},{10,... | collective-permute-start | bytes 196616 | tf_op jit(solution)/shard_map/ppermute | solution.py:25
  11.9 0.1 order.1
  13.3 0.2 mask.1.refs_9_
  13.5 0.0 collective-permute-done.3.refs_4_
  13.6 0.0 collective-permute-done.1.refs_2_
  13.6 0.0 collective-permute-done.6.refs_7_
  13.6 0.0 collective-permute-done.4.refs_5_
  13.6 2.3 %collective-permute-done.2.refs_3_ = bf16[8,32,128]{2,1,0:T(8,128)(2,1)S(1)} collective-permute-done((bf16[8,32,128]{2,1,0:T(8,128)(2,1)S(1)}, bf16[8,32,128]{2,1,0:T(8,128)(2,1)S(1)}, u32[]{:S(2)}, u32[]{:S(2)}) %collective-permute-start.2) | collective-permute-done | bytes 65568 | tf_op jit(solution)/shard_map/ppermute | solution.py:25
  15.9 1.7 %attend.5 = bf16[528,128]{1,0:T(8,128)(2,1)S(1)} custom-call(bf16[8,32,128]{2,1,0:T(8,128)(2,1)S(1)} %bitcast.13, bf16[8,32,128]{2,1,0:T(8,128)(2,1)S(1)} %collective-permute-done.refs_1_, bf16[8,32,128]{2,1,0:T(8,128)(2,1)S(1)} %collective-permute-done.1.refs_2_, bf16[8,32,128]{2,1,0:T(8,128)(2,1)S(1)} %collective-permute-done.2.refs_3_, ...), custom_call_target="tpu_custom_call" | custom-call | flops 536870912 | bytes 2097152 | tf_op jit(solution)/shard_map/attend/pallas_call | solution.py:203
  17.6 0.0 slice-start
  17.6 0.0 slice-start.1
  17.6 1.2 %collective-permute-start.7 = (bf16[528,128]{1,0:T(8,128)(2,1)S(1)}, bf16[528,128]{1,0:T(8,128)(2,1)S(1)}, u32[]{:S(2)}, u32[]{:S(2)}) collective-permute-start(bf16[528,128]{1,0:T(8,128)(2,1)S(1)} %attend.5), channel_id=1, source_target_pairs={{0,3},{1,2},{2,1},{3,0},{4,7},{5,6},{6,5},{7,4},{8,11},{9,10},{10,... | collective-permute-start | bytes 405512 | tf_op jit(solution)/shard_map/ppermute | solution.py:25
  18.9 1.7 %attend.6 = bf16[528,128]{1,0:T(8,128)(2,1)S(1)} custom-call(bf16[8,32,128]{2,1,0:T(8,128)(2,1)S(1)} %bitcast.14, bf16[8,32,128]{2,1,0:T(8,128)(2,1)S(1)} %collective-permute-done.refs_1_, bf16[8,32,128]{2,1,0:T(8,128)(2,1)S(1)} %collective-permute-done.1.refs_2_, bf16[8,32,128]{2,1,0:T(8,128)(2,1)S(1)} %collective-permute-done.2.refs_3_, ...), custom_call_target="tpu_custom_call" | custom-call | flops 536870912 | bytes 2097152 | tf_op jit(solution)/shard_map/attend/pallas_call | solution.py:203
  20.6 0.0 slice-start.2
  20.6 0.8 %collective-permute-start.8 = (bf16[528,128]{1,0:T(8,128)(2,1)S(1)}, bf16[528,128]{1,0:T(8,128)(2,1)S(1)}, u32[]{:S(2)}, u32[]{:S(2)}) collective-permute-start(bf16[528,128]{1,0:T(8,128)(2,1)S(1)} %attend.6), channel_id=1, source_target_pairs={{0,2},{1,3},{2,0},{3,1},{4,6},{5,7},{6,4},{7,5},{8,10},{9,11},{10,... | collective-permute-start | bytes 405512 | tf_op jit(solution)/shard_map/ppermute | solution.py:25
  21.4 1.7 %attend.7 = bf16[528,128]{1,0:T(8,128)(2,1)S(1)} custom-call(bf16[8,32,128]{2,1,0:T(8,128)(2,1)S(1)} %bitcast.15, bf16[8,32,128]{2,1,0:T(8,128)(2,1)S(1)} %collective-permute-done.refs_1_, bf16[8,32,128]{2,1,0:T(8,128)(2,1)S(1)} %collective-permute-done.1.refs_2_, bf16[8,32,128]{2,1,0:T(8,128)(2,1)S(1)} %collective-permute-done.2.refs_3_, ...), custom_call_target="tpu_custom_call" | custom-call | flops 536870912 | bytes 2097152 | tf_op jit(solution)/shard_map/attend/pallas_call | solution.py:203
  23.1 0.0 slice-start.3
  23.1 1.5 %collective-permute-start.9 = (bf16[528,128]{1,0:T(8,128)(2,1)S(1)}, bf16[528,128]{1,0:T(8,128)(2,1)S(1)}, u32[]{:S(2)}, u32[]{:S(2)}) collective-permute-start(bf16[528,128]{1,0:T(8,128)(2,1)S(1)} %attend.7), channel_id=1, source_target_pairs={{0,1},{1,0},{2,3},{3,2},{4,5},{5,4},{6,7},{7,6},{8,9},{9,8},{10,11... | collective-permute-start | bytes 405512 | tf_op jit(solution)/shard_map/ppermute | solution.py:25
  24.6 1.6 %attend.4 = (f32[512,128]{1,0:T(8,128)S(1)}, bf16[16,128]{1,0:T(8,128)(2,1)S(1)}) custom-call(bf16[8,32,128]{2,1,0:T(8,128)(2,1)S(1)} %bitcast.16, bf16[8,32,128]{2,1,0:T(8,128)(2,1)S(1)} %collective-permute-done.refs_1_, bf16[8,32,128]{2,1,0:T(8,128)(2,1)S(1)} %collective-permute-done.1.refs_2_, bf16[8,32,128]{2,1,0:T(8,128)(2,1)S(1)} %collective-permute-done.2.refs_3_, ...), custom_call_target="tpu_custom_call" | custom-call | flops 536870912 | bytes 2097152 | tf_op jit(solution)/shard_map/attend/pallas_call | solution.py:203
  26.3 0.0 collective-permute-done.7.refs_0_
  26.3 0.0 collective-permute-done.8.refs_1_
  26.3 0.4 merge.2
  26.7 1.5 %collective-permute-done.9.refs_0_ = bf16[528,128]{1,0:T(8,128)(2,1)S(1)} collective-permute-done((bf16[528,128]{1,0:T(8,128)(2,1)S(1)}, bf16[528,128]{1,0:T(8,128)(2,1)S(1)}, u32[]{:S(2)}, u32[]{:S(2)}) %collective-permute-start.9) | collective-permute-done | bytes 135200 | tf_op jit(solution)/shard_map/ppermute | solution.py:25
  28.2 0.3 merge.3
  28.5 3.0 %collective-permute-start.10 = (bf16[528,128]{1,0:T(8,128)(2,1)S(1)}, bf16[528,128]{1,0:T(8,128)(2,1)S(1)}, u32[]{:S(2)}, u32[]{:S(2)}) collective-permute-start(bf16[528,128]{1,0:T(8,128)(2,1)S(1)} %get-tuple-element.20.own_ref), channel_id=1, source_target_pairs={{0,6},{1,7},{2,4},{3,5},{4,2},{5,3},{6,0},{7,1},{8,14},{9,15},{10,... | collective-permute-start | bytes 405512 | tf_op jit(solution)/shard_map/ppermute | solution.py:25
  31.5 4.0 %collective-permute-done.10.other_ref = bf16[528,128]{1,0:T(8,128)(2,1)S(1)} collective-permute-done((bf16[528,128]{1,0:T(8,128)(2,1)S(1)}, bf16[528,128]{1,0:T(8,128)(2,1)S(1)}, u32[]{:S(2)}, u32[]{:S(2)}) %collective-permute-start.10) | collective-permute-done | bytes 135200 | tf_op jit(solution)/shard_map/ppermute | solution.py:25
  35.5 0.6 %settle.1.refs_0_ = bf16[32,2048]{1,0:T(8,128)(2,1)S(1)} custom-call(f32[512,128]{1,0:T(8,128)S(1)} %get-tuple-element.19.wide_ref, bf16[528,128]{1,0:T(8,128)(2,1)S(1)} %get-tuple-element.20.own_ref, bf16[528,128]{1,0:T(8,128)(2,1)S(1)} %collective-permute-done.10.other_ref, bf16[256,256]{1,0:T(8,128)(2,1)S(1)} %get-tuple-element.13.refs_10_.order_ref), custom_call_target="tpu_custom_call" | custom-call | tf_op jit(solution)/shard_map/settle/pallas_call | solution.py:302
  36.1 1.6 %collective-permute-start.13 = (bf16[32,2048]{1,0:T(8,128)(2,1)S(1)}, bf16[32,2048]{1,0:T(8,128)(2,1)S(1)}, u32[]{:S(2)}, u32[]{:S(2)}) collective-permute-start(bf16[32,2048]{1,0:T(8,128)(2,1)S(1)} %settle.1.refs_0_), channel_id=1, source_target_pairs={{0,1},{1,0},{2,3},{3,2},{4,5},{5,4},{6,7},{7,6},{8,9},{9,8},{10,11... | collective-permute-start | bytes 393224 | tf_op jit(solution)/shard_map/ppermute | solution.py:25
  37.7 0.9 %collective-permute-start.12 = (bf16[32,2048]{1,0:T(8,128)(2,1)S(1)}, bf16[32,2048]{1,0:T(8,128)(2,1)S(1)}, u32[]{:S(2)}, u32[]{:S(2)}) collective-permute-start(bf16[32,2048]{1,0:T(8,128)(2,1)S(1)} %settle.1.refs_0_), channel_id=1, source_target_pairs={{0,2},{1,3},{2,0},{3,1},{4,6},{5,7},{6,4},{7,5},{8,10},{9,11},{10,... | collective-permute-start | bytes 393224 | tf_op jit(solution)/shard_map/ppermute | solution.py:25
  38.5 1.1 %collective-permute-start.11 = (bf16[32,2048]{1,0:T(8,128)(2,1)S(1)}, bf16[32,2048]{1,0:T(8,128)(2,1)S(1)}, u32[]{:S(2)}, u32[]{:S(2)}) collective-permute-start(bf16[32,2048]{1,0:T(8,128)(2,1)S(1)} %settle.1.refs_0_), channel_id=1, source_target_pairs={{0,3},{1,2},{2,1},{3,0},{4,7},{5,6},{6,5},{7,4},{8,11},{9,10},{10,... | collective-permute-start | bytes 393224 | tf_op jit(solution)/shard_map/ppermute | solution.py:25
  39.7 0.8 %project.4.refs_2_ = f32[32,1024]{1,0:T(8,128)S(1)} custom-call(bf16[32,2048]{1,0:T(8,128)(2,1)S(1)} %settle.1.refs_0_, bf16[8192,1024]{1,0:T(8,128)(2,1)S(1)} %bitcast.6), custom_call_target="tpu_custom_call" | custom-call | tf_op jit(solution)/shard_map/project/pallas_call | solution.py:322
  40.5 0.6 %collective-permute-done.13.refs_0_ = bf16[32,2048]{1,0:T(8,128)(2,1)S(1)} collective-permute-done((bf16[32,2048]{1,0:T(8,128)(2,1)S(1)}, bf16[32,2048]{1,0:T(8,128)(2,1)S(1)}, u32[]{:S(2)}, u32[]{:S(2)}) %collective-permute-start.13) | collective-permute-done | bytes 131104 | tf_op jit(solution)/shard_map/ppermute | solution.py:25
  41.1 0.8 %project.5.refs_2_ = f32[32,1024]{1,0:T(8,128)S(1)} custom-call(bf16[32,2048]{1,0:T(8,128)(2,1)S(1)} %collective-permute-done.13.refs_0_, bf16[8192,1024]{1,0:T(8,128)(2,1)S(1)} %bitcast.6, f32[32,1024]{1,0:T(8,128)S(1)} %project.4.refs_2_), custom_call_target="tpu_custom_call" | custom-call | tf_op jit(solution)/shard_map/project/pallas_call | solution.py:322
  41.9 0.7 %collective-permute-done.12.refs_0_ = bf16[32,2048]{1,0:T(8,128)(2,1)S(1)} collective-permute-done((bf16[32,2048]{1,0:T(8,128)(2,1)S(1)}, bf16[32,2048]{1,0:T(8,128)(2,1)S(1)}, u32[]{:S(2)}, u32[]{:S(2)}) %collective-permute-start.12) | collective-permute-done | bytes 131104 | tf_op jit(solution)/shard_map/ppermute | solution.py:25
  42.6 0.8 %project.6.refs_2_ = f32[32,1024]{1,0:T(8,128)S(1)} custom-call(bf16[32,2048]{1,0:T(8,128)(2,1)S(1)} %collective-permute-done.12.refs_0_, bf16[8192,1024]{1,0:T(8,128)(2,1)S(1)} %bitcast.6, f32[32,1024]{1,0:T(8,128)S(1)} %project.5.refs_2_), custom_call_target="tpu_custom_call" | custom-call | tf_op jit(solution)/shard_map/project/pallas_call | solution.py:322
  43.5 0.9 %collective-permute-done.11.refs_0_ = bf16[32,2048]{1,0:T(8,128)(2,1)S(1)} collective-permute-done((bf16[32,2048]{1,0:T(8,128)(2,1)S(1)}, bf16[32,2048]{1,0:T(8,128)(2,1)S(1)}, u32[]{:S(2)}, u32[]{:S(2)}) %collective-permute-start.11) | collective-permute-done | bytes 131104 | tf_op jit(solution)/shard_map/ppermute | solution.py:25
  44.4 0.8 %project.7 = bf16[32,1024]{1,0:T(8,128)(2,1)S(1)} custom-call(bf16[32,2048]{1,0:T(8,128)(2,1)S(1)} %collective-permute-done.11.refs_0_, bf16[8192,1024]{1,0:T(8,128)(2,1)S(1)} %bitcast.6, f32[32,1024]{1,0:T(8,128)S(1)} %project.6.refs_2_), custom_call_target="tpu_custom_call" | custom-call | tf_op jit(solution)/shard_map/project/pallas_call | solution.py:322
  45.2 0.0 collective-permute-start.14
  45.2 3.7 %collective-permute-done.14 = bf16[32,1024]{1,0:T(8,128)(2,1)S(1)} collective-permute-done((bf16[32,1024]{1,0:T(8,128)(2,1)S(1)}, bf16[32,1024]{1,0:T(8,128)(2,1)S(1)}, u32[]{:S(2)}, u32[]{:S(2)}) %collective-permute-start.14) | collective-permute-done | bytes 65568 | tf_op jit(solution)/shard_map/ppermute | solution.py:30
  48.9 0.6 %copy.10 = bf16[32,1024]{1,0:T(8,128)(2,1)} copy(bf16[32,1024]{1,0:T(8,128)(2,1)S(1)} %collective-permute-done.14) | data formatting | bytes 131072
  (12 shorter events, 0.0 us)
Async XLA Ops:
  0.0 15.8 %copy-start = (bf16[4,8192]{1,0:T(4,128)(2,1)S(1)}, bf16[4,8192]{1,0:T(4,128)(2,1)}, u32[]{:S(2)}) copy-start(bf16[4,8192]{1,0:T(4,128)(2,1)} %param.5) | copy-start | bytes 196612
  0.0 15.8 %slice-start.4 = ((s8[8388608]{0:T(1024)(128)(4,1)}), s8[4194304]{0:T(1024)(128)(4,1)S(1)}, s32[]{:S(2)}) async-start(s8[8388608]{0:T(1024)(128)(4,1)} %bitcast.7), calls=%async_computation.4 | async-start | bytes 8388608
  0.0 15.8 %slice-start.5 = ((s8[8388608]{0:T(1024)(128)(4,1)}), s8[4194304]{0:T(1024)(128)(4,1)S(1)}, s32[]{:S(2)}) async-start(s8[8388608]{0:T(1024)(128)(4,1)} %bitcast.7), calls=%async_computation.5 | async-start | bytes 8388608
  0.0 7.6 %collective-permute-start = (bf16[8,32,128]{2,1,0:T(8,128)(2,1)}, bf16[8,32,128]{2,1,0:T(8,128)(2,1)S(1)}, u32[]{:S(2)}, u32[]{:S(2)}) collective-permute-start(bf16[8,32,128]{2,1,0:T(8,128)(2,1)} %bitcast.9), channel_id=1, source_target_pairs={{0,4},{1,5},{2,6},{3,7},{4,0},{5,1},{6,2},{7,3},{8,12},{9,13},{10,... | collective-permute-start | bytes 196616 | tf_op jit(solution)/shard_map/ppermute | solution.py:25
  4.1 6.6 %collective-permute-start.5 = (bf16[8,32,128]{2,1,0:T(8,128)(2,1)}, bf16[8,32,128]{2,1,0:T(8,128)(2,1)S(1)}, u32[]{:S(2)}, u32[]{:S(2)}) collective-permute-start(bf16[8,32,128]{2,1,0:T(8,128)(2,1)} %bitcast.10), channel_id=1, source_target_pairs={{0,1},{1,0},{2,3},{3,2},{4,5},{5,4},{6,7},{7,6},{8,9},{9,8},{10,11... | collective-permute-start | bytes 196616 | tf_op jit(solution)/shard_map/ppermute | solution.py:25
  5.6 7.9 %collective-permute-start.3 = (bf16[8,32,128]{2,1,0:T(8,128)(2,1)}, bf16[8,32,128]{2,1,0:T(8,128)(2,1)S(1)}, u32[]{:S(2)}, u32[]{:S(2)}) collective-permute-start(bf16[8,32,128]{2,1,0:T(8,128)(2,1)} %bitcast.11), channel_id=1, source_target_pairs={{0,2},{1,3},{2,0},{3,1},{4,6},{5,7},{6,4},{7,5},{8,10},{9,11},{10,... | collective-permute-start | bytes 196616 | tf_op jit(solution)/shard_map/ppermute | solution.py:25
  7.2 6.4 %collective-permute-start.1 = (bf16[8,32,128]{2,1,0:T(8,128)(2,1)}, bf16[8,32,128]{2,1,0:T(8,128)(2,1)S(1)}, u32[]{:S(2)}, u32[]{:S(2)}) collective-permute-start(bf16[8,32,128]{2,1,0:T(8,128)(2,1)} %bitcast.12), channel_id=1, source_target_pairs={{0,3},{1,2},{2,1},{3,0},{4,7},{5,6},{6,5},{7,4},{8,11},{9,10},{10,... | collective-permute-start | bytes 196616 | tf_op jit(solution)/shard_map/ppermute | solution.py:25
  7.6 6.0 %collective-permute-start.6 = (bf16[8,32,128]{2,1,0:T(8,128)(2,1)S(1)}, bf16[8,32,128]{2,1,0:T(8,128)(2,1)S(1)}, u32[]{:S(2)}, u32[]{:S(2)}) collective-permute-start(bf16[8,32,128]{2,1,0:T(8,128)(2,1)S(1)} %collective-permute-done.refs_1_), channel_id=1, source_target_pairs={{0,1},{1,0},{2,3},{3,2},{4,5},{5,4},{6,7},{7,6},{8,9},{9,8},{10,11... | collective-permute-start | bytes 196616 | tf_op jit(solution)/shard_map/ppermute | solution.py:25
  9.2 4.4 %collective-permute-start.4 = (bf16[8,32,128]{2,1,0:T(8,128)(2,1)S(1)}, bf16[8,32,128]{2,1,0:T(8,128)(2,1)S(1)}, u32[]{:S(2)}, u32[]{:S(2)}) collective-permute-start(bf16[8,32,128]{2,1,0:T(8,128)(2,1)S(1)} %collective-permute-done.refs_1_), channel_id=1, source_target_pairs={{0,2},{1,3},{2,0},{3,1},{4,6},{5,7},{6,4},{7,5},{8,10},{9,11},{10,... | collective-permute-start | bytes 196616 | tf_op jit(solution)/shard_map/ppermute | solution.py:25
  10.7 5.2 %collective-permute-start.2 = (bf16[8,32,128]{2,1,0:T(8,128)(2,1)S(1)}, bf16[8,32,128]{2,1,0:T(8,128)(2,1)S(1)}, u32[]{:S(2)}, u32[]{:S(2)}) collective-permute-start(bf16[8,32,128]{2,1,0:T(8,128)(2,1)S(1)} %collective-permute-done.refs_1_), channel_id=1, source_target_pairs={{0,3},{1,2},{2,1},{3,0},{4,7},{5,6},{6,5},{7,4},{8,11},{9,10},{10,... | collective-permute-start | bytes 196616 | tf_op jit(solution)/shard_map/ppermute | solution.py:25
  17.6 22.1 %slice-start = ((s8[16777216]{0:T(1024)(128)(4,1)}), s8[4194304]{0:T(1024)(128)(4,1)S(1)}, s32[]{:S(2)}) async-start(s8[16777216]{0:T(1024)(128)(4,1)} %bitcast.5), calls=%async_computation | async-start | bytes 8388608
  17.6 22.0 %slice-start.1 = ((s8[16777216]{0:T(1024)(128)(4,1)}), s8[4194304]{0:T(1024)(128)(4,1)S(1)}, s32[]{:S(2)}) async-start(s8[16777216]{0:T(1024)(128)(4,1)} %bitcast.5), calls=%async_computation.1 | async-start | bytes 8388608
  17.6 8.7 %collective-permute-start.7 = (bf16[528,128]{1,0:T(8,128)(2,1)S(1)}, bf16[528,128]{1,0:T(8,128)(2,1)S(1)}, u32[]{:S(2)}, u32[]{:S(2)}) collective-permute-start(bf16[528,128]{1,0:T(8,128)(2,1)S(1)} %attend.5), channel_id=1, source_target_pairs={{0,3},{1,2},{2,1},{3,0},{4,7},{5,6},{6,5},{7,4},{8,11},{9,10},{10,... | collective-permute-start | bytes 405512 | tf_op jit(solution)/shard_map/ppermute | solution.py:25
  20.6 19.1 %slice-start.2 = ((s8[16777216]{0:T(1024)(128)(4,1)}), s8[4194304]{0:T(1024)(128)(4,1)S(1)}, s32[]{:S(2)}) async-start(s8[16777216]{0:T(1024)(128)(4,1)} %bitcast.5), calls=%async_computation.2 | async-start | bytes 8388608
  20.6 5.7 %collective-permute-start.8 = (bf16[528,128]{1,0:T(8,128)(2,1)S(1)}, bf16[528,128]{1,0:T(8,128)(2,1)S(1)}, u32[]{:S(2)}, u32[]{:S(2)}) collective-permute-start(bf16[528,128]{1,0:T(8,128)(2,1)S(1)} %attend.6), channel_id=1, source_target_pairs={{0,2},{1,3},{2,0},{3,1},{4,6},{5,7},{6,4},{7,5},{8,10},{9,11},{10,... | collective-permute-start | bytes 405512 | tf_op jit(solution)/shard_map/ppermute | solution.py:25
  23.1 16.5 %slice-start.3 = ((s8[16777216]{0:T(1024)(128)(4,1)}), s8[4194304]{0:T(1024)(128)(4,1)S(1)}, s32[]{:S(2)}) async-start(s8[16777216]{0:T(1024)(128)(4,1)} %bitcast.5), calls=%async_computation.3 | async-start | bytes 8388608
  23.1 5.1 %collective-permute-start.9 = (bf16[528,128]{1,0:T(8,128)(2,1)S(1)}, bf16[528,128]{1,0:T(8,128)(2,1)S(1)}, u32[]{:S(2)}, u32[]{:S(2)}) collective-permute-start(bf16[528,128]{1,0:T(8,128)(2,1)S(1)} %attend.7), channel_id=1, source_target_pairs={{0,1},{1,0},{2,3},{3,2},{4,5},{5,4},{6,7},{7,6},{8,9},{9,8},{10,11... | collective-permute-start | bytes 405512 | tf_op jit(solution)/shard_map/ppermute | solution.py:25
  28.5 7.0 %collective-permute-start.10 = (bf16[528,128]{1,0:T(8,128)(2,1)S(1)}, bf16[528,128]{1,0:T(8,128)(2,1)S(1)}, u32[]{:S(2)}, u32[]{:S(2)}) collective-permute-start(bf16[528,128]{1,0:T(8,128)(2,1)S(1)} %get-tuple-element.20.own_ref), channel_id=1, source_target_pairs={{0,6},{1,7},{2,4},{3,5},{4,2},{5,3},{6,0},{7,1},{8,14},{9,15},{10,... | collective-permute-start | bytes 405512 | tf_op jit(solution)/shard_map/ppermute | solution.py:25
  36.1 5.0 %collective-permute-start.13 = (bf16[32,2048]{1,0:T(8,128)(2,1)S(1)}, bf16[32,2048]{1,0:T(8,128)(2,1)S(1)}, u32[]{:S(2)}, u32[]{:S(2)}) collective-permute-start(bf16[32,2048]{1,0:T(8,128)(2,1)S(1)} %settle.1.refs_0_), channel_id=1, source_target_pairs={{0,1},{1,0},{2,3},{3,2},{4,5},{5,4},{6,7},{7,6},{8,9},{9,8},{10,11... | collective-permute-start | bytes 393224 | tf_op jit(solution)/shard_map/ppermute | solution.py:25
  37.7 5.0 %collective-permute-start.12 = (bf16[32,2048]{1,0:T(8,128)(2,1)S(1)}, bf16[32,2048]{1,0:T(8,128)(2,1)S(1)}, u32[]{:S(2)}, u32[]{:S(2)}) collective-permute-start(bf16[32,2048]{1,0:T(8,128)(2,1)S(1)} %settle.1.refs_0_), channel_id=1, source_target_pairs={{0,2},{1,3},{2,0},{3,1},{4,6},{5,7},{6,4},{7,5},{8,10},{9,11},{10,... | collective-permute-start | bytes 393224 | tf_op jit(solution)/shard_map/ppermute | solution.py:25
  38.5 5.9 %collective-permute-start.11 = (bf16[32,2048]{1,0:T(8,128)(2,1)S(1)}, bf16[32,2048]{1,0:T(8,128)(2,1)S(1)}, u32[]{:S(2)}, u32[]{:S(2)}) collective-permute-start(bf16[32,2048]{1,0:T(8,128)(2,1)S(1)} %settle.1.refs_0_), channel_id=1, source_target_pairs={{0,3},{1,2},{2,1},{3,0},{4,7},{5,6},{6,5},{7,4},{8,11},{9,10},{10,... | collective-permute-start | bytes 393224 | tf_op jit(solution)/shard_map/ppermute | solution.py:25
  45.2 3.7 %collective-permute-start.14 = (bf16[32,1024]{1,0:T(8,128)(2,1)S(1)}, bf16[32,1024]{1,0:T(8,128)(2,1)S(1)}, u32[]{:S(2)}, u32[]{:S(2)}) collective-permute-start(bf16[32,1024]{1,0:T(8,128)(2,1)S(1)} %project.7), channel_id=1, source_target_pairs={{0,8},{8,16},{16,24},{24,0},{1,9},{9,17},{17,25},{25,1},{2,10},{10... | collective-permute-start | bytes 196616 | tf_op jit(solution)/shard_map/ppermute | solution.py:30
